TPU v7x, 32 devices: a whole 2x2x4 slice. The times are simulated.
32 devices in a mesh: seq: 16 (over z, y, x), fsdp: 2 (over core).
Axes of the slice: x: 2, y: 2, z: 4, core: 2. Of those that a mesh axis runs over, the one named last changes fastest.
Arguments:
- tokens: bfloat16 [4096, 2048], P(('fsdp', 'seq')), may hold values from -6 to 6
- cotangent: bfloat16 [4096, 2048], P(('fsdp', 'seq')), may hold values from -6 to 6
- lengths: int32 [2, 4], P('fsdp'), may hold values from 1 to 2045, as said below
- routes: int32 [4096, 6], P(('fsdp', 'seq')), may hold values from 0 to 15, all different within a row; in each aligned block of 128 rows (0 to 127, 128 to 255, ...) at most 96 rows name the same one
- g_attn: bfloat16 [2048], P('fsdp'), may hold values from 0.5 to 1.5
- w_q: bfloat16 [2048, 3072], P('fsdp')
- w_kva: bfloat16 [2048, 576], P('fsdp'), may hold values from -0.125 to 0.125
- g_kv: bfloat16 [512], P('fsdp'), may hold values from 0.5 to 1.5
- w_kvb: bfloat16 [512, 4096], P('fsdp'), may hold values from -0.25 to 0.25
- w_o: bfloat16 [2048, 2048], P('fsdp'), may hold values from -1 to 1
- g_ffn: bfloat16 [2048], P('fsdp'), may hold values from 0.5 to 1.5
- w_router: bfloat16 [2048, 16], P('fsdp'), may hold values from -0.0625 to 0.0625
- w_shared_in: bfloat16 [2048, 5632], P('fsdp'), may hold values from -0.125 to 0.125
- w_shared_out: bfloat16 [2816, 2048], P('fsdp'), may hold values from -0.109375 to 0.109375
- w_expert_in: bfloat16 [16, 2048, 2816], P('seq', 'fsdp'), may hold values from -0.125 to 0.125
- w_expert_out: bfloat16 [16, 1408, 2048], P('seq', 'fsdp'), may hold values from -1.25 to 1.25
Outputs:
- mixed: bfloat16 [4096, 2048], P(('fsdp', 'seq'))
- grad_tokens: float32 [4096, 2048], P(('fsdp', 'seq'))
- grad_g_attn: float32 [2048], P('fsdp')
- grad_w_q: float32 [2048, 3072], P('fsdp')
- grad_w_kva: float32 [2048, 576], P('fsdp')
- grad_g_kv: float32 [512], P('fsdp')
- grad_w_kvb: float32 [512, 4096], P('fsdp')
- grad_w_o: float32 [2048, 2048], P('fsdp')
- grad_g_ffn: float32 [2048], P('fsdp')
- grad_w_router: float32 [2048, 16], P('fsdp')
- grad_w_shared_in: float32 [2048, 5632], P('fsdp')
- grad_w_shared_out: float32 [2816, 2048], P('fsdp')
- grad_w_expert_in: float32 [16, 2048, 2816], P('seq', 'fsdp')
- grad_w_expert_out: float32 [16, 1408, 2048], P('seq', 'fsdp')
- clipped_w_q: bfloat16 [2048, 3072], P('fsdp')
Inputs may be any that keep to these rules, and one draw needn't show every extreme that they name: Row f holds the lengths of the 4 sequences of group f, which sum to at most 2048. One sequence of each group begins on the group's first device and ends on its last. Some group in every draw is filled with no padding, all its other sequences of length 1. `routes`: the rows of one device (128 aligned rows) name no expert more than 96 times, a bound that some block reaches.
All inputs are finite; a program needn't handle non-finite values.
Results may differ from a plain program's by a relative error of at most 0.025.
Values may be sent and summed in bfloat16 or wider, within the bound.
A program may use at most 384 MiB of HBM per device.

v0:
```python
import jax
import jax.numpy as jnp
from jax import lax
from jax.sharding import PartitionSpec as P

D = 2048
H = 16
DN = 128
DR = 64
DV = 128
KVR = 512
FF = 1408
TOP = 6
SH = 2816


EPSILON = 1e-06
CLIP_LIMIT = 8.0
ROPE_BASE = 10000.0
MASK_VALUE = -1e30


def rms_norm(values, gain_vector):
    return (
        values
        * lax.rsqrt(jnp.mean(values * values, axis=-1, keepdims=True) + EPSILON)
        * gain_vector
    )


def rotate(values, angles):
    half_width = values.shape[-1] // 2
    first_half = values[..., :half_width]
    second_half = values[..., half_width:]
    cosine = jnp.cos(angles)
    sine_part = jnp.sin(angles)
    return jnp.concatenate(
        [
            first_half * cosine - second_half * sine_part,
            second_half * cosine + first_half * sine_part,
        ],
        axis=-1,
    )


def frequencies(count):
    exponent = jnp.arange(count // 2, dtype=jnp.float32) * 2.0 / count
    return ROPE_BASE ** (-exponent)


def layout(lengths_row, slot_ids):
    seq_ends = jnp.cumsum(lengths_row)
    seq_starts = seq_ends - lengths_row
    inside = (slot_ids[:, None] >= seq_starts[None, :]) & (slot_ids[:, None] < seq_ends[None, :])
    is_valid = jnp.any(inside, axis=1)
    numbers = jnp.arange(lengths_row.shape[0], dtype=jnp.int32)
    seq_number = jnp.sum(jnp.where(inside, numbers[None, :], 0), axis=1)
    first_slot = jnp.sum(jnp.where(inside, seq_starts[None, :], 0), axis=1)
    segment = jnp.where(is_valid, seq_number, lengths_row.shape[0] + slot_ids)
    position = jnp.where(is_valid, slot_ids - first_slot, 0)
    return (segment, position, is_valid)


def silu_back(gate_part, up_part, hidden_grad):
    sigmoid_gate = jax.nn.sigmoid(gate_part)
    gate_grad = hidden_grad * up_part * sigmoid_gate * (1.0 + gate_part * (1.0 - sigmoid_gate))
    up_grad = hidden_grad * gate_part * sigmoid_gate
    return jnp.concatenate([gate_grad, up_grad], axis=1)


def expert_weights(weight_in, weight_out):
    return (
        lax.all_gather(weight_in, "fsdp", axis=1, tiled=True),
        lax.all_gather(weight_out, "fsdp", axis=1, tiled=True),
    )


def on_device(
    tokens,
    cotangent,
    lengths,
    routes,
    g_attn,
    w_q,
    w_kva,
    g_kv,
    w_kvb,
    w_o,
    g_ffn,
    w_router,
    w_shared_in,
    w_shared_out,
    w_expert_in,
    w_expert_out,
):
    seq_count = lax.axis_size("seq")
    seq_rank = lax.axis_index("seq")
    tok_count = tokens.shape[0]
    group_size = tok_count * seq_count
    local_heads = H // seq_count
    query_width = DN + DR
    score_scale = query_width ** (-0.5)
    expert_local = w_expert_in.shape[0]
    experts = expert_local * seq_count
    capacity = min(tok_count, 2 * tok_count * TOP // experts)
    gathered = (
        lax.all_gather(g_attn, "fsdp", axis=0, tiled=True),
        lax.all_gather(w_q, "fsdp", axis=0, tiled=True),
        lax.all_gather(w_kva, "fsdp", axis=0, tiled=True),
        lax.all_gather(g_kv, "fsdp", axis=0, tiled=True),
        lax.all_gather(w_kvb, "fsdp", axis=0, tiled=True),
        lax.all_gather(w_o, "fsdp", axis=0, tiled=True),
        lax.all_gather(g_ffn, "fsdp", axis=0, tiled=True),
        lax.all_gather(w_router, "fsdp", axis=0, tiled=True),
        lax.all_gather(w_shared_in, "fsdp", axis=0, tiled=True),
        lax.all_gather(w_shared_out, "fsdp", axis=0, tiled=True),
    )
    gain_attn = gathered[0].astype(jnp.float32)
    query_weight = gathered[1]
    latent_weight = gathered[2]
    gain_latent = gathered[3].astype(jnp.float32)
    expand_weight = gathered[4]
    output_weight = gathered[5]
    gain_ffn = gathered[6].astype(jnp.float32)
    router_weight = gathered[7]
    shared_in = gathered[8]
    shared_out = gathered[9]
    slot_ids = jnp.arange(group_size, dtype=jnp.int32)
    segment, position_all, valid_all = layout(lengths[0], slot_ids)
    offset = seq_rank * tok_count
    position = lax.dynamic_slice_in_dim(position_all, offset, tok_count, 0)
    valid_rows = lax.dynamic_slice_in_dim(valid_all, offset, tok_count, 0)
    angles = position[:, None].astype(jnp.float32) * frequencies(DR)[None, :]
    inputs = tokens.astype(jnp.float32)
    normed_low = rms_norm(inputs, gain_attn).astype(jnp.bfloat16)
    query_pre = jnp.dot(normed_low, query_weight, preferred_element_type=jnp.float32).reshape(
        tok_count, H, query_width
    )
    latent_full = jnp.dot(normed_low, latent_weight, preferred_element_type=jnp.float32)
    latent_low = rms_norm(latent_full[:, :KVR], gain_latent).astype(jnp.bfloat16)
    expanded = jnp.dot(latent_low, expand_weight, preferred_element_type=jnp.float32).reshape(
        tok_count, H, DN + DV
    )
    query_low = jnp.concatenate(
        [query_pre[..., :DN], rotate(query_pre[..., DN:], angles[:, None, :])], axis=-1
    ).astype(jnp.bfloat16)
    key_rope = rotate(latent_full[:, KVR:], angles)
    key_low = jnp.concatenate(
        [expanded[..., :DN], jnp.broadcast_to(key_rope[:, None, :], (tok_count, H, DR))], axis=-1
    ).astype(jnp.bfloat16)
    value_low = expanded[..., DN:].astype(jnp.bfloat16)
    head_query, head_key, head_value = (
        lax.all_to_all(
            query_low.reshape(tok_count, H * query_width),
            "seq",
            split_axis=1,
            concat_axis=0,
            tiled=True,
        ),
        lax.all_to_all(
            key_low.reshape(tok_count, H * query_width),
            "seq",
            split_axis=1,
            concat_axis=0,
            tiled=True,
        ),
        lax.all_to_all(
            value_low.reshape(tok_count, H * DV), "seq", split_axis=1, concat_axis=0, tiled=True
        ),
    )
    head_query = head_query.reshape(group_size, local_heads, query_width)
    head_key = head_key.reshape(group_size, local_heads, query_width)
    head_value = head_value.reshape(group_size, local_heads, DV)
    block_rows = 512
    starts = jnp.arange(group_size // block_rows, dtype=jnp.int32) * block_rows

    def block_scores(first_row):
        row_query = lax.dynamic_slice_in_dim(head_query, first_row, block_rows, 0)
        scores = (
            jnp.einsum("qhd,khd->hqk", row_query, head_key, preferred_element_type=jnp.float32)
            * score_scale
        )
        row_slots = first_row + jnp.arange(block_rows, dtype=jnp.int32)
        row_segment = lax.dynamic_slice_in_dim(segment, first_row, block_rows, 0)
        allowed = (row_segment[:, None] == segment[None, :]) & (
            slot_ids[None, :] <= row_slots[:, None]
        )
        return (row_query, scores, allowed)

    def forward_block(first_row):
        row_query, scores, allowed = block_scores(first_row)
        masked = jnp.where(allowed[None], scores, MASK_VALUE)
        row_max = jnp.max(masked, axis=-1, keepdims=True)
        exponent = jnp.exp(masked - row_max)
        row_sum = jnp.sum(exponent, axis=-1, keepdims=True)
        probs_low = (exponent / row_sum).astype(jnp.bfloat16)
        context = jnp.einsum(
            "hqk,khd->qhd", probs_low, head_value, preferred_element_type=jnp.float32
        )
        row_valid = lax.dynamic_slice_in_dim(valid_all, first_row, block_rows, 0)
        largest = jnp.max(
            jnp.where((allowed & row_valid[:, None])[None], scores, MASK_VALUE), axis=(1, 2)
        )
        return (context, (row_max + jnp.log(row_sum))[..., 0], largest)

    context, log_total, largest = lax.map(forward_block, starts)
    context = context.reshape(group_size, local_heads * DV).astype(jnp.bfloat16)
    attn_low = lax.all_to_all(context, "seq", split_axis=0, concat_axis=1, tiled=True)
    head_largest = jnp.max(largest, axis=0)
    spread_max = lax.dynamic_update_slice(
        jnp.full((H,), MASK_VALUE, jnp.float32), head_largest, (seq_rank * local_heads,)
    )
    global_max = lax.pmax(spread_max, ("seq", "fsdp"))
    attended = jnp.dot(attn_low, output_weight, preferred_element_type=jnp.float32)
    middle = inputs + attended
    ffn_low = rms_norm(middle, gain_ffn).astype(jnp.bfloat16)
    logits = jnp.dot(ffn_low, router_weight, preferred_element_type=jnp.float32)
    router_probs = jax.nn.softmax(logits, axis=-1)
    gate_values = jnp.take_along_axis(router_probs, routes, axis=1)
    shared_both = jnp.dot(ffn_low, shared_in, preferred_element_type=jnp.float32)
    shared_hidden = (jax.nn.silu(shared_both[:, :SH]) * shared_both[:, SH:]).astype(jnp.bfloat16)
    shared_result = jnp.dot(shared_hidden, shared_out, preferred_element_type=jnp.float32)
    flat_routes = routes.reshape(-1)
    expert_ids = jnp.arange(experts, dtype=jnp.int32)
    onehot = (flat_routes[:, None] == expert_ids[None, :]).astype(jnp.int32)
    slot_index = jnp.sum((jnp.cumsum(onehot, axis=0) - 1) * onehot, axis=1)
    send_rows = (
        jnp.zeros((experts, capacity, D), jnp.bfloat16)
        .at[flat_routes, slot_index]
        .set(jnp.repeat(ffn_low, TOP, axis=0))
    )
    arrived = lax.all_to_all(send_rows, "seq", split_axis=0, concat_axis=1, tiled=True)
    expert_in, expert_out = expert_weights(w_expert_in, w_expert_out)
    expert_index = 0
    gate_up = jnp.dot(
        arrived[expert_index], expert_in[expert_index], preferred_element_type=jnp.float32
    )
    hidden = (jax.nn.silu(gate_up[:, :FF]) * gate_up[:, FF:]).astype(jnp.bfloat16)
    kept_gate_up = [gate_up]
    kept_hidden = [hidden]
    results = [
        jnp.dot(hidden, expert_out[expert_index], preferred_element_type=jnp.float32).astype(
            jnp.bfloat16
        )
    ]
    returned = lax.all_to_all(jnp.stack(results), "seq", split_axis=1, concat_axis=0, tiled=True)
    picked = returned[flat_routes, slot_index].reshape(tok_count, TOP, D).astype(jnp.float32)
    routed = jnp.sum(gate_values[:, :, None] * picked, axis=1)
    mixed = (middle + shared_result + routed).astype(jnp.bfloat16)
    upstream = cotangent.astype(jnp.float32) * valid_rows[:, None].astype(jnp.float32)
    upstream_low = upstream.astype(jnp.bfloat16)
    gate_grads = jnp.sum(upstream[:, None, :] * picked, axis=2)
    result_grads = (
        (gate_values[:, :, None] * upstream[:, None, :])
        .reshape(tok_count * TOP, D)
        .astype(jnp.bfloat16)
    )
    grad_send = (
        jnp.zeros((experts, capacity, D), jnp.bfloat16)
        .at[flat_routes, slot_index]
        .set(result_grads)
    )
    grad_arrived = lax.all_to_all(grad_send, "seq", split_axis=0, concat_axis=1, tiled=True)
    expert_in, expert_out = expert_weights(w_expert_in, w_expert_out)
    expert_index = 0
    d_hidden = jnp.dot(
        grad_arrived[expert_index], expert_out[expert_index].T, preferred_element_type=jnp.float32
    )
    grads_out = [
        jnp.dot(
            kept_hidden[expert_index].T,
            grad_arrived[expert_index],
            preferred_element_type=jnp.float32,
        )
    ]
    gate_up = kept_gate_up[expert_index]
    d_gate_up = silu_back(gate_up[:, :FF], gate_up[:, FF:], d_hidden).astype(jnp.bfloat16)
    grads_in = [jnp.dot(arrived[expert_index].T, d_gate_up, preferred_element_type=jnp.float32)]
    row_grads = [
        jnp.dot(d_gate_up, expert_in[expert_index].T, preferred_element_type=jnp.float32).astype(
            jnp.bfloat16
        )
    ]
    grad_returned = lax.all_to_all(
        jnp.stack(row_grads), "seq", split_axis=1, concat_axis=0, tiled=True
    )
    ffn_grad = jnp.sum(
        grad_returned[flat_routes, slot_index].reshape(tok_count, TOP, D).astype(jnp.float32),
        axis=1,
    )
    route_match = (routes[:, :, None] == expert_ids[None, None, :]).astype(jnp.float32)
    prob_grads = jnp.sum(route_match * gate_grads[:, :, None], axis=1)
    logit_grads = (
        router_probs * (prob_grads - jnp.sum(router_probs * prob_grads, axis=-1, keepdims=True))
    ).astype(jnp.bfloat16)
    grad_router = jnp.dot(ffn_low.T, logit_grads, preferred_element_type=jnp.float32)
    ffn_grad = ffn_grad + jnp.dot(logit_grads, router_weight.T, preferred_element_type=jnp.float32)
    shared_hidden_grad = jnp.dot(upstream_low, shared_out.T, preferred_element_type=jnp.float32)
    grad_shared_out = jnp.dot(shared_hidden.T, upstream_low, preferred_element_type=jnp.float32)
    shared_both_grad = silu_back(
        shared_both[:, :SH], shared_both[:, SH:], shared_hidden_grad
    ).astype(jnp.bfloat16)
    grad_shared_in = jnp.dot(ffn_low.T, shared_both_grad, preferred_element_type=jnp.float32)
    ffn_grad = ffn_grad + jnp.dot(shared_both_grad, shared_in.T, preferred_element_type=jnp.float32)
    ffn_pull = jax.vjp(rms_norm, middle, gain_ffn)[1]
    middle_norm_grad, grad_gain_ffn = ffn_pull(ffn_grad)
    middle_grad = upstream + middle_norm_grad
    middle_low = middle_grad.astype(jnp.bfloat16)
    grad_output = jnp.dot(attn_low.T, middle_low, preferred_element_type=jnp.float32)
    context_grad = jnp.dot(middle_low, output_weight.T, preferred_element_type=jnp.float32).astype(
        jnp.bfloat16
    )
    head_grad = lax.all_to_all(
        context_grad, "seq", split_axis=1, concat_axis=0, tiled=True
    ).reshape(group_size, local_heads, DV)

    def backward_block(sums, operands):
        first_row, row_log = operands
        row_query, scores, allowed = block_scores(first_row)
        probs = jnp.exp(jnp.where(allowed[None], scores, MASK_VALUE) - row_log[..., None])
        probs_low = probs.astype(jnp.bfloat16)
        row_grad = lax.dynamic_slice_in_dim(head_grad, first_row, block_rows, 0)
        prob_grad = jnp.einsum(
            "qhd,khd->hqk", row_grad, head_value, preferred_element_type=jnp.float32
        )
        score_grad = (
            probs * (prob_grad - jnp.sum(probs * prob_grad, axis=-1, keepdims=True))
        ).astype(jnp.bfloat16)
        query_grad = (
            jnp.einsum("hqk,khd->qhd", score_grad, head_key, preferred_element_type=jnp.float32)
            * score_scale
        )
        key_sum = (
            sums[0]
            + jnp.einsum("hqk,qhd->khd", score_grad, row_query, preferred_element_type=jnp.float32)
            * score_scale
        )
        value_sum = sums[1] + jnp.einsum(
            "hqk,qhd->khd", probs_low, row_grad, preferred_element_type=jnp.float32
        )
        return ((key_sum, value_sum), query_grad)

    zero_sums = (
        jnp.zeros((group_size, local_heads, query_width), jnp.float32),
        jnp.zeros((group_size, local_heads, DV), jnp.float32),
    )
    (key_grad, value_grad), query_grad = lax.scan(backward_block, zero_sums, (starts, log_total))
    back_query, back_key, back_value = (
        lax.all_to_all(
            query_grad.reshape(group_size, local_heads * query_width).astype(jnp.bfloat16),
            "seq",
            split_axis=0,
            concat_axis=1,
            tiled=True,
        ),
        lax.all_to_all(
            key_grad.reshape(group_size, local_heads * query_width).astype(jnp.bfloat16),
            "seq",
            split_axis=0,
            concat_axis=1,
            tiled=True,
        ),
        lax.all_to_all(
            value_grad.reshape(group_size, local_heads * DV).astype(jnp.bfloat16),
            "seq",
            split_axis=0,
            concat_axis=1,
            tiled=True,
        ),
    )
    back_query = back_query.reshape(tok_count, H, query_width).astype(jnp.float32)
    pre_grad = jnp.concatenate(
        [back_query[..., :DN], rotate(back_query[..., DN:], -angles[:, None, :])], axis=-1
    )
    pre_grad = pre_grad.reshape(tok_count, H * query_width).astype(jnp.bfloat16)
    grad_query = jnp.dot(normed_low.T, pre_grad, preferred_element_type=jnp.float32)
    normed_grad = jnp.dot(pre_grad, query_weight.T, preferred_element_type=jnp.float32)
    back_key = back_key.reshape(tok_count, H, query_width)
    expand_grad = jnp.concatenate(
        [back_key[..., :DN], back_value.reshape(tok_count, H, DV)], axis=-1
    ).reshape(tok_count, H * (DN + DV))
    grad_expand = jnp.dot(latent_low.T, expand_grad, preferred_element_type=jnp.float32)
    latent_grad = jnp.dot(expand_grad, expand_weight.T, preferred_element_type=jnp.float32)
    rope_grad = rotate(jnp.sum(back_key[..., DN:].astype(jnp.float32), axis=1), -angles)
    latent_pull = jax.vjp(rms_norm, latent_full[:, :KVR], gain_latent)[1]
    compressed_grad, grad_gain_latent = latent_pull(latent_grad)
    full_grad = jnp.concatenate([compressed_grad, rope_grad], axis=1).astype(jnp.bfloat16)
    grad_latent = jnp.dot(normed_low.T, full_grad, preferred_element_type=jnp.float32)
    normed_grad = normed_grad + jnp.dot(
        full_grad, latent_weight.T, preferred_element_type=jnp.float32
    )
    input_pull = jax.vjp(rms_norm, inputs, gain_attn)[1]
    input_norm_grad, grad_gain_attn = input_pull(normed_grad)
    grad_inputs = middle_grad + input_norm_grad
    dense_sums = (
        lax.psum_scatter(
            grad_gain_attn.astype(jnp.bfloat16), "fsdp", scatter_dimension=0, tiled=True
        ).astype(jnp.float32),
        lax.psum_scatter(
            grad_query.astype(jnp.bfloat16), "fsdp", scatter_dimension=0, tiled=True
        ).astype(jnp.float32),
        lax.psum_scatter(
            grad_latent.astype(jnp.bfloat16), "fsdp", scatter_dimension=0, tiled=True
        ).astype(jnp.float32),
        lax.psum_scatter(
            grad_gain_latent.astype(jnp.bfloat16), "fsdp", scatter_dimension=0, tiled=True
        ).astype(jnp.float32),
        lax.psum_scatter(
            grad_expand.astype(jnp.bfloat16), "fsdp", scatter_dimension=0, tiled=True
        ).astype(jnp.float32),
        lax.psum_scatter(
            grad_output.astype(jnp.bfloat16), "fsdp", scatter_dimension=0, tiled=True
        ).astype(jnp.float32),
        lax.psum_scatter(
            grad_gain_ffn.astype(jnp.bfloat16), "fsdp", scatter_dimension=0, tiled=True
        ).astype(jnp.float32),
        lax.psum_scatter(
            grad_router.astype(jnp.bfloat16), "fsdp", scatter_dimension=0, tiled=True
        ).astype(jnp.float32),
        lax.psum_scatter(
            grad_shared_in.astype(jnp.bfloat16), "fsdp", scatter_dimension=0, tiled=True
        ).astype(jnp.float32),
        lax.psum_scatter(
            grad_shared_out.astype(jnp.bfloat16), "fsdp", scatter_dimension=0, tiled=True
        ).astype(jnp.float32),
    )
    dense_sums = (
        lax.psum(dense_sums[0].astype(jnp.bfloat16), "seq").astype(jnp.float32),
        lax.psum(dense_sums[1].astype(jnp.bfloat16), "seq").astype(jnp.float32),
        lax.psum(dense_sums[2].astype(jnp.bfloat16), "seq").astype(jnp.float32),
        lax.psum(dense_sums[3].astype(jnp.bfloat16), "seq").astype(jnp.float32),
        lax.psum(dense_sums[4].astype(jnp.bfloat16), "seq").astype(jnp.float32),
        lax.psum(dense_sums[5].astype(jnp.bfloat16), "seq").astype(jnp.float32),
        lax.psum(dense_sums[6].astype(jnp.bfloat16), "seq").astype(jnp.float32),
        lax.psum(dense_sums[7].astype(jnp.bfloat16), "seq").astype(jnp.float32),
        lax.psum(dense_sums[8].astype(jnp.bfloat16), "seq").astype(jnp.float32),
        lax.psum(dense_sums[9].astype(jnp.bfloat16), "seq").astype(jnp.float32),
    )
    expert_sums = (
        lax.psum_scatter(
            jnp.stack(grads_in).astype(jnp.bfloat16), "fsdp", scatter_dimension=1, tiled=True
        ).astype(jnp.float32),
        lax.psum_scatter(
            jnp.stack(grads_out).astype(jnp.bfloat16), "fsdp", scatter_dimension=1, tiled=True
        ).astype(jnp.float32),
    )
    clip_gamma = CLIP_LIMIT / jnp.maximum(global_max, CLIP_LIMIT)
    clip_root = jnp.sqrt(clip_gamma)
    query_factor = jnp.concatenate(
        [
            jnp.broadcast_to(clip_root[:, None], (H, DN)),
            jnp.broadcast_to(clip_gamma[:, None], (H, DR)),
        ],
        axis=1,
    ).reshape(1, -1)
    clipped_query = (w_q.astype(jnp.float32) * query_factor).astype(jnp.bfloat16)
    return (
        mixed,
        grad_inputs,
        dense_sums[0],
        dense_sums[1],
        dense_sums[2],
        dense_sums[3],
        dense_sums[4],
        dense_sums[5],
        dense_sums[6],
        dense_sums[7],
        dense_sums[8],
        dense_sums[9],
        expert_sums[0],
        expert_sums[1],
        clipped_query,
    )


def solution(mesh):
    in_specs = (
        P(("fsdp", "seq"), None),
        P(("fsdp", "seq"), None),
        P("fsdp", None),
        P(("fsdp", "seq"), None),
        P("fsdp"),
        P("fsdp", None),
        P("fsdp", None),
        P("fsdp"),
        P("fsdp", None),
        P("fsdp", None),
        P("fsdp"),
        P("fsdp", None),
        P("fsdp", None),
        P("fsdp", None),
        P("seq", "fsdp", None),
        P("seq", "fsdp", None),
    )
    out_specs = (
        P(("fsdp", "seq"), None),
        P(("fsdp", "seq"), None),
        P("fsdp"),
        P("fsdp", None),
        P("fsdp", None),
        P("fsdp"),
        P("fsdp", None),
        P("fsdp", None),
        P("fsdp"),
        P("fsdp", None),
        P("fsdp", None),
        P("fsdp", None),
        P("seq", "fsdp", None),
        P("seq", "fsdp", None),
        P("fsdp", None),
    )
    return jax.shard_map(
        on_device, mesh=mesh, in_specs=in_specs, out_specs=out_specs, check_vma=False
    )
```

profile of v0, /device:TPU:0, one launch (start us, length us, event | category | flops | bytes accessed | tf_op | source)
XLA Modules:
  0.0 2346.7 jit_solution(5809181595819549959)
XLA Ops:
  14.5 8.8 all-gather.12.cloned.1.call-done
  26.1 13.6 all-gather.14.cloned.1.call-done
  51.6 15.7 all-gather.10.cloned.1.call-done
  84.3 19.2 all-to-all-done
  112.7 10.2 all-to-all-done.2
  122.9 57.2 %while.30 = (s32[]{:T(128)}, bf16[4,512,1,128]{3,1,2,0:T(8,128)(2,1)}, f32[4,1,512]{2,1,0:T(1,128)}, f32[4,1]{0,1:T(1,128)S(1)}, s32[4]{0:T(128)S(1)}, /*index=5...) while((s32[]{:T(128)}, ...), condition=%wide.region_10.11_spmd.clone, body=%wide.region_6.10_spmd.clone.sunk | while | flops 696254464 | bytes 14417627 | solution.py:206
  189.2 9.3 all-to-all-done.3
  217.5 137.3 %scatter_fusion = bf16[16,96,2048]{2,1,0:T(8,128)(2,1)} fusion(bf16[16,96,2048]{2,1,0:T(8,128)(2,1)} %broadcast.307.clone, s32[768]{0:T(1024)S(1)} %get-tuple-element.215, bf16[768,2048]{1,0:T(8,128)(2,1)} %reshape.560), kind=kCustom, calls=%fused_computation.3 | custom fusion | bytes 9443328 | tf_op jit(solution)/shard_map/scatter | solution.py:230
  365.8 8.6 mul.491
  390.9 132.4 %scatter_fusion.1 = bf16[16,96,2048]{2,1,0:T(8,128)(2,1)} fusion(bf16[16,96,2048]{2,1,0:T(8,128)(2,1)} %broadcast.307.clone.1, s32[768]{0:T(1024)S(1)} %get-tuple-element.215, bf16[768,2048]{1,0:T(8,128)(2,1)S(1)} %multiply_convert_fusion.5), kind=kCustom, calls=%fused_computation.4 | custom fusion | bytes 9443328 | tf_op jit(solution)/shard_map/scatter | solution.py:261
  531.0 26.9 %fusion.41 = f32[1536,2816]{1,0:T(8,128)} fusion(bf16[1536,2048]{1,0:T(8,128)(2,1)} %bitcast.16, bf16[1,2048,2816]{2,1,0:T(8,128)(2,1)} %all-gather.22.cloned.1.call-done), kind=kOutput, calls=%fused_computation.63 | convolution fusion | flops 17716740096 | bytes 35127296 | tf_op jit(solution)/shard_map/dot_general | solution.py:235
  557.9 92.3 %all-to-all-done.6 = bf16[16,96,2048]{2,1,0:T(8,128)(2,1)} async-done(((bf16[16,96,2048]{2,1,0:T(8,128)(2,1)}), bf16[16,96,2048]{2,1,0:T(8,128)(2,1)}, u32[]{:S(2)}, u32[]{:S(2)}) %all-to-all-start.6) | async-done | bytes 6291488 | tf_op jit(solution)/shard_map/all_to_all | solution.py:263
  650.2 23.0 multiply_convert_fusion.3
  673.3 13.5 fusion.46
  686.8 36.5 %copy.253 = bf16[1,1536,2048]{2,0,1:T(2,128)(2,1)} copy(bf16[1,1536,2048]{2,1,0:T(8,128)(2,1)S(1)} %fusion.46) | data formatting | bytes 12582912 | tf_op jit(solution)/shard_map/stack | solution.py:246
  723.8 39.0 %reduce.19 = bf16[1536,2048]{1,0:T(8,128)(2,1)} reduce(bf16[1536,1,2048]{2,1,0:T(2,128)(2,1)} %bitcast.264, bf16[]{:T(256)} %broadcast.516), dimensions={1}, to_apply=%bitcast.214.reduce_sub_computation | reduce | bytes 12582914
  762.7 12.9 reshape.592
  775.7 29.3 %all-to-all-start.5 = ((bf16[16,2,98304]{2,1,0:T(2,128)(2,1)}), bf16[16,2,98304]{2,1,0:T(2,128)(2,1)}, u32[]{:S(2)}, u32[]{:S(2)}) async-start(bf16[16,2,98304]{2,1,0:T(2,128)(2,1)} %reshape.592), calls=%async_computation.5 | async-start | bytes 12582912 | tf_op jit(solution)/shard_map/all_to_all | solution.py:246
  805.7 24.0 %fusion.48 = bf16[1,1536,2048]{2,1,0:T(8,128)(2,1)S(1)} fusion(bf16[1,2048,2816]{2,1,0:T(8,128)(2,1)} %all-gather.22.cloned.1.call-done, bf16[1536,1408]{1,0:T(8,128)(2,1)} %get-tuple-element.280, bf16[1536,1408]{1,0:T(8,128)(2,1)} %get-tuple-element.279), kind=kOutput, calls=%fused_computation.81 | convolution fusion | flops 17737187328 | bytes 26476544 | tf_op jit(solution)/shard_map/dot_general | solution.py:280
  829.8 36.5 %copy.252 = bf16[1,1536,2048]{2,0,1:T(2,128)(2,1)} copy(bf16[1,1536,2048]{2,1,0:T(8,128)(2,1)S(1)} %fusion.48) | data formatting | bytes 12582912 | tf_op jit(solution)/shard_map/stack | solution.py:285
  866.2 39.0 %reduce.20 = bf16[1536,2048]{1,0:T(8,128)(2,1)} reduce(bf16[1536,1,2048]{2,1,0:T(2,128)(2,1)} %bitcast.265, bf16[]{:T(256)} %broadcast.516), dimensions={1}, to_apply=%bitcast.213.reduce_sub_computation | reduce | bytes 12582914
  905.2 12.9 reshape.594
  921.4 28.9 %all-to-all-start.7 = ((bf16[16,2,98304]{2,1,0:T(2,128)(2,1)}), bf16[16,2,98304]{2,1,0:T(2,128)(2,1)}, u32[]{:S(2)}, u32[]{:S(2)}) async-start(bf16[16,2,98304]{2,1,0:T(2,128)(2,1)} %reshape.594), calls=%async_computation.7 | async-start | bytes 12582912 | tf_op jit(solution)/shard_map/all_to_all | solution.py:284
  950.4 12.4 fusion.106
  962.8 10.2 multiply_convert_fusion.7
  974.0 12.9 fusion.66
  986.9 14.5 reshape.593
  1001.4 11.3 copy.239
  1012.7 12.0 gather_fusion
  1035.9 30.3 %all-to-all-done.7 = bf16[16,2,98304]{2,1,0:T(2,128)(2,1)} async-done(((bf16[16,2,98304]{2,1,0:T(2,128)(2,1)}), bf16[16,2,98304]{2,1,0:T(2,128)(2,1)}, u32[]{:S(2)}, u32[]{:S(2)}) %all-to-all-start.7) | async-done | bytes 6291488 | tf_op jit(solution)/shard_map/all_to_all | solution.py:284
  1066.2 14.7 reshape.595
  1080.9 11.3 copy.240
  1092.2 12.0 gather_fusion.1
  1123.8 28.6 %all-to-all-start.8 = ((bf16[128,16,128]{2,0,1:T(8,128)(2,1)}), bf16[128,16,128]{2,0,1:T(8,128)(2,1)}, u32[]{:S(2)}, u32[]{:S(2)}) async-start(bf16[128,16,128]{2,0,1:T(8,128)(2,1)} %bitcast.212), calls=%async_computation.8 | async-start | bytes 1048576 | tf_op jit(solution)/shard_map/all_to_all | solution.py:313
  1152.4 14.4 all-to-all-done.8
  1166.8 75.9 %while.31 = (s32[]{:T(128)}, f32[2048,1,192]{0,2,1:T(8,128)}, f32[2048,1,128]{0,2,1:T(8,128)S(1)}, bf16[4,512,1,192]{1,3,2,0:T(8,128)(2,1)}, s32[4]{0:T(128)S(1)...) while((s32[]{:T(128)}, f32[2048,1,192]{0,2,1:T(8,128)}, ...), condition=%wide.region_27.28_spmd.clone, body=%wide.region_25.27_spmd.clone.sunk | while | flops 1759215616 | bytes 79720784 | solution.py:347
  1250.8 17.6 all-to-all-done.10
  1274.4 12.9 all-to-all-done.11
  1314.3 23.5 %all_to_all.149 = bf16[16,128,192]{1,2,0:T(8,128)(2,1)S(1)} all-to-all(bf16[16,128,192]{1,2,0:T(8,128)(2,1)S(1)} %copy.230), channel_id=1, replica_groups=mesh['seq'=16,'fsdp'=2] {'seq'}, dimensions={0} | all-to-all | bytes 1572864 | tf_op jit(solution)/shard_map/all_to_all | solution.py:349
  1346.0 15.2 convolution_convert_fusion
  1361.4 14.9 fusion.47
  1377.9 27.3 %convert_bitcast_fusion = bf16[1,2048,2816]{2,1,0:T(8,128)(2,1)} fusion(bf16[1536,2048]{1,0:T(8,128)(2,1)} %bitcast.16, bf16[1536,1408]{1,0:T(8,128)(2,1)} %get-tuple-element.280, bf16[1536,1408]{1,0:T(8,128)(2,1)} %get-tuple-element.279), kind=kOutput, calls=%fused_computation.65 | convolution fusion | flops 17739808768 | bytes 26476544 | tf_op jit(solution)/shard_map/dot_general | solution.py:278
  1405.3 22.1 reduce-scatter.29.cloned.1.call-done
  1431.3 40.8 %pmax.7 = f32[16]{0:T(128)S(1)} all-reduce(f32[16]{0:T(128)S(1)} %dynamic_update_slice.19), channel_id=1, replica_groups=mesh['seq'=16,'fsdp'=2] {'seq','fsdp'}, use_global_device_ids=true, to_apply=%region_57.58 | all-reduce | flops 16 | bytes 128 | tf_op jit(solution)/shard_map/pmax | solution.py:213
  1472.4 8.7 multiply_convert_fusion.1
  1503.7 80.8 %all-reduce.4 = (bf16[1024]{0:T(1024)(128)(2,1)S(1)}, bf16[256]{0:T(256)(128)(2,1)S(1)}, bf16[1024]{0:T(1024)(128)(2,1)S(1)}, bf16[1024,16]{0,1:T(8,128)(2,1)S(1)}) all-reduce(bf16[1024]{0:T(1024)(128)(2,1)S(1)} %dynamic-slice.1, bf16[256]{0:T(256)(128)(2,1)S(1)} %dynamic-slice.3, ...), channel_id=1, replica_groups=mesh['seq'=16,'fsdp'=2] {'seq'}, use_global_device_ids=true, to_apply=%region_33.34 | all-reduce | flops 18688 | bytes 74752 | tf_op jit(solution)/shard_map/psum | solution.py:428
  1597.4 707.6 %all-reduce.9.cloned.1.call-done = (bf16[1024,3072]{1,0:T(8,128)(2,1)}, bf16[1024,576]{0,1:T(8,128)(2,1)}, bf16[256,4096]{1,0:T(8,128)(2,1)}, bf16[1024,2048]{1,...) async-done(((bf16[1024,3072]{1,0:T(8,128)(2,1)}, bf16[1024,576]{0,1:T(8,128)(2,1)}, bf16[256,4096]{1,0:T(8,128)(2,1)}, ...) | async-done | bytes 31064080 | tf_op jit(solution)/shard_map/psum | solution.py:429
  2305.0 9.4 convert_element_type.291
  (518 shorter events, 378.3 us)
Async XLA Ops:
  7.2 16.1 all-gather.12.cloned.1.call-start
  7.9 31.8 %all-gather.14.cloned.1.call-start = ((), (), s32[]{:S(2)}) async-start(), calls=%async_computation.23 | async-start | bytes 6291456 | tf_op jit(solution)/shard_map/all_gather | solution.py:111
  8.7 58.6 %all-gather.10.cloned.1.call-start = ((), (), s32[]{:S(2)}) async-start(), calls=%async_computation.21 | async-start | bytes 18874368 | tf_op jit(solution)/shard_map/all_gather | solution.py:108
  9.4 189.4 %all-gather.16.cloned.1.call-start = ((), (), s32[]{:S(2)}) async-start(), calls=%async_computation.24 | async-start | bytes 12582912 | tf_op jit(solution)/shard_map/all_gather | solution.py:112
  12.0 55.4 %copy-start.35 = (f32[2048]{0:T(1024)}, f32[2048]{0:T(1024)S(1)}, u32[]{:S(2)}) copy-start(f32[2048]{0:T(1024)S(1)} %convert_element_type.252) | copy-start | bytes 24580
  13.9 28.8 %copy-start.47 = (f32[2,1,256]{2,1,0:T(1,128)}, f32[2,1,256]{2,1,0:T(1,128)S(1)}, u32[]{:S(2)}) copy-start(f32[2,1,256]{2,1,0:T(1,128)S(1)} %convert_element_type.318) | copy-start | bytes 6148
  13.9 37.5 %copy-start.76 = (f32[32]{0:T(128)}, f32[32]{0:T(128)S(1)}, u32[]{:S(2)}) copy-start(f32[32]{0:T(128)S(1)} %negate_power_fusion) | copy-start | bytes 388
  14.3 37.2 %copy-start.68 = (f32[128]{0:T(128)}, f32[128]{0:T(128)S(1)}, u32[]{:S(2)}) copy-start(f32[128]{0:T(128)S(1)} %fusion.85) | copy-start | bytes 1540
  14.5 52.9 %copy-start.58 = (f32[128]{0:T(128)}, f32[128]{0:T(128)S(1)}, u32[]{:S(2)}) copy-start(f32[128]{0:T(128)S(1)} %fusion.86) | copy-start | bytes 1540
  44.7 31.9 %all-to-all-start.1 = ((bf16[128,16,192]{0,2,1:T(8,128)(2,1)}), bf16[128,16,192]{0,2,1:T(8,128)(2,1)S(1)}, u32[]{:S(2)}, u32[]{:S(2)}) async-start(bf16[128,16,192]{0,2,1:T(8,128)(2,1)} %pad_maximum_fusion.8), calls=%async_computation.1 | async-start | bytes 1572864 | tf_op jit(solution)/shard_map/all_to_all | solution.py:160
  76.6 26.9 %all-to-all-start = ((bf16[128,16,192]{0,2,1:T(8,128)(2,1)}), bf16[128,16,192]{0,2,1:T(8,128)(2,1)S(1)}, u32[]{:S(2)}, u32[]{:S(2)}) async-start(bf16[128,16,192]{0,2,1:T(8,128)(2,1)} %pad_maximum_fusion.7), calls=%async_computation | async-start | bytes 1572864 | tf_op jit(solution)/shard_map/all_to_all | solution.py:153
  103.5 19.4 all-to-all-start.2
  108.6 422.4 %all-gather.22.cloned.1.call-start = ((), (), s32[]{:S(2)}) async-start(), calls=%async_computation.27 | async-start | bytes 17301504 | tf_op jit(solution)/shard_map/all_gather | solution.py:73
  122.8 61.3 %copy-start.51 = (s32[128,6]{0,1:T(8,128)S(1)}, s32[128,6]{0,1:T(8,128)}, u32[]{:S(2)}) copy-start(s32[128,6]{0,1:T(8,128)} %param.23) | copy-start | bytes 9220
  122.9 63.9 %copy-start.79 = (bf16[1024]{0:T(1024)(128)(2,1)S(1)}, bf16[1024]{0:T(1024)(128)(2,1)}, u32[]{:S(2)}) copy-start(bf16[1024]{0:T(1024)(128)(2,1)} %param.30) | copy-start | bytes 6148
  180.1 18.4 all-to-all-start.3
  204.9 171.7 %copy-start.8 = (bf16[128,2048]{1,0:T(8,128)(2,1)}, bf16[128,2048]{1,0:T(8,128)(2,1)S(1)}, u32[]{:S(2)}) copy-start(bf16[128,2048]{1,0:T(8,128)(2,1)S(1)} %multiply_convert_fusion.9) | copy-start | bytes 1572868
  354.8 168.5 %all-to-all-start.4 = ((bf16[16,96,2048]{2,1,0:T(8,128)(2,1)}), bf16[16,96,2048]{2,1,0:T(8,128)(2,1)}, u32[]{:S(2)}, u32[]{:S(2)}) async-start(bf16[16,96,2048]{2,1,0:T(8,128)(2,1)} %scatter_fusion), calls=%async_computation.4 | async-start | bytes 12582912 | tf_op jit(solution)/shard_map/all_to_all | solution.py:232
  359.6 198.3 %all-gather.24.cloned.1.call-start = ((), (), s32[]{:S(2)}) async-start(), calls=%async_computation.28 | async-start | bytes 8650752 | tf_op jit(solution)/shard_map/all_gather | solution.py:74
  523.3 126.9 %all-to-all-start.6 = ((bf16[16,96,2048]{2,1,0:T(8,128)(2,1)}), bf16[16,96,2048]{2,1,0:T(8,128)(2,1)}, u32[]{:S(2)}, u32[]{:S(2)}) async-start(bf16[16,96,2048]{2,1,0:T(8,128)(2,1)} %scatter_fusion.1), calls=%async_computation.6 | async-start | bytes 12582912 | tf_op jit(solution)/shard_map/all_to_all | solution.py:263
  530.2 420.2 %all-gather.18.cloned.1.call-start = ((), (), s32[]{:S(2)}) async-start(), calls=%async_computation.25 | async-start | bytes 34603008 | tf_op jit(solution)/shard_map/all_gather | solution.py:115
  775.7 145.7 %all-to-all-start.5 = ((bf16[16,2,98304]{2,1,0:T(2,128)(2,1)}), bf16[16,2,98304]{2,1,0:T(2,128)(2,1)}, u32[]{:S(2)}, u32[]{:S(2)}) async-start(bf16[16,2,98304]{2,1,0:T(2,128)(2,1)} %reshape.592), calls=%async_computation.5 | async-start | bytes 12582912 | tf_op jit(solution)/shard_map/all_to_all | solution.py:246
  805.0 157.8 %all-gather.20.cloned.1.call-start = ((), (), s32[]{:S(2)}) async-start(), calls=%async_computation.26 | async-start | bytes 17301504 | tf_op jit(solution)/shard_map/all_gather | solution.py:116
  918.1 32.2 %copy-start.9 = (bf16[128,2048]{1,0:T(8,128)(2,1)S(1)}, bf16[128,2048]{1,0:T(8,128)(2,1)}, u32[]{:S(2)}) copy-start(bf16[128,2048]{1,0:T(8,128)(2,1)} %copy-done.8) | copy-start | bytes 1572868
  921.4 144.8 %all-to-all-start.7 = ((bf16[16,2,98304]{2,1,0:T(2,128)(2,1)}), bf16[16,2,98304]{2,1,0:T(2,128)(2,1)}, u32[]{:S(2)}, u32[]{:S(2)}) async-start(bf16[16,2,98304]{2,1,0:T(2,128)(2,1)} %reshape.594), calls=%async_computation.7 | async-start | bytes 12582912 | tf_op jit(solution)/shard_map/all_to_all | solution.py:284
  1116.1 50.6 %copy-start.38 = (s32[2048]{0:T(1024)S(1)}, s32[2048]{0:T(1024)}, u32[]{:S(2)}) copy-start(s32[2048]{0:T(1024)} %copy-done.37) | copy-start | bytes 24580
  1116.1 50.6 %copy-start.93 = (s32[4]{0:T(128)S(1)}, s32[4]{0:T(128)}, u32[]{:S(2)}) copy-start(s32[4]{0:T(128)} %copy-done.92) | copy-start | bytes 52
  1123.8 43.0 %all-to-all-start.8 = ((bf16[128,16,128]{2,0,1:T(8,128)(2,1)}), bf16[128,16,128]{2,0,1:T(8,128)(2,1)}, u32[]{:S(2)}, u32[]{:S(2)}) async-start(bf16[128,16,128]{2,0,1:T(8,128)(2,1)} %bitcast.212), calls=%async_computation.8 | async-start | bytes 1048576 | tf_op jit(solution)/shard_map/all_to_all | solution.py:313
  1244.4 29.2 %copy-start.69 = (f32[128]{0:T(128)S(1)}, f32[128]{0:T(128)}, u32[]{:S(2)}) copy-start(f32[128]{0:T(128)} %copy-done.68) | copy-start | bytes 1540
  1244.4 29.2 %copy-start.77 = (f32[32]{0:T(128)S(1)}, f32[32]{0:T(128)}, u32[]{:S(2)}) copy-start(f32[32]{0:T(128)} %copy-done.76) | copy-start | bytes 388
  1245.5 42.8 %copy-start.17 = (f32[128,576]{0,1:T(8,128)S(1)}, f32[128,576]{0,1:T(8,128)}, u32[]{:S(2)}) copy-start(f32[128,576]{0,1:T(8,128)} %copy-done.16) | copy-start | bytes 884740
  1245.5 42.8 %copy-start.48 = (f32[2,1,256]{2,1,0:T(1,128)S(1)}, f32[2,1,256]{2,1,0:T(1,128)}, u32[]{:S(2)}) copy-start(f32[2,1,256]{2,1,0:T(1,128)} %copy-done.47) | copy-start | bytes 6148
  1245.5 42.8 %copy-start.71 = (f32[128]{0:T(128)S(1)}, f32[128]{0:T(128)}, u32[]{:S(2)}) copy-start(f32[128]{0:T(128)} %copy-done.70) | copy-start | bytes 1540
  1245.5 22.8 all-to-all-start.10
  1268.4 18.9 all-to-all-start.11
  1273.5 131.8 %reduce-scatter.15.cloned.1.call-start = ((), (), s32[]{:S(2)}) async-start(), calls=%async_computation.30 | async-start | bytes 3538944 | tf_op jit(solution)/shard_map/reduce_scatter | solution.py:402
  1294.9 110.3 %reduce-scatter.23.cloned.1.call-start = ((), (), s32[]{:S(2)}) async-start(), calls=%async_computation.34 | async-start | bytes 17301504 | tf_op jit(solution)/shard_map/reduce_scatter | solution.py:423
  1301.3 103.9 %reduce-scatter.17.cloned.1.call-start = ((), (), s32[]{:S(2)}) async-start(), calls=%async_computation.31 | async-start | bytes 6291456 | tf_op jit(solution)/shard_map/reduce_scatter | solution.py:408
  1306.2 99.2 %reduce-scatter.19.cloned.1.call-start = ((), (), s32[]{:S(2)}) async-start(), calls=%async_computation.32 | async-start | bytes 12582912 | tf_op jit(solution)/shard_map/reduce_scatter | solution.py:411
  1312.0 93.4 %reduce-scatter.13.cloned.1.call-start = ((), (), s32[]{:S(2)}) async-start(), calls=%async_computation.29 | async-start | bytes 18874368 | tf_op jit(solution)/shard_map/reduce_scatter | solution.py:399
  1313.7 24.2 %copy-start.53 = (f32[128,32]{0,1:T(8,128)S(1)}, f32[128,32]{0,1:T(8,128)}, u32[]{:S(2)}) copy-start(f32[128,32]{0,1:T(8,128)} %get-tuple-element.295) | copy-start | bytes 49156
  1345.0 82.4 %reduce-scatter.29.cloned.1.call-start = ((), (), s32[]{:S(2)}) async-start(), calls=%async_computation.37 | async-start | bytes 34603008
  1361.3 119.8 %reduce-scatter.27.cloned.1.call-start = ((), (), s32[]{:S(2)}) async-start(), calls=%async_computation.36 | async-start | bytes 8650752 | tf_op jit(solution)/shard_map/reduce_scatter | solution.py:443
  1376.3 127.4 %reduce-scatter.21.cloned.1.call-start = ((), (), s32[]{:S(2)}) async-start(), calls=%async_computation.33 | async-start | bytes 98304 | tf_op jit(solution)/shard_map/reduce_scatter | solution.py:417
  1377.8 211.7 %reduce-scatter.25.cloned.1.call-start = ((), (), s32[]{:S(2)}) async-start(), calls=%async_computation.35 | async-start | bytes 17301504 | tf_op jit(solution)/shard_map/reduce_scatter | solution.py:440
  1405.2 899.9 %all-reduce.9.cloned.1.call-start = ((), (), s32[]{:S(2)}) async-start(), calls=%async_computation.38 | async-start | bytes 62128128 | tf_op jit(solution)/shard_map/psum | solution.py:429
  1497.7 89.3 %copy-start.84 = (f32[128]{0:T(128)S(1)}, f32[128]{0:T(128)}, u32[]{:S(2)}) copy-start(f32[128]{0:T(128)} %copy-done.83) | copy-start | bytes 1540
  1497.7 89.3 %copy-start.62 = (f32[128]{0:T(128)S(1)}, f32[128]{0:T(128)}, u32[]{:S(2)}) copy-start(f32[128]{0:T(128)} %copy-done.58) | copy-start | bytes 1540
  (95 other events, 654.2 us)
Sparse Core Ops, SparseCore 0:
  9.6 13.6 all-gather.11
  24.8 14.8 all-gather.13
  41.2 26.0 all-gather.9
  68.7 21.0 all-gather.15
  110.7 25.1 all-gather.21
  361.6 17.2 all-gather.23
  532.6 39.1 all-gather.17
  807.4 25.1 all-gather.19
  1295.1 8.1 reduce-scatter.14
  1306.1 21.3 reduce-scatter.22
  1330.4 13.2 reduce-scatter.16
  1346.5 18.0 reduce-scatter.18
  1367.6 22.7 reduce-scatter.12
  1393.2 34.1 reduce-scatter.28
  1430.2 15.1 reduce-scatter.26
  1448.0 8.5 reduce-scatter.20
  1459.4 21.3 reduce-scatter.24
  1487.1 817.9 all-reduce.8
where the time goes:
time: 2360 us; the launch traced here: 2350 us
  waiting for transfers between devices  982 us (42%)
  local copies, waits for them, and re-layouts  534 us (23%)
  matrix products  327 us (14%)
  other arithmetic  184 us (8%)
  blocking collectives  155 us (7%)
  starting transfers between devices  132 us (6%)
    psum x1, waiting for transfers between devices, on_device(): lax.psum(dense_sums[1].astype(jnp.bfloat16), 'seq').astype(jnp.float32)  708 us
    scatter x1, local copies, waits for them, and re-layouts, on_device(): send_rows = jnp.zeros((experts, capacity, D), jnp.bfloat16).at[flat_route...  137 us
    scatter x1, local copies, waits for them, and re-layouts, on_device(): grad_send = jnp.zeros((experts, capacity, D), jnp.bfloat16).at[flat_route...  132 us
    all_to_all x1, waiting for transfers between devices, on_device(): lax.all_to_all(grad_send, 'seq', split_axis=0, concat_axis=1, tiled=True)  92.3 us
    unnamed x213, local copies, waits for them, and re-layouts  91.2 us
    psum x1, blocking collectives, on_device(): lax.psum(dense_sums[0].astype(jnp.bfloat16), 'seq').astype(jnp.float32)  80.8 us
    unnamed x8, other arithmetic  79.5 us
  transfers between devices with their start and end apart: 29, of which 14 were waited for; matrix products, arithmetic and copies ran while one was open for 37% of the time, Pallas kernels for 0%

commit v1 on v0

v1 whole, which is shorter than its diff:
```python
import functools

import jax
import jax.numpy as jnp
from jax import lax
from jax.experimental import pallas as pl
from jax.experimental.pallas import tpu as pltpu
from jax.sharding import PartitionSpec as P

D = 2048
H = 16
DN = 128
DR = 64
DV = 128
KVR = 512
FF = 1408
TOP = 6
SH = 2816

EPSILON = 1e-06
CLIP_LIMIT = 8.0
ROPE_BASE = 10000.0
MASK_VALUE = -1e30
BF16 = jnp.bfloat16
F32 = jnp.float32


def rms_norm(values, gain_vector):
    return (
        values
        * lax.rsqrt(jnp.mean(values * values, axis=-1, keepdims=True) + EPSILON)
        * gain_vector
    )


def rotate(values, angles):
    half_width = values.shape[-1] // 2
    first_half = values[..., :half_width]
    second_half = values[..., half_width:]
    cosine = jnp.cos(angles)
    sine_part = jnp.sin(angles)
    return jnp.concatenate(
        [
            first_half * cosine - second_half * sine_part,
            second_half * cosine + first_half * sine_part,
        ],
        axis=-1,
    )


def frequencies(count):
    exponent = jnp.arange(count // 2, dtype=jnp.float32) * 2.0 / count
    return ROPE_BASE ** (-exponent)


def layout(lengths_row, slot_ids):
    seq_ends = jnp.cumsum(lengths_row)
    seq_starts = seq_ends - lengths_row
    inside = (slot_ids[:, None] >= seq_starts[None, :]) & (slot_ids[:, None] < seq_ends[None, :])
    is_valid = jnp.any(inside, axis=1)
    numbers = jnp.arange(lengths_row.shape[0], dtype=jnp.int32)
    seq_number = jnp.sum(jnp.where(inside, numbers[None, :], 0), axis=1)
    first_slot = jnp.sum(jnp.where(inside, seq_starts[None, :], 0), axis=1)
    segment = jnp.where(is_valid, seq_number, lengths_row.shape[0] + slot_ids)
    position = jnp.where(is_valid, slot_ids - first_slot, 0)
    return (segment, position, is_valid)


def silu_back(gate_part, up_part, hidden_grad):
    sigmoid_gate = jax.nn.sigmoid(gate_part)
    gate_grad = hidden_grad * up_part * sigmoid_gate * (1.0 + gate_part * (1.0 - sigmoid_gate))
    up_grad = hidden_grad * gate_part * sigmoid_gate
    return jnp.concatenate([gate_grad, up_grad], axis=1)


def dot(left, right):
    return jnp.dot(left, right, preferred_element_type=F32)


def dot_tn(left, right):
    return lax.dot_general(left, right, (((0,), (0,)), ((), ())), preferred_element_type=F32)


def dot_nt(left, right):
    return lax.dot_general(left, right, (((1,), (1,)), ((), ())), preferred_element_type=F32)


ROWS = 256


def masked_scores(query, key, seg_col, seg_row, first, scale):
    scores = dot_nt(query, key) * scale
    shape = scores.shape
    row_slot = first + lax.broadcasted_iota(jnp.int32, shape, 0)
    key_slot = lax.broadcasted_iota(jnp.int32, shape, 1)
    allowed = (seg_col == seg_row) & (key_slot <= row_slot)
    return jnp.where(allowed, scores, MASK_VALUE)


def attention_forward_kernel(scale, q_ref, k_ref, v_ref, segc_ref, segr_ref, valid_ref, ctx_ref, lse_ref, max_ref):
    count = q_ref.shape[0]
    best = jnp.full((1, 1), MASK_VALUE, F32)
    for first in range(0, count, ROWS):
        rows, keys = pl.ds(first, ROWS), pl.ds(0, first + ROWS)
        masked = masked_scores(q_ref[rows, :], k_ref[keys, :], segc_ref[rows, :], segr_ref[:, keys], first, scale)
        row_max = jnp.max(masked, axis=1, keepdims=True)
        exponent = jnp.exp(masked - row_max)
        row_sum = jnp.sum(exponent, axis=1, keepdims=True)
        probs = (exponent * (1.0 / row_sum)).astype(BF16)
        ctx_ref[rows, :] = dot(probs, v_ref[keys, :]).astype(BF16)
        lse_ref[rows, :] = row_max + jnp.log(row_sum)
        counted = jnp.where(valid_ref[rows, :] > 0, row_max, MASK_VALUE)
        best = jnp.maximum(best, jnp.max(counted, axis=0, keepdims=True))
    max_ref[...] = jnp.broadcast_to(best, max_ref.shape)


def attention_forward(query, key, value, segment, valid):
    count, width = query.shape
    return pl.pallas_call(
        functools.partial(attention_forward_kernel, width ** (-0.5)),
        out_shape=(
            jax.ShapeDtypeStruct((count, value.shape[1]), BF16),
            jax.ShapeDtypeStruct((count, 1), F32),
            jax.ShapeDtypeStruct((8, 128), F32),
        ),
        compiler_params=pltpu.CompilerParams(vmem_limit_bytes=48 * 2**20),
        cost_estimate=pl.CostEstimate(flops=count * count * 320, bytes_accessed=4 * 2**20, transcendentals=count * count // 2),
        name="attention_forward",
    )(query, key, value, segment[:, None], segment[None, :], valid[:, None].astype(jnp.int32))


def attention_backward_kernel(scale, q_ref, k_ref, v_ref, g_ref, segc_ref, segr_ref, lse_ref, dq_ref, dk_ref, dv_ref, dk_sum, dv_sum):
    count = q_ref.shape[0]
    dk_sum[...] = jnp.zeros_like(dk_sum)
    dv_sum[...] = jnp.zeros_like(dv_sum)
    for first in range(0, count, ROWS):
        rows, keys = pl.ds(first, ROWS), pl.ds(0, first + ROWS)
        query, grad = q_ref[rows, :], g_ref[rows, :]
        masked = masked_scores(query, k_ref[keys, :], segc_ref[rows, :], segr_ref[:, keys], first, scale)
        probs = jnp.exp(masked - lse_ref[rows, :])
        prob_grad = dot_nt(grad, v_ref[keys, :])
        mean = jnp.sum(probs * prob_grad, axis=1, keepdims=True)
        score_grad = (probs * (prob_grad - mean)).astype(BF16)
        dq_ref[rows, :] = (dot(score_grad, k_ref[keys, :]) * scale).astype(BF16)
        dk_sum[keys, :] += dot_tn(score_grad, query)
        dv_sum[keys, :] += dot_tn(probs.astype(BF16), grad)
    dk_ref[...] = (dk_sum[...] * scale).astype(BF16)
    dv_ref[...] = dv_sum[...].astype(BF16)


def attention_backward(query, key, value, grad, segment, log_total):
    count, width = query.shape
    return pl.pallas_call(
        functools.partial(attention_backward_kernel, width ** (-0.5)),
        out_shape=(
            jax.ShapeDtypeStruct(query.shape, BF16),
            jax.ShapeDtypeStruct(key.shape, BF16),
            jax.ShapeDtypeStruct(value.shape, BF16),
        ),
        scratch_shapes=[pltpu.VMEM(key.shape, F32), pltpu.VMEM(value.shape, F32)],
        compiler_params=pltpu.CompilerParams(vmem_limit_bytes=48 * 2**20),
        cost_estimate=pl.CostEstimate(flops=count * count * 832, bytes_accessed=6 * 2**20, transcendentals=count * count // 2),
        name="attention_backward",
    )(query, key, value, grad, segment[:, None], segment[None, :], log_total)


def gather_seq(rows):
    return lax.all_gather(rows, "seq", axis=0, tiled=True)


def scatter_seq(partial):
    return lax.psum_scatter(partial, "seq", scatter_dimension=0, tiled=True)


def gather_fsdp(rows, axis=0):
    return lax.all_gather(rows, "fsdp", axis=axis, tiled=True)


def scatter_fsdp(partial, axis=0):
    return lax.psum_scatter(partial, "fsdp", scatter_dimension=axis, tiled=True)


def on_device(
    tokens,
    cotangent,
    lengths,
    routes,
    g_attn,
    w_q,
    w_kva,
    g_kv,
    w_kvb,
    w_o,
    g_ffn,
    w_router,
    w_shared_in,
    w_shared_out,
    w_expert_in,
    w_expert_out,
):
    seq_count = lax.axis_size("seq")
    fsdp_count = lax.axis_size("fsdp")
    rank = lax.axis_index("seq")
    tok_count = tokens.shape[0]
    group_size = tok_count * seq_count
    query_width = DN + DR
    kv_width = DN + DV
    experts = seq_count
    capacity = min(tok_count, 2 * tok_count * TOP // experts)
    buffer_rows = seq_count * capacity
    unit = SH // (seq_count * fsdp_count)
    units = unit * fsdp_count
    row_part = w_q.shape[0]

    def own(rows, axis=0):
        return lax.dynamic_slice_in_dim(rows, rank * tok_count, tok_count, axis)

    token_all = gather_seq(tokens)
    routes_all = gather_seq(routes)
    cotangent_all = gather_seq(cotangent)

    small = gather_fsdp(jnp.concatenate([g_attn, g_kv, g_ffn, w_router.reshape(-1)])[None])
    cuts = [0, g_attn.size, g_kv.size, g_ffn.size, w_router.size]
    ends = [sum(cuts[: i + 1]) for i in range(len(cuts))]
    gain_attn = small[:, ends[0] : ends[1]].reshape(-1).astype(F32)
    gain_latent = small[:, ends[1] : ends[2]].reshape(-1).astype(F32)
    gain_ffn = small[:, ends[2] : ends[3]].reshape(-1).astype(F32)
    router_weight = small[:, ends[3] : ends[4]].reshape(D, experts)
    head_query_part = lax.dynamic_slice_in_dim(w_q, rank * query_width, query_width, 1)
    shared_in_part = lax.dynamic_slice_in_dim(
        w_shared_in.reshape(row_part, 2, fsdp_count, seq_count, unit), rank, 1, 3
    ).reshape(row_part, 2 * units)
    head_expand = gather_fsdp(lax.dynamic_slice_in_dim(w_kvb, rank * kv_width, kv_width, 1))
    head_weights = gather_fsdp(jnp.concatenate([w_kva, head_query_part], axis=1))
    latent_weight = head_weights[:, : KVR + DR]
    head_query = head_weights[:, KVR + DR :]
    shared_in = gather_fsdp(shared_in_part)
    shared_out = gather_fsdp(lax.dynamic_slice_in_dim(w_shared_out, rank * unit, unit, 0))
    output_weight = gather_fsdp(w_o)
    expert_in = gather_fsdp(w_expert_in[0])
    expert_out = gather_fsdp(w_expert_out[0])
    query_weight = gather_fsdp(w_q)
    expand_weight = gather_fsdp(w_kvb)

    slot_ids = jnp.arange(group_size, dtype=jnp.int32)
    segment, position, valid_all = layout(lengths[0], slot_ids)
    angles_all = position[:, None].astype(F32) * frequencies(DR)[None, :]
    angles = own(angles_all)

    normed_all = rms_norm(token_all.astype(F32), gain_attn).astype(BF16)
    query_pre = dot(normed_all, head_query)
    latent_full = dot(normed_all, latent_weight)
    latent_all = rms_norm(latent_full[:, :KVR], gain_latent).astype(BF16)
    expanded = dot(latent_all, head_expand)
    query = jnp.concatenate([query_pre[:, :DN], rotate(query_pre[:, DN:], angles_all)], axis=1).astype(BF16)
    key_rope = rotate(latent_full[:, KVR:], angles_all)
    key = jnp.concatenate([expanded[:, :DN], key_rope], axis=1).astype(BF16)
    value = expanded[:, DN:].astype(BF16)
    context, log_total, head_largest = attention_forward(query, key, value, segment, valid_all)
    largest_all = lax.all_gather(head_largest[:1], ("fsdp", "seq"), axis=0, tiled=False)
    global_max = jnp.max(largest_all.reshape(fsdp_count, seq_count, -1)[:, :, 0], axis=0)

    context_low = lax.all_to_all(context, "seq", split_axis=0, concat_axis=1, tiled=True)
    inputs = tokens.astype(F32)
    middle = inputs + dot(context_low, output_weight)
    ffn_low = rms_norm(middle, gain_ffn).astype(BF16)
    ffn_all = gather_seq(ffn_low)

    router_probs = jax.nn.softmax(dot(ffn_all, router_weight), axis=-1)
    chosen = jnp.any(routes_all == rank, axis=1).reshape(seq_count, tok_count)
    gates = lax.dynamic_slice_in_dim(router_probs, rank, 1, 1).reshape(seq_count, tok_count)
    place = jnp.cumsum(chosen.astype(jnp.int32), axis=1) - 1
    place = jnp.where(chosen, place, capacity)
    picks = lax.broadcasted_iota(jnp.int32, (seq_count, capacity, tok_count), 1) == place[:, None, :]
    pick = picks.astype(BF16)
    row_gate = jnp.sum(jnp.where(picks, gates[:, None, :], 0.0), axis=2).reshape(buffer_rows, 1)

    def to_slots(rows):
        return lax.dot_general(
            pick,
            rows.reshape(seq_count, tok_count, D),
            (((2,), (1,)), ((0,), (0,))),
            preferred_element_type=F32,
        ).reshape(buffer_rows, D)

    def to_tokens(rows):
        return lax.dot_general(
            pick,
            rows.reshape(seq_count, capacity, D),
            (((1,), (1,)), ((0,), (0,))),
            preferred_element_type=F32,
        ).reshape(group_size, D)

    arrived = to_slots(ffn_all).astype(BF16)
    gate_up = dot(arrived, expert_in)
    hidden = (jax.nn.silu(gate_up[:, :FF]) * gate_up[:, FF:]).astype(BF16)
    result = dot(hidden, expert_out).astype(BF16).astype(F32)
    shared_both = dot(ffn_all, shared_in)
    shared_hidden = (jax.nn.silu(shared_both[:, :units]) * shared_both[:, units:]).astype(BF16)
    mixed_part = to_tokens((row_gate * result).astype(BF16)) + dot(shared_hidden, shared_out)
    mixed_sum = scatter_seq(mixed_part.astype(BF16))
    mixed = (middle + mixed_sum.astype(F32)).astype(BF16)

    upstream_all = jnp.where(valid_all[:, None], cotangent_all, 0).astype(BF16)
    upstream_rows = to_slots(upstream_all)
    row_gate_grad = jnp.sum(upstream_rows * result, axis=1).reshape(seq_count, capacity)
    gate_grad = jnp.sum(jnp.where(picks, row_gate_grad[:, :, None], 0.0), axis=1).reshape(1, group_size)
    prob_grads = gather_seq(gate_grad).T
    result_grad = (row_gate * upstream_rows).astype(BF16)
    d_hidden = dot_nt(result_grad, expert_out)
    grad_expert_out = dot_tn(hidden, result_grad)
    d_gate_up = silu_back(gate_up[:, :FF], gate_up[:, FF:], d_hidden).astype(BF16)
    grad_expert_in = dot_tn(arrived, d_gate_up)
    row_grad = dot_nt(d_gate_up, expert_in).astype(BF16)
    shared_hidden_grad = dot_nt(upstream_all, shared_out)
    shared_grad = silu_back(shared_both[:, :units], shared_both[:, units:], shared_hidden_grad).astype(BF16)
    ffn_part = to_tokens(row_grad) + dot_nt(shared_grad, shared_in)
    ffn_sum = scatter_seq(ffn_part.astype(BF16))
    grad_shared_out = dot_tn(shared_hidden, upstream_all)
    grad_shared_in = dot_tn(shared_grad, ffn_all)
    sum_expert_in = scatter_fsdp(grad_expert_in.astype(BF16)).astype(F32)[None]
    sum_expert_out = scatter_fsdp(grad_expert_out.astype(BF16)).astype(F32)[None]
    sum_shared_out = gather_seq(scatter_fsdp(grad_shared_out.astype(BF16))).astype(F32)
    sum_shared_in = gather_seq(scatter_fsdp(grad_shared_in.astype(BF16), 1))
    sum_shared_in = (
        sum_shared_in.reshape(seq_count, 2, fsdp_count, unit, row_part)
        .transpose(4, 1, 2, 0, 3)
        .reshape(row_part, 2 * SH)
        .astype(F32)
    )

    logit_grads = (
        router_probs * (prob_grads - jnp.sum(router_probs * prob_grads, axis=-1, keepdims=True))
    ).astype(BF16)
    grad_router = dot_tn(ffn_all, logit_grads)
    sum_router = scatter_fsdp(grad_router.astype(BF16)).astype(F32)
    ffn_grad = ffn_sum.astype(F32) + dot_nt(own(logit_grads), router_weight)

    ffn_pull = jax.vjp(rms_norm, middle, gain_ffn)[1]
    middle_norm_grad, grad_gain_ffn = ffn_pull(ffn_grad)
    upstream = own(upstream_all).astype(F32)
    middle_grad = upstream + middle_norm_grad
    middle_low = middle_grad.astype(BF16)
    context_grad = dot_nt(middle_low, output_weight).astype(BF16)
    head_grad = lax.all_to_all(context_grad, "seq", split_axis=1, concat_axis=0, tiled=True)
    grad_output = scatter_fsdp(dot_tn(context_low, middle_low).astype(BF16))
    sum_output = lax.psum(grad_output, "seq").astype(F32)

    query_grad, key_grad, value_grad = attention_backward(query, key, value, head_grad, segment, log_total)
    back = lax.all_to_all(
        jnp.concatenate([query_grad, key_grad, value_grad], axis=1).reshape(seq_count, tok_count, -1),
        "seq",
        split_axis=0,
        concat_axis=0,
        tiled=True,
    )
    query_grad_32 = query_grad.astype(F32)
    head_pre_grad = jnp.concatenate(
        [query_grad_32[:, :DN], rotate(query_grad_32[:, DN:], -angles_all)], axis=1
    ).astype(BF16)
    grad_query = scatter_fsdp(dot_tn(head_pre_grad, normed_all).astype(BF16), 1)
    sum_query = gather_seq(grad_query).T.astype(F32)
    head_expand_grad = jnp.concatenate([key_grad[:, :DN], value_grad], axis=1)
    grad_expand = scatter_fsdp(dot_tn(head_expand_grad, latent_all).astype(BF16), 1)
    sum_expand = gather_seq(grad_expand).T.astype(F32)

    back = back.transpose(1, 0, 2)
    back_query = back[..., :query_width].astype(F32)
    back_key = back[..., query_width : 2 * query_width]
    back_value = back[..., 2 * query_width :]
    pre_grad = (
        jnp.concatenate([back_query[..., :DN], rotate(back_query[..., DN:], -angles[:, None, :])], axis=-1)
        .reshape(tok_count, H * query_width)
        .astype(BF16)
    )
    expand_grad = jnp.concatenate([back_key[..., :DN], back_value], axis=-1).reshape(tok_count, H * kv_width)
    latent_grad = dot_nt(expand_grad, expand_weight)
    rope_grad = rotate(jnp.sum(back_key[..., DN:].astype(F32), axis=1), -angles)
    latent_pull = jax.vjp(rms_norm, own(latent_full)[:, :KVR], gain_latent)[1]
    compressed_grad, grad_gain_latent = latent_pull(latent_grad)
    full_grad = jnp.concatenate([compressed_grad, rope_grad], axis=1).astype(BF16)
    full_all = gather_seq(full_grad)
    sum_latent = scatter_fsdp(dot_tn(normed_all, full_all).astype(BF16)).astype(F32)
    normed_grad = dot_nt(pre_grad, query_weight) + dot_nt(full_grad, latent_weight)
    input_pull = jax.vjp(rms_norm, inputs, gain_attn)[1]
    input_norm_grad, grad_gain_attn = input_pull(normed_grad)
    grad_inputs = middle_grad + input_norm_grad

    gain_grads = jnp.concatenate([grad_gain_attn, grad_gain_latent, grad_gain_ffn])
    gain_sum = jnp.sum(lax.all_gather(gain_grads[None], ("fsdp", "seq"), axis=0, tiled=True), axis=0)
    fsdp_rank = lax.axis_index("fsdp")

    def own_part(first, like):
        return lax.dynamic_slice_in_dim(gain_sum, first + fsdp_rank * like.size, like.size, 0)

    sum_gain_attn = own_part(0, g_attn)
    sum_gain_latent = own_part(D, g_kv)
    sum_gain_ffn = own_part(D + KVR, g_ffn)

    clip_gamma = CLIP_LIMIT / jnp.maximum(global_max, CLIP_LIMIT)
    clip_root = jnp.sqrt(clip_gamma)
    query_factor = jnp.concatenate(
        [
            jnp.broadcast_to(clip_root[:, None], (H, DN)),
            jnp.broadcast_to(clip_gamma[:, None], (H, DR)),
        ],
        axis=1,
    ).reshape(1, -1)
    clipped_query = (w_q.astype(F32) * query_factor).astype(BF16)
    return (
        mixed,
        grad_inputs,
        sum_gain_attn,
        sum_query,
        sum_latent,
        sum_gain_latent,
        sum_expand,
        sum_output,
        sum_gain_ffn,
        sum_router,
        sum_shared_in,
        sum_shared_out,
        sum_expert_in,
        sum_expert_out,
        clipped_query,
    )


def solution(mesh):
    in_specs = (
        P(("fsdp", "seq"), None),
        P(("fsdp", "seq"), None),
        P("fsdp", None),
        P(("fsdp", "seq"), None),
        P("fsdp"),
        P("fsdp", None),
        P("fsdp", None),
        P("fsdp"),
        P("fsdp", None),
        P("fsdp", None),
        P("fsdp"),
        P("fsdp", None),
        P("fsdp", None),
        P("fsdp", None),
        P("seq", "fsdp", None),
        P("seq", "fsdp", None),
    )
    out_specs = (
        P(("fsdp", "seq"), None),
        P(("fsdp", "seq"), None),
        P("fsdp"),
        P("fsdp", None),
        P("fsdp", None),
        P("fsdp"),
        P("fsdp", None),
        P("fsdp", None),
        P("fsdp"),
        P("fsdp", None),
        P("fsdp", None),
        P("fsdp", None),
        P("seq", "fsdp", None),
        P("seq", "fsdp", None),
        P("fsdp", None),
    )
    return jax.shard_map(
        on_device, mesh=mesh, in_specs=in_specs, out_specs=out_specs, check_vma=False
    )
```

time: 2360 us -> 1840 us (0.78)
  local copies, waits for them, and re-layouts: 534 us -> 108 us
  starting transfers between devices: 132 us -> 10.7 us
  blocking collectives: 155 us -> 260 us
  other arithmetic: 184 us -> 128 us
  matrix products: 327 us -> 296 us
    psum x1, waiting for transfers between devices: 708 us -> 151 us  [on_device(): sum_output = lax.psum(grad_output, 'seq').astype(F32)]
    all_gather x8 -> x15, waiting for transfers between devices: 38.1 us -> 482 us  [the longest x8 455 us: gather_seq(): return lax.all_gather(rows, 'seq', axis=0, tiled=True)]
    reduce_scatter x8 -> x11, waiting for transfers between devices: 0.1 us -> 310 us  [the longest x2 297 us: scatter_seq(): return lax.psum_scatter(partial, 'seq', scatter_dimension=0, tiled=True)]
    scatter x2 -> x0, local copies, waits for them, and re-layouts: 270 us -> none  [the longest x1 137 us: on_device(): send_rows = jnp.zeros((experts, capacity, D), jnp.bfloat16).at[flat_route...]
    all_gather x4 -> x7, blocking collectives: 7.39 us -> 237 us  [the longest x2 89.5 us: gather_seq(): return lax.all_gather(rows, 'seq', axis=0, tiled=True)]
    all_to_all x10 -> x1, waiting for transfers between devices: 200 us -> 16.2 us  [on_device(): lax.all_to_all(jnp.concatenate([query_grad, key_grad, value_grad], axis=1...]
    all_to_all x10 -> x1, starting transfers between devices: 126 us -> 4.46 us  [on_device(): lax.all_to_all(jnp.concatenate([query_grad, key_grad, value_grad], axis=1...]
    psum x1 -> x0, blocking collectives: 80.8 us -> none  [on_device(): lax.psum(dense_sums[0].astype(jnp.bfloat16), 'seq').astype(jnp.float32)]
  transfers between devices with their start and end apart: 29 -> 29, of which waited for: 14 -> 15; matrix products, arithmetic and copies ran while one was open for 37% -> 27% of each run, Pallas kernels for 0% -> 1%
where the time goes in v1:
time: 1840 us; the launch traced here: 1830 us
  waiting for transfers between devices  989 us (54%)
  matrix products  296 us (16%)
  blocking collectives  260 us (14%)
  other arithmetic  128 us (7%)
  local copies, waits for them, and re-layouts  108 us (6%)
  Pallas kernels  20 us (1%)
    all_gather x8, waiting for transfers between devices, gather_seq(): return lax.all_gather(rows, 'seq', axis=0, tiled=True)  455 us
    reduce_scatter x2, waiting for transfers between devices, scatter_seq(): return lax.psum_scatter(partial, 'seq', scatter_dimension=0, tiled=True)  297 us
    psum x1, waiting for transfers between devices, on_device(): sum_output = lax.psum(grad_output, 'seq').astype(F32)  151 us
    all_gather x2, blocking collectives, gather_seq(): return lax.all_gather(rows, 'seq', axis=0, tiled=True)  89.5 us
    dot_general x9, matrix products, dot(): return jnp.dot(left, right, preferred_element_type=F32)  88.6 us
    dot_general x9, matrix products, dot_nt(): lax.dot_general(left, right, (((1,), (1,)), ((), ())), preferred_element_...  84.9 us
    dot_general x9, matrix products, dot_tn(): lax.dot_general(left, right, (((0,), (0,)), ((), ())), preferred_element_...  83.5 us
    unnamed x132, local copies, waits for them, and re-layouts  77.6 us
  transfers between devices with their start and end apart: 29, of which 15 were waited for; matrix products, arithmetic and copies ran while one was open for 27% of the time, Pallas kernels for 1%

profile of v1, /device:TPU:0, one launch (start us, length us, event | category | flops | bytes accessed | tf_op | source)
XLA Modules:
  0.0 1827.3 jit_solution(12710161343453239649)
XLA Ops:
  21.8 104.6 %all-gather.25.cloned.1.call-done = bf16[2048,2048]{1,0:T(8,128)(2,1)} async-done(((bf16[128,2048]{1,0:T(8,128)(2,1)}), bf16[2048,2048]{1,0:T(8,128)(2,1)}) %all-gather.25.cloned.1.call-update) | async-done | bytes 8388624 | tf_op jit(solution)/shard_map/all_gather | solution.py:168
  131.5 9.7 fusion.2
  141.2 8.2 fusion.19
  152.6 8.1 fusion.62
  180.0 8.3 attention_forward.1
  195.6 22.7 %all-to-all-done = bf16[16,128,128]{1,2,0:T(8,128)(2,1)S(1)} async-done(((bf16[16,128,128]{1,2,0:T(8,128)(2,1)}), bf16[16,128,128]{1,2,0:T(8,128)(2,1)S(1)}, u32[]{:S(2)}, u32[]{:S(2)}) %all-to-all-start) | async-done | bytes 524320 | tf_op jit(solution)/shard_map/all_to_all | solution.py:263
  226.6 15.7 copy.146
  244.9 47.5 %all_gather.74 = s32[2048,6]{0,1:T(8,128)S(1)} all-gather(s32[128,6]{0,1:T(8,128)S(1)} %copy-done.47), channel_id=1, replica_groups=mesh['seq'=16,'fsdp'=2] {'seq'}, dimensions={0}, use_global_device_ids=true | all-gather | bytes 52224 | tf_op jit(solution)/shard_map/all_gather | solution.py:168
  296.2 7.8 broadcast_select_fusion
  304.0 10.0 fusion.65
  314.0 89.2 %all-gather.31.cloned.1.call-done = bf16[2048,2048]{1,0:T(8,128)(2,1)} async-done(((bf16[128,2048]{1,0:T(8,128)(2,1)}), bf16[2048,2048]{1,0:T(8,128)(2,1)}) %all-gather.31.cloned.1.call-update) | async-done | bytes 8388624 | tf_op jit(solution)/shard_map/all_gather | solution.py:168
  403.1 8.8 convolution_convert_fusion.4
  411.9 14.7 all-gather.51.cloned.1.call-done
  426.7 23.6 %fusion.10 = f32[1536,2816]{1,0:T(8,128)S(1)} fusion(bf16[1536,2048]{1,0:T(8,128)(2,1)} %bitcast.157, bf16[1,2048,2816]{2,1,0:T(8,128)(2,1)} %all-gather.51.cloned.1.call-done), kind=kOutput, calls=%fused_computation.19 | convolution fusion | flops 17716740096 | bytes 35127296 | tf_op jit(solution)/shard_map/dot_general | solution.py:77
  460.7 17.1 fusion.6
  484.3 13.3 fusion.7
  497.6 21.8 %multiply_convert_fusion.2 = (bf16[1536,1408]{1,0:T(8,128)(2,1)}, bf16[1536,1408]{1,0:T(8,128)(2,1)}) fusion(f32[1536,2816]{1,0:T(8,128)} %copy-done.10, bf16[1536,2048]{1,0:T(8,128)(2,1)} %get-tuple-element.150, bf16[1,1408,2048]{2,1,0:T(8,128)(2,1)} %all-gather.53.cloned.1.call-done), kind=kOutput, calls=%fused_computation.24 | convolution fusion | flops 8886484992 | bytes 38010880 | tf_op jit(solution)/shard_map/dot_general | solution.py:85
  519.4 24.0 %fusion.12 = bf16[1536,2048]{1,0:T(8,128)(2,1)S(1)} fusion(bf16[1,2048,2816]{2,1,0:T(8,128)(2,1)} %all-gather.51.cloned.1.call-done, bf16[1536,1408]{1,0:T(8,128)(2,1)} %get-tuple-element.118, bf16[1536,1408]{1,0:T(8,128)(2,1)} %get-tuple-element.117), kind=kOutput, calls=%fused_computation.28 | convolution fusion | flops 17737187328 | bytes 26476544 | tf_op jit(solution)/shard_map/dot_general | solution.py:85
  543.4 8.5 fusion.64
  566.1 10.2 fusion.3
  576.5 11.3 fusion.66
  587.8 11.6 fusion.4
  600.3 42.0 %all-gather.6 = f32[16,1,2048]{2,1,0:T(1,128)S(1)} all-gather(f32[1,1,2048]{2,1,0:T(1,128)S(1)} %bitcast.181), channel_id=1, replica_groups=mesh['seq'=16,'fsdp'=2] {'seq'}, dimensions={0}, use_global_device_ids=true | all-gather | bytes 139264 | tf_op jit(solution)/shard_map/all_gather | solution.py:168
  642.4 115.7 %reduce-scatter.14.cloned.1.call-done = bf16[128,2048]{1,0:T(8,128)(2,1)} async-done(((bf16[2048,2048]{1,0:T(8,128)(2,1)}), bf16[128,2048]{1,0:T(8,128)(2,1)}) %reduce-scatter.14.cloned.1.call-update) | async-done | bytes 524304 | tf_op jit(solution)/shard_map/reduce_scatter | solution.py:172
  759.8 181.3 %reduce-scatter.12.cloned.1.call-done = bf16[128,2048]{1,0:T(8,128)(2,1)} async-done(((bf16[2048,2048]{1,0:T(8,128)(2,1)}), bf16[128,2048]{1,0:T(8,128)(2,1)}) %reduce-scatter.12.cloned.1.call-update) | async-done | bytes 524304 | tf_op jit(solution)/shard_map/reduce_scatter | solution.py:172
  950.3 22.8 %all_to_all.43 = bf16[128,16,128]{2,0,1:T(8,128)(2,1)S(1)} all-to-all(bf16[128,16,128]{2,0,1:T(8,128)(2,1)S(1)} %bitcast.167), channel_id=1, replica_groups=mesh['seq'=16,'fsdp'=2] {'seq'}, dimensions={1} | all-to-all | bytes 1048576 | tf_op jit(solution)/shard_map/all_to_all | solution.py:345
  973.2 11.7 attention_backward.1
  1007.1 8.4 convolution_convert_fusion.6
  1021.4 16.2 all-to-all-done.2
  1059.6 14.3 convolution_convert_fusion.1
  1081.9 24.5 %convolution_convert_fusion = bf16[2048,2816]{1,0:T(8,128)(2,1)} fusion(bf16[1536,2048]{1,0:T(8,128)(2,1)} %bitcast.158, bf16[1536,1408]{1,0:T(8,128)(2,1)} %get-tuple-element.118, bf16[1536,1408]{1,0:T(8,128)(2,1)} %get-tuple-element.117), kind=kOutput, calls=%fused_computation.21 | convolution fusion | flops 17739808768 | bytes 26476544 | tf_op jit(solution)/shard_map/dot_general | solution.py:81
  1107.2 11.1 all-gather.43.cloned.1.call-done
  1118.3 9.2 convolution_convert_fusion.5
  1128.4 67.8 %all-gather.8 = f32[32,1,128]{2,1,0:T(1,128)S(1)} all-gather(f32[1,1,128]{2,1,0:T(1,128)S(1)} %slice_bitcast_fusion), channel_id=6, replica_groups=mesh['seq'=16,'fsdp'=2] {'fsdp','seq'}, dimensions={0}, use_global_device_ids=true | all-gather | bytes 16896 | tf_op jit(solution)/shard_map/all_gather | solution.py:260
  1210.2 40.2 %all-gather.49.cloned.1.call-done = bf16[1408,2048]{1,0:T(8,128)(2,1)} async-done(((bf16[88,2048]{1,0:T(8,128)(2,1)}), bf16[1408,2048]{1,0:T(8,128)(2,1)}) %all-gather.49.cloned.1.call-update) | async-done | bytes 5767184 | tf_op jit(solution)/shard_map/all_gather | solution.py:168
  1250.4 10.8 convert_element_type.265
  1262.9 12.3 all-gather.37.cloned.1.call-done
  1275.2 9.1 fusion.106
  1285.2 72.8 %all-gather.7 = f32[32,1,4608]{2,1,0:T(1,128)S(1)} all-gather(f32[1,1,4608]{2,1,0:T(1,128)S(1)} %reshape.335), channel_id=5, replica_groups=mesh['seq'=16,'fsdp'=2] {'fsdp','seq'}, dimensions={0}, use_global_device_ids=true | all-gather | bytes 608256 | tf_op jit(solution)/shard_map/all_gather | solution.py:390
  1372.2 13.0 reduce-scatter.30.cloned.1.call-done
  1385.2 7.9 bitcast_convert_fusion
  1393.1 138.1 %all-gather.47.cloned.1.call-done = bf16[5632,1024]{1,0:T(8,128)(2,1)} async-done(((bf16[352,1024]{1,0:T(8,128)(2,1)}), bf16[5632,1024]{1,0:T(8,128)(2,1)}) %all-gather.47.cloned.1.call-update) | async-done | bytes 11534352 | tf_op jit(solution)/shard_map/all_gather | solution.py:168
  1531.2 12.8 copy.159
  1544.1 23.6 %copy.162 = f32[1024,5632]{1,0:T(8,128)} copy(f32[1024,5632]{0,1:T(8,128)} %bitcast.154) | data formatting | bytes 46137344
  1570.6 69.9 %all-gather.41.cloned.1.call-done = bf16[3072,1024]{1,0:T(8,128)(2,1)} async-done(((bf16[192,1024]{1,0:T(8,128)(2,1)}), bf16[3072,1024]{1,0:T(8,128)(2,1)}) %all-gather.41.cloned.1.call-update) | async-done | bytes 6291472 | tf_op jit(solution)/shard_map/all_gather | solution.py:168
  1640.5 8.9 convert_bitcast_fusion
  1649.4 12.7 copy.160
  1662.0 151.3 %all-reduce.2.cloned.1.call-done = bf16[1024,2048]{1,0:T(8,128)(2,1)} async-done(((bf16[1024,2048]{1,0:T(8,128)(2,1)}), bf16[1024,2048]{1,0:T(8,128)(2,1)}) %all-reduce.2.cloned.1.call-update) | async-done | bytes 4194320 | tf_op jit(solution)/shard_map/psum | solution.py:347
  (312 shorter events, 206.2 us)
Async XLA Ops:
  7.2 119.2 %all-gather.25.cloned.1.call-start = ((), (), s32[]{:S(2)}) async-start(), calls=%async_computation.14 | async-start | bytes 8912896 | tf_op jit(solution)/shard_map/all_gather | solution.py:168
  7.9 133.2 %all-gather.27.cloned.1.call-start = ((), (), s32[]{:S(2)}) async-start(), calls=%async_computation.15 | async-start | bytes 4718592 | tf_op jit(solution)/shard_map/all_gather | solution.py:176
  12.2 183.4 %all-gather.29.cloned.1.call-start = ((), (), s32[]{:S(2)}) async-start(), calls=%async_computation.16 | async-start | bytes 12582912 | tf_op jit(solution)/shard_map/all_gather | solution.py:176
  12.9 283.2 %all-gather.35.cloned.1.call-start = ((), (), s32[]{:S(2)}) async-start(), calls=%async_computation.20 | async-start | bytes 8912896 | tf_op jit(solution)/shard_map/all_gather | solution.py:168
  16.1 115.3 %copy-start.34 = (f32[1,8,2,128]{3,1,2,0:T(8,128)}, f32[1,8,2,128]{3,1,2,0:T(8,128)S(1)}, u32[]{:S(2)}) copy-start(f32[1,8,2,128]{3,1,2,0:T(8,128)S(1)} %copy.189) | copy-start | bytes 24580
  16.3 154.3 %copy-start.41 = (f32[1,2,2,128]{3,1,2,0:T(2,128)}, f32[1,2,2,128]{3,1,2,0:T(2,128)S(1)}, u32[]{:S(2)}) copy-start(f32[1,2,2,128]{3,1,2,0:T(2,128)S(1)} %copy.178) | copy-start | bytes 6148
  21.4 152.6 %copy-start.48 = (f32[32]{0:T(128)}, f32[32]{0:T(128)S(1)}, u32[]{:S(2)}) copy-start(f32[32]{0:T(128)S(1)} %negate_power_fusion) | copy-start | bytes 388
  21.4 152.5 %copy-start.38 = (f32[2048]{0:T(1024)}, f32[2048]{0:T(1024)S(1)}, u32[]{:S(2)}) copy-start(f32[2048]{0:T(1024)S(1)} %select_convert_fusion) | copy-start | bytes 24580
  21.4 158.6 %copy-start.7 = (s32[1,2048]{1,0:T(1,128)}, s32[1,2048]{1,0:T(1,128)S(1)}, u32[]{:S(2)}) copy-start(s32[1,2048]{1,0:T(1,128)S(1)} %reshape_select_fusion.segr_ref) | copy-start | bytes 24580
  21.8 158.2 %copy-start.4 = (s32[2048,1]{1,0:T(8,128)}, s32[2048,1]{1,0:T(8,128)S(1)}, u32[]{:S(2)}) copy-start(s32[2048,1]{1,0:T(8,128)S(1)} %add_select_fusion.segc_ref) | copy-start | bytes 24580
  179.3 39.0 %copy-start.15 = (bf16[128,2048]{1,0:T(8,128)(2,1)S(1)}, bf16[128,2048]{1,0:T(8,128)(2,1)}, u32[]{:S(2)}) copy-start(bf16[128,2048]{1,0:T(8,128)(2,1)} %param.16) | copy-start | bytes 1572868
  191.2 27.0 %all-to-all-start = ((bf16[16,128,128]{1,2,0:T(8,128)(2,1)}), bf16[16,128,128]{1,2,0:T(8,128)(2,1)S(1)}, u32[]{:S(2)}, u32[]{:S(2)}) async-start(bf16[16,128,128]{1,2,0:T(8,128)(2,1)} %copy.145), calls=%async_computation | async-start | bytes 1048576 | tf_op jit(solution)/shard_map/all_to_all | solution.py:263
  195.5 207.7 %all-gather.31.cloned.1.call-start = ((), (), s32[]{:S(2)}) async-start(), calls=%async_computation.17 | async-start | bytes 8912896 | tf_op jit(solution)/shard_map/all_gather | solution.py:168
  195.5 27.8 %copy-start.36 = (f32[1,8,2,128]{3,1,2,0:T(8,128)}, f32[1,8,2,128]{3,1,2,0:T(8,128)S(1)}, u32[]{:S(2)}) copy-start(f32[1,8,2,128]{3,1,2,0:T(8,128)S(1)} %copy.188) | copy-start | bytes 24580
  225.2 201.5 %all-gather.51.cloned.1.call-start = ((), (), s32[]{:S(2)}) async-start(), calls=%async_computation.39 | async-start | bytes 17301504 | tf_op jit(solution)/shard_map/all_gather | solution.py:176
  225.8 234.9 %all-gather.53.cloned.1.call-start = ((), (), s32[]{:S(2)}) async-start(), calls=%async_computation.40 | async-start | bytes 8650752 | tf_op jit(solution)/shard_map/all_gather | solution.py:176
  226.5 325.5 %all-gather.33.cloned.1.call-start = ((), (), s32[]{:S(2)}) async-start(), calls=%async_computation.18 | async-start | bytes 2162688 | tf_op jit(solution)/shard_map/all_gather | solution.py:176
  244.4 513.7 %reduce-scatter.14.cloned.1.call-start = ((), (), s32[]{:S(2)}) async-start(), calls=%async_computation.21 | async-start | bytes 8912896 | tf_op jit(solution)/shard_map/reduce_scatter | solution.py:172
  244.8 233.0 %copy-start.20 = (bf16[2048,16]{1,0:T(8,128)(2,1)}, bf16[2048,16]{1,0:T(8,128)(2,1)S(1)}, u32[]{:S(2)}) copy-start(bf16[2048,16]{1,0:T(8,128)(2,1)S(1)} %reshape.304) | copy-start | bytes 196612
  564.9 22.9 %copy-start.28 = (bf16[2048,176]{0,1:T(8,128)(2,1)}, bf16[2048,176]{0,1:T(8,128)(2,1)S(1)}, u32[]{:S(2)}) copy-start(bf16[2048,176]{0,1:T(8,128)(2,1)S(1)} %get-tuple-element.123) | copy-start | bytes 2162692
  576.3 364.8 %reduce-scatter.12.cloned.1.call-start = ((), (), s32[]{:S(2)}) async-start(), calls=%async_computation.19 | async-start | bytes 8912896 | tf_op jit(solution)/shard_map/reduce_scatter | solution.py:172
  599.5 158.6 %copy-start.12 = (f32[128,2048]{1,0:T(8,128)S(1)}, f32[128,2048]{1,0:T(8,128)}, u32[]{:S(2)}) copy-start(f32[128,2048]{1,0:T(8,128)} %copy-done.11) | copy-start | bytes 3145732
  599.5 158.6 %copy-start.21 = (bf16[2048,16]{1,0:T(8,128)(2,1)S(1)}, bf16[2048,16]{1,0:T(8,128)(2,1)}, u32[]{:S(2)}) copy-start(bf16[2048,16]{1,0:T(8,128)(2,1)} %copy-done.20) | copy-start | bytes 196612
  599.5 158.6 %copy-start.37 = (f32[1,8,2,128]{3,1,2,0:T(8,128)S(1)}, f32[1,8,2,128]{3,1,2,0:T(8,128)}, u32[]{:S(2)}) copy-start(f32[1,8,2,128]{3,1,2,0:T(8,128)} %copy-done.36) | copy-start | bytes 24580
  599.5 158.6 %copy-start.46 = (f32[128]{0:T(128)S(1)}, f32[128]{0:T(128)}, u32[]{:S(2)}) copy-start(f32[128]{0:T(128)} %copy-done.45) | copy-start | bytes 1540
  599.5 160.2 %copy-start.53 = (f32[128]{0:T(128)S(1)}, f32[128]{0:T(128)}, u32[]{:S(2)}) copy-start(f32[128]{0:T(128)} %copy-done.52) | copy-start | bytes 1540
  599.5 442.3 %all-gather.39.cloned.1.call-start = ((), (), s32[]{:S(2)}) async-start(), calls=%async_computation.23 | async-start | bytes 6291456 | tf_op jit(solution)/shard_map/all_gather | solution.py:176
  943.5 29.7 %copy-start.1 = (bf16[2048,192]{1,0:T(8,128)(2,1)S(1)}, bf16[2048,192]{1,0:T(8,128)(2,1)}, u32[]{:S(2)}) copy-start(bf16[2048,192]{1,0:T(8,128)(2,1)} %copy-done) | copy-start | bytes 2359300
  943.5 29.7 %copy-start.3 = (bf16[2048,192]{1,0:T(8,128)(2,1)S(1)}, bf16[2048,192]{1,0:T(8,128)(2,1)}, u32[]{:S(2)}) copy-start(bf16[2048,192]{1,0:T(8,128)(2,1)} %copy-done.2) | copy-start | bytes 2359300
  943.5 29.7 %copy-start.6 = (bf16[2048,128]{1,0:T(8,128)(2,1)S(1)}, bf16[2048,128]{1,0:T(8,128)(2,1)}, u32[]{:S(2)}) copy-start(bf16[2048,128]{1,0:T(8,128)(2,1)} %copy-done.5) | copy-start | bytes 1572868
  943.5 29.7 %copy-start.8 = (s32[1,2048]{1,0:T(1,128)S(1)}, s32[1,2048]{1,0:T(1,128)}, u32[]{:S(2)}) copy-start(s32[1,2048]{1,0:T(1,128)} %copy-done.7) | copy-start | bytes 24580
  991.1 46.6 %all-to-all-start.2 = ((bf16[16,128,512]{1,2,0:T(8,128)(2,1)}), bf16[16,128,512]{1,2,0:T(8,128)(2,1)}, u32[]{:S(2)}, u32[]{:S(2)}) async-start(bf16[16,128,512]{1,2,0:T(8,128)(2,1)} %copy.150), calls=%async_computation.4 | async-start | bytes 4194304 | tf_op jit(solution)/shard_map/all_to_all | solution.py:350
  995.6 78.4 %reduce-scatter.28.cloned.1.call-start = ((), (), s32[]{:S(2)}) async-start(), calls=%async_computation.35 | async-start | bytes 1081344 | tf_op jit(solution)/shard_map/reduce_scatter | solution.py:180
  1002.0 79.1 %reduce-scatter.20.cloned.1.call-start = ((), (), s32[]{:S(2)}) async-start(), calls=%async_computation.28 | async-start | bytes 393216 | tf_op jit(solution)/shard_map/reduce_scatter | solution.py:180
  1007.1 99.4 %reduce-scatter.26.cloned.1.call-start = ((), (), s32[]{:S(2)}) async-start(), calls=%async_computation.33 | async-start | bytes 2162688 | tf_op jit(solution)/shard_map/reduce_scatter | solution.py:180
  1015.5 102.8 %all-gather.43.cloned.1.call-start = ((), (), s32[]{:S(2)}) async-start(), calls=%async_computation.26 | async-start | bytes 2506752 | tf_op jit(solution)/shard_map/all_gather | solution.py:168
  1047.5 80.1 %reduce-scatter.16.cloned.1.call-start = ((), (), s32[]{:S(2)}) async-start(), calls=%async_computation.24 | async-start | bytes 1179648 | tf_op jit(solution)/shard_map/reduce_scatter | solution.py:180
  1054.1 149.6 %reduce-scatter.24.cloned.1.call-start = ((), (), s32[]{:S(2)}) async-start(), calls=%async_computation.32 | async-start | bytes 98304 | tf_op jit(solution)/shard_map/reduce_scatter | solution.py:180
  1059.4 145.7 %reduce-scatter.32.cloned.1.call-start = ((), (), s32[]{:S(2)}) async-start(), calls=%async_computation.38 | async-start | bytes 8650752 | tf_op jit(solution)/shard_map/reduce_scatter | solution.py:180
  1073.9 176.5 %all-gather.49.cloned.1.call-start = ((), (), s32[]{:S(2)}) async-start(), calls=%async_computation.36 | async-start | bytes 6127616 | tf_op jit(solution)/shard_map/all_gather | solution.py:168
  1074.7 200.6 %all-gather.37.cloned.1.call-start = ((), (), s32[]{:S(2)}) async-start(), calls=%async_computation.22 | async-start | bytes 18874368 | tf_op jit(solution)/shard_map/all_gather | solution.py:176
  1075.2 283.8 %reduce-scatter.22.cloned.1.call-start = ((), (), s32[]{:S(2)}) async-start(), calls=%async_computation.30 | async-start | bytes 12582912 | tf_op jit(solution)/shard_map/reduce_scatter | solution.py:180
  1081.1 281.6 %all-gather.45.cloned.1.call-start = ((), (), s32[]{:S(2)}) async-start(), calls=%async_computation.29 | async-start | bytes 2228224 | tf_op jit(solution)/shard_map/all_gather | solution.py:168
  1081.8 303.4 %reduce-scatter.30.cloned.1.call-start = ((), (), s32[]{:S(2)}) async-start(), calls=%async_computation.37 | async-start | bytes 17301504 | tf_op jit(solution)/shard_map/reduce_scatter | solution.py:180
  1106.4 424.9 %all-gather.47.cloned.1.call-start = ((), (), s32[]{:S(2)}) async-start(), calls=%async_computation.34 | async-start | bytes 12255232 | tf_op jit(solution)/shard_map/all_gather | solution.py:168
  1106.9 460.7 %reduce-scatter.18.cloned.1.call-start = ((), (), s32[]{:S(2)}) async-start(), calls=%async_computation.27 | async-start | bytes 3538944 | tf_op jit(solution)/shard_map/reduce_scatter | solution.py:180
  1127.5 513.0 %all-gather.41.cloned.1.call-start = ((), (), s32[]{:S(2)}) async-start(), calls=%async_computation.25 | async-start | bytes 6684672 | tf_op jit(solution)/shard_map/all_gather | solution.py:168
  1128.1 685.2 %all-reduce.2.cloned.1.call-start = ((), (), s32[]{:S(2)}) async-start(), calls=%async_computation.31 | async-start | bytes 8388608 | tf_op jit(solution)/shard_map/psum | solution.py:347
  (37 other events, 246.2 us)
Sparse Core Ops, SparseCore 0:
  10.8 115.5 all-gather.24
  128.5 10.3 all-gather.26
  140.4 21.0 all-gather.28
  164.1 124.6 all-gather.34
  292.0 111.1 all-gather.30
  404.6 22.0 all-gather.50
  428.2 17.1 all-gather.52
  446.9 10.7 all-gather.32
  576.4 181.6 reduce-scatter.13
  760.8 180.2 reduce-scatter.11
  942.6 16.0 all-gather.38
  1002.1 9.3 reduce-scatter.27
  1014.4 8.8 reduce-scatter.19
  1025.9 10.1 reduce-scatter.25
  1047.6 70.6 all-gather.42
  1121.1 6.4 reduce-scatter.15
  1130.2 8.5 reduce-scatter.23
  1141.5 14.9 reduce-scatter.31
  1159.6 90.7 all-gather.48
  1251.9 23.2 all-gather.36
  1278.2 17.9 reduce-scatter.21
  1299.0 63.6 all-gather.44
  1365.5 19.5 reduce-scatter.29
  1387.8 143.3 all-gather.46
  1534.0 8.0 reduce-scatter.17
  1545.2 95.2 all-gather.40
  1646.9 166.4 all-reduce.1

commit v2 on v1

--- a/solution.py
+++ b/solution.py
@@ -164,6 +164,360 @@
     )(query, key, value, grad, segment[:, None], segment[None, :], log_total)
 
 
+LINE = 4
+MESH = pl.DeviceIdType.MESH
+
+
+def place():
+    rank = lax.axis_index("seq")
+    return rank, lax.div(rank, 4), lax.rem(lax.div(rank, 2), 2), lax.rem(rank, 2)
+
+
+def rank_at(z, y, x, dz, dy, dx):
+    across = y + dy * (1 - 2 * y)
+    along = x + dx * (1 - 2 * x)
+    return (z + dz) * 4 + across * 2 + along
+
+
+OFFSETS = [(dz, dy, dx) for dz in (0, -1, 1, -2, 2, -3, 3) for dy in (0, 1) for dx in (0, 1)]
+
+
+def hops(offset):
+    return abs(offset[0]) + offset[1] + offset[2]
+
+
+def onward(order, offset):
+    rel = dict(zip("zyx", offset))
+    moved = [i for i, dim in enumerate(order) if rel[dim]]
+    last = moved[-1] if moved else -1
+    steps = []
+    if last >= 0 and order[last] == "z":
+        steps.append((1 if rel["z"] < 0 else -1, 0, 0))
+    for dim in order[last + 1 :]:
+        steps += {"z": [(1, 0, 0), (-1, 0, 0)], "y": [(0, 1, 0)], "x": [(0, 0, 1)]}[dim]
+    return [s for s in steps if any(0 <= z + offset[0] < LINE and 0 <= z + s[0] < LINE for z in range(LINE))]
+
+
+def inside(z, dz):
+    return (z + dz >= 0) & (z + dz < LINE)
+
+
+def guarded(z, steps, body):
+    steps = [dz for dz in steps if dz]
+    if not steps:
+        body()
+        return
+    good = inside(z, steps[0])
+    for dz in steps[1:]:
+        good = good & inside(z, dz)
+    pl.when(good)(body)
+
+
+def greet_all():
+    rank = lax.axis_index("seq")
+    count = lax.axis_size("seq")
+    barrier = pltpu.get_barrier_semaphore()
+    for k in range(1, count):
+        peer = lax.rem(rank + k, count)
+        pl.semaphore_signal(barrier, inc=1, device_id={"seq": peer}, device_id_type=MESH)
+    pl.semaphore_wait(barrier, count - 1)
+
+
+def gather_kernel(streams, n_main, n_small, *refs):
+    n = n_main + n_small
+    ins, outs = refs[:n], refs[n : 2 * n]
+    send_sems, recv_sems, small_send, small_recv, local_sems = refs[2 * n :]
+    rank, z, y, x = place()
+    count = lax.axis_size("seq")
+    greet_all()
+    locals_ = [pltpu.make_async_copy(ins[i], outs[i].at[rank], local_sems.at[i]) for i in range(n)]
+    slots = {}
+
+    def copy(stream, offset, step):
+        index, first, rows, order = streams[stream]
+        part = pl.ds(first, rows)
+        source = rank_at(z, y, x, *offset)
+        slot = slots.setdefault((stream, offset, step), len(slots))
+        block = outs[index].at[source, part]
+        own = offset == (0, 0, 0)
+        return pltpu.make_async_remote_copy(
+            src_ref=ins[index].at[part] if own else block,
+            dst_ref=block,
+            send_sem=send_sems.at[slot],
+            recv_sem=recv_sems.at[stream * count + source],
+            device_id={"seq": rank_at(z, y, x, *step)},
+            device_id_type=MESH,
+        )
+
+    def small_copy(i, k):
+        peer = lax.rem(rank + k, count)
+        return pltpu.make_async_remote_copy(
+            src_ref=ins[n_main + i],
+            dst_ref=outs[n_main + i].at[rank],
+            send_sem=small_send.at[i * count + k],
+            recv_sem=small_recv.at[i * count + rank],
+            device_id={"seq": peer},
+            device_id_type=MESH,
+        )
+
+    def arrived(stream, offset):
+        index, first, rows, order = streams[stream]
+        source = rank_at(z, y, x, *offset)
+        block = outs[index].at[source, pl.ds(first, rows)]
+        pltpu.make_async_remote_copy(
+            src_ref=block,
+            dst_ref=block,
+            send_sem=send_sems.at[0],
+            recv_sem=recv_sems.at[stream * count + source],
+            device_id={"seq": rank},
+            device_id_type=MESH,
+        ).wait_recv()
+
+    todo = sorted(
+        ((stream, offset) for stream in range(len(streams)) for offset in OFFSETS),
+        key=lambda it: (hops(it[1]), it[0]),
+    )
+    for stream, offset in todo:
+        def forward(stream=stream, offset=offset):
+            if hops(offset):
+                arrived(stream, offset)
+            for step in onward(streams[stream][3], offset):
+                guarded(z, [step[0]], lambda: copy(stream, offset, step).start())
+        guarded(z, [offset[0]], forward)
+        if stream == len(streams) - 1 and offset == (0, 0, 0):
+            for c in locals_:
+                c.start()
+            for i in range(n_small):
+                for k in range(1, count):
+                    small_copy(i, k).start()
+    for stream, offset in todo:
+        for step in onward(streams[stream][3], offset):
+            guarded(z, [offset[0], step[0]], lambda: copy(stream, offset, step).wait_send())
+    for i in range(n_small):
+        for k in range(1, count):
+            small_copy(i, k).wait_send()
+        for k in range(1, count):
+            source = lax.rem(rank + k, count)
+            block = outs[n_main + i].at[source]
+            pltpu.make_async_remote_copy(
+                src_ref=block, dst_ref=block, send_sem=small_send.at[0],
+                recv_sem=small_recv.at[i * count + source], device_id={"seq": rank}, device_id_type=MESH,
+            ).wait_recv()
+    for c in locals_:
+        c.wait()
+
+
+def n_sends(streams):
+    return sum(len(onward(s[3], o)) for s in streams for o in OFFSETS)
+
+
+def gather_all(main, parts, small, collective_id, count=16):
+    streams = []
+    for i, pieces in enumerate(parts):
+        first = 0
+        for rows, order in pieces:
+            streams.append((i, first, rows, order))
+            first += rows
+        assert first == main[i].shape[0]
+    arrays = list(main) + list(small)
+    any_spec = pl.BlockSpec(memory_space=pl.ANY)
+    return pl.pallas_call(
+        functools.partial(gather_kernel, streams, len(main), len(small)),
+        out_shape=tuple(jax.ShapeDtypeStruct((count,) + a.shape, a.dtype) for a in arrays),
+        in_specs=[any_spec] * len(arrays),
+        out_specs=tuple([any_spec] * len(arrays)),
+        scratch_shapes=[
+            pltpu.SemaphoreType.DMA((n_sends(streams),)),
+            pltpu.SemaphoreType.DMA((len(streams) * count,)),
+            pltpu.SemaphoreType.DMA((max(1, len(small)) * count,)),
+            pltpu.SemaphoreType.DMA((max(1, len(small)) * count,)),
+            pltpu.SemaphoreType.DMA((len(arrays),)),
+        ],
+        compiler_params=pltpu.CompilerParams(collective_id=collective_id, has_side_effects=True),
+        name="gather_all",
+    )(*arrays)
+
+
+def toward(order, offset):
+    rel = dict(zip("zyx", offset))
+    dim = [d for d in order if rel[d]][-1]
+    return {"z": (1 if rel["z"] > 0 else -1, 0, 0), "y": (0, 1, 0), "x": (0, 0, 1)}[dim]
+
+
+def seen_from(offset, step):
+    return (offset[0] - step[0], offset[1] ^ step[1], offset[2] ^ step[2])
+
+
+def back(step):
+    return (-step[0], step[1], step[2])
+
+
+ADD_ROWS = 16
+
+
+def scatter_kernel(streams, n_main, n_small, *refs):
+    n = n_main + n_small
+    ins, outs = refs[:n], refs[n : 2 * n]
+    scratch = refs[2 * n :]
+    bufs, accs = scratch[: len(streams)], scratch[len(streams) : 2 * len(streams)]
+    send_sems, recv_sems, small_send, small_recv, local_sems = scratch[2 * len(streams) :]
+    rank, z, y, x = place()
+    count = lax.axis_size("seq")
+    slot_of, acc_of = {}, {}
+    for s, stream in enumerate(streams):
+        k = 0
+        a = 0
+        for offset in OFFSETS:
+            for step in onward(stream[3], offset):
+                slot_of[s, offset, step] = (k, len(slot_of))
+                k += 1
+            if hops(offset) and onward(stream[3], offset):
+                acc_of[s, offset] = a
+                a += 1
+    greet_all()
+
+    def small_copy(i, k):
+        peer = lax.rem(rank + k, count)
+        return pltpu.make_async_remote_copy(
+            src_ref=ins[n_main + i],
+            dst_ref=outs[n_main + i].at[rank],
+            send_sem=small_send.at[i * count + k],
+            recv_sem=small_recv.at[i * count + rank],
+            device_id={"seq": peer},
+            device_id_type=MESH,
+        )
+
+    todo = sorted(
+        ((s, offset) for s in range(len(streams)) for offset in OFFSETS),
+        key=lambda it: (-hops(it[1]), it[0]),
+    )
+    send_slot = {key: i for i, key in enumerate(k for k in todo if hops(k[1]))}
+
+    def send_copy(s, offset, source):
+        order = streams[s][3]
+        step = toward(order, offset)
+        k, sem = slot_of[s, seen_from(offset, step), back(step)]
+        return pltpu.make_async_remote_copy(
+            src_ref=source,
+            dst_ref=bufs[s].at[k],
+            send_sem=send_sems.at[send_slot[s, offset]],
+            recv_sem=recv_sems.at[sem],
+            device_id={"seq": rank_at(z, y, x, *step)},
+            device_id_type=MESH,
+        )
+
+    def wait_child(s, offset, step):
+        k, sem = slot_of[s, offset, step]
+        pltpu.make_async_remote_copy(
+            src_ref=bufs[s].at[k],
+            dst_ref=bufs[s].at[k],
+            send_sem=send_sems.at[0],
+            recv_sem=recv_sems.at[sem],
+            device_id={"seq": rank},
+            device_id_type=MESH,
+        ).wait_recv()
+
+    for s, offset in todo:
+        index, first, rows, order = streams[s]
+        children = onward(order, offset)
+        dest = rank_at(z, y, x, *offset)
+        always = [c for c in children if not c[0]]
+        sometimes = [c for c in children if c[0]]
+
+        def run(present, s=s, offset=offset, index=index, first=first, rows=rows, dest=dest):
+            own = ins[index].at[dest, pl.ds(first, rows)]
+            if not present:
+                send_copy(s, offset, own).start()
+                return
+            for step in present:
+                wait_child(s, offset, step)
+            final = not hops(offset)
+            target = outs[index].at[pl.ds(first, rows)] if final else accs[s].at[acc_of[s, offset]]
+            slots = [slot_of[s, offset, step][0] for step in present]
+
+            def add(i, carry):
+                part = pl.ds(pl.multiple_of(i * ADD_ROWS, ADD_ROWS), ADD_ROWS)
+                total = own[part, :].astype(F32)
+                for k in slots:
+                    total = total + bufs[s][k, part, :].astype(F32)
+                target[part, :] = total.astype(target.dtype)
+                return carry
+
+            lax.fori_loop(0, rows // ADD_ROWS, add, 0)
+            if not final:
+                send_copy(s, offset, target).start()
+
+        def cases(run=run, always=always, sometimes=sometimes):
+            if not sometimes:
+                run(always)
+                return
+            for mask in range(2 ** len(sometimes)):
+                present = [c for i, c in enumerate(sometimes) if mask >> i & 1]
+                good = None
+                for i, c in enumerate(sometimes):
+                    here = inside(z, c[0]) if mask >> i & 1 else jnp.logical_not(inside(z, c[0]))
+                    good = here if good is None else good & here
+                pl.when(good)(functools.partial(run, present + always))
+
+        guarded(z, [offset[0]], cases)
+        if (s, offset) == todo[0]:
+            for i in range(n_small):
+                for k in range(1, count):
+                    small_copy(i, k).start()
+                pltpu.make_async_copy(ins[n_main + i], outs[n_main + i].at[rank], local_sems.at[i]).start()
+    for s, offset in todo:
+        if hops(offset):
+            index, first, rows, order = streams[s]
+            own = ins[index].at[rank_at(z, y, x, *offset), pl.ds(first, rows)]
+            guarded(z, [offset[0]], lambda: send_copy(s, offset, own).wait_send())
+    for i in range(n_small):
+        for k in range(1, count):
+            small_copy(i, k).wait_send()
+        for k in range(1, count):
+            source = lax.rem(rank + k, count)
+            block = outs[n_main + i].at[source]
+            pltpu.make_async_remote_copy(
+                src_ref=block, dst_ref=block, send_sem=small_send.at[0],
+                recv_sem=small_recv.at[i * count + source], device_id={"seq": rank}, device_id_type=MESH,
+            ).wait_recv()
+        pltpu.make_async_copy(ins[n_main + i], outs[n_main + i].at[rank], local_sems.at[i]).wait()
+
+
+def scatter_sum(main, parts, small, collective_id, count=16):
+    streams = []
+    for i, pieces in enumerate(parts):
+        first = 0
+        for rows, order in pieces:
+            streams.append((i, first, rows, order))
+            first += rows
+        assert first == main[i].shape[1]
+    arrays = list(main) + list(small)
+    any_spec = pl.BlockSpec(memory_space=pl.ANY)
+    vmem = pl.BlockSpec(memory_space=pltpu.VMEM)
+    buffers, sums = [], []
+    for index, first, rows, order in streams:
+        columns = main[index].shape[2]
+        slots = sum(len(onward(order, o)) for o in OFFSETS)
+        held = sum(1 for o in OFFSETS if hops(o) and onward(order, o))
+        buffers.append(pltpu.VMEM((slots, rows, columns), main[index].dtype))
+        sums.append(pltpu.VMEM((held, rows, columns), main[index].dtype))
+    return pl.pallas_call(
+        functools.partial(scatter_kernel, streams, len(main), len(small)),
+        out_shape=tuple([jax.ShapeDtypeStruct(a.shape[1:], F32) for a in main] + [jax.ShapeDtypeStruct((count,) + a.shape, a.dtype) for a in small]),
+        in_specs=[vmem] * len(main) + [any_spec] * len(small),
+        out_specs=tuple([vmem] * len(main) + [any_spec] * len(small)),
+        scratch_shapes=buffers + sums + [
+            pltpu.SemaphoreType.DMA((len(streams) * len(OFFSETS),)),
+            pltpu.SemaphoreType.DMA((n_sends(streams),)),
+            pltpu.SemaphoreType.DMA((max(1, len(small)) * count,)),
+            pltpu.SemaphoreType.DMA((max(1, len(small)) * count,)),
+            pltpu.SemaphoreType.DMA((max(1, len(small)),)),
+        ],
+        compiler_params=pltpu.CompilerParams(collective_id=collective_id, has_side_effects=True, vmem_limit_bytes=60 * 2**20),
+        name="scatter_sum",
+    )(*arrays)
+
+
 def gather_seq(rows):
     return lax.all_gather(rows, "seq", axis=0, tiled=True)
 
@@ -178,6 +532,24 @@
 
 def scatter_fsdp(partial, axis=0):
     return lax.psum_scatter(partial, "fsdp", scatter_dimension=axis, tiled=True)
+
+
+def shift_fsdp(rows, k):
+    count = lax.axis_size("fsdp")
+    return lax.ppermute(rows, "fsdp", [(i, (i + k) % count) for i in range(count)])
+
+
+ROW_PARTS = [(48, "zxy"), (48, "zyx"), (16, "xyz"), (16, "yxz")]
+
+
+def split_rows(rows):
+    tile = 16
+    tiles = rows // tile
+    short = tiles // 8
+    long = (tiles - 2 * short) // 2
+    sizes = [tiles - 2 * short - long, long, short, short]
+    orders = ["zxy", "zyx", "xyz", "yxz"]
+    return [(n * tile, order) for n, order in zip(sizes, orders) if n]
 
 
 def on_device(
@@ -215,8 +587,10 @@
     def own(rows, axis=0):
         return lax.dynamic_slice_in_dim(rows, rank * tok_count, tok_count, axis)
 
-    token_all = gather_seq(tokens)
-    routes_all = gather_seq(routes)
+    expert_ids = jnp.arange(experts, dtype=jnp.int32)
+    route_mask = jnp.any(routes[None] == expert_ids[:, None, None], axis=2).astype(BF16)
+    token_all, mask_all = gather_all([tokens], [ROW_PARTS], [route_mask], 1)
+    token_all = token_all.reshape(group_size, D)
     cotangent_all = gather_seq(cotangent)
 
     small = gather_fsdp(jnp.concatenate([g_attn, g_kv, g_ffn, w_router.reshape(-1)])[None])
@@ -227,9 +601,13 @@
     gain_ffn = small[:, ends[2] : ends[3]].reshape(-1).astype(F32)
     router_weight = small[:, ends[3] : ends[4]].reshape(D, experts)
     head_query_part = lax.dynamic_slice_in_dim(w_q, rank * query_width, query_width, 1)
-    shared_in_part = lax.dynamic_slice_in_dim(
-        w_shared_in.reshape(row_part, 2, fsdp_count, seq_count, unit), rank, 1, 3
-    ).reshape(row_part, 2 * units)
+    shared_in_part = jnp.concatenate(
+        [
+            lax.dynamic_slice_in_dim(w_shared_in, i * (SH // fsdp_count) + rank * unit, unit, 1)
+            for i in range(2 * fsdp_count)
+        ],
+        axis=1,
+    )
     head_expand = gather_fsdp(lax.dynamic_slice_in_dim(w_kvb, rank * kv_width, kv_width, 1))
     head_weights = gather_fsdp(jnp.concatenate([w_kva, head_query_part], axis=1))
     latent_weight = head_weights[:, : KVR + DR]
@@ -257,17 +635,19 @@
     key = jnp.concatenate([expanded[:, :DN], key_rope], axis=1).astype(BF16)
     value = expanded[:, DN:].astype(BF16)
     context, log_total, head_largest = attention_forward(query, key, value, segment, valid_all)
-    largest_all = lax.all_gather(head_largest[:1], ("fsdp", "seq"), axis=0, tiled=False)
-    global_max = jnp.max(largest_all.reshape(fsdp_count, seq_count, -1)[:, :, 0], axis=0)
-
     context_low = lax.all_to_all(context, "seq", split_axis=0, concat_axis=1, tiled=True)
     inputs = tokens.astype(F32)
     middle = inputs + dot(context_low, output_weight)
     ffn_low = rms_norm(middle, gain_ffn).astype(BF16)
-    ffn_all = gather_seq(ffn_low)
+    ffn_all, largest_all = gather_all([ffn_low], [ROW_PARTS], [head_largest], 2)
+    ffn_all = ffn_all.reshape(group_size, D)
+    head_max = largest_all[:, 0, :]
+    for k in range(1, fsdp_count):
+        head_max = jnp.maximum(head_max, shift_fsdp(largest_all[:, 0, :], k))
+    global_max = head_max[:, 0]
 
     router_probs = jax.nn.softmax(dot(ffn_all, router_weight), axis=-1)
-    chosen = jnp.any(routes_all == rank, axis=1).reshape(seq_count, tok_count)
+    chosen = lax.dynamic_slice_in_dim(mask_all, rank, 1, 1).reshape(seq_count, tok_count) > 0
     gates = lax.dynamic_slice_in_dim(router_probs, rank, 1, 1).reshape(seq_count, tok_count)
     place = jnp.cumsum(chosen.astype(jnp.int32), axis=1) - 1
     place = jnp.where(chosen, place, capacity)
@@ -304,8 +684,7 @@
     upstream_all = jnp.where(valid_all[:, None], cotangent_all, 0).astype(BF16)
     upstream_rows = to_slots(upstream_all)
     row_gate_grad = jnp.sum(upstream_rows * result, axis=1).reshape(seq_count, capacity)
-    gate_grad = jnp.sum(jnp.where(picks, row_gate_grad[:, :, None], 0.0), axis=1).reshape(1, group_size)
-    prob_grads = gather_seq(gate_grad).T
+    gate_grad = jnp.sum(jnp.where(picks, row_gate_grad[:, :, None], 0.0), axis=1)
     result_grad = (row_gate * upstream_rows).astype(BF16)
     d_hidden = dot_nt(result_grad, expert_out)
     grad_expert_out = dot_tn(hidden, result_grad)
@@ -315,26 +694,23 @@
     shared_hidden_grad = dot_nt(upstream_all, shared_out)
     shared_grad = silu_back(shared_both[:, :units], shared_both[:, units:], shared_hidden_grad).astype(BF16)
     ffn_part = to_tokens(row_grad) + dot_nt(shared_grad, shared_in)
-    ffn_sum = scatter_seq(ffn_part.astype(BF16))
+    ffn_sum, prob_grads = scatter_sum(
+        [ffn_part.astype(BF16).reshape(seq_count, tok_count, D)], [ROW_PARTS], [gate_grad], 3
+    )
+    prob_grads = prob_grads.reshape(experts, group_size).T
     grad_shared_out = dot_tn(shared_hidden, upstream_all)
     grad_shared_in = dot_tn(shared_grad, ffn_all)
     sum_expert_in = scatter_fsdp(grad_expert_in.astype(BF16)).astype(F32)[None]
     sum_expert_out = scatter_fsdp(grad_expert_out.astype(BF16)).astype(F32)[None]
-    sum_shared_out = gather_seq(scatter_fsdp(grad_shared_out.astype(BF16))).astype(F32)
-    sum_shared_in = gather_seq(scatter_fsdp(grad_shared_in.astype(BF16), 1))
-    sum_shared_in = (
-        sum_shared_in.reshape(seq_count, 2, fsdp_count, unit, row_part)
-        .transpose(4, 1, 2, 0, 3)
-        .reshape(row_part, 2 * SH)
-        .astype(F32)
-    )
+    part_shared_out = scatter_fsdp(grad_shared_out.astype(BF16))
+    part_shared_in = scatter_fsdp(grad_shared_in.astype(BF16), 1)
 
     logit_grads = (
         router_probs * (prob_grads - jnp.sum(router_probs * prob_grads, axis=-1, keepdims=True))
     ).astype(BF16)
     grad_router = dot_tn(ffn_all, logit_grads)
     sum_router = scatter_fsdp(grad_router.astype(BF16)).astype(F32)
-    ffn_grad = ffn_sum.astype(F32) + dot_nt(own(logit_grads), router_weight)
+    ffn_grad = ffn_sum + dot_nt(own(logit_grads), router_weight)
 
     ffn_pull = jax.vjp(rms_norm, middle, gain_ffn)[1]
     middle_norm_grad, grad_gain_ffn = ffn_pull(ffn_grad)
@@ -344,7 +720,7 @@
     context_grad = dot_nt(middle_low, output_weight).astype(BF16)
     head_grad = lax.all_to_all(context_grad, "seq", split_axis=1, concat_axis=0, tiled=True)
     grad_output = scatter_fsdp(dot_tn(context_low, middle_low).astype(BF16))
-    sum_output = lax.psum(grad_output, "seq").astype(F32)
+    part_output = scatter_seq(grad_output)
 
     query_grad, key_grad, value_grad = attention_backward(query, key, value, head_grad, segment, log_total)
     back = lax.all_to_all(
@@ -358,11 +734,9 @@
     head_pre_grad = jnp.concatenate(
         [query_grad_32[:, :DN], rotate(query_grad_32[:, DN:], -angles_all)], axis=1
     ).astype(BF16)
-    grad_query = scatter_fsdp(dot_tn(head_pre_grad, normed_all).astype(BF16), 1)
-    sum_query = gather_seq(grad_query).T.astype(F32)
+    part_query = scatter_fsdp(dot_tn(head_pre_grad, normed_all).astype(BF16), 1)
     head_expand_grad = jnp.concatenate([key_grad[:, :DN], value_grad], axis=1)
-    grad_expand = scatter_fsdp(dot_tn(head_expand_grad, latent_all).astype(BF16), 1)
-    sum_expand = gather_seq(grad_expand).T.astype(F32)
+    part_expand = scatter_fsdp(dot_tn(head_expand_grad, latent_all).astype(BF16), 1)
 
     back = back.transpose(1, 0, 2)
     back_query = back[..., :query_width].astype(F32)
@@ -386,8 +760,27 @@
     input_norm_grad, grad_gain_attn = input_pull(normed_grad)
     grad_inputs = middle_grad + input_norm_grad
 
-    gain_grads = jnp.concatenate([grad_gain_attn, grad_gain_latent, grad_gain_ffn])
-    gain_sum = jnp.sum(lax.all_gather(gain_grads[None], ("fsdp", "seq"), axis=0, tiled=True), axis=0)
+    gain_grads = jnp.concatenate([grad_gain_attn, grad_gain_latent, grad_gain_ffn]).reshape(-1, 128)
+    gain_grads = jnp.pad(gain_grads, ((0, -gain_grads.shape[0] % 8), (0, 0)))
+    part_shared_out = jnp.pad(part_shared_out, ((0, -unit % 16), (0, 0)))
+    weight_parts = [part_shared_in, part_query, part_shared_out, part_output, part_expand]
+    *sums, gain_all = gather_all(weight_parts, [split_rows(p.shape[0]) for p in weight_parts], [gain_grads], 4)
+    sum_shared_in = (
+        sums[0]
+        .reshape(seq_count, 2, fsdp_count, unit, row_part)
+        .transpose(4, 1, 2, 0, 3)
+        .reshape(row_part, 2 * SH)
+        .astype(F32)
+    )
+    sum_query = sums[1].reshape(-1, row_part).T.astype(F32)
+    sum_shared_out = sums[2][:, :unit].reshape(w_shared_out.shape).astype(F32)
+    sum_output = sums[3].reshape(w_o.shape).astype(F32)
+    sum_expand = sums[4].reshape(-1, w_kvb.shape[0]).T.astype(F32)
+    gain_seq = jnp.sum(gain_all, axis=0)
+    gain_sum = gain_seq
+    for k in range(1, fsdp_count):
+        gain_sum = gain_sum + shift_fsdp(gain_seq, k)
+    gain_sum = gain_sum.reshape(-1)
     fsdp_rank = lax.axis_index("fsdp")
 
     def own_part(first, like):

time: 1840 us -> 1410 us (0.77)
  waiting for transfers between devices: 989 us -> 273 us
  Pallas kernels: 20 us -> 558 us
  blocking collectives: 260 us -> 29.7 us
    pallas_call x0 -> x4, Pallas kernels: none -> 539 us  [the longest x3 393 us: gather_all(): pl.pallas_call(functools.partial(gather_kernel, streams, len(main), len(s...]
    all_gather x8 -> x2, waiting for transfers between devices: 455 us -> 12.7 us  [gather_seq(): return lax.all_gather(rows, 'seq', axis=0, tiled=True)]
    all_gather x4 -> x0, blocking collectives: 230 us -> none  [the longest x2 89.5 us: gather_seq(): return lax.all_gather(rows, 'seq', axis=0, tiled=True)]
    reduce_scatter x2, waiting for transfers between devices: 297 us -> 114 us  [scatter_seq(): return lax.psum_scatter(partial, 'seq', scatter_dimension=0, tiled=True)]
    psum x1 -> x0, waiting for transfers between devices: 151 us -> none  [on_device(): sum_output = lax.psum(grad_output, 'seq').astype(F32)]
    reduce_scatter x9, waiting for transfers between devices: 13.1 us -> 67.5 us  [scatter_fsdp(): return lax.psum_scatter(partial, 'fsdp', scatter_dimension=axis, tiled=True)]
    unnamed x132 -> x153, local copies, waits for them, and re-layouts: 77.6 us -> 42.3 us
  transfers between devices with their start and end apart: 29 -> 24, of which waited for: 15 -> 13; matrix products, arithmetic and copies ran while one was open for 27% -> 29% of each run, Pallas kernels for 1% -> 22%
where the time goes in v2:
time: 1410 us; the launch traced here: 1400 us
  Pallas kernels  558 us (40%)
  matrix products  295 us (21%)
  waiting for transfers between devices  273 us (19%)
  other arithmetic  126 us (9%)
  local copies, waits for them, and re-layouts  96.9 us (7%)
  blocking collectives  29.7 us (2%)
  between operations  16 us (1%)
    pallas_call x3, Pallas kernels, gather_all(): pl.pallas_call(functools.partial(gather_kernel, streams, len(main), len(s...  393 us
    pallas_call x1, Pallas kernels, scatter_sum(): pl.pallas_call(functools.partial(scatter_kernel, streams, len(main), len(...  146 us
    reduce_scatter x2, waiting for transfers between devices, scatter_seq(): return lax.psum_scatter(partial, 'seq', scatter_dimension=0, tiled=True)  114 us
    dot_general x9, matrix products, dot_nt(): lax.dot_general(left, right, (((1,), (1,)), ((), ())), preferred_element_...  88.9 us
    dot_general x9, matrix products, dot(): return jnp.dot(left, right, preferred_element_type=F32)  88.2 us
    dot_general x9, matrix products, dot_tn(): lax.dot_general(left, right, (((0,), (0,)), ((), ())), preferred_element_...  86.6 us
    reduce_scatter x9, waiting for transfers between devices, scatter_fsdp(): return lax.psum_scatter(partial, 'fsdp', scatter_dimension=axis, tiled=True)  67.5 us
    unnamed x153, local copies, waits for them, and re-layouts  42.3 us
  transfers between devices with their start and end apart: 24, of which 13 were waited for; matrix products, arithmetic and copies ran while one was open for 29% of the time, Pallas kernels for 22%

profile of v2, /device:TPU:0, one launch (start us, length us, event | category | flops | bytes accessed | tf_op | source)
XLA Modules:
  0.0 1403.6 jit_solution(18298841222138363939)
XLA Ops:
  21.1 74.1 %gather_all.3 = (bf16[16,128,2048]{2,1,0:T(8,128)(2,1)}, bf16[16,16,128]{2,1,0:T(8,128)(2,1)}) custom-call(bf16[128,2048]{1,0:T(8,128)(2,1)} %refs_0_.1, bf16[16,128]{1,0:T(8,128)(2,1)} %convert_element_type.231.refs_1_), custom_call_target="tpu_custom_call" | custom-call | tf_op jit(solution)/shard_map/gather_all/pallas_call | solution.py:324
  106.1 9.0 fusion.3
  115.9 8.5 fusion.18
  142.6 7.6 fusion.44
  151.0 8.2 attention_forward.1
  171.4 18.0 %all-to-all-done = bf16[16,128,128]{1,2,0:T(8,128)(2,1)S(1)} async-done(((bf16[16,128,128]{1,2,0:T(8,128)(2,1)}), bf16[16,128,128]{1,2,0:T(8,128)(2,1)S(1)}, u32[]{:S(2)}, u32[]{:S(2)}) %all-to-all-start) | async-done | bytes 524320 | tf_op jit(solution)/shard_map/all_to_all | solution.py:638
  196.2 77.4 %gather_all.4 = (bf16[16,128,2048]{2,1,0:T(8,128)(2,1)}, f32[16,8,128]{2,1,0:T(8,128)}) custom-call(bf16[128,2048]{1,0:T(8,128)(2,1)} %multiply_convert_fusion.8.refs_0_, f32[8,128]{1,0:T(8,128)} %copy-done.9), custom_call_target="tpu_custom_call" | custom-call | tf_op jit(solution)/shard_map/gather_all/pallas_call | solution.py:324
  284.7 8.6 fusion.108
  293.3 23.6 %fusion.9 = f32[1536,2816]{1,0:T(8,128)S(1)} fusion(bf16[1536,2048]{1,0:T(8,128)(2,1)} %bitcast.194, bf16[1,2048,2816]{2,1,0:T(8,128)(2,1)} %all-gather.28.cloned.1.call-done), kind=kOutput, calls=%fused_computation.17 | convolution fusion | flops 17716740096 | bytes 35127296 | tf_op jit(solution)/shard_map/dot_general | solution.py:77
  327.2 7.4 broadcast_select_fusion
  334.6 9.9 fusion.64
  344.5 17.1 %fusion.5 = (f32[1536]{0:T(1024)S(1)}, bf16[1536,2048]{1,0:T(8,128)(2,1)}) fusion(f32[16,96,2048]{2,1,0:T(8,128)} %fusion.64, bf16[1536,1408]{1,0:T(8,128)(2,1)} %multiply_convert_fusion.3, bf16[1,1408,2048]{2,1,0:T(8,128)(2,1)} %all-gather.30.cloned.1.call-done), kind=kOutput, calls=%fused_computation.11 | convolution fusion | flops 8870950912 | bytes 28973056 | tf_op jit(solution)/shard_map/dot_general | solution.py:77
  362.7 11.2 fusion.6
  373.9 8.2 fusion.65
  386.6 11.8 fusion.1
  398.4 22.4 %multiply_convert_fusion.2 = (bf16[1536,1408]{1,0:T(8,128)(2,1)}, bf16[1536,1408]{1,0:T(8,128)(2,1)}) fusion(f32[1536,2816]{1,0:T(8,128)} %copy-done.12, bf16[1536,2048]{1,0:T(8,128)(2,1)} %get-tuple-element.163, bf16[1,1408,2048]{2,1,0:T(8,128)(2,1)} %all-gather.30.cloned.1.call-done), kind=kOutput, calls=%fused_computation.22 | convolution fusion | flops 8886484992 | bytes 38010880 | tf_op jit(solution)/shard_map/dot_general | solution.py:85
  420.8 23.9 %fusion.11 = bf16[1536,2048]{1,0:T(8,128)(2,1)S(1)} fusion(bf16[1,2048,2816]{2,1,0:T(8,128)(2,1)} %all-gather.28.cloned.1.call-done, bf16[1536,1408]{1,0:T(8,128)(2,1)} %get-tuple-element.127, bf16[1536,1408]{1,0:T(8,128)(2,1)} %get-tuple-element.126), kind=kOutput, calls=%fused_computation.26 | convolution fusion | flops 17737187328 | bytes 26476544 | tf_op jit(solution)/shard_map/dot_general | solution.py:85
  444.7 8.5 fusion.63
  453.2 14.8 %fusion = bf16[2048,2048]{1,0:T(8,128)(2,1)} fusion(f32[16,128,2048]{2,1,0:T(8,128)} %fusion.63, bf16[2048,352]{1,0:T(8,128)(2,1)} %all-gather.18.cloned.1.call-done, bf16[2048,176]{0,1:T(8,128)(2,1)} %get-tuple-element.135, bf16[2048,176]{0,1:T(8,128)(2,1)} %get-tuple-element.134), kind=kOutput, calls=%fused_computation.1 | convolution fusion | flops 2964062208 | bytes 28049408 | tf_op jit(solution)/shard_map/dot_general | solution.py:85
  468.1 145.8 %scatter_sum.1 = (f32[128,2048]{1,0:T(8,128)}, f32[16,16,128]{2,1,0:T(8,128)}) custom-call(bf16[16,128,2048]{2,1,0:T(8,128)(2,1)} %bitcast.193, f32[16,128]{1,0:T(8,128)} %get-tuple-element.119.refs_1_), custom_call_target="tpu_custom_call" | custom-call | tf_op jit(solution)/shard_map/scatter_sum/pallas_call | solution.py:504
  617.6 15.7 %reduce-scatter.12.cloned.1.call-done = bf16[128,2048]{1,0:T(8,128)(2,1)} async-done(((bf16[2048,2048]{1,0:T(8,128)(2,1)}), bf16[128,2048]{1,0:T(8,128)(2,1)}) %reduce-scatter.12.cloned.1.call-update) | async-done | bytes 524304 | tf_op jit(solution)/shard_map/reduce_scatter | solution.py:526
  635.7 6.7 fusion.34
  642.6 22.5 %all_to_all.43 = bf16[128,16,128]{2,0,1:T(8,128)(2,1)S(1)} all-to-all(bf16[128,16,128]{2,0,1:T(8,128)(2,1)S(1)} %bitcast.204), channel_id=1, replica_groups=mesh['seq'=16,'fsdp'=2] {'seq'}, dimensions={1} | all-to-all | bytes 1048576 | tf_op jit(solution)/shard_map/all_to_all | solution.py:721
  665.1 11.3 attention_backward.1
  695.2 34.1 %all-to-all-done.2 = bf16[16,128,512]{1,2,0:T(8,128)(2,1)} async-done(((bf16[16,128,512]{1,2,0:T(8,128)(2,1)}), bf16[16,128,512]{1,2,0:T(8,128)(2,1)}, u32[]{:S(2)}, u32[]{:S(2)}) %all-to-all-start.2) | async-done | bytes 2097184 | tf_op jit(solution)/shard_map/all_to_all | solution.py:726
  742.7 7.0 convolution_convert_fusion.3
  761.5 14.2 %convolution_convert_fusion.1 = bf16[1408,2048]{1,0:T(8,128)(2,1)} fusion(bf16[1536,1408]{1,0:T(8,128)(2,1)} %multiply_convert_fusion.3, bf16[1536,2048]{1,0:T(8,128)(2,1)} %get-tuple-element.163), kind=kOutput, calls=%fused_computation.27 | convolution fusion | flops 8861253632 | bytes 16384000 | tf_op jit(solution)/shard_map/dot_general | solution.py:81
  776.4 24.5 %convolution_convert_fusion = bf16[2048,2816]{1,0:T(8,128)(2,1)} fusion(bf16[1536,2048]{1,0:T(8,128)(2,1)} %bitcast.195, bf16[1536,1408]{1,0:T(8,128)(2,1)} %get-tuple-element.127, bf16[1536,1408]{1,0:T(8,128)(2,1)} %get-tuple-element.126), kind=kOutput, calls=%fused_computation.19 | convolution fusion | flops 17739808768 | bytes 26476544 | tf_op jit(solution)/shard_map/dot_general | solution.py:81
  800.9 12.7 all-gather.26.cloned.1.call-done
  813.5 9.2 convolution_convert_fusion.5
  822.8 10.3 convolution_convert_fusion.6
  846.7 7.2 multiply_convert_fusion
  857.0 16.0 %reduce-scatter.32.cloned.1.call-done = bf16[704,2048]{1,0:T(8,128)(2,1)} async-done(((bf16[1408,2048]{1,0:T(8,128)(2,1)}), bf16[704,2048]{1,0:T(8,128)(2,1)}) %reduce-scatter.32.cloned.1.call-update) | async-done | bytes 2883600 | tf_op jit(solution)/shard_map/reduce_scatter | solution.py:534
  879.7 20.9 %all-gather.22.cloned.1.call-done = bf16[2048,3072]{1,0:T(8,128)(2,1)} async-done(((bf16[1024,3072]{1,0:T(8,128)(2,1)}), bf16[2048,3072]{1,0:T(8,128)(2,1)}) %all-gather.22.cloned.1.call-update) | async-done | bytes 12582928 | tf_op jit(solution)/shard_map/all_gather | solution.py:530
  900.6 9.0 fusion.109
  912.5 12.4 reduce-scatter.30.cloned.1.call-done
  924.9 7.9 bitcast_convert_fusion.1
  941.8 9.8 reduce-scatter.14.cloned.1.call-done.refs_0_
  951.6 11.1 reduce-scatter.24.cloned.1.call-done.refs_4_
  962.7 12.3 reduce-scatter.16.cloned.1.call-done.refs_1_
  975.0 98.5 %reduce-scatter.22.cloned.1.call-done.refs_3_ = bf16[64,2048]{1,0:T(8,128)(2,1)} async-done(((bf16[1024,2048]{1,0:T(8,128)(2,1)}), bf16[64,2048]{1,0:T(8,128)(2,1)}) %reduce-scatter.22.cloned.1.call-update) | async-done | bytes 262160 | tf_op jit(solution)/shard_map/reduce_scatter | solution.py:526
  1073.5 241.3 %gather_all.5 = (bf16[16,352,1024]{2,1,0:T(8,128)(2,1)}, bf16[16,192,1024]{2,1,0:T(8,128)(2,1)}, bf16[16,96,2048]{2,1,0:T(8,128)(2,1)}, bf16[16,64,2048]{2,1,0:T...) custom-call(bf16[352,1024]{1,0:T(8,128)(2,1)} %reduce-scatter.14.cloned.1.call-done.refs_0_, ...), custom_call_target="tpu_custom_call" | custom-call | tf_op jit(solution)/shard_map/gather_all/pallas_call | solution.py:324
  1314.8 9.3 bitcast_convert_fusion
  1325.1 6.4 bitcast_convert_fusion.2
  1334.0 6.7 bitcast_convert_fusion.3
  1340.7 12.7 copy.174
  1353.4 23.5 %copy.175 = f32[1024,5632]{1,0:T(8,128)} copy(f32[1024,5632]{0,1:T(8,128)} %bitcast.188) | data formatting | bytes 46137344
  1376.8 12.6 copy.172
  (327 shorter events, 186.2 us)
Async XLA Ops:
  7.2 108.7 %all-gather.14.cloned.1.call-start = ((), (), s32[]{:S(2)}) async-start(), calls=%async_computation.14 | async-start | bytes 4718592 | tf_op jit(solution)/shard_map/all_gather | solution.py:530
  11.4 178.0 %all-gather.16.cloned.1.call-start = ((), (), s32[]{:S(2)}) async-start(), calls=%async_computation.15 | async-start | bytes 12582912 | tf_op jit(solution)/shard_map/all_gather | solution.py:530
  12.1 272.6 %all-gather.18.cloned.1.call-start = ((), (), s32[]{:S(2)}) async-start(), calls=%async_computation.16 | async-start | bytes 2359296 | tf_op jit(solution)/shard_map/all_gather | solution.py:530
  15.6 277.8 %all-gather.28.cloned.1.call-start = ((), (), s32[]{:S(2)}) async-start(), calls=%async_computation.32 | async-start | bytes 17301504 | tf_op jit(solution)/shard_map/all_gather | solution.py:530
  16.1 311.0 %all-gather.20.cloned.1.call-start = ((), (), s32[]{:S(2)}) async-start(), calls=%async_computation.18 | async-start | bytes 8912896 | tf_op jit(solution)/shard_map/all_gather | solution.py:522
  16.7 327.8 %all-gather.30.cloned.1.call-start = ((), (), s32[]{:S(2)}) async-start(), calls=%async_computation.33 | async-start | bytes 8650752 | tf_op jit(solution)/shard_map/all_gather | solution.py:530
  17.8 124.8 %copy-start.56 = (f32[32]{0:T(128)}, f32[32]{0:T(128)S(1)}, u32[]{:S(2)}) copy-start(f32[32]{0:T(128)S(1)} %negate_power_fusion) | copy-start | bytes 388
  20.4 85.6 %copy-start.39 = (f32[1,8,2,128]{3,1,2,0:T(8,128)}, f32[1,8,2,128]{3,1,2,0:T(8,128)S(1)}, u32[]{:S(2)}) copy-start(f32[1,8,2,128]{3,1,2,0:T(8,128)S(1)} %copy.203) | copy-start | bytes 24580
  100.3 42.3 %copy-start.45 = (f32[2048]{0:T(1024)}, f32[2048]{0:T(1024)S(1)}, u32[]{:S(2)}) copy-start(f32[2048]{0:T(1024)S(1)} %select_convert_fusion) | copy-start | bytes 24580
  103.6 32.8 %copy-start.48 = (f32[1,2,2,128]{3,1,2,0:T(2,128)}, f32[1,2,2,128]{3,1,2,0:T(2,128)S(1)}, u32[]{:S(2)}) copy-start(f32[1,2,2,128]{3,1,2,0:T(2,128)S(1)} %copy.190) | copy-start | bytes 6148
  104.3 46.6 %copy-start.4 = (s32[2048,1]{1,0:T(8,128)}, s32[2048,1]{1,0:T(8,128)S(1)}, u32[]{:S(2)}) copy-start(s32[2048,1]{1,0:T(8,128)S(1)} %add_select_fusion.segc_ref) | copy-start | bytes 24580
  104.3 46.6 %copy-start.7 = (s32[1,2048]{1,0:T(1,128)}, s32[1,2048]{1,0:T(1,128)S(1)}, u32[]{:S(2)}) copy-start(s32[1,2048]{1,0:T(1,128)S(1)} %reshape_select_fusion.segr_ref) | copy-start | bytes 24580
  105.7 88.7 %copy-start.43 = (f32[1,8,2,128]{3,1,2,0:T(8,128)}, f32[1,8,2,128]{3,1,2,0:T(8,128)S(1)}, u32[]{:S(2)}) copy-start(f32[1,8,2,128]{3,1,2,0:T(8,128)S(1)} %copy.202) | copy-start | bytes 24580
  106.1 167.6 %copy-start.24 = (bf16[2048,16]{1,0:T(8,128)(2,1)}, bf16[2048,16]{1,0:T(8,128)(2,1)S(1)}, u32[]{:S(2)}) copy-start(bf16[2048,16]{1,0:T(8,128)(2,1)S(1)} %reshape.312) | copy-start | bytes 196612
  150.9 38.4 %copy-start.17 = (bf16[128,2048]{1,0:T(8,128)(2,1)S(1)}, bf16[128,2048]{1,0:T(8,128)(2,1)}, u32[]{:S(2)}) copy-start(bf16[128,2048]{1,0:T(8,128)(2,1)} %refs_0_.1) | copy-start | bytes 1572868
  162.7 26.7 %all-to-all-start = ((bf16[16,128,128]{1,2,0:T(8,128)(2,1)}), bf16[16,128,128]{1,2,0:T(8,128)(2,1)S(1)}, u32[]{:S(2)}, u32[]{:S(2)}) async-start(bf16[16,128,128]{1,2,0:T(8,128)(2,1)} %copy.157), calls=%async_computation | async-start | bytes 1048576 | tf_op jit(solution)/shard_map/all_to_all | solution.py:638
  166.5 466.9 %reduce-scatter.12.cloned.1.call-start = ((), (), s32[]{:S(2)}) async-start(), calls=%async_computation.17 | async-start | bytes 8912896 | tf_op jit(solution)/shard_map/reduce_scatter | solution.py:526
  194.3 85.2 %copy-start.61 = (f32[128]{0:T(128)}, f32[128]{0:T(128)S(1)}, u32[]{:S(2)}) copy-start(f32[128]{0:T(128)S(1)} %get-tuple-element.165) | copy-start | bytes 1540
  194.3 85.2 %copy-start.53 = (f32[128]{0:T(128)}, f32[128]{0:T(128)S(1)}, u32[]{:S(2)}) copy-start(f32[128]{0:T(128)S(1)} %fusion.89) | copy-start | bytes 1540
  468.0 145.8 %copy-start.27 = (f32[2048,16]{0,1:T(8,128)S(1)}, f32[2048,16]{0,1:T(8,128)}, u32[]{:S(2)}) copy-start(f32[2048,16]{0,1:T(8,128)} %copy-done.26) | copy-start | bytes 393220
  468.0 145.8 %copy-start.38 = (f32[2048]{0:T(1024)S(1)}, f32[2048]{0:T(1024)}, u32[]{:S(2)}) copy-start(f32[2048]{0:T(1024)} %copy-done.37) | copy-start | bytes 24580
  468.0 145.8 %copy-start.42 = (f32[2048]{0:T(1024)S(1)}, f32[2048]{0:T(1024)}, u32[]{:S(2)}) copy-start(f32[2048]{0:T(1024)} %copy-done.41) | copy-start | bytes 24580
  468.0 147.8 %copy-start.16 = (f32[128,2048]{1,0:T(8,128)S(1)}, f32[128,2048]{1,0:T(8,128)}, u32[]{:S(2)}) copy-start(f32[128,2048]{1,0:T(8,128)} %copy-done.15) | copy-start | bytes 3145732
  468.0 147.8 %copy-start.25 = (bf16[2048,16]{1,0:T(8,128)(2,1)S(1)}, bf16[2048,16]{1,0:T(8,128)(2,1)}, u32[]{:S(2)}) copy-start(bf16[2048,16]{1,0:T(8,128)(2,1)} %copy-done.24) | copy-start | bytes 196612
  468.0 147.8 %copy-start.44 = (f32[1,8,2,128]{3,1,2,0:T(8,128)S(1)}, f32[1,8,2,128]{3,1,2,0:T(8,128)}, u32[]{:S(2)}) copy-start(f32[1,8,2,128]{3,1,2,0:T(8,128)} %copy-done.43) | copy-start | bytes 24580
  468.0 147.8 %copy-start.54 = (f32[128]{0:T(128)S(1)}, f32[128]{0:T(128)}, u32[]{:S(2)}) copy-start(f32[128]{0:T(128)} %copy-done.53) | copy-start | bytes 1540
  468.1 149.6 %copy-start.62 = (f32[128]{0:T(128)S(1)}, f32[128]{0:T(128)}, u32[]{:S(2)}) copy-start(f32[128]{0:T(128)} %copy-done.61) | copy-start | bytes 1540
  635.7 29.4 %copy-start.3 = (bf16[2048,192]{1,0:T(8,128)(2,1)S(1)}, bf16[2048,192]{1,0:T(8,128)(2,1)}, u32[]{:S(2)}) copy-start(bf16[2048,192]{1,0:T(8,128)(2,1)} %copy-done.2) | copy-start | bytes 2359300
  635.7 29.4 %copy-start.6 = (bf16[2048,128]{1,0:T(8,128)(2,1)S(1)}, bf16[2048,128]{1,0:T(8,128)(2,1)}, u32[]{:S(2)}) copy-start(bf16[2048,128]{1,0:T(8,128)(2,1)} %copy-done.5) | copy-start | bytes 1572868
  635.7 29.4 %copy-start.8 = (s32[1,2048]{1,0:T(1,128)S(1)}, s32[1,2048]{1,0:T(1,128)}, u32[]{:S(2)}) copy-start(s32[1,2048]{1,0:T(1,128)} %copy-done.7) | copy-start | bytes 24580
  682.6 46.7 %all-to-all-start.2 = ((bf16[16,128,512]{1,2,0:T(8,128)(2,1)}), bf16[16,128,512]{1,2,0:T(8,128)(2,1)}, u32[]{:S(2)}, u32[]{:S(2)}) async-start(bf16[16,128,512]{1,2,0:T(8,128)(2,1)} %copy.163), calls=%async_computation.3 | async-start | bytes 4194304 | tf_op jit(solution)/shard_map/all_to_all | solution.py:726
  687.2 46.5 %all-gather.24.cloned.1.call-start = ((), (), s32[]{:S(2)}) async-start(), calls=%async_computation.20 | async-start | bytes 6291456 | tf_op jit(solution)/shard_map/all_gather | solution.py:530
  687.9 125.6 %all-gather.26.cloned.1.call-start = ((), (), s32[]{:S(2)}) async-start(), calls=%async_computation.27 | async-start | bytes 2506752 | tf_op jit(solution)/shard_map/all_gather | solution.py:522
  689.4 44.3 %copy-start.64 = (f32[128]{0:T(128)}, f32[128]{0:T(128)S(1)}, u32[]{:S(2)}) copy-start(f32[128]{0:T(128)S(1)} %fusion.90) | copy-start | bytes 1540
  689.4 44.3 %copy-start.49 = (f32[1,2,2,128]{3,1,2,0:T(2,128)S(1)}, f32[1,2,2,128]{3,1,2,0:T(2,128)}, u32[]{:S(2)}) copy-start(f32[1,2,2,128]{3,1,2,0:T(2,128)} %copy-done.48) | copy-start | bytes 6148
  742.7 101.1 %reduce-scatter.20.cloned.1.call-start = ((), (), s32[]{:S(2)}) async-start(), calls=%async_computation.24 | async-start | bytes 12582912 | tf_op jit(solution)/shard_map/reduce_scatter | solution.py:534
  749.7 104.1 %reduce-scatter.28.cloned.1.call-start = ((), (), s32[]{:S(2)}) async-start(), calls=%async_computation.29 | async-start | bytes 98304 | tf_op jit(solution)/shard_map/reduce_scatter | solution.py:534
  755.0 100.2 %reduce-scatter.18.cloned.1.call-start = ((), (), s32[]{:S(2)}) async-start(), calls=%async_computation.23 | async-start | bytes 1081344 | tf_op jit(solution)/shard_map/reduce_scatter | solution.py:534
  761.3 111.7 %reduce-scatter.32.cloned.1.call-start = ((), (), s32[]{:S(2)}) async-start(), calls=%async_computation.31 | async-start | bytes 8650752 | tf_op jit(solution)/shard_map/reduce_scatter | solution.py:534
  775.7 124.9 %all-gather.22.cloned.1.call-start = ((), (), s32[]{:S(2)}) async-start(), calls=%async_computation.19 | async-start | bytes 18874368 | tf_op jit(solution)/shard_map/all_gather | solution.py:530
  776.3 148.6 %reduce-scatter.30.cloned.1.call-start = ((), (), s32[]{:S(2)}) async-start(), calls=%async_computation.30 | async-start | bytes 17301504 | tf_op jit(solution)/shard_map/reduce_scatter | solution.py:534
  800.8 138.0 %reduce-scatter.26.cloned.1.call-start = ((), (), s32[]{:S(2)}) async-start(), calls=%async_computation.28 | async-start | bytes 3538944 | tf_op jit(solution)/shard_map/reduce_scatter | solution.py:534
  822.8 128.9 %reduce-scatter.14.cloned.1.call-start = ((), (), s32[]{:S(2)}) async-start(), calls=%async_computation.21 | async-start | bytes 2162688 | tf_op jit(solution)/shard_map/reduce_scatter | solution.py:534
  833.2 129.5 %reduce-scatter.24.cloned.1.call-start = ((), (), s32[]{:S(2)}) async-start(), calls=%async_computation.26 | async-start | bytes 393216 | tf_op jit(solution)/shard_map/reduce_scatter | solution.py:534
  837.2 137.8 %reduce-scatter.16.cloned.1.call-start = ((), (), s32[]{:S(2)}) async-start(), calls=%async_computation.22 | async-start | bytes 1179648 | tf_op jit(solution)/shard_map/reduce_scatter | solution.py:534
  843.5 230.0 %reduce-scatter.22.cloned.1.call-start = ((), (), s32[]{:S(2)}) async-start(), calls=%async_computation.25 | async-start | bytes 4456448 | tf_op jit(solution)/shard_map/reduce_scatter | solution.py:526
  845.1 1.2 collective-permute-start.1
  1333.9 61.1 %collective-permute-start = (f32[40,128]{1,0:T(8,128)S(1)}, f32[40,128]{1,0:T(8,128)S(1)}, u32[]{:S(2)}, u32[]{:S(2)}) collective-permute-start(f32[40,128]{1,0:T(8,128)S(1)} %reduce_sum.233), channel_id=1, source_target_pairs={{0,1},{1,0},{2,3},{3,2},{4,5},{5,4},{6,7},{7,6},{8,9},{9,8},{10,11... | collective-permute-start | bytes 61448 | tf_op jit(solution)/shard_map/ppermute | solution.py:539
  (45 other events, 354.5 us)
Sparse Core Ops, SparseCore 0:
  11.5 14.7 all-gather.13
  27.8 21.0 all-gather.15
  51.0 10.9 all-gather.17
  63.4 25.0 all-gather.27
  91.1 127.1 all-gather.19
  219.8 15.5 all-gather.29
  398.5 234.8 reduce-scatter.11
  689.6 14.8 all-gather.23
  742.8 70.6 all-gather.25
  816.2 14.9 reduce-scatter.19
  834.1 8.7 reduce-scatter.27
  845.7 9.3 reduce-scatter.17
  857.9 14.9 reduce-scatter.31
  874.4 26.1 all-gather.21
  903.5 21.4 reduce-scatter.29
  927.7 11.1 reduce-scatter.25
  941.5 10.0 reduce-scatter.13
  953.8 8.8 reduce-scatter.23
  965.5 9.4 reduce-scatter.15
  977.2 96.2 reduce-scatter.21

commit v3 on v2

--- a/solution.py
+++ b/solution.py
@@ -162,6 +162,99 @@
         cost_estimate=pl.CostEstimate(flops=count * count * 832, bytes_accessed=6 * 2**20, transcendentals=count * count // 2),
         name="attention_backward",
     )(query, key, value, grad, segment[:, None], segment[None, :], log_total)
+
+
+def swap_halves(values):
+    half = DR // 2
+    pieces = [values[:, i * half : (i + 1) * half] for i in (1, 0, 3, 2)]
+    return jnp.concatenate(pieces, axis=1)
+
+
+def project_kernel(x_ref, gain_ref, w_ref, gain_kv_ref, expand_ref, cos_ref, sin_ref, normed_ref, q_ref, k_ref, v_ref, raw_ref, latent_ref):
+    normed = rms_norm(x_ref[...].astype(F32), gain_ref[...]).astype(BF16)
+    normed_ref[...] = normed
+    both = dot(normed, w_ref[...])
+    raw = both[:, :KVR]
+    raw_ref[...] = raw
+    latent = rms_norm(raw, gain_kv_ref[...]).astype(BF16)
+    latent_ref[...] = latent
+    expanded = dot(latent, expand_ref[...])
+    rope = both[:, KVR + DN :]
+    rope = rope * cos_ref[...] + swap_halves(rope) * sin_ref[...]
+    q_ref[...] = jnp.concatenate([both[:, KVR : KVR + DN], rope[:, :DR]], axis=1).astype(BF16)
+    k_ref[...] = jnp.concatenate([expanded[:, :DN], rope[:, DR:]], axis=1).astype(BF16)
+    v_ref[...] = expanded[:, DN:].astype(BF16)
+
+
+def project(rows, gain, weight, gain_kv, expand, angles):
+    count = rows.shape[0]
+    tile = 256
+    cosine, sine = jnp.cos(angles), jnp.sin(angles)
+    cosines = jnp.concatenate([cosine] * 4, axis=1)
+    sines = jnp.concatenate([-sine, sine] * 2, axis=1)
+
+    def by_rows(columns):
+        return pl.BlockSpec((tile, columns), lambda i: (i, 0))
+
+    def whole(array):
+        return pl.BlockSpec(array.shape, lambda i: (0, 0))
+
+    outs = [(D, BF16), (DN + DR, BF16), (DN + DR, BF16), (DV, BF16), (KVR, F32), (KVR, BF16)]
+    return pl.pallas_call(
+        project_kernel,
+        grid=(count // tile,),
+        in_specs=[
+            by_rows(D),
+            whole(gain[None]),
+            whole(weight),
+            whole(gain_kv[None]),
+            whole(expand),
+            by_rows(2 * DR),
+            by_rows(2 * DR),
+        ],
+        out_specs=tuple(by_rows(c) for c, _ in outs),
+        out_shape=tuple(jax.ShapeDtypeStruct((count, c), t) for c, t in outs),
+        compiler_params=pltpu.CompilerParams(vmem_limit_bytes=48 * 2**20),
+        cost_estimate=pl.CostEstimate(flops=2 * count * D * 900, bytes_accessed=24 * 2**20, transcendentals=count),
+        name="project",
+    )(rows, gain[None], weight, gain_kv[None], expand, cosines, sines)
+
+
+def turn_kernel(in_ref, out_ref):
+    block = in_ref[...].astype(F32)
+    out_ref[...] = block.reshape(-1, block.shape[-1]).T
+
+
+def turn_rows(rows, tile):
+    count, columns = rows.shape
+    return pl.pallas_call(
+        turn_kernel,
+        grid=(count // tile,),
+        in_specs=[pl.BlockSpec((tile, columns), lambda i: (i, 0))],
+        out_specs=pl.BlockSpec((columns, tile), lambda i: (0, i)),
+        out_shape=jax.ShapeDtypeStruct((columns, count), F32),
+        compiler_params=pltpu.CompilerParams(vmem_limit_bytes=48 * 2**20),
+        cost_estimate=pl.CostEstimate(flops=0, bytes_accessed=6 * rows.size, transcendentals=0),
+        name="turn_rows",
+    )(rows)
+
+
+def turn_units(parts):
+    seq_count, groups, unit, columns = parts.shape
+    if unit % 8 or (seq_count * unit) % 128:
+        return parts.transpose(3, 1, 0, 2).reshape(columns, -1).astype(F32)
+    wide = seq_count * unit
+    tile = 256
+    return pl.pallas_call(
+        turn_kernel,
+        grid=(groups, columns // tile),
+        in_specs=[pl.BlockSpec((seq_count, None, unit, tile), lambda g, i: (0, g, 0, i))],
+        out_specs=pl.BlockSpec((tile, wide), lambda g, i: (i, g)),
+        out_shape=jax.ShapeDtypeStruct((columns, groups * wide), F32),
+        compiler_params=pltpu.CompilerParams(vmem_limit_bytes=48 * 2**20),
+        cost_estimate=pl.CostEstimate(flops=0, bytes_accessed=6 * parts.size, transcendentals=0),
+        name="turn_units",
+    )(parts)
 
 
 LINE = 4
@@ -531,7 +624,13 @@
 
 
 def scatter_fsdp(partial, axis=0):
-    return lax.psum_scatter(partial, "fsdp", scatter_dimension=axis, tiled=True)
+    count, me = lax.axis_size("fsdp"), lax.axis_index("fsdp")
+    size = partial.shape[axis] // count
+    total = lax.dynamic_slice_in_dim(partial, me * size, size, axis).astype(F32)
+    for k in range(1, count):
+        piece = lax.dynamic_slice_in_dim(partial, lax.rem(me + k, count) * size, size, axis)
+        total = total + shift_fsdp(piece, k).astype(F32)
+    return total
 
 
 def shift_fsdp(rows, k):
@@ -591,7 +690,6 @@
     route_mask = jnp.any(routes[None] == expert_ids[:, None, None], axis=2).astype(BF16)
     token_all, mask_all = gather_all([tokens], [ROW_PARTS], [route_mask], 1)
     token_all = token_all.reshape(group_size, D)
-    cotangent_all = gather_seq(cotangent)
 
     small = gather_fsdp(jnp.concatenate([g_attn, g_kv, g_ffn, w_router.reshape(-1)])[None])
     cuts = [0, g_attn.size, g_kv.size, g_ffn.size, w_router.size]
@@ -609,9 +707,9 @@
         axis=1,
     )
     head_expand = gather_fsdp(lax.dynamic_slice_in_dim(w_kvb, rank * kv_width, kv_width, 1))
-    head_weights = gather_fsdp(jnp.concatenate([w_kva, head_query_part], axis=1))
-    latent_weight = head_weights[:, : KVR + DR]
-    head_query = head_weights[:, KVR + DR :]
+    head_weights = gather_fsdp(
+        jnp.concatenate([w_kva[:, :KVR], head_query_part, w_kva[:, KVR:]], axis=1)
+    )
     shared_in = gather_fsdp(shared_in_part)
     shared_out = gather_fsdp(lax.dynamic_slice_in_dim(w_shared_out, rank * unit, unit, 0))
     output_weight = gather_fsdp(w_o)
@@ -625,15 +723,12 @@
     angles_all = position[:, None].astype(F32) * frequencies(DR)[None, :]
     angles = own(angles_all)
 
-    normed_all = rms_norm(token_all.astype(F32), gain_attn).astype(BF16)
-    query_pre = dot(normed_all, head_query)
-    latent_full = dot(normed_all, latent_weight)
-    latent_all = rms_norm(latent_full[:, :KVR], gain_latent).astype(BF16)
-    expanded = dot(latent_all, head_expand)
-    query = jnp.concatenate([query_pre[:, :DN], rotate(query_pre[:, DN:], angles_all)], axis=1).astype(BF16)
-    key_rope = rotate(latent_full[:, KVR:], angles_all)
-    key = jnp.concatenate([expanded[:, :DN], key_rope], axis=1).astype(BF16)
-    value = expanded[:, DN:].astype(BF16)
+    upstream_own = jnp.where(own(valid_all)[:, None], cotangent, 0).astype(BF16)
+    upstream_all = gather_seq(upstream_own)
+
+    normed_all, query, key, value, latent_full, latent_all = project(
+        token_all, gain_attn, head_weights, gain_latent, head_expand, angles_all
+    )
     context, log_total, head_largest = attention_forward(query, key, value, segment, valid_all)
     context_low = lax.all_to_all(context, "seq", split_axis=0, concat_axis=1, tiled=True)
     inputs = tokens.astype(F32)
@@ -681,7 +776,6 @@
     mixed_sum = scatter_seq(mixed_part.astype(BF16))
     mixed = (middle + mixed_sum.astype(F32)).astype(BF16)
 
-    upstream_all = jnp.where(valid_all[:, None], cotangent_all, 0).astype(BF16)
     upstream_rows = to_slots(upstream_all)
     row_gate_grad = jnp.sum(upstream_rows * result, axis=1).reshape(seq_count, capacity)
     gate_grad = jnp.sum(jnp.where(picks, row_gate_grad[:, :, None], 0.0), axis=1)
@@ -700,27 +794,33 @@
     prob_grads = prob_grads.reshape(experts, group_size).T
     grad_shared_out = dot_tn(shared_hidden, upstream_all)
     grad_shared_in = dot_tn(shared_grad, ffn_all)
-    sum_expert_in = scatter_fsdp(grad_expert_in.astype(BF16)).astype(F32)[None]
-    sum_expert_out = scatter_fsdp(grad_expert_out.astype(BF16)).astype(F32)[None]
-    part_shared_out = scatter_fsdp(grad_shared_out.astype(BF16))
-    part_shared_in = scatter_fsdp(grad_shared_in.astype(BF16), 1)
+    sum_expert_in = scatter_fsdp(grad_expert_in.astype(BF16))[None]
+    sum_expert_out = scatter_fsdp(grad_expert_out.astype(BF16))[None]
+    part_shared_out = scatter_fsdp(grad_shared_out.astype(BF16)).astype(BF16)
+    part_shared_in = scatter_fsdp(grad_shared_in.astype(BF16), 1).astype(BF16)
+    sum_shared_out = gather_seq(part_shared_out).astype(F32)
+    sum_shared_in = turn_units(
+        gather_seq(part_shared_in).reshape(seq_count, 2 * fsdp_count, unit, row_part)
+    )
 
     logit_grads = (
         router_probs * (prob_grads - jnp.sum(router_probs * prob_grads, axis=-1, keepdims=True))
     ).astype(BF16)
     grad_router = dot_tn(ffn_all, logit_grads)
-    sum_router = scatter_fsdp(grad_router.astype(BF16)).astype(F32)
+    sum_router = scatter_fsdp(grad_router.astype(BF16))
     ffn_grad = ffn_sum + dot_nt(own(logit_grads), router_weight)
 
     ffn_pull = jax.vjp(rms_norm, middle, gain_ffn)[1]
     middle_norm_grad, grad_gain_ffn = ffn_pull(ffn_grad)
-    upstream = own(upstream_all).astype(F32)
-    middle_grad = upstream + middle_norm_grad
+    middle_grad = upstream_own.astype(F32) + middle_norm_grad
     middle_low = middle_grad.astype(BF16)
     context_grad = dot_nt(middle_low, output_weight).astype(BF16)
     head_grad = lax.all_to_all(context_grad, "seq", split_axis=1, concat_axis=0, tiled=True)
-    grad_output = scatter_fsdp(dot_tn(context_low, middle_low).astype(BF16))
-    part_output = scatter_seq(grad_output)
+    grad_output = scatter_fsdp(dot_tn(context_low, middle_low).astype(BF16)).astype(BF16)
+    output_rows = row_part // seq_count
+    (part_output,) = scatter_sum(
+        [grad_output.reshape(seq_count, output_rows, D)], [split_rows(output_rows)], [], 5
+    )
 
     query_grad, key_grad, value_grad = attention_backward(query, key, value, head_grad, segment, log_total)
     back = lax.all_to_all(
@@ -734,9 +834,9 @@
     head_pre_grad = jnp.concatenate(
         [query_grad_32[:, :DN], rotate(query_grad_32[:, DN:], -angles_all)], axis=1
     ).astype(BF16)
-    part_query = scatter_fsdp(dot_tn(head_pre_grad, normed_all).astype(BF16), 1)
+    part_query = scatter_fsdp(dot_tn(head_pre_grad, normed_all).astype(BF16), 1).astype(BF16)
     head_expand_grad = jnp.concatenate([key_grad[:, :DN], value_grad], axis=1)
-    part_expand = scatter_fsdp(dot_tn(head_expand_grad, latent_all).astype(BF16), 1)
+    part_expand = scatter_fsdp(dot_tn(head_expand_grad, latent_all).astype(BF16), 1).astype(BF16)
 
     back = back.transpose(1, 0, 2)
     back_query = back[..., :query_width].astype(F32)
@@ -754,28 +854,21 @@
     compressed_grad, grad_gain_latent = latent_pull(latent_grad)
     full_grad = jnp.concatenate([compressed_grad, rope_grad], axis=1).astype(BF16)
     full_all = gather_seq(full_grad)
-    sum_latent = scatter_fsdp(dot_tn(normed_all, full_all).astype(BF16)).astype(F32)
-    normed_grad = dot_nt(pre_grad, query_weight) + dot_nt(full_grad, latent_weight)
+    sum_latent = scatter_fsdp(dot_tn(normed_all, full_all).astype(BF16))
+    spread_grad = jnp.pad(full_grad[:, :KVR], ((0, 0), (0, query_width + DR)))
+    spread_grad = spread_grad + jnp.pad(full_grad[:, KVR:], ((0, 0), (KVR + query_width, 0)))
+    normed_grad = dot_nt(pre_grad, query_weight) + dot_nt(spread_grad, head_weights)
     input_pull = jax.vjp(rms_norm, inputs, gain_attn)[1]
     input_norm_grad, grad_gain_attn = input_pull(normed_grad)
     grad_inputs = middle_grad + input_norm_grad
 
     gain_grads = jnp.concatenate([grad_gain_attn, grad_gain_latent, grad_gain_ffn]).reshape(-1, 128)
     gain_grads = jnp.pad(gain_grads, ((0, -gain_grads.shape[0] % 8), (0, 0)))
-    part_shared_out = jnp.pad(part_shared_out, ((0, -unit % 16), (0, 0)))
-    weight_parts = [part_shared_in, part_query, part_shared_out, part_output, part_expand]
+    weight_parts = [part_query, part_output.astype(BF16), part_expand]
     *sums, gain_all = gather_all(weight_parts, [split_rows(p.shape[0]) for p in weight_parts], [gain_grads], 4)
-    sum_shared_in = (
-        sums[0]
-        .reshape(seq_count, 2, fsdp_count, unit, row_part)
-        .transpose(4, 1, 2, 0, 3)
-        .reshape(row_part, 2 * SH)
-        .astype(F32)
-    )
-    sum_query = sums[1].reshape(-1, row_part).T.astype(F32)
-    sum_shared_out = sums[2][:, :unit].reshape(w_shared_out.shape).astype(F32)
-    sum_output = sums[3].reshape(w_o.shape).astype(F32)
-    sum_expand = sums[4].reshape(-1, w_kvb.shape[0]).T.astype(F32)
+    sum_query = turn_rows(sums[0].reshape(-1, row_part), 384)
+    sum_output = sums[1].reshape(w_o.shape).astype(F32)
+    sum_expand = turn_rows(sums[2].reshape(-1, w_kvb.shape[0]), 512)
     gain_seq = jnp.sum(gain_all, axis=0)
     gain_sum = gain_seq
     for k in range(1, fsdp_count):

time: 1410 us -> 1170 us (0.83)
  waiting for transfers between devices: 273 us -> 85.2 us
  local copies, waits for them, and re-layouts: 96.9 us -> 51.9 us
  Pallas kernels: 558 us -> 592 us
  matrix products: 295 us -> 264 us
  other arithmetic: 126 us -> 111 us
    reduce_scatter x2 -> x1, waiting for transfers between devices: 114 us -> 6.2 us  [scatter_seq(): return lax.psum_scatter(partial, 'seq', scatter_dimension=0, tiled=True)]
    pallas_call x3, Pallas kernels: 393 us -> 308 us  [gather_all(): pl.pallas_call(functools.partial(gather_kernel, streams, len(main), len(s...]
    pallas_call x1 -> x2, Pallas kernels: 146 us -> 217 us  [scatter_sum(): pl.pallas_call(functools.partial(scatter_kernel, streams, len(main), len(...]
    reduce_scatter x9 -> x0, waiting for transfers between devices: 67.5 us -> none  [scatter_fsdp(): return lax.psum_scatter(partial, 'fsdp', scatter_dimension=axis, tiled=True)]
    pallas_call x0 -> x4, Pallas kernels: none -> 47.1 us  [the longest x1 17.6 us: turn_units(): pl.pallas_call(turn_kernel, grid=(groups, columns // tile), in_specs=[pl....]
    convert_element_type x3 -> x0, local copies, waits for them, and re-layouts: 30.9 us -> none  [the longest x1 12.7 us: on_device(): sum_shared_in = sums[0].reshape(seq_count, 2, fsdp_count, unit, row_part)...]
    all_to_all x1, waiting for transfers between devices: 34.1 us -> 60.6 us  [on_device(): lax.all_to_all(jnp.concatenate([query_grad, key_grad, value_grad], axis=1...]
    unnamed x153 -> x172, local copies, waits for them, and re-layouts: 42.3 us -> 18.5 us
  transfers between devices with their start and end apart: 24 -> 25, of which waited for: 13 -> 5; matrix products, arithmetic and copies ran while one was open for 29% -> 30% of each run, Pallas kernels for 22% -> 51%
where the time goes in v3:
time: 1170 us; the launch traced here: 1160 us
  Pallas kernels  592 us (51%)
  matrix products  264 us (23%)
  other arithmetic  111 us (9%)
  waiting for transfers between devices  85.2 us (7%)
  local copies, waits for them, and re-layouts  51.9 us (4%)
  blocking collectives  29.3 us (3%)
  between operations  15.8 us (1%)
    pallas_call x3, Pallas kernels, gather_all(): pl.pallas_call(functools.partial(gather_kernel, streams, len(main), len(s...  308 us
    pallas_call x2, Pallas kernels, scatter_sum(): pl.pallas_call(functools.partial(scatter_kernel, streams, len(main), len(...  217 us
    dot_general x9, matrix products, dot_nt(): lax.dot_general(left, right, (((1,), (1,)), ((), ())), preferred_element_...  85 us
    dot_general x9, matrix products, dot_tn(): lax.dot_general(left, right, (((0,), (0,)), ((), ())), preferred_element_...  71.4 us
    dot_general x6, matrix products, dot(): return jnp.dot(left, right, preferred_element_type=F32)  69.9 us
    all_to_all x1, waiting for transfers between devices, on_device(): lax.all_to_all(jnp.concatenate([query_grad, key_grad, value_grad], axis=1...  60.6 us
  transfers between devices with their start and end apart: 25, of which 5 were waited for; matrix products, arithmetic and copies ran while one was open for 30% of the time, Pallas kernels for 51%

profile of v3, /device:TPU:0, one launch (start us, length us, event | category | flops | bytes accessed | tf_op | source)
XLA Modules:
  0.0 1160.2 jit_solution(13844578980983005500)
XLA Ops:
  29.7 73.9 %gather_all.3 = (bf16[16,128,2048]{2,1,0:T(8,128)(2,1)}, bf16[16,16,128]{2,1,0:T(8,128)(2,1)}) custom-call(bf16[128,2048]{1,0:T(8,128)(2,1)} %refs_0_.1, bf16[16,128]{1,0:T(8,128)(2,1)} %convert_element_type.264.refs_1_), custom_call_target="tpu_custom_call" | custom-call | tf_op jit(solution)/shard_map/gather_all/pallas_call | solution.py:417
  103.6 5.7 fusion.49
  110.1 5.3 pad_maximum_fusion.6
  115.5 16.1 %project.1 = (bf16[2048,2048]{1,0:T(8,128)(2,1)}, bf16[2048,192]{1,0:T(8,128)(2,1)S(1)}, bf16[2048,192]{1,0:T(8,128)(2,1)S(1)}, bf16[2048,128]{1,0:T(8,128)(2,1)...) custom-call(bf16[2048,2048]{1,0:T(8,128)(2,1)} %bitcast.223, f32[1,2048]{1,0:T(1,128)S(1)} %bitcast.171, ...), custom_call_target="tpu_custom_call" | custom-call | flops 7549747200 | bytes 25165824 | tf_op jit(solution)/shard_map/project/pallas_call | solution.py:203
  131.6 8.6 attention_forward.1
  151.2 11.0 all-to-all-done
  162.2 6.0 multiply_reduce_fusion.2
  169.4 102.9 %gather_all.4 = (bf16[16,128,2048]{2,1,0:T(8,128)(2,1)}, f32[16,8,128]{2,1,0:T(8,128)}) custom-call(bf16[128,2048]{1,0:T(8,128)(2,1)} %multiply_convert_fusion.7.refs_0_, f32[8,128]{1,0:T(8,128)} %copy-done.2), custom_call_target="tpu_custom_call" | custom-call | tf_op jit(solution)/shard_map/gather_all/pallas_call | solution.py:417
  272.3 8.0 convolution_convert_fusion.4
  283.4 8.6 fusion.95
  292.0 23.8 %fusion.7 = f32[1536,2816]{1,0:T(8,128)S(1)} fusion(bf16[1536,2048]{1,0:T(8,128)(2,1)} %bitcast.181, bf16[1,2048,2816]{2,1,0:T(8,128)(2,1)} %all-gather.34.cloned.1.call-done), kind=kOutput, calls=%fused_computation.13 | convolution fusion | flops 17716740096 | bytes 35127296 | tf_op jit(solution)/shard_map/dot_general | solution.py:77
  315.9 6.3 copy-done.12
  326.1 9.9 fusion.41
  336.1 17.1 %fusion.3 = (f32[1536]{0:T(1024)S(1)}, bf16[1536,2048]{1,0:T(8,128)(2,1)}) fusion(f32[16,96,2048]{2,1,0:T(8,128)} %fusion.41, bf16[1536,1408]{1,0:T(8,128)(2,1)} %multiply_convert_fusion.3, bf16[1,1408,2048]{2,1,0:T(8,128)(2,1)} %all-gather.36.cloned.1.call-done), kind=kOutput, calls=%fused_computation.7 | convolution fusion | flops 8870950912 | bytes 28973056 | tf_op jit(solution)/shard_map/dot_general | solution.py:77
  354.2 11.3 fusion.4
  365.5 8.2 fusion.42
  377.1 12.1 %fusion.1 = bf16[2048,2048]{1,0:T(8,128)(2,1)} fusion(f32[16,128,2048]{2,1,0:T(8,128)} %fusion.42, bf16[2048,176]{0,1:T(8,128)(2,1)S(1)} %get-tuple-element.82, bf16[176,2048]{1,0:T(8,128)(2,1)S(1)} %copy-done.30), kind=kOutput, calls=%fused_computation.3 | convolution fusion | flops 1484783616 | bytes 26607616 | tf_op jit(solution)/shard_map/dot_general | solution.py:77
  390.3 5.1 convolution_convert_fusion.8
  398.6 21.8 %multiply_convert_fusion.2 = (bf16[1536,1408]{1,0:T(8,128)(2,1)}, bf16[1536,1408]{1,0:T(8,128)(2,1)}) fusion(f32[1536,2816]{1,0:T(8,128)} %copy-done.12, bf16[1536,2048]{1,0:T(8,128)(2,1)} %get-tuple-element.105, bf16[1,1408,2048]{2,1,0:T(8,128)(2,1)} %all-gather.36.cloned.1.call-done), kind=kOutput, calls=%fused_computation.19 | convolution fusion | flops 8886484992 | bytes 38010880 | tf_op jit(solution)/shard_map/dot_general | solution.py:85
  420.3 24.9 %fusion.9 = bf16[1536,2048]{1,0:T(8,128)(2,1)} fusion(bf16[1,2048,2816]{2,1,0:T(8,128)(2,1)} %all-gather.34.cloned.1.call-done, bf16[1536,1408]{1,0:T(8,128)(2,1)} %get-tuple-element.75, bf16[1536,1408]{1,0:T(8,128)(2,1)} %get-tuple-element.74), kind=kOutput, calls=%fused_computation.23 | convolution fusion | flops 17737187328 | bytes 26476544 | tf_op jit(solution)/shard_map/dot_general | solution.py:85
  445.2 11.5 fusion.40
  456.7 10.7 fusion
  467.5 145.5 %scatter_sum.2 = (f32[128,2048]{1,0:T(8,128)}, f32[16,16,128]{2,1,0:T(8,128)}) custom-call(bf16[16,128,2048]{2,1,0:T(8,128)(2,1)} %bitcast.178, f32[16,128]{1,0:T(8,128)} %get-tuple-element.67.refs_1_), custom_call_target="tpu_custom_call" | custom-call | tf_op jit(solution)/shard_map/scatter_sum/pallas_call | solution.py:597
  617.5 6.2 reduce-scatter.2.cloned.1.call-done
  626.0 6.7 fusion.21
  632.8 22.5 %all_to_all.43 = bf16[128,16,128]{2,0,1:T(8,128)(2,1)S(1)} all-to-all(bf16[128,16,128]{2,0,1:T(8,128)(2,1)S(1)} %bitcast.197), channel_id=1, replica_groups=mesh['seq'=16,'fsdp'=2] {'seq'}, dimensions={1} | all-to-all | bytes 1048576 | tf_op jit(solution)/shard_map/all_to_all | solution.py:818
  655.3 11.2 attention_backward.1
  672.8 4.5 all-to-all-start.2
  678.6 6.0 fusion.23
  684.6 60.6 %all-to-all-done.2 = bf16[16,128,512]{1,2,0:T(8,128)(2,1)} async-done(((bf16[16,128,512]{1,2,0:T(8,128)(2,1)}), bf16[16,128,512]{1,2,0:T(8,128)(2,1)}, u32[]{:S(2)}, u32[]{:S(2)}) %all-to-all-start.2) | async-done | bytes 2097184 | tf_op jit(solution)/shard_map/all_to_all | solution.py:826
  749.8 4.7 multiply_reduce_fusion.3
  757.6 7.0 convolution_convert_fusion.6
  773.4 24.4 %convolution_convert_fusion = bf16[2048,2816]{1,0:T(8,128)(2,1)S(1)} fusion(bf16[1536,2048]{1,0:T(8,128)(2,1)} %bitcast.182, bf16[1536,1408]{1,0:T(8,128)(2,1)} %get-tuple-element.75, bf16[1536,1408]{1,0:T(8,128)(2,1)} %get-tuple-element.74), kind=kOutput, calls=%fused_computation.16 | convolution fusion | flops 17739808768 | bytes 26476544 | tf_op jit(solution)/shard_map/dot_general | solution.py:81
  804.4 12.9 %convolution_convert_fusion.1 = bf16[1408,2048]{1,0:T(8,128)(2,1)S(1)} fusion(bf16[1536,1408]{1,0:T(8,128)(2,1)} %multiply_convert_fusion.3, bf16[1536,2048]{1,0:T(8,128)(2,1)} %get-tuple-element.105), kind=kOutput, calls=%fused_computation.24 | convolution fusion | flops 8861253632 | bytes 16384000 | tf_op jit(solution)/shard_map/dot_general | solution.py:81
  824.0 4.7 convolution_convert_fusion.10
  837.5 4.4 multiply_convert_fusion
  842.6 5.6 add_bitcast_fusion.1
  848.3 5.5 convolution_convert_fusion.7
  855.9 10.0 add_bitcast_fusion
  865.9 8.8 convert_element_type.329
  876.3 8.0 add_convert_fusion
  884.3 71.5 %scatter_sum.3 = f32[64,2048]{1,0:T(8,128)} custom-call(bf16[16,64,2048]{2,1,0:T(8,128)(2,1)} %bitcast.186), custom_call_target="tpu_custom_call" | custom-call | tf_op jit(solution)/shard_map/scatter_sum/pallas_call | solution.py:597
  959.2 9.1 fusion.96
  970.3 130.7 %gather_all.5 = (bf16[16,192,1024]{2,1,0:T(8,128)(2,1)}, bf16[16,64,2048]{2,1,0:T(8,128)(2,1)}, bf16[16,256,256]{2,1,0:T(8,128)(2,1)}, f32[16,40,128]{2,1,0:T(8,128)}) custom-call(bf16[192,1024]{1,0:T(8,128)(2,1)} %add_convert_fusion.3.refs_0_, bf16[64,2048]{1,0:T(8,128)(2,1)} %convert_element_type.308.refs_1_, bf16[256,256]{1,0:T(8,128)(2,1)} %add_convert_fusion.5.refs_2_, ...), custom_call_target="tpu_custom_call" | custom-call | tf_op jit(solution)/shard_map/gather_all/pallas_call | solution.py:417
  1102.2 8.7 convolution_convert_fusion.5
  1112.7 4.7 bitcast_convert_fusion
  1118.8 9.6 turn_rows.2
  1133.6 17.6 %turn_units.1 = f32[1024,5632]{1,0:T(8,128)} custom-call(bf16[16,4,88,1024]{3,2,1,0:T(8,128)(2,1)} %bitcast.188), custom_call_target="tpu_custom_call" | custom-call | bytes 34603008 | tf_op jit(solution)/shard_map/turn_units/pallas_call | solution.py:248
  (344 shorter events, 124.3 us)
Async XLA Ops:
  7.2 108.3 %all-gather.16.cloned.1.call-start = ((), (), s32[]{:S(2)}) async-start(), calls=%async_computation.4 | async-start | bytes 4718592 | tf_op jit(solution)/shard_map/all_gather | solution.py:623
  12.9 149.3 %all-gather.18.cloned.1.call-start = ((), (), s32[]{:S(2)}) async-start(), calls=%async_computation.5 | async-start | bytes 12582912 | tf_op jit(solution)/shard_map/all_gather | solution.py:623
  13.7 269.7 %all-gather.20.cloned.1.call-start = ((), (), s32[]{:S(2)}) async-start(), calls=%async_computation.6 | async-start | bytes 2359296 | tf_op jit(solution)/shard_map/all_gather | solution.py:623
  17.2 274.8 %all-gather.34.cloned.1.call-start = ((), (), s32[]{:S(2)}) async-start(), calls=%async_computation.14 | async-start | bytes 17301504 | tf_op jit(solution)/shard_map/all_gather | solution.py:623
  17.7 308.4 %all-gather.22.cloned.1.call-start = ((), (), s32[]{:S(2)}) async-start(), calls=%async_computation.8 | async-start | bytes 8912896 | tf_op jit(solution)/shard_map/all_gather | solution.py:615
  19.1 317.0 %all-gather.36.cloned.1.call-start = ((), (), s32[]{:S(2)}) async-start(), calls=%async_computation.15 | async-start | bytes 8650752 | tf_op jit(solution)/shard_map/all_gather | solution.py:623
  23.5 86.7 %copy-start.64 = (f32[32]{0:T(128)}, f32[32]{0:T(128)S(1)}, u32[]{:S(2)}) copy-start(f32[32]{0:T(128)S(1)} %negate_power_fusion) | copy-start | bytes 388
  27.6 82.5 %copy-start.48 = (f32[2048]{0:T(1024)}, f32[2048]{0:T(1024)S(1)}, u32[]{:S(2)}) copy-start(f32[2048]{0:T(1024)S(1)} %select_convert_fusion) | copy-start | bytes 24580
  28.3 103.3 %copy-start.1 = (s32[2048,1]{1,0:T(8,128)}, s32[2048,1]{1,0:T(8,128)S(1)}, u32[]{:S(2)}) copy-start(s32[2048,1]{1,0:T(8,128)S(1)} %add_select_fusion.segc_ref) | copy-start | bytes 24580
  29.7 138.6 %copy-start.46 = (f32[1,8,2,128]{3,1,2,0:T(8,128)}, f32[1,8,2,128]{3,1,2,0:T(8,128)S(1)}, u32[]{:S(2)}) copy-start(f32[1,8,2,128]{3,1,2,0:T(8,128)S(1)} %copy.154) | copy-start | bytes 24580
  131.6 30.6 %copy-start.18 = (bf16[128,2048]{1,0:T(8,128)(2,1)S(1)}, bf16[128,2048]{1,0:T(8,128)(2,1)}, u32[]{:S(2)}) copy-start(bf16[128,2048]{1,0:T(8,128)(2,1)} %refs_0_.1) | copy-start | bytes 1572868
  141.4 20.8 %all-to-all-start = ((bf16[16,128,128]{1,2,0:T(8,128)(2,1)}), bf16[16,128,128]{1,2,0:T(8,128)(2,1)S(1)}, u32[]{:S(2)}, u32[]{:S(2)}) async-start(bf16[16,128,128]{1,2,0:T(8,128)(2,1)} %copy.120), calls=%async_computation | async-start | bytes 1048576 | tf_op jit(solution)/shard_map/all_to_all | solution.py:733
  145.2 478.5 %reduce-scatter.2.cloned.1.call-start = ((), (), s32[]{:S(2)}) async-start(), calls=%async_computation.7 | async-start | bytes 8912896 | tf_op jit(solution)/shard_map/reduce_scatter | solution.py:619
  168.2 112.1 %copy-start.16 = (f32[128,2048]{1,0:T(8,128)}, f32[128,2048]{1,0:T(8,128)S(1)}, u32[]{:S(2)}) copy-start(f32[128,2048]{1,0:T(8,128)S(1)} %get-tuple-element.108) | copy-start | bytes 3145732
  168.2 112.1 %copy-start.66 = (f32[128]{0:T(128)}, f32[128]{0:T(128)S(1)}, u32[]{:S(2)}) copy-start(f32[128]{0:T(128)S(1)} %get-tuple-element.107) | copy-start | bytes 1540
  168.3 112.1 %copy-start.56 = (f32[128]{0:T(128)}, f32[128]{0:T(128)S(1)}, u32[]{:S(2)}) copy-start(f32[128]{0:T(128)S(1)} %fusion.76) | copy-start | bytes 1540
  377.1 79.6 %copy-start.38 = (bf16[2048,176]{0,1:T(8,128)(2,1)}, bf16[2048,176]{0,1:T(8,128)(2,1)S(1)}, u32[]{:S(2)}) copy-start(bf16[2048,176]{0,1:T(8,128)(2,1)S(1)} %get-tuple-element.80) | copy-start | bytes 2162692
  377.1 79.6 %copy-start.39 = (bf16[2048,176]{0,1:T(8,128)(2,1)}, bf16[2048,176]{0,1:T(8,128)(2,1)S(1)}, u32[]{:S(2)}) copy-start(bf16[2048,176]{0,1:T(8,128)(2,1)S(1)} %get-tuple-element.81) | copy-start | bytes 2162692
  389.2 360.6 %all-gather.26.cloned.1.call-start = ((), (), s32[]{:S(2)}) async-start(), calls=%async_computation.10 | async-start | bytes 6291456 | tf_op jit(solution)/shard_map/all_gather | solution.py:623
  390.0 475.9 %all-gather.32.cloned.1.call-start = ((), (), s32[]{:S(2)}) async-start(), calls=%async_computation.13 | async-start | bytes 6127616 | tf_op jit(solution)/shard_map/all_gather | solution.py:615
  395.4 1.7 collective-permute-start.7
  398.0 561.2 %all-gather.24.cloned.1.call-start = ((), (), s32[]{:S(2)}) async-start(), calls=%async_computation.9 | async-start | bytes 18874368 | tf_op jit(solution)/shard_map/all_gather | solution.py:623
  467.4 145.6 %copy-start.28 = (f32[2048,16]{0,1:T(8,128)S(1)}, f32[2048,16]{0,1:T(8,128)}, u32[]{:S(2)}) copy-start(f32[2048,16]{0,1:T(8,128)} %copy-done.27) | copy-start | bytes 393220
  467.4 145.6 %copy-start.43 = (f32[2048]{0:T(1024)S(1)}, f32[2048]{0:T(1024)}, u32[]{:S(2)}) copy-start(f32[2048]{0:T(1024)} %copy-done.42) | copy-start | bytes 24580
  467.4 145.7 %copy-start.45 = (f32[2048]{0:T(1024)S(1)}, f32[2048]{0:T(1024)}, u32[]{:S(2)}) copy-start(f32[2048]{0:T(1024)} %copy-done.44) | copy-start | bytes 24580
  467.4 147.6 %copy-start.17 = (f32[128,2048]{1,0:T(8,128)S(1)}, f32[128,2048]{1,0:T(8,128)}, u32[]{:S(2)}) copy-start(f32[128,2048]{1,0:T(8,128)} %copy-done.16) | copy-start | bytes 3145732
  467.4 147.6 %copy-start.25 = (bf16[2048,16]{1,0:T(8,128)(2,1)S(1)}, bf16[2048,16]{1,0:T(8,128)(2,1)}, u32[]{:S(2)}) copy-start(bf16[2048,16]{1,0:T(8,128)(2,1)} %reshape.301) | copy-start | bytes 196612
  467.5 147.6 %copy-start.47 = (f32[1,8,2,128]{3,1,2,0:T(8,128)S(1)}, f32[1,8,2,128]{3,1,2,0:T(8,128)}, u32[]{:S(2)}) copy-start(f32[1,8,2,128]{3,1,2,0:T(8,128)} %copy-done.46) | copy-start | bytes 24580
  467.5 147.6 %copy-start.57 = (f32[128]{0:T(128)S(1)}, f32[128]{0:T(128)}, u32[]{:S(2)}) copy-start(f32[128]{0:T(128)} %copy-done.56) | copy-start | bytes 1540
  467.5 150.0 %copy-start.67 = (f32[128]{0:T(128)S(1)}, f32[128]{0:T(128)}, u32[]{:S(2)}) copy-start(f32[128]{0:T(128)} %copy-done.66) | copy-start | bytes 1540
  467.5 156.2 %copy-start.35 = (bf16[128,2048]{1,0:T(8,128)(2,1)S(1)}, bf16[128,2048]{1,0:T(8,128)(2,1)}, u32[]{:S(2)}) copy-start(bf16[128,2048]{1,0:T(8,128)(2,1)} %param.17) | copy-start | bytes 1572868
  467.5 156.2 %copy-start.60 = (pred[128]{0:T(512)(128)(4,1)S(1)}, pred[128]{0:T(512)(128)(4,1)}, u32[]{:S(2)}) copy-start(pred[128]{0:T(512)(128)(4,1)} %copy-done.59) | copy-start | bytes 388
  626.0 29.4 %copy-start.6 = (bf16[2048,192]{1,0:T(8,128)(2,1)S(1)}, bf16[2048,192]{1,0:T(8,128)(2,1)}, u32[]{:S(2)}) copy-start(bf16[2048,192]{1,0:T(8,128)(2,1)} %copy-done.5) | copy-start | bytes 2359300
  626.0 29.4 %copy-start.9 = (bf16[2048,128]{1,0:T(8,128)(2,1)S(1)}, bf16[2048,128]{1,0:T(8,128)(2,1)}, u32[]{:S(2)}) copy-start(bf16[2048,128]{1,0:T(8,128)(2,1)} %copy-done.8) | copy-start | bytes 1572868
  672.8 72.4 %all-to-all-start.2 = ((bf16[16,128,512]{1,2,0:T(8,128)(2,1)}), bf16[16,128,512]{1,2,0:T(8,128)(2,1)}, u32[]{:S(2)}, u32[]{:S(2)}) async-start(bf16[16,128,512]{1,2,0:T(8,128)(2,1)} %copy.126), calls=%async_computation.3 | async-start | bytes 4194304 | tf_op jit(solution)/shard_map/all_to_all | solution.py:826
  677.2 424.9 %all-gather.28.cloned.1.call-start = ((), (), s32[]{:S(2)}) async-start(), calls=%async_computation.11 | async-start | bytes 2785280 | tf_op jit(solution)/shard_map/all_gather | solution.py:615
  757.5 376.0 %all-gather.30.cloned.1.call-start = ((), (), s32[]{:S(2)}) async-start(), calls=%async_computation.12 | async-start | bytes 12255232 | tf_op jit(solution)/shard_map/all_gather | solution.py:615
  766.7 2.5 collective-permute-start.6
  773.3 48.4 %collective-permute-start.10 = (f32[16,128]{1,0:T(8,128)S(1)}, f32[16,128]{1,0:T(8,128)S(1)}, u32[]{:S(2)}, u32[]{:S(2)}) collective-permute-start(f32[16,128]{1,0:T(8,128)S(1)} %bitcast.217), channel_id=1, source_target_pairs={{0,1},{1,0},{2,3},{3,2},{4,5},{5,4},{6,7},{7,6},{8,9},{9,8},{10,11... | collective-permute-start | bytes 24584 | tf_op jit(solution)/shard_map/ppermute | solution.py:638
  804.0 51.9 %collective-permute-start.8 = (bf16[1024,2816]{1,0:T(8,128)(2,1)}, bf16[1024,2816]{1,0:T(8,128)(2,1)}, u32[]{:S(2)}, u32[]{:S(2)}) collective-permute-start(bf16[1024,2816]{1,0:T(8,128)(2,1)} %constant_dynamic-slice_fusion.1), channel_id=1, source_target_pairs={{0,1},{1,0},{2,3},{3,2},{4,5},{5,4},{6,7},{7,6},{8,9},{9,8},{10,11... | collective-permute-start | bytes 17301512 | tf_op jit(solution)/shard_map/ppermute | solution.py:638
  821.6 20.9 %collective-permute-start.9 = (bf16[704,2048]{1,0:T(8,128)(2,1)}, bf16[704,2048]{1,0:T(8,128)(2,1)}, u32[]{:S(2)}, u32[]{:S(2)}) collective-permute-start(bf16[704,2048]{1,0:T(8,128)(2,1)} %constant_dynamic-slice_fusion), channel_id=1, source_target_pairs={{0,1},{1,0},{2,3},{3,2},{4,5},{5,4},{6,7},{7,6},{8,9},{9,8},{10,11... | collective-permute-start | bytes 8650760 | tf_op jit(solution)/shard_map/ppermute | solution.py:638
  828.7 13.2 %collective-permute-start.5 = (bf16[1024,16]{0,1:T(8,128)(2,1)S(1)}, bf16[1024,16]{0,1:T(8,128)(2,1)S(1)}, u32[]{:S(2)}, u32[]{:S(2)}) collective-permute-start(bf16[1024,16]{0,1:T(8,128)(2,1)S(1)} %constant_dynamic-slice_fusion.4), channel_id=1, source_target_pairs={{0,1},{1,0},{2,3},{3,2},{4,5},{5,4},{6,7},{7,6},{8,9},{9,8},{10,11... | collective-permute-start | bytes 98312 | tf_op jit(solution)/shard_map/ppermute | solution.py:638
  837.4 38.8 %collective-permute-start.1 = (bf16[1024,2048]{1,0:T(8,128)(2,1)}, bf16[1024,2048]{1,0:T(8,128)(2,1)}, u32[]{:S(2)}, u32[]{:S(2)}) collective-permute-start(bf16[1024,2048]{1,0:T(8,128)(2,1)} %constant_dynamic-slice_fusion.7), channel_id=1, source_target_pairs={{0,1},{1,0},{2,3},{3,2},{4,5},{5,4},{6,7},{7,6},{8,9},{9,8},{10,11... | collective-permute-start | bytes 12582920 | tf_op jit(solution)/shard_map/ppermute | solution.py:638
  854.5 20.8 %collective-permute-start = (bf16[192,1024]{1,0:T(8,128)(2,1)}, bf16[192,1024]{1,0:T(8,128)(2,1)S(1)}, u32[]{:S(2)}, u32[]{:S(2)}) collective-permute-start(bf16[192,1024]{1,0:T(8,128)(2,1)} %constant_dynamic-slice_fusion.8), channel_id=1, source_target_pairs={{0,1},{1,0},{2,3},{3,2},{4,5},{5,4},{6,7},{7,6},{8,9},{9,8},{10,11... | collective-permute-start | bytes 1179656 | tf_op jit(solution)/shard_map/ppermute | solution.py:638
  855.7 19.0 %collective-permute-start.2 = (bf16[256,256]{1,0:T(8,128)(2,1)S(1)}, bf16[256,256]{1,0:T(8,128)(2,1)S(1)}, u32[]{:S(2)}, u32[]{:S(2)}) collective-permute-start(bf16[256,256]{1,0:T(8,128)(2,1)S(1)} %constant_dynamic-slice_fusion.6), channel_id=1, source_target_pairs={{0,1},{1,0},{2,3},{3,2},{4,5},{5,4},{6,7},{7,6},{8,9},{9,8},{10,11... | collective-permute-start | bytes 393224 | tf_op jit(solution)/shard_map/ppermute | solution.py:638
  884.2 74.8 %copy-start.33 = (bf16[128,16,128]{0,2,1:T(8,128)(2,1)S(1)}, bf16[128,16,128]{0,2,1:T(8,128)(2,1)}, u32[]{:S(2)}) copy-start(bf16[128,16,128]{0,2,1:T(8,128)(2,1)} %get-tuple-element.87) | copy-start | bytes 1572868
  1102.1 30.2 %collective-permute-start.3 = (f32[40,128]{1,0:T(8,128)S(1)}, f32[40,128]{1,0:T(8,128)S(1)}, u32[]{:S(2)}, u32[]{:S(2)}) collective-permute-start(f32[40,128]{1,0:T(8,128)S(1)} %reduce_sum.213), channel_id=1, source_target_pairs={{0,1},{1,0},{2,3},{3,2},{4,5},{5,4},{6,7},{7,6},{8,9},{9,8},{10,11... | collective-permute-start | bytes 61448 | tf_op jit(solution)/shard_map/ppermute | solution.py:638
  1112.3 38.9 %collective-permute-start.4 = (bf16[1024,576]{0,1:T(8,128)(2,1)}, bf16[1024,576]{0,1:T(8,128)(2,1)S(1)}, u32[]{:S(2)}, u32[]{:S(2)}) collective-permute-start(bf16[1024,576]{0,1:T(8,128)(2,1)} %constant_dynamic-slice_fusion.5), channel_id=1, source_target_pairs={{0,1},{1,0},{2,3},{3,2},{4,5},{5,4},{6,7},{7,6},{8,9},{9,8},{10,11... | collective-permute-start | bytes 3538952 | tf_op jit(solution)/shard_map/ppermute | solution.py:638
  (57 other events, 462.0 us)
Sparse Core Ops, SparseCore 0:
  13.0 14.9 all-gather.15
  29.5 20.8 all-gather.17
  52.5 10.9 all-gather.19
  65.0 25.0 all-gather.33
  93.2 151.3 all-gather.21
  246.0 14.7 all-gather.35
  389.4 234.2 reduce-scatter.1
  625.2 15.7 all-gather.25
  643.7 123.5 all-gather.31
  768.8 25.5 all-gather.23
  797.1 65.2 all-gather.27
  865.0 189.3 all-gather.29

commit v4 on v3

--- a/solution.py
+++ b/solution.py
@@ -64,13 +64,6 @@
     segment = jnp.where(is_valid, seq_number, lengths_row.shape[0] + slot_ids)
     position = jnp.where(is_valid, slot_ids - first_slot, 0)
     return (segment, position, is_valid)
-
-
-def silu_back(gate_part, up_part, hidden_grad):
-    sigmoid_gate = jax.nn.sigmoid(gate_part)
-    gate_grad = hidden_grad * up_part * sigmoid_gate * (1.0 + gate_part * (1.0 - sigmoid_gate))
-    up_grad = hidden_grad * gate_part * sigmoid_gate
-    return jnp.concatenate([gate_grad, up_grad], axis=1)
 
 
 def dot(left, right):
@@ -129,7 +122,10 @@
     )(query, key, value, segment[:, None], segment[None, :], valid[:, None].astype(jnp.int32))
 
 
-def attention_backward_kernel(scale, q_ref, k_ref, v_ref, g_ref, segc_ref, segr_ref, lse_ref, dq_ref, dk_ref, dv_ref, dk_sum, dv_sum):
+def attention_backward_kernel(
+    scale, q_ref, k_ref, v_ref, g_ref, segc_ref, segr_ref, lse_ref, cos_ref, sin_ref, out_ref, dk_sum, dv_sum
+):
+    half = DR // 2
     count = q_ref.shape[0]
     dk_sum[...] = jnp.zeros_like(dk_sum)
     dv_sum[...] = jnp.zeros_like(dv_sum)
@@ -141,27 +137,30 @@
         prob_grad = dot_nt(grad, v_ref[keys, :])
         mean = jnp.sum(probs * prob_grad, axis=1, keepdims=True)
         score_grad = (probs * (prob_grad - mean)).astype(BF16)
-        dq_ref[rows, :] = (dot(score_grad, k_ref[keys, :]) * scale).astype(BF16)
+        query_grad = (dot(score_grad, k_ref[keys, :]) * scale).astype(BF16)
+        out_ref[rows, :DN] = query_grad[:, :DN]
+        rope = query_grad[:, DN:].astype(F32)
+        swapped = jnp.concatenate([rope[:, half:], rope[:, :half]], axis=1)
+        rope = rope * cos_ref[rows, :DR] - swapped * sin_ref[rows, :DR]
+        out_ref[rows, 2 * DN + DV : 2 * DN + DV + DR] = rope.astype(BF16)
         dk_sum[keys, :] += dot_tn(score_grad, query)
         dv_sum[keys, :] += dot_tn(probs.astype(BF16), grad)
-    dk_ref[...] = (dk_sum[...] * scale).astype(BF16)
-    dv_ref[...] = dv_sum[...].astype(BF16)
-
-
-def attention_backward(query, key, value, grad, segment, log_total):
+    key_grad = (dk_sum[...] * scale).astype(BF16)
+    out_ref[:, DN : 2 * DN] = key_grad[:, :DN]
+    out_ref[:, 2 * DN : 2 * DN + DV] = dv_sum[...].astype(BF16)
+    out_ref[:, 2 * DN + DV + DR :] = key_grad[:, DN:]
+
+
+def attention_backward(query, key, value, grad, segment, log_total, cosines, sines):
     count, width = query.shape
     return pl.pallas_call(
         functools.partial(attention_backward_kernel, width ** (-0.5)),
-        out_shape=(
-            jax.ShapeDtypeStruct(query.shape, BF16),
-            jax.ShapeDtypeStruct(key.shape, BF16),
-            jax.ShapeDtypeStruct(value.shape, BF16),
-        ),
+        out_shape=jax.ShapeDtypeStruct((count, 2 * width + value.shape[1]), BF16),
         scratch_shapes=[pltpu.VMEM(key.shape, F32), pltpu.VMEM(value.shape, F32)],
         compiler_params=pltpu.CompilerParams(vmem_limit_bytes=48 * 2**20),
         cost_estimate=pl.CostEstimate(flops=count * count * 832, bytes_accessed=6 * 2**20, transcendentals=count * count // 2),
         name="attention_backward",
-    )(query, key, value, grad, segment[:, None], segment[None, :], log_total)
+    )(query, key, value, grad, segment[:, None], segment[None, :], log_total, cosines, sines)
 
 
 def swap_halves(values):
@@ -186,12 +185,9 @@
     v_ref[...] = expanded[:, DN:].astype(BF16)
 
 
-def project(rows, gain, weight, gain_kv, expand, angles):
+def project(rows, gain, weight, gain_kv, expand, cosines, sines):
     count = rows.shape[0]
     tile = 256
-    cosine, sine = jnp.cos(angles), jnp.sin(angles)
-    cosines = jnp.concatenate([cosine] * 4, axis=1)
-    sines = jnp.concatenate([-sine, sine] * 2, axis=1)
 
     def by_rows(columns):
         return pl.BlockSpec((tile, columns), lambda i: (i, 0))
@@ -218,6 +214,160 @@
         cost_estimate=pl.CostEstimate(flops=2 * count * D * 900, bytes_accessed=24 * 2**20, transcendentals=count),
         name="project",
     )(rows, gain[None], weight, gain_kv[None], expand, cosines, sines)
+
+
+BLOCKS = 4
+
+
+def silu_grads(gate, up, grad):
+    sig = jax.nn.sigmoid(gate)
+    return grad * up * sig * (1.0 + gate * (1.0 - sig)), grad * gate * sig
+
+
+def pick_of(place_ref, b, capacity):
+    tok = place_ref.shape[1]
+    return lax.broadcasted_iota(jnp.int32, (capacity, tok), 0) == place_ref[b : b + 1, :]
+
+
+def as_weights(match):
+    return jnp.where(match, 1.0, 0.0).astype(BF16)
+
+
+def spread_kernel(
+    ffn_ref, up_ref, place_ref, gate_ref, in_ref, out_ref,
+    x_ref, rg_ref, hidden_ref, grad_ref, gout_ref, gin_ref,
+    sum_out, sum_in,
+):
+    step = pl.program_id(0)
+    blocks, tok = place_ref.shape
+    capacity = x_ref.shape[0] // blocks
+    units = out_ref.shape[0]
+    for b in range(blocks):
+        match = pick_of(place_ref, b, capacity)
+        pick = as_weights(match)
+        gate = jnp.sum(jnp.where(match, gate_ref[b : b + 1, :], 0.0), axis=1, keepdims=True)
+        tokens, rows = pl.ds(b * tok, tok), pl.ds(b * capacity, capacity)
+        x_ref[rows, :] = dot(pick, ffn_ref[tokens, :]).astype(BF16)
+        rg_ref[rows, :] = (gate * dot(pick, up_ref[tokens, :])).astype(BF16)
+    both = dot(ffn_ref[...], in_ref[...])
+    gate, up = both[:, :units], both[:, units:]
+    hidden = (gate * jax.nn.sigmoid(gate) * up).astype(BF16)
+    hidden_ref[...] = hidden
+    grads = silu_grads(gate, up, dot_nt(up_ref[...], out_ref[...]))
+    grad = jnp.concatenate(grads, axis=1).astype(BF16)
+    grad_ref[...] = grad
+
+    @pl.when(step == 0)
+    def _():
+        sum_out[...] = jnp.zeros_like(sum_out)
+        sum_in[...] = jnp.zeros_like(sum_in)
+
+    sum_out[...] += dot_tn(hidden, up_ref[...])
+    sum_in[...] += dot_tn(grad, ffn_ref[...])
+
+    @pl.when(step == pl.num_programs(0) - 1)
+    def _():
+        gout_ref[...] = sum_out[...].astype(BF16)
+        gin_ref[...] = sum_in[...].astype(BF16)
+
+
+def by_rows(size, columns):
+    return pl.BlockSpec((size, columns), lambda i: (i, 0))
+
+
+def whole(array):
+    return pl.BlockSpec(array.shape, lambda i: (0, 0), pipeline_mode=pl.Buffered(1))
+
+
+def by_step(tok):
+    return pl.BlockSpec((None, BLOCKS, tok), lambda i: (i, 0, 0))
+
+
+def in_steps(rows):
+    return rows.reshape(-1, BLOCKS, rows.shape[1])
+
+
+def spread(ffn, upstream, place, gates, shared_in, shared_out, capacity):
+    count = ffn.shape[0]
+    seq, tok = place.shape
+    steps = seq // BLOCKS
+    units = shared_out.shape[0]
+    t, rows = BLOCKS * tok, BLOCKS * capacity
+    outs = [(rows, D), (rows, D), (t, units), (t, 2 * units)]
+    fixed = [(units, D), (2 * units, D)]
+    flops = 4 * seq * capacity * tok * D + 2 * count * 6 * D * units
+    return pl.pallas_call(
+        spread_kernel,
+        grid=(steps,),
+        in_specs=[by_rows(t, D), by_rows(t, D), by_step(tok), by_step(tok), whole(shared_in), whole(shared_out)],
+        out_specs=tuple(by_rows(*o) for o in outs) + tuple(pl.BlockSpec(o, lambda i: (0, 0)) for o in fixed),
+        out_shape=tuple(jax.ShapeDtypeStruct((r * steps, c), BF16) for r, c in outs)
+        + tuple(jax.ShapeDtypeStruct(o, BF16) for o in fixed),
+        scratch_shapes=[pltpu.VMEM(o, F32) for o in fixed],
+        compiler_params=pltpu.CompilerParams(vmem_limit_bytes=56 * 2**20),
+        cost_estimate=pl.CostEstimate(flops=flops, bytes_accessed=40 * 2**20, transcendentals=2 * count * units),
+        name="spread",
+    )(ffn, upstream, in_steps(place), in_steps(gates), shared_in, shared_out)
+
+
+def collect_forward_kernel(res_ref, up_ref, place_ref, gate_ref, hidden_ref, out_ref, mixed_ref, dots_ref):
+    blocks, tok = place_ref.shape
+    capacity = res_ref.shape[0] // blocks
+    for b in range(blocks):
+        pick = as_weights(pick_of(place_ref, b, capacity))
+        tokens, rows = pl.ds(b * tok, tok), pl.ds(b * capacity, capacity)
+        mine = dot_tn(pick, res_ref[rows, :])
+        dots_ref[tokens, :] = jnp.sum(up_ref[tokens, :].astype(F32) * mine, axis=1, keepdims=True)
+        shared = dot(hidden_ref[tokens, :], out_ref[...])
+        mixed_ref[tokens, :] = (gate_ref[tokens, :] * mine + shared).astype(BF16)
+
+
+def collect_forward(results, upstream, place, gates, hidden, shared_out, capacity):
+    count = upstream.shape[0]
+    seq, tok = place.shape
+    steps = seq // BLOCKS
+    t, rows = BLOCKS * tok, BLOCKS * capacity
+    units = shared_out.shape[0]
+    flops = 2 * seq * capacity * tok * D + 2 * count * D * units
+    return pl.pallas_call(
+        collect_forward_kernel,
+        grid=(steps,),
+        in_specs=[by_rows(rows, D), by_rows(t, D), by_step(tok), by_rows(t, 1), by_rows(t, units), whole(shared_out)],
+        out_specs=(by_rows(t, D), by_rows(t, 1)),
+        out_shape=(jax.ShapeDtypeStruct((count, D), BF16), jax.ShapeDtypeStruct((count, 1), F32)),
+        compiler_params=pltpu.CompilerParams(vmem_limit_bytes=48 * 2**20),
+        cost_estimate=pl.CostEstimate(flops=flops, bytes_accessed=24 * 2**20, transcendentals=0),
+        name="collect_forward",
+    )(results, upstream, in_steps(place), gates.reshape(-1, 1), hidden, shared_out)
+
+
+def collect_backward_kernel(rows_ref, place_ref, grad_ref, in_ref, back_ref):
+    blocks, tok = place_ref.shape
+    capacity = rows_ref.shape[0] // blocks
+    shared = dot_nt(grad_ref[...], in_ref[...])
+    for b in range(blocks):
+        pick = as_weights(pick_of(place_ref, b, capacity))
+        tokens, rows = pl.ds(b * tok, tok), pl.ds(b * capacity, capacity)
+        mine = dot_tn(pick, rows_ref[rows, :])
+        back_ref[tokens, :] = (mine + shared[b * tok : (b + 1) * tok]).astype(BF16)
+
+
+def collect_backward(row_grads, place, grads, shared_in, capacity):
+    count = grads.shape[0]
+    seq, tok = place.shape
+    steps = seq // BLOCKS
+    t, rows = BLOCKS * tok, BLOCKS * capacity
+    flops = 2 * seq * capacity * tok * D + 2 * count * D * grads.shape[1]
+    return pl.pallas_call(
+        collect_backward_kernel,
+        grid=(steps,),
+        in_specs=[by_rows(rows, D), by_step(tok), by_rows(t, grads.shape[1]), whole(shared_in)],
+        out_specs=by_rows(t, D),
+        out_shape=jax.ShapeDtypeStruct((count, D), BF16),
+        compiler_params=pltpu.CompilerParams(vmem_limit_bytes=48 * 2**20),
+        cost_estimate=pl.CostEstimate(flops=flops, bytes_accessed=18 * 2**20, transcendentals=0),
+        name="collect_backward",
+    )(row_grads, in_steps(place), grads, shared_in)
 
 
 def turn_kernel(in_ref, out_ref):
@@ -448,25 +598,46 @@
 ADD_ROWS = 16
 
 
+def slot_table(order):
+    table, used = {}, 0
+    for dy in (0, 1):
+        for dx in (0, 1):
+            for kind in ("x", "y", "up", "down"):
+                step = {"x": (0, 0, 1), "y": (0, 1, 0), "up": (1, 0, 0), "down": (-1, 0, 0)}[kind]
+                met = [o[0] for o in OFFSETS if o[1:] == (dy, dx) and step in onward(order, o)]
+                if not met:
+                    continue
+                if kind == "down":
+                    table[dy, dx, "down"] = (used, False)
+                    used += 1
+                    continue
+                spread = any(met)
+                table[dy, dx, kind] = (used, spread)
+                used += LINE if spread else 1
+    return table, used
+
+
+def slot_at(table, z, offset, step):
+    dz, dy, dx = offset
+    kind = "x" if step[2] else "y" if step[1] else "down" if step[0] < 0 and dz == 0 else "up"
+    first, spread = table[dy, dx, kind]
+    return first + (z + dz) if spread else first
+
+
 def scatter_kernel(streams, n_main, n_small, *refs):
     n = n_main + n_small
     ins, outs = refs[:n], refs[n : 2 * n]
     scratch = refs[2 * n :]
-    bufs, accs = scratch[: len(streams)], scratch[len(streams) : 2 * len(streams)]
-    send_sems, recv_sems, small_send, small_recv, local_sems = scratch[2 * len(streams) :]
+    bufs = scratch[: len(streams)]
+    send_sems, recv_sems, small_send, small_recv, local_sems = scratch[len(streams) :]
     rank, z, y, x = place()
     count = lax.axis_size("seq")
-    slot_of, acc_of = {}, {}
-    for s, stream in enumerate(streams):
-        k = 0
-        a = 0
-        for offset in OFFSETS:
-            for step in onward(stream[3], offset):
-                slot_of[s, offset, step] = (k, len(slot_of))
-                k += 1
-            if hops(offset) and onward(stream[3], offset):
-                acc_of[s, offset] = a
-                a += 1
+    tables, bases, base = [], [], 0
+    for stream in streams:
+        table, used = slot_table(stream[3])
+        tables.append(table)
+        bases.append(base)
+        base += used
     greet_all()
 
     def small_copy(i, k):
@@ -487,25 +658,23 @@
     send_slot = {key: i for i, key in enumerate(k for k in todo if hops(k[1]))}
 
     def send_copy(s, offset, source):
-        order = streams[s][3]
-        step = toward(order, offset)
-        k, sem = slot_of[s, seen_from(offset, step), back(step)]
+        step = toward(streams[s][3], offset)
+        k = slot_at(tables[s], z + step[0], seen_from(offset, step), back(step))
         return pltpu.make_async_remote_copy(
             src_ref=source,
             dst_ref=bufs[s].at[k],
             send_sem=send_sems.at[send_slot[s, offset]],
-            recv_sem=recv_sems.at[sem],
+            recv_sem=recv_sems.at[bases[s] + k],
             device_id={"seq": rank_at(z, y, x, *step)},
             device_id_type=MESH,
         )
 
-    def wait_child(s, offset, step):
-        k, sem = slot_of[s, offset, step]
+    def wait_child(s, k):
         pltpu.make_async_remote_copy(
             src_ref=bufs[s].at[k],
             dst_ref=bufs[s].at[k],
             send_sem=send_sems.at[0],
-            recv_sem=recv_sems.at[sem],
+            recv_sem=recv_sems.at[bases[s] + k],
             device_id={"seq": rank},
             device_id_type=MESH,
         ).wait_recv()
@@ -522,11 +691,11 @@
             if not present:
                 send_copy(s, offset, own).start()
                 return
-            for step in present:
-                wait_child(s, offset, step)
+            slots = [slot_at(tables[s], z, offset, step) for step in present]
+            for k in slots:
+                wait_child(s, k)
             final = not hops(offset)
-            target = outs[index].at[pl.ds(first, rows)] if final else accs[s].at[acc_of[s, offset]]
-            slots = [slot_of[s, offset, step][0] for step in present]
+            target = outs[index].at[pl.ds(first, rows)] if final else bufs[s].at[slots[0]]
 
             def add(i, carry):
                 part = pl.ds(pl.multiple_of(i * ADD_ROWS, ADD_ROWS), ADD_ROWS)
@@ -570,8 +739,12 @@
             source = lax.rem(rank + k, count)
             block = outs[n_main + i].at[source]
             pltpu.make_async_remote_copy(
-                src_ref=block, dst_ref=block, send_sem=small_send.at[0],
-                recv_sem=small_recv.at[i * count + source], device_id={"seq": rank}, device_id_type=MESH,
+                src_ref=block,
+                dst_ref=block,
+                send_sem=small_send.at[0],
+                recv_sem=small_recv.at[i * count + source],
+                device_id={"seq": rank},
+                device_id_type=MESH,
             ).wait_recv()
         pltpu.make_async_copy(ins[n_main + i], outs[n_main + i].at[rank], local_sems.at[i]).wait()
 
@@ -587,26 +760,30 @@
     arrays = list(main) + list(small)
     any_spec = pl.BlockSpec(memory_space=pl.ANY)
     vmem = pl.BlockSpec(memory_space=pltpu.VMEM)
-    buffers, sums = [], []
-    for index, first, rows, order in streams:
-        columns = main[index].shape[2]
-        slots = sum(len(onward(order, o)) for o in OFFSETS)
-        held = sum(1 for o in OFFSETS if hops(o) and onward(order, o))
-        buffers.append(pltpu.VMEM((slots, rows, columns), main[index].dtype))
-        sums.append(pltpu.VMEM((held, rows, columns), main[index].dtype))
+    places = [slot_table(stream[3])[1] for stream in streams]
+    buffers = [
+        pltpu.VMEM((used, rows, main[index].shape[2]), main[index].dtype)
+        for used, (index, first, rows, order) in zip(places, streams)
+    ]
     return pl.pallas_call(
         functools.partial(scatter_kernel, streams, len(main), len(small)),
-        out_shape=tuple([jax.ShapeDtypeStruct(a.shape[1:], F32) for a in main] + [jax.ShapeDtypeStruct((count,) + a.shape, a.dtype) for a in small]),
+        out_shape=tuple(
+            [jax.ShapeDtypeStruct(a.shape[1:], F32) for a in main]
+            + [jax.ShapeDtypeStruct((count,) + a.shape, a.dtype) for a in small]
+        ),
         in_specs=[vmem] * len(main) + [any_spec] * len(small),
         out_specs=tuple([vmem] * len(main) + [any_spec] * len(small)),
-        scratch_shapes=buffers + sums + [
+        scratch_shapes=buffers
+        + [
             pltpu.SemaphoreType.DMA((len(streams) * len(OFFSETS),)),
-            pltpu.SemaphoreType.DMA((n_sends(streams),)),
+            pltpu.SemaphoreType.DMA((sum(places),)),
             pltpu.SemaphoreType.DMA((max(1, len(small)) * count,)),
             pltpu.SemaphoreType.DMA((max(1, len(small)) * count,)),
             pltpu.SemaphoreType.DMA((max(1, len(small)),)),
         ],
-        compiler_params=pltpu.CompilerParams(collective_id=collective_id, has_side_effects=True, vmem_limit_bytes=60 * 2**20),
+        compiler_params=pltpu.CompilerParams(
+            collective_id=collective_id, has_side_effects=True, vmem_limit_bytes=60 * 2**20
+        ),
         name="scatter_sum",
     )(*arrays)
 
@@ -699,12 +876,14 @@
     gain_ffn = small[:, ends[2] : ends[3]].reshape(-1).astype(F32)
     router_weight = small[:, ends[3] : ends[4]].reshape(D, experts)
     head_query_part = lax.dynamic_slice_in_dim(w_q, rank * query_width, query_width, 1)
+    lanes = -(-units // 128) * 128
+    unit_slices = [
+        lax.dynamic_slice_in_dim(w_shared_in, i * (SH // fsdp_count) + rank * unit, unit, 1)
+        for i in range(2 * fsdp_count)
+    ]
+    filler = jnp.zeros((row_part, lanes - units), BF16)
     shared_in_part = jnp.concatenate(
-        [
-            lax.dynamic_slice_in_dim(w_shared_in, i * (SH // fsdp_count) + rank * unit, unit, 1)
-            for i in range(2 * fsdp_count)
-        ],
-        axis=1,
+        unit_slices[:fsdp_count] + [filler] + unit_slices[fsdp_count:] + [filler], axis=1
     )
     head_expand = gather_fsdp(lax.dynamic_slice_in_dim(w_kvb, rank * kv_width, kv_width, 1))
     head_weights = gather_fsdp(
@@ -712,6 +891,7 @@
     )
     shared_in = gather_fsdp(shared_in_part)
     shared_out = gather_fsdp(lax.dynamic_slice_in_dim(w_shared_out, rank * unit, unit, 0))
+    shared_out = jnp.pad(shared_out, ((0, lanes - units), (0, 0)))
     output_weight = gather_fsdp(w_o)
     expert_in = gather_fsdp(w_expert_in[0])
     expert_out = gather_fsdp(w_expert_out[0])
@@ -720,14 +900,17 @@
 
     slot_ids = jnp.arange(group_size, dtype=jnp.int32)
     segment, position, valid_all = layout(lengths[0], slot_ids)
-    angles_all = position[:, None].astype(F32) * frequencies(DR)[None, :]
-    angles = own(angles_all)
+    angles = own(position)[:, None].astype(F32) * frequencies(DR)[None, :]
+    wide_angles = position[:, None].astype(F32) * jnp.tile(frequencies(DR), 4)[None, :]
+    cosines = jnp.cos(wide_angles)
+    signs = jnp.where(jnp.arange(2 * DR) % DR < DR // 2, -1.0, 1.0).astype(F32)
+    sines = jnp.sin(wide_angles) * signs[None, :]
 
     upstream_own = jnp.where(own(valid_all)[:, None], cotangent, 0).astype(BF16)
     upstream_all = gather_seq(upstream_own)
 
     normed_all, query, key, value, latent_full, latent_all = project(
-        token_all, gain_attn, head_weights, gain_latent, head_expand, angles_all
+        token_all, gain_attn, head_weights, gain_latent, head_expand, cosines, sines
     )
     context, log_total, head_largest = attention_forward(query, key, value, segment, valid_all)
     context_low = lax.all_to_all(context, "seq", split_axis=0, concat_axis=1, tiled=True)
@@ -746,62 +929,37 @@
     gates = lax.dynamic_slice_in_dim(router_probs, rank, 1, 1).reshape(seq_count, tok_count)
     place = jnp.cumsum(chosen.astype(jnp.int32), axis=1) - 1
     place = jnp.where(chosen, place, capacity)
-    picks = lax.broadcasted_iota(jnp.int32, (seq_count, capacity, tok_count), 1) == place[:, None, :]
-    pick = picks.astype(BF16)
-    row_gate = jnp.sum(jnp.where(picks, gates[:, None, :], 0.0), axis=2).reshape(buffer_rows, 1)
-
-    def to_slots(rows):
-        return lax.dot_general(
-            pick,
-            rows.reshape(seq_count, tok_count, D),
-            (((2,), (1,)), ((0,), (0,))),
-            preferred_element_type=F32,
-        ).reshape(buffer_rows, D)
-
-    def to_tokens(rows):
-        return lax.dot_general(
-            pick,
-            rows.reshape(seq_count, capacity, D),
-            (((1,), (1,)), ((0,), (0,))),
-            preferred_element_type=F32,
-        ).reshape(group_size, D)
-
-    arrived = to_slots(ffn_all).astype(BF16)
-    gate_up = dot(arrived, expert_in)
-    hidden = (jax.nn.silu(gate_up[:, :FF]) * gate_up[:, FF:]).astype(BF16)
-    result = dot(hidden, expert_out).astype(BF16).astype(F32)
-    shared_both = dot(ffn_all, shared_in)
-    shared_hidden = (jax.nn.silu(shared_both[:, :units]) * shared_both[:, units:]).astype(BF16)
-    mixed_part = to_tokens((row_gate * result).astype(BF16)) + dot(shared_hidden, shared_out)
-    mixed_sum = scatter_seq(mixed_part.astype(BF16))
-    mixed = (middle + mixed_sum.astype(F32)).astype(BF16)
-
-    upstream_rows = to_slots(upstream_all)
-    row_gate_grad = jnp.sum(upstream_rows * result, axis=1).reshape(seq_count, capacity)
-    gate_grad = jnp.sum(jnp.where(picks, row_gate_grad[:, :, None], 0.0), axis=1)
-    result_grad = (row_gate * upstream_rows).astype(BF16)
-    d_hidden = dot_nt(result_grad, expert_out)
-    grad_expert_out = dot_tn(hidden, result_grad)
-    d_gate_up = silu_back(gate_up[:, :FF], gate_up[:, FF:], d_hidden).astype(BF16)
-    grad_expert_in = dot_tn(arrived, d_gate_up)
-    row_grad = dot_nt(d_gate_up, expert_in).astype(BF16)
-    shared_hidden_grad = dot_nt(upstream_all, shared_out)
-    shared_grad = silu_back(shared_both[:, :units], shared_both[:, units:], shared_hidden_grad).astype(BF16)
-    ffn_part = to_tokens(row_grad) + dot_nt(shared_grad, shared_in)
-    ffn_sum, prob_grads = scatter_sum(
-        [ffn_part.astype(BF16).reshape(seq_count, tok_count, D)], [ROW_PARTS], [gate_grad], 3
-    )
-    prob_grads = prob_grads.reshape(experts, group_size).T
-    grad_shared_out = dot_tn(shared_hidden, upstream_all)
-    grad_shared_in = dot_tn(shared_grad, ffn_all)
-    sum_expert_in = scatter_fsdp(grad_expert_in.astype(BF16))[None]
-    sum_expert_out = scatter_fsdp(grad_expert_out.astype(BF16))[None]
-    part_shared_out = scatter_fsdp(grad_shared_out.astype(BF16)).astype(BF16)
-    part_shared_in = scatter_fsdp(grad_shared_in.astype(BF16), 1).astype(BF16)
+
+    arrived, result_grad, shared_hidden, shared_grad, grad_shared_out, grad_shared_in = spread(
+        ffn_all, upstream_all, place, gates, shared_in, shared_out, capacity
+    )
+    part_shared_out = scatter_fsdp(grad_shared_out[:units]).astype(BF16)
+    part_shared_in = jnp.concatenate([grad_shared_in[:units], grad_shared_in[lanes : lanes + units]], axis=0)
+    part_shared_in = scatter_fsdp(part_shared_in, 1).astype(BF16)
     sum_shared_out = gather_seq(part_shared_out).astype(F32)
     sum_shared_in = turn_units(
         gather_seq(part_shared_in).reshape(seq_count, 2 * fsdp_count, unit, row_part)
     )
+
+    gate_up = dot(arrived, expert_in).astype(BF16)
+    gate_part, up_part = gate_up[:, :FF].astype(F32), gate_up[:, FF:].astype(F32)
+    hidden = (jax.nn.silu(gate_part) * up_part).astype(BF16)
+    result = dot(hidden, expert_out).astype(BF16)
+    d_hidden = dot_nt(result_grad, expert_out)
+    d_gate_up = jnp.concatenate(silu_grads(gate_part, up_part, d_hidden), axis=1).astype(BF16)
+    row_grad = dot_nt(d_gate_up, expert_in).astype(BF16)
+    mixed_part, gate_grad = collect_forward(
+        result, upstream_all, place, gates, shared_hidden, shared_out, capacity
+    )
+    ffn_part = collect_backward(row_grad, place, shared_grad, shared_in, capacity)
+    mixed_sum, ffn_sum, prob_grads = scatter_sum(
+        [part.reshape(seq_count, tok_count, D) for part in (mixed_part, ffn_part)],
+        [ROW_PARTS, ROW_PARTS],
+        [gate_grad.reshape(seq_count, tok_count)],
+        3,
+    )
+    mixed = (middle + mixed_sum).astype(BF16)
+    prob_grads = prob_grads.reshape(experts, group_size).T
 
     logit_grads = (
         router_probs * (prob_grads - jnp.sum(router_probs * prob_grads, axis=-1, keepdims=True))
@@ -822,35 +980,34 @@
         [grad_output.reshape(seq_count, output_rows, D)], [split_rows(output_rows)], [], 5
     )
 
-    query_grad, key_grad, value_grad = attention_backward(query, key, value, head_grad, segment, log_total)
+    head_back = attention_backward(query, key, value, head_grad, segment, log_total, cosines, sines)
+    head_back, arrived, result_grad, hidden, d_gate_up = lax.optimization_barrier(
+        (head_back, arrived, result_grad, hidden, d_gate_up)
+    )
     back = lax.all_to_all(
-        jnp.concatenate([query_grad, key_grad, value_grad], axis=1).reshape(seq_count, tok_count, -1),
-        "seq",
-        split_axis=0,
-        concat_axis=0,
-        tiled=True,
-    )
-    query_grad_32 = query_grad.astype(F32)
-    head_pre_grad = jnp.concatenate(
-        [query_grad_32[:, :DN], rotate(query_grad_32[:, DN:], -angles_all)], axis=1
-    ).astype(BF16)
-    part_query = scatter_fsdp(dot_tn(head_pre_grad, normed_all).astype(BF16), 1).astype(BF16)
-    head_expand_grad = jnp.concatenate([key_grad[:, :DN], value_grad], axis=1)
-    part_expand = scatter_fsdp(dot_tn(head_expand_grad, latent_all).astype(BF16), 1).astype(BF16)
+        head_back.reshape(seq_count, tok_count, -1), "seq", split_axis=0, concat_axis=0, tiled=True
+    )
+    grad_expert_out = dot_tn(hidden, result_grad).astype(BF16)
+    grad_expert_in = dot_tn(arrived, d_gate_up).astype(BF16)
+    rope_at = 2 * DN + DV
+    head_pre_grad = jnp.concatenate([head_back[:, :DN], head_back[:, rope_at : rope_at + DR]], axis=1)
+    grad_query = dot_tn(head_pre_grad, normed_all).astype(BF16)
+    grad_expand = dot_tn(head_back[:, DN:rope_at], latent_all).astype(BF16)
+    back, grad_expert_out, grad_expert_in, grad_query, grad_expand = lax.optimization_barrier(
+        (back, grad_expert_out, grad_expert_in, grad_query, grad_expand)
+    )
+    sum_expert_in = scatter_fsdp(grad_expert_in)[None]
+    sum_expert_out = scatter_fsdp(grad_expert_out)[None]
+    part_query = scatter_fsdp(grad_query, 1).astype(BF16)
+    part_expand = scatter_fsdp(grad_expand, 1).astype(BF16)
 
     back = back.transpose(1, 0, 2)
-    back_query = back[..., :query_width].astype(F32)
-    back_key = back[..., query_width : 2 * query_width]
-    back_value = back[..., 2 * query_width :]
-    pre_grad = (
-        jnp.concatenate([back_query[..., :DN], rotate(back_query[..., DN:], -angles[:, None, :])], axis=-1)
-        .reshape(tok_count, H * query_width)
-        .astype(BF16)
-    )
-    expand_grad = jnp.concatenate([back_key[..., :DN], back_value], axis=-1).reshape(tok_count, H * kv_width)
+    pre_grad = jnp.concatenate([back[..., :DN], back[..., rope_at : rope_at + DR]], axis=-1)
+    pre_grad = pre_grad.reshape(tok_count, H * query_width)
+    expand_grad = back[..., DN:rope_at].reshape(tok_count, H * kv_width)
     latent_grad = dot_nt(expand_grad, expand_weight)
-    rope_grad = rotate(jnp.sum(back_key[..., DN:].astype(F32), axis=1), -angles)
-    latent_pull = jax.vjp(rms_norm, own(latent_full)[:, :KVR], gain_latent)[1]
+    rope_grad = rotate(jnp.sum(back[..., rope_at + DR :].astype(F32), axis=1), -angles)
+    latent_pull = jax.vjp(rms_norm, own(latent_full), gain_latent)[1]
     compressed_grad, grad_gain_latent = latent_pull(latent_grad)
     full_grad = jnp.concatenate([compressed_grad, rope_grad], axis=1).astype(BF16)
     full_all = gather_seq(full_grad)

time: 1170 us -> 1050 us (0.90)
  matrix products: 264 us -> 180 us
  waiting for transfers between devices: 85.2 us -> 49 us
  Pallas kernels: 592 us -> 623 us
  blocking collectives: 29.3 us -> 6.39 us
  other arithmetic: 111 us -> 88.8 us
    all_to_all x1 -> x2, waiting for transfers between devices: 60.6 us -> 2.99 us  [the longest x1 2.98 us: on_device(): lax.all_to_all(context_grad, 'seq', split_axis=1, concat_axis=0, tiled=True)]
    pallas_call x0 -> x3, Pallas kernels: none -> 53.8 us  [the longest x1 31.8 us: spread(): pl.pallas_call(spread_kernel, grid=(steps,), in_specs=[by_rows(t, D), by_...]
    pallas_call x2, Pallas kernels: 217 us -> 178 us  [scatter_sum(): pl.pallas_call(functools.partial(scatter_kernel, streams, len(main), len(...]
    dot_general x4 -> x0, matrix products: 37.7 us -> none  [the longest x2 19.7 us: to_tokens(): lax.dot_general(pick, rows.reshape(seq_count, capacity, D), (((1,), (1,))...]
    all_gather x4, waiting for transfers between devices: 0.03 us -> 23.7 us  [gather_seq(): return lax.all_gather(rows, 'seq', axis=0, tiled=True)]
    all_to_all x1 -> x0, blocking collectives: 22.5 us -> none  [on_device(): lax.all_to_all(context_grad, 'seq', split_axis=1, concat_axis=0, tiled=True)]
    dot_general x6 -> x4, matrix products: 69.9 us -> 50.3 us  [dot(): return jnp.dot(left, right, preferred_element_type=F32)]
    dot_general x9 -> x7, matrix products: 85 us -> 70.5 us  [dot_nt(): lax.dot_general(left, right, (((1,), (1,)), ((), ())), preferred_element_...]
  transfers between devices with their start and end apart: 25 -> 25, of which waited for: 5 -> 6; matrix products, arithmetic and copies ran while one was open for 30% -> 30% of each run, Pallas kernels for 51% -> 58%
where the time goes in v4:
time: 1050 us; the launch traced here: 1040 us
  Pallas kernels  623 us (59%)
  matrix products  180 us (17%)
  other arithmetic  88.8 us (8%)
  local copies, waits for them, and re-layouts  57.8 us (6%)
  waiting for transfers between devices  49 us (5%)
  starting transfers between devices  16.2 us (2%)
  between operations  15.4 us (1%)
    pallas_call x3, Pallas kernels, gather_all(): pl.pallas_call(functools.partial(gather_kernel, streams, len(main), len(s...  321 us
    pallas_call x2, Pallas kernels, scatter_sum(): pl.pallas_call(functools.partial(scatter_kernel, streams, len(main), len(...  178 us
    dot_general x7, matrix products, dot_nt(): lax.dot_general(left, right, (((1,), (1,)), ((), ())), preferred_element_...  70.5 us
    dot_general x7, matrix products, dot_tn(): lax.dot_general(left, right, (((0,), (0,)), ((), ())), preferred_element_...  59.5 us
    dot_general x4, matrix products, dot(): return jnp.dot(left, right, preferred_element_type=F32)  50.3 us
    pallas_call x1, Pallas kernels, spread(): pl.pallas_call(spread_kernel, grid=(steps,), in_specs=[by_rows(t, D), by_...  31.8 us
    all_gather x4, waiting for transfers between devices, gather_seq(): return lax.all_gather(rows, 'seq', axis=0, tiled=True)  23.7 us
  transfers between devices with their start and end apart: 25, of which 6 were waited for; matrix products, arithmetic and copies ran while one was open for 30% of the time, Pallas kernels for 58%

profile of v4, /device:TPU:0, one launch (start us, length us, event | category | flops | bytes accessed | tf_op | source)
XLA Modules:
  0.0 1037.2 jit_solution(11945724542925655746)
XLA Ops:
  15.7 3.3 concatenate.37
  32.3 103.1 %gather_all.3 = (bf16[16,128,2048]{2,1,0:T(8,128)(2,1)}, bf16[16,16,128]{2,1,0:T(8,128)(2,1)}) custom-call(bf16[128,2048]{1,0:T(8,128)(2,1)} %refs_0_.1, bf16[16,128]{1,0:T(8,128)(2,1)} %convert_element_type.233.refs_1_), custom_call_target="tpu_custom_call" | custom-call | tf_op jit(solution)/shard_map/gather_all/pallas_call | solution.py:567
  135.4 3.7 fusion.24
  139.1 17.1 %project.1 = (bf16[2048,2048]{1,0:T(8,128)(2,1)}, bf16[2048,192]{1,0:T(8,128)(2,1)S(1)}, bf16[2048,192]{1,0:T(8,128)(2,1)S(1)}, bf16[2048,128]{1,0:T(8,128)(2,1)...) custom-call(bf16[2048,2048]{1,0:T(8,128)(2,1)} %bitcast.175, f32[1,2048]{1,0:T(1,128)S(1)} %bitcast.128, ...), custom_call_target="tpu_custom_call" | custom-call | flops 7549747200 | bytes 25165824 | tf_op jit(solution)/shard_map/project/pallas_call | solution.py:199
  156.3 8.6 attention_forward.1
  166.9 3.6 all-to-all-start
  181.1 9.2 all-to-all-done
  190.3 4.9 multiply_reduce_fusion.2
  197.2 65.7 %gather_all.4 = (bf16[16,128,2048]{2,1,0:T(8,128)(2,1)}, f32[16,8,128]{2,1,0:T(8,128)}) custom-call(bf16[128,2048]{1,0:T(8,128)(2,1)} %multiply_convert_fusion.1.refs_0_, f32[8,128]{1,0:T(8,128)} %copy-done.11), custom_call_target="tpu_custom_call" | custom-call | tf_op jit(solution)/shard_map/gather_all/pallas_call | solution.py:567
  262.9 5.7 fusion.78
  272.1 31.8 %spread.1 = (bf16[1536,2048]{1,0:T(8,128)(2,1)}, bf16[1536,2048]{1,0:T(8,128)(2,1)}, bf16[2048,256]{1,0:T(8,128)(2,1)}, bf16[2048,512]{1,0:T(8,128)(2,1)}, bf16[...) custom-call(bf16[2048,2048]{1,0:T(8,128)(2,1)} %bitcast.131, bf16[2048,2048]{1,0:T(8,128)(2,1)} %all-gather.20.cloned.1.call-done.up_ref, ...), custom_call_target="tpu_custom_call" | custom-call | flops 14495514624 | bytes 41943040 | tf_op jit(solution)/shard_map/spread/pallas_call | solution.py:299
  304.0 24.6 %fusion.4 = bf16[1536,2816]{1,0:T(8,128)(2,1)} fusion(bf16[1536,2048]{1,0:T(8,128)(2,1)} %get-tuple-element.74, bf16[1,2048,2816]{2,1,0:T(8,128)(2,1)} %all-gather.34.cloned.1.call-done), kind=kOutput, calls=%fused_computation.11 | convolution fusion | flops 17721065472 | bytes 26476544 | tf_op jit(solution)/shard_map/dot_general | solution.py:70
  328.6 22.3 %fusion.10 = (bf16[1536,1408]{1,0:T(8,128)(2,1)}, bf16[1536,1408]{1,0:T(8,128)(2,1)}, bf16[1536,1408]{1,0:T(8,128)(2,1)}) fusion(bf16[1536,2816]{1,0:T(8,128)(2,1)} %fusion.4, bf16[1536,2048]{1,0:T(8,128)(2,1)} %get-tuple-element.73, bf16[1,1408,2048]{2,1,0:T(8,128)(2,1)} %all-gather.36.cloned.1.call-done), kind=kOutput, calls=%fused_computation.17 | convolution fusion | flops 8897298432 | bytes 33685504 | tf_op jit(solution)/shard_map/dot_general | solution.py:78
  350.9 15.0 %convolution_convert_fusion.2.res_ref = bf16[1536,2048]{1,0:T(8,128)(2,1)} fusion(bf16[1536,1408]{1,0:T(8,128)(2,1)} %get-tuple-element.72, bf16[1,1408,2048]{2,1,0:T(8,128)(2,1)} %all-gather.36.cloned.1.call-done), kind=kOutput, calls=%fused_computation.28 | convolution fusion | flops 8861515776 | bytes 16384000 | tf_op jit(solution)/shard_map/dot_general | solution.py:70
  366.0 24.9 %fusion.17.rows_ref = bf16[1536,2048]{1,0:T(8,128)(2,1)} fusion(bf16[1,2048,2816]{2,1,0:T(8,128)(2,1)} %all-gather.34.cloned.1.call-done, bf16[1536,1408]{1,0:T(8,128)(2,1)} %get-tuple-element.106, bf16[1536,1408]{1,0:T(8,128)(2,1)} %get-tuple-element.105), kind=kOutput, calls=%fused_computation.26 | convolution fusion | flops 17737187328 | bytes 26476544 | tf_op jit(solution)/shard_map/dot_general | solution.py:78
  390.9 11.5 %collect_forward.1 = (bf16[2048,2048]{1,0:T(8,128)(2,1)}, f32[2048,1]{1,0:T(8,128)S(1)}) custom-call(bf16[1536,2048]{1,0:T(8,128)(2,1)} %convolution_convert_fusion.2.res_ref, bf16[2048,2048]{1,0:T(8,128)(2,1)} %all-gather.20.cloned.1.call-done.up_ref, s32[4,4,128]{2,1,0:T(4,128)S(1)} %copy-done.10, f32[2048,1]{1,0:T(8,128)S(1)} %get-tuple-element.102.gate_ref, ...), custom_call_target="tpu_custom_call" | custom-call | flops 2952790016 | bytes 25165824 | tf_op jit(solution)/shard_map/collect_forward/pallas_call | solution.py:332
  407.1 10.5 %collect_backward.1 = bf16[2048,2048]{1,0:T(8,128)(2,1)} custom-call(bf16[1536,2048]{1,0:T(8,128)(2,1)} %fusion.17.rows_ref, s32[4,4,128]{2,1,0:T(4,128)S(1)} %copy-done.10, bf16[2048,512]{1,0:T(8,128)(2,1)S(1)} %copy-done.2, bf16[2048,512]{1,0:T(8,128)(2,1)S(1)} %copy-done.1), custom_call_target="tpu_custom_call" | custom-call | flops 5100273664 | bytes 18874368 | tf_op jit(solution)/shard_map/collect_backward/pallas_call | solution.py:361
  417.6 126.8 %scatter_sum.2 = (f32[128,2048]{1,0:T(8,128)}, f32[128,2048]{1,0:T(8,128)}, f32[16,16,128]{2,1,0:T(8,128)}) custom-call(bf16[16,128,2048]{2,1,0:T(8,128)(2,1)} %bitcast.146, bf16[16,128,2048]{2,1,0:T(8,128)(2,1)} %bitcast.135, f32[16,128]{1,0:T(8,128)} %bitcast.165), custom_call_target="tpu_custom_call" | custom-call | tf_op jit(solution)/shard_map/scatter_sum/pallas_call | solution.py:768
  551.4 6.7 fusion.23
  559.0 5.5 all-to-all-start.1
  564.5 7.8 pad_maximum_fusion
  572.2 3.0 all-to-all-done.1
  577.7 12.7 %attention_backward.1 = bf16[2048,512]{1,0:T(8,128)(2,1)} custom-call(bf16[2048,192]{1,0:T(8,128)(2,1)S(1)} %copy-done.13, bf16[2048,192]{1,0:T(8,128)(2,1)S(1)} %copy-done.15, bf16[2048,128]{1,0:T(8,128)(2,1)S(1)} %copy-done.19, bf16[2048,128]{1,0:T(8,128)(2,1)S(1)} %bitcast.126, s32[2048,1]{1,0:T(8,128)S(1)} %copy-done.6, ...), custom_call_target="tpu_custom_call" | custom-call | flops 3489660928 | bytes 6291456 | tf_op jit(solution)/shard_map/attention_backward/pallas_call | solution.py:156
  592.6 3.9 copy.112
  596.5 4.0 all-to-all-start.2
  600.6 6.2 convolution_convert_fusion.5
  606.9 14.5 %convolution_convert_fusion.1 = bf16[1408,2048]{1,0:T(8,128)(2,1)} fusion(bf16[1536,1408]{1,0:T(8,128)(2,1)} %get-tuple-element.72, bf16[1536,2048]{1,0:T(8,128)(2,1)} %get-tuple-element.73), kind=kOutput, calls=%fused_computation.27 | convolution fusion | flops 8861253632 | bytes 16384000 | tf_op jit(solution)/shard_map/dot_general | solution.py:74
  622.9 21.6 %convolution_convert_fusion = bf16[2048,2816]{1,0:T(8,128)(2,1)} fusion(bf16[1536,2048]{1,0:T(8,128)(2,1)S(1)} %bitcast.178, bf16[1536,2816]{1,0:T(8,128)(2,1)S(1)} %bitcast.141), kind=kOutput, calls=%fused_computation.10 | convolution fusion | flops 17722507264 | bytes 26476544 | tf_op jit(solution)/shard_map/dot_general | solution.py:74
  644.9 4.1 multiply_reduce_fusion.3
  659.0 2.4 collective-permute-done.6
  666.1 3.4 copy-done.20
  673.4 5.6 collective-permute-done.10
  679.3 4.8 convolution_convert_fusion.7
  684.3 7.3 multiply_convert_fusion
  692.3 6.1 add_convert_fusion
  698.4 51.1 %scatter_sum.3 = f32[64,2048]{1,0:T(8,128)} custom-call(bf16[16,64,2048]{2,1,0:T(8,128)(2,1)} %bitcast.136), custom_call_target="tpu_custom_call" | custom-call | tf_op jit(solution)/shard_map/scatter_sum/pallas_call | solution.py:768
  755.5 6.1 constant_dynamic-slice_fusion.1
  764.0 9.1 fusion.79
  779.0 152.1 %gather_all.5 = (bf16[16,192,1024]{2,1,0:T(8,128)(2,1)}, bf16[16,64,2048]{2,1,0:T(8,128)(2,1)}, bf16[16,256,256]{2,1,0:T(8,128)(2,1)}, f32[16,40,128]{2,1,0:T(8,128)}) custom-call(bf16[192,1024]{1,0:T(8,128)(2,1)} %add_convert_fusion.3.refs_0_, bf16[64,2048]{1,0:T(8,128)(2,1)} %convert_element_type.272.refs_1_, bf16[256,256]{1,0:T(8,128)(2,1)} %add_convert_fusion.5.refs_2_, ...), custom_call_target="tpu_custom_call" | custom-call | tf_op jit(solution)/shard_map/gather_all/pallas_call | solution.py:567
  932.2 8.7 convolution_convert_fusion.4
  941.5 5.7 bitcast_convert_fusion
  947.2 10.9 %turn_rows.2 = f32[1024,3072]{1,0:T(8,128)} custom-call(bf16[3072,1024]{1,0:T(8,128)(2,1)} %bitcast.147), custom_call_target="tpu_custom_call" | custom-call | bytes 18874368 | tf_op jit(solution)/shard_map/turn_rows/pallas_call | solution.py:380
  958.1 3.9 turn_rows.3
  963.3 5.6 add_bitcast_fusion.1
  970.7 10.0 add_bitcast_fusion
  980.7 8.7 convert_element_type.290
  989.4 23.7 %all-gather.30.cloned.1.call-done = bf16[5632,1024]{1,0:T(8,128)(2,1)} async-done(((bf16[352,1024]{1,0:T(8,128)(2,1)}), bf16[5632,1024]{1,0:T(8,128)(2,1)}) %all-gather.30.cloned.1.call-update) | async-done | bytes 11534352 | tf_op jit(solution)/shard_map/all_gather | solution.py:792
  1013.1 17.4 %turn_units.1 = f32[1024,5632]{1,0:T(8,128)} custom-call(bf16[16,4,88,1024]{3,2,1,0:T(8,128)(2,1)} %bitcast.137), custom_call_target="tpu_custom_call" | custom-call | bytes 34603008 | tf_op jit(solution)/shard_map/turn_units/pallas_call | solution.py:398
  (332 shorter events, 96.9 us)
Async XLA Ops:
  7.2 132.0 %all-gather.16.cloned.1.call-start = ((), (), s32[]{:S(2)}) async-start(), calls=%async_computation.3 | async-start | bytes 4718592 | tf_op jit(solution)/shard_map/all_gather | solution.py:800
  12.9 177.3 %all-gather.18.cloned.1.call-start = ((), (), s32[]{:S(2)}) async-start(), calls=%async_computation.4 | async-start | bytes 12582912 | tf_op jit(solution)/shard_map/all_gather | solution.py:800
  13.7 258.4 %all-gather.22.cloned.1.call-start = ((), (), s32[]{:S(2)}) async-start(), calls=%async_computation.6 | async-start | bytes 3145728 | tf_op jit(solution)/shard_map/all_gather | solution.py:800
  19.0 253.1 %all-gather.20.cloned.1.call-start = ((), (), s32[]{:S(2)}) async-start(), calls=%async_computation.5 | async-start | bytes 8912896 | tf_op jit(solution)/shard_map/all_gather | solution.py:792
  20.4 283.6 %all-gather.34.cloned.1.call-start = ((), (), s32[]{:S(2)}) async-start(), calls=%async_computation.12 | async-start | bytes 17301504 | tf_op jit(solution)/shard_map/all_gather | solution.py:800
  21.0 307.6 %all-gather.36.cloned.1.call-start = ((), (), s32[]{:S(2)}) async-start(), calls=%async_computation.13 | async-start | bytes 8650752 | tf_op jit(solution)/shard_map/all_gather | solution.py:800
  21.6 623.3 %all-gather.26.cloned.1.call-start = ((), (), s32[]{:S(2)}) async-start(), calls=%async_computation.8 | async-start | bytes 6291456 | tf_op jit(solution)/shard_map/all_gather | solution.py:800
  22.4 741.6 %all-gather.24.cloned.1.call-start = ((), (), s32[]{:S(2)}) async-start(), calls=%async_computation.7 | async-start | bytes 18874368 | tf_op jit(solution)/shard_map/all_gather | solution.py:800
  26.3 109.0 %copy-start.54 = (f32[32]{0:T(128)}, f32[32]{0:T(128)S(1)}, u32[]{:S(2)}) copy-start(f32[32]{0:T(128)S(1)} %negate_power_fusion) | copy-start | bytes 388
  30.9 125.4 %copy-start.5 = (s32[2048,1]{1,0:T(8,128)}, s32[2048,1]{1,0:T(8,128)S(1)}, u32[]{:S(2)}) copy-start(s32[2048,1]{1,0:T(8,128)S(1)} %add_select_fusion.segc_ref) | copy-start | bytes 24580
  139.1 17.1 %copy-start.8 = (f32[2048,128]{1,0:T(8,128)}, f32[2048,128]{1,0:T(8,128)S(1)}, u32[]{:S(2)}) copy-start(f32[2048,128]{1,0:T(8,128)S(1)} %get-tuple-element.127.sin_ref) | copy-start | bytes 3145732
  139.1 17.1 %copy-start.9 = (f32[2048,128]{1,0:T(8,128)}, f32[2048,128]{1,0:T(8,128)S(1)}, u32[]{:S(2)}) copy-start(f32[2048,128]{1,0:T(8,128)S(1)} %get-tuple-element.128.cos_ref) | copy-start | bytes 3145732
  156.3 34.0 %copy-start.27 = (bf16[128,2048]{1,0:T(8,128)(2,1)S(1)}, bf16[128,2048]{1,0:T(8,128)(2,1)}, u32[]{:S(2)}) copy-start(bf16[128,2048]{1,0:T(8,128)(2,1)} %refs_0_.1) | copy-start | bytes 1572868
  165.9 29.4 %copy-start.11 = (f32[8,128]{1,0:T(8,128)}, f32[8,128]{1,0:T(8,128)S(1)}, u32[]{:S(2)}) copy-start(f32[8,128]{1,0:T(8,128)S(1)} %get-tuple-element.58.refs_1_) | copy-start | bytes 12292
  166.9 23.4 %all-to-all-start = ((bf16[16,128,128]{1,2,0:T(8,128)(2,1)}), bf16[16,128,128]{1,2,0:T(8,128)(2,1)S(1)}, u32[]{:S(2)}, u32[]{:S(2)}) async-start(bf16[16,128,128]{1,2,0:T(8,128)(2,1)} %copy.106), calls=%async_computation | async-start | bytes 1048576 | tf_op jit(solution)/shard_map/all_to_all | solution.py:916
  171.3 24.0 %copy-start.44 = (f32[1,8,2,128]{3,1,2,0:T(8,128)}, f32[1,8,2,128]{3,1,2,0:T(8,128)S(1)}, u32[]{:S(2)}) copy-start(f32[1,8,2,128]{3,1,2,0:T(8,128)S(1)} %copy.137) | copy-start | bytes 24580
  173.0 90.0 %copy-start.33 = (bf16[2048,16]{1,0:T(8,128)(2,1)}, bf16[2048,16]{1,0:T(8,128)(2,1)S(1)}, u32[]{:S(2)}) copy-start(bf16[2048,16]{1,0:T(8,128)(2,1)S(1)} %reshape.294) | copy-start | bytes 196612
  195.3 73.4 %copy-start.59 = (f32[128]{0:T(128)}, f32[128]{0:T(128)S(1)}, u32[]{:S(2)}) copy-start(f32[128]{0:T(128)S(1)} %get-tuple-element.129) | copy-start | bytes 1540
  195.3 73.4 %copy-start.49 = (f32[128]{0:T(128)}, f32[128]{0:T(128)S(1)}, u32[]{:S(2)}) copy-start(f32[128]{0:T(128)S(1)} %fusion.65) | copy-start | bytes 1540
  366.0 24.9 %copy-start = (bf16[256,2048]{1,0:T(8,128)(2,1)S(1)}, bf16[256,2048]{1,0:T(8,128)(2,1)}, u32[]{:S(2)}) copy-start(bf16[256,2048]{1,0:T(8,128)(2,1)} %pad.16.out_ref) | copy-start | bytes 3145732
  366.0 24.9 %copy-start.4 = (bf16[2048,256]{1,0:T(8,128)(2,1)S(1)}, bf16[2048,256]{1,0:T(8,128)(2,1)}, u32[]{:S(2)}) copy-start(bf16[2048,256]{1,0:T(8,128)(2,1)} %get-tuple-element.62.hidden_ref) | copy-start | bytes 3145732
  366.0 24.9 %copy-start.10 = (s32[4,4,128]{2,1,0:T(4,128)S(1)}, s32[4,4,128]{2,1,0:T(4,128)}, u32[]{:S(2)}) copy-start(s32[4,4,128]{2,1,0:T(4,128)} %add_select_fusion.1.place_ref) | copy-start | bytes 24580
  417.6 128.2 %copy-start.22 = (f32[2048,16]{1,0:T(8,128)S(1)}, f32[2048,16]{1,0:T(8,128)}, u32[]{:S(2)}) copy-start(f32[2048,16]{1,0:T(8,128)} %copy-done.21) | copy-start | bytes 393220
  559.0 16.2 %all-to-all-start.1 = ((bf16[128,16,128]{2,0,1:T(8,128)(2,1)}), bf16[128,16,128]{2,0,1:T(8,128)(2,1)S(1)}, u32[]{:S(2)}, u32[]{:S(2)}) async-start(bf16[128,16,128]{2,0,1:T(8,128)(2,1)} %bitcast.121), calls=%async_computation.1 | async-start | bytes 1048576 | tf_op jit(solution)/shard_map/all_to_all | solution.py:976
  596.5 48.0 %all-to-all-start.2 = ((bf16[16,128,512]{1,2,0:T(8,128)(2,1)}), bf16[16,128,512]{1,2,0:T(8,128)(2,1)S(1)}, u32[]{:S(2)}, u32[]{:S(2)}) async-start(bf16[16,128,512]{1,2,0:T(8,128)(2,1)} %copy.112), calls=%async_computation.2 | async-start | bytes 4194304 | tf_op jit(solution)/shard_map/all_to_all | solution.py:987
  600.6 331.6 %all-gather.28.cloned.1.call-start = ((), (), s32[]{:S(2)}) async-start(), calls=%async_computation.9 | async-start | bytes 2785280 | tf_op jit(solution)/shard_map/all_gather | solution.py:792
  600.6 22.2 %slice-start.2 = ((s8[8650752]{0:T(1024)(128)(4,1)}), s8[4194304]{0:T(1024)(128)(4,1)S(1)}, s32[]{:S(2)}) async-start(s8[8650752]{0:T(1024)(128)(4,1)} %bitcast.140), calls=%async_computation.16 | async-start | bytes 8388608
  600.6 22.2 %slice-start.9 = ((s8[6291456]{0:T(1024)(128)(4,1)}), s8[4194304]{0:T(1024)(128)(4,1)S(1)}, s32[]{:S(2)}) async-start(s8[6291456]{0:T(1024)(128)(4,1)} %bitcast.177), calls=%async_computation.23 | async-start | bytes 8388608
  606.9 16.0 %slice-start.10 = ((s8[6291456]{0:T(1024)(128)(4,1)}), s8[2097152]{0:T(1024)(128)(4,1)S(1)}, s32[]{:S(2)}) async-start(s8[6291456]{0:T(1024)(128)(4,1)} %bitcast.177), calls=%async_computation.24 | async-start | bytes 4194304
  622.9 22.0 %copy-start.48 = (f32[1,2,2,128]{3,1,2,0:T(2,128)S(1)}, f32[1,2,2,128]{3,1,2,0:T(2,128)}, u32[]{:S(2)}) copy-start(f32[1,2,2,128]{3,1,2,0:T(2,128)} %copy.128) | copy-start | bytes 6148
  622.9 22.0 %copy-start.58 = (f32[128]{0:T(128)S(1)}, f32[128]{0:T(128)}, u32[]{:S(2)}) copy-start(f32[128]{0:T(128)} %fusion.66) | copy-start | bytes 1540
  651.3 329.5 %all-gather.32.cloned.1.call-start = ((), (), s32[]{:S(2)}) async-start(), calls=%async_computation.11 | async-start | bytes 6127616 | tf_op jit(solution)/shard_map/all_gather | solution.py:792
  652.6 1.9 collective-permute-start.7
  656.3 356.8 %all-gather.30.cloned.1.call-start = ((), (), s32[]{:S(2)}) async-start(), calls=%async_computation.10 | async-start | bytes 12255232 | tf_op jit(solution)/shard_map/all_gather | solution.py:792
  658.9 2.5 collective-permute-start.6
  671.8 20.5 %collective-permute-start.1 = (bf16[1024,2048]{1,0:T(8,128)(2,1)}, bf16[1024,2048]{1,0:T(8,128)(2,1)}, u32[]{:S(2)}, u32[]{:S(2)}) collective-permute-start(bf16[1024,2048]{1,0:T(8,128)(2,1)} %constant_dynamic-slice_fusion.6), channel_id=1, source_target_pairs={{0,1},{1,0},{2,3},{3,2},{4,5},{5,4},{6,7},{7,6},{8,9},{9,8},{10,11... | collective-permute-start | bytes 12582920 | tf_op jit(solution)/shard_map/ppermute | solution.py:815
  673.0 6.0 collective-permute-start.10
  684.1 7.5 collective-permute-start.5
  698.4 55.1 %copy-start.35 = (bf16[192,2048]{1,0:T(8,128)(2,1)S(1)}, bf16[192,2048]{1,0:T(8,128)(2,1)}, u32[]{:S(2)}) copy-start(bf16[192,2048]{1,0:T(8,128)(2,1)} %convolution_convert_fusion.5) | copy-start | bytes 2359300
  698.4 55.9 %copy-start.42 = (bf16[256,512]{1,0:T(8,128)(2,1)S(1)}, bf16[256,512]{1,0:T(8,128)(2,1)}, u32[]{:S(2)}) copy-start(bf16[256,512]{1,0:T(8,128)(2,1)} %convolution_convert_fusion.8) | copy-start | bytes 786436
  754.3 22.8 %collective-permute-start = (bf16[192,1024]{1,0:T(8,128)(2,1)}, bf16[192,1024]{1,0:T(8,128)(2,1)}, u32[]{:S(2)}, u32[]{:S(2)}) collective-permute-start(bf16[192,1024]{1,0:T(8,128)(2,1)} %constant_dynamic-slice_fusion.7), channel_id=1, source_target_pairs={{0,1},{1,0},{2,3},{3,2},{4,5},{5,4},{6,7},{7,6},{8,9},{9,8},{10,11... | collective-permute-start | bytes 1179656 | tf_op jit(solution)/shard_map/ppermute | solution.py:815
  755.0 21.5 %collective-permute-start.2 = (bf16[256,256]{1,0:T(8,128)(2,1)}, bf16[256,256]{1,0:T(8,128)(2,1)S(1)}, u32[]{:S(2)}, u32[]{:S(2)}) collective-permute-start(bf16[256,256]{1,0:T(8,128)(2,1)} %constant_dynamic-slice_fusion.5), channel_id=1, source_target_pairs={{0,1},{1,0},{2,3},{3,2},{4,5},{5,4},{6,7},{7,6},{8,9},{9,8},{10,11... | collective-permute-start | bytes 393224 | tf_op jit(solution)/shard_map/ppermute | solution.py:815
  761.6 209.1 %collective-permute-start.8 = (bf16[1024,2816]{1,0:T(8,128)(2,1)}, bf16[1024,2816]{1,0:T(8,128)(2,1)}, u32[]{:S(2)}, u32[]{:S(2)}) collective-permute-start(bf16[1024,2816]{1,0:T(8,128)(2,1)} %constant_dynamic-slice_fusion.1), channel_id=1, source_target_pairs={{0,1},{1,0},{2,3},{3,2},{4,5},{5,4},{6,7},{7,6},{8,9},{9,8},{10,11... | collective-permute-start | bytes 17301512 | tf_op jit(solution)/shard_map/ppermute | solution.py:815
  763.4 199.9 %collective-permute-start.9 = (bf16[704,2048]{1,0:T(8,128)(2,1)}, bf16[704,2048]{1,0:T(8,128)(2,1)}, u32[]{:S(2)}, u32[]{:S(2)}) collective-permute-start(bf16[704,2048]{1,0:T(8,128)(2,1)} %constant_dynamic-slice_fusion), channel_id=1, source_target_pairs={{0,1},{1,0},{2,3},{3,2},{4,5},{5,4},{6,7},{7,6},{8,9},{9,8},{10,11... | collective-permute-start | bytes 8650760 | tf_op jit(solution)/shard_map/ppermute | solution.py:815
  932.1 29.9 %collective-permute-start.3 = (f32[40,128]{1,0:T(8,128)S(1)}, f32[40,128]{1,0:T(8,128)S(1)}, u32[]{:S(2)}, u32[]{:S(2)}) collective-permute-start(f32[40,128]{1,0:T(8,128)S(1)} %reduce_sum.183), channel_id=1, source_target_pairs={{0,1},{1,0},{2,3},{3,2},{4,5},{5,4},{6,7},{7,6},{8,9},{9,8},{10,11... | collective-permute-start | bytes 61448 | tf_op jit(solution)/shard_map/ppermute | solution.py:815
  941.0 27.9 %collective-permute-start.4 = (bf16[1024,576]{0,1:T(8,128)(2,1)S(1)}, bf16[1024,576]{0,1:T(8,128)(2,1)S(1)}, u32[]{:S(2)}, u32[]{:S(2)}) collective-permute-start(bf16[1024,576]{0,1:T(8,128)(2,1)S(1)} %constant_dynamic-slice_fusion.4), channel_id=1, source_target_pairs={{0,1},{1,0},{2,3},{3,2},{4,5},{5,4},{6,7},{7,6},{8,9},{9,8},{10,11... | collective-permute-start | bytes 3538952 | tf_op jit(solution)/shard_map/ppermute | solution.py:815
  947.2 16.1 %slice-start.7 = ((s8[5767168]{0:T(1024)(128)(4,1)}), s8[4194304]{0:T(1024)(128)(4,1)S(1)}, s32[]{:S(2)}) async-start(s8[5767168]{0:T(1024)(128)(4,1)} %bitcast.150), calls=%async_computation.21 | async-start | bytes 8388608
  947.2 16.1 %slice-start.8 = ((s8[5767168]{0:T(1024)(128)(4,1)}), s8[1572864]{0:T(1024)(128)(4,1)S(1)}, s32[]{:S(2)}) async-start(s8[5767168]{0:T(1024)(128)(4,1)} %bitcast.150), calls=%async_computation.22 | async-start | bytes 3145728
  (55 other events, 360.5 us)
Sparse Core Ops, SparseCore 0:
  13.0 14.7 all-gather.15
  29.4 21.1 all-gather.17
  52.7 11.7 all-gather.21
  67.6 132.0 all-gather.19
  201.1 23.2 all-gather.33
  225.8 17.1 all-gather.35
  244.5 14.8 all-gather.25
  261.0 26.0 all-gather.23
  651.4 66.5 all-gather.27
  720.5 119.0 all-gather.31
  842.4 170.6 all-gather.29

commit v5 on v4

--- a/solution.py
+++ b/solution.py
@@ -815,6 +815,19 @@
     return lax.ppermute(rows, "fsdp", [(i, (i + k) % count) for i in range(count)])
 
 
+def sum_everywhere(rows):
+    count = lax.axis_size("seq")
+    total = rows
+    bit = 1
+    while bit < count:
+        total = total + lax.ppermute(total, "seq", [(i, i ^ bit) for i in range(count)])
+        bit *= 2
+    kept = total
+    for k in range(1, lax.axis_size("fsdp")):
+        total = total + shift_fsdp(kept, k)
+    return total
+
+
 ROW_PARTS = [(48, "zxy"), (48, "zyx"), (16, "xyz"), (16, "yxz")]
 
 
@@ -876,22 +889,10 @@
     gain_ffn = small[:, ends[2] : ends[3]].reshape(-1).astype(F32)
     router_weight = small[:, ends[3] : ends[4]].reshape(D, experts)
     head_query_part = lax.dynamic_slice_in_dim(w_q, rank * query_width, query_width, 1)
-    lanes = -(-units // 128) * 128
-    unit_slices = [
-        lax.dynamic_slice_in_dim(w_shared_in, i * (SH // fsdp_count) + rank * unit, unit, 1)
-        for i in range(2 * fsdp_count)
-    ]
-    filler = jnp.zeros((row_part, lanes - units), BF16)
-    shared_in_part = jnp.concatenate(
-        unit_slices[:fsdp_count] + [filler] + unit_slices[fsdp_count:] + [filler], axis=1
-    )
     head_expand = gather_fsdp(lax.dynamic_slice_in_dim(w_kvb, rank * kv_width, kv_width, 1))
     head_weights = gather_fsdp(
         jnp.concatenate([w_kva[:, :KVR], head_query_part, w_kva[:, KVR:]], axis=1)
     )
-    shared_in = gather_fsdp(shared_in_part)
-    shared_out = gather_fsdp(lax.dynamic_slice_in_dim(w_shared_out, rank * unit, unit, 0))
-    shared_out = jnp.pad(shared_out, ((0, lanes - units), (0, 0)))
     output_weight = gather_fsdp(w_o)
     expert_in = gather_fsdp(w_expert_in[0])
     expert_out = gather_fsdp(w_expert_out[0])
@@ -913,6 +914,20 @@
         token_all, gain_attn, head_weights, gain_latent, head_expand, cosines, sines
     )
     context, log_total, head_largest = attention_forward(query, key, value, segment, valid_all)
+    late_rank, context, upstream_all = lax.optimization_barrier((rank, context, upstream_all))
+    lanes = -(-units // 128) * 128
+    unit_slices = [
+        lax.dynamic_slice_in_dim(w_shared_in, i * (SH // fsdp_count) + late_rank * unit, unit, 1)
+        for i in range(2 * fsdp_count)
+    ]
+    filler = jnp.zeros((row_part, lanes - units), BF16)
+    shared_in_part = jnp.concatenate(
+        unit_slices[:fsdp_count] + [filler] + unit_slices[fsdp_count:] + [filler], axis=1
+    )
+    shared_in = gather_fsdp(shared_in_part)
+    shared_out = gather_fsdp(lax.dynamic_slice_in_dim(w_shared_out, late_rank * unit, unit, 0))
+    shared_out = jnp.pad(shared_out, ((0, lanes - units), (0, 0)))
+
     context_low = lax.all_to_all(context, "seq", split_axis=0, concat_axis=1, tiled=True)
     inputs = tokens.astype(F32)
     middle = inputs + dot(context_low, output_weight)
@@ -936,22 +951,24 @@
     part_shared_out = scatter_fsdp(grad_shared_out[:units]).astype(BF16)
     part_shared_in = jnp.concatenate([grad_shared_in[:units], grad_shared_in[lanes : lanes + units]], axis=0)
     part_shared_in = scatter_fsdp(part_shared_in, 1).astype(BF16)
-    sum_shared_out = gather_seq(part_shared_out).astype(F32)
-    sum_shared_in = turn_units(
-        gather_seq(part_shared_in).reshape(seq_count, 2 * fsdp_count, unit, row_part)
-    )
+    arrived, part_shared_out, part_shared_in = lax.optimization_barrier(
+        (arrived, part_shared_out, part_shared_in)
+    )
+    all_shared_out = gather_seq(part_shared_out)
+    all_shared_in = gather_seq(part_shared_in)
 
     gate_up = dot(arrived, expert_in).astype(BF16)
     gate_part, up_part = gate_up[:, :FF].astype(F32), gate_up[:, FF:].astype(F32)
     hidden = (jax.nn.silu(gate_part) * up_part).astype(BF16)
     result = dot(hidden, expert_out).astype(BF16)
     d_hidden = dot_nt(result_grad, expert_out)
-    d_gate_up = jnp.concatenate(silu_grads(gate_part, up_part, d_hidden), axis=1).astype(BF16)
-    row_grad = dot_nt(d_gate_up, expert_in).astype(BF16)
+    d_gate, d_up = [g.astype(BF16) for g in silu_grads(gate_part, up_part, d_hidden)]
+    row_grad = dot_nt(jnp.concatenate([d_gate, d_up], axis=1), expert_in).astype(BF16)
     mixed_part, gate_grad = collect_forward(
         result, upstream_all, place, gates, shared_hidden, shared_out, capacity
     )
     ffn_part = collect_backward(row_grad, place, shared_grad, shared_in, capacity)
+    mixed_part, ffn_part, all_shared_out = lax.optimization_barrier((mixed_part, ffn_part, all_shared_out))
     mixed_sum, ffn_sum, prob_grads = scatter_sum(
         [part.reshape(seq_count, tok_count, D) for part in (mixed_part, ffn_part)],
         [ROW_PARTS, ROW_PARTS],
@@ -980,15 +997,16 @@
         [grad_output.reshape(seq_count, output_rows, D)], [split_rows(output_rows)], [], 5
     )
 
+    head_grad, all_shared_in = lax.optimization_barrier((head_grad, all_shared_in))
     head_back = attention_backward(query, key, value, head_grad, segment, log_total, cosines, sines)
-    head_back, arrived, result_grad, hidden, d_gate_up = lax.optimization_barrier(
-        (head_back, arrived, result_grad, hidden, d_gate_up)
+    head_back, arrived, result_grad, hidden, d_gate, d_up = lax.optimization_barrier(
+        (head_back, arrived, result_grad, hidden, d_gate, d_up)
     )
     back = lax.all_to_all(
         head_back.reshape(seq_count, tok_count, -1), "seq", split_axis=0, concat_axis=0, tiled=True
     )
     grad_expert_out = dot_tn(hidden, result_grad).astype(BF16)
-    grad_expert_in = dot_tn(arrived, d_gate_up).astype(BF16)
+    grad_expert_in = dot_tn(arrived, jnp.concatenate([d_gate, d_up], axis=1)).astype(BF16)
     rope_at = 2 * DN + DV
     head_pre_grad = jnp.concatenate([head_back[:, :DN], head_back[:, rope_at : rope_at + DR]], axis=1)
     grad_query = dot_tn(head_pre_grad, normed_all).astype(BF16)
@@ -1019,18 +1037,14 @@
     input_norm_grad, grad_gain_attn = input_pull(normed_grad)
     grad_inputs = middle_grad + input_norm_grad
 
-    gain_grads = jnp.concatenate([grad_gain_attn, grad_gain_latent, grad_gain_ffn]).reshape(-1, 128)
-    gain_grads = jnp.pad(gain_grads, ((0, -gain_grads.shape[0] % 8), (0, 0)))
-    weight_parts = [part_query, part_output.astype(BF16), part_expand]
-    *sums, gain_all = gather_all(weight_parts, [split_rows(p.shape[0]) for p in weight_parts], [gain_grads], 4)
-    sum_query = turn_rows(sums[0].reshape(-1, row_part), 384)
-    sum_output = sums[1].reshape(w_o.shape).astype(F32)
-    sum_expand = turn_rows(sums[2].reshape(-1, w_kvb.shape[0]), 512)
-    gain_seq = jnp.sum(gain_all, axis=0)
-    gain_sum = gain_seq
-    for k in range(1, fsdp_count):
-        gain_sum = gain_sum + shift_fsdp(gain_seq, k)
-    gain_sum = gain_sum.reshape(-1)
+    gain_sum = sum_everywhere(
+        jnp.concatenate([grad_gain_attn, grad_gain_latent, grad_gain_ffn]).reshape(-1, 128)
+    ).reshape(-1)
+    sum_shared_out = all_shared_out.astype(F32)
+    sum_shared_in = turn_units(all_shared_in.reshape(seq_count, 2 * fsdp_count, unit, row_part))
+    sum_query = turn_rows(gather_seq(part_query), 384)
+    sum_expand = turn_rows(gather_seq(part_expand), 512)
+    sum_output = gather_seq(part_output.astype(BF16)).astype(F32)
     fsdp_rank = lax.axis_index("fsdp")
 
     def own_part(first, like):

time: 1050 us -> 1110 us (1.057)
  waiting for transfers between devices: 49 us -> 145 us
  Pallas kernels: 623 us -> 577 us
  starting transfers between devices: 16.2 us -> 33.9 us
    pallas_call x3 -> x2, Pallas kernels: 321 us -> 187 us  [gather_all(): pl.pallas_call(functools.partial(gather_kernel, streams, len(main), len(s...]
    pallas_call x2, Pallas kernels: 178 us -> 271 us  [scatter_sum(): pl.pallas_call(functools.partial(scatter_kernel, streams, len(main), len(...]
    all_gather x4 -> x7, waiting for transfers between devices: 23.7 us -> 99.8 us  [gather_seq(): return lax.all_gather(rows, 'seq', axis=0, tiled=True)]
    all_to_all x1, waiting for transfers between devices: 0.01 us -> 26.1 us  [on_device(): lax.all_to_all(head_back.reshape(seq_count, tok_count, -1), 'seq', split_...]
    ppermute x0 -> x4, starting transfers between devices: none -> 16.2 us  [sum_everywhere(): lax.ppermute(total, 'seq', [(i, i ^ bit) for i in range(count)])]
  transfers between devices with their start and end apart: 25 -> 32, of which waited for: 6 -> 9; matrix products, arithmetic and copies ran while one was open for 30% -> 28% of each run, Pallas kernels for 58% -> 52%
where the time goes in v5:
time: 1110 us; the launch traced here: 1100 us
  Pallas kernels  577 us (52%)
  matrix products  180 us (16%)
  waiting for transfers between devices  145 us (13%)
  other arithmetic  86 us (8%)
  local copies, waits for them, and re-layouts  57.3 us (5%)
  starting transfers between devices  33.9 us (3%)
  between operations  15.6 us (1%)
    pallas_call x2, Pallas kernels, scatter_sum(): pl.pallas_call(functools.partial(scatter_kernel, streams, len(main), len(...  271 us
    pallas_call x2, Pallas kernels, gather_all(): pl.pallas_call(functools.partial(gather_kernel, streams, len(main), len(s...  187 us
    all_gather x7, waiting for transfers between devices, gather_seq(): return lax.all_gather(rows, 'seq', axis=0, tiled=True)  99.8 us
    dot_general x7, matrix products, dot_nt(): lax.dot_general(left, right, (((1,), (1,)), ((), ())), preferred_element_...  66.2 us
    dot_general x7, matrix products, dot_tn(): lax.dot_general(left, right, (((0,), (0,)), ((), ())), preferred_element_...  61.6 us
    dot_general x4, matrix products, dot(): return jnp.dot(left, right, preferred_element_type=F32)  52.1 us
    pallas_call x1, Pallas kernels, spread(): pl.pallas_call(spread_kernel, grid=(steps,), in_specs=[by_rows(t, D), by_...  30 us
    all_to_all x1, waiting for transfers between devices, on_device(): lax.all_to_all(head_back.reshape(seq_count, tok_count, -1), 'seq', split_...  26.1 us
  transfers between devices with their start and end apart: 32, of which 9 were waited for; matrix products, arithmetic and copies ran while one was open for 28% of the time, Pallas kernels for 52%

profile of v5, /device:TPU:0, one launch (start us, length us, event | category | flops | bytes accessed | tf_op | source)
XLA Modules:
  0.0 1101.1 jit_solution(10578663456248216744)
XLA Ops:
  22.1 117.3 %gather_all.2 = (bf16[16,128,2048]{2,1,0:T(8,128)(2,1)}, bf16[16,16,128]{2,1,0:T(8,128)(2,1)}) custom-call(bf16[128,2048]{1,0:T(8,128)(2,1)} %refs_0_.1, bf16[16,128]{1,0:T(8,128)(2,1)} %convert_element_type.233.refs_1_), custom_call_target="tpu_custom_call" | custom-call | tf_op jit(solution)/shard_map/gather_all/pallas_call | solution.py:567
  143.3 3.7 fusion.32
  147.0 16.7 %project.1 = (bf16[2048,2048]{1,0:T(8,128)(2,1)}, bf16[2048,192]{1,0:T(8,128)(2,1)S(1)}, bf16[2048,192]{1,0:T(8,128)(2,1)S(1)}, bf16[2048,128]{1,0:T(8,128)(2,1)...) custom-call(bf16[2048,2048]{1,0:T(8,128)(2,1)} %bitcast.167, f32[1,2048]{1,0:T(1,128)S(1)} %bitcast.125, ...), custom_call_target="tpu_custom_call" | custom-call | flops 7549747200 | bytes 25165824 | tf_op jit(solution)/shard_map/project/pallas_call | solution.py:199
  163.7 7.7 attention_forward.1
  177.5 3.3 concatenate.39
  182.4 3.6 all-to-all-start
  194.5 7.0 all-to-all-done
  201.4 4.9 multiply_reduce_fusion.2
  208.3 69.6 %gather_all.3 = (bf16[16,128,2048]{2,1,0:T(8,128)(2,1)}, f32[16,8,128]{2,1,0:T(8,128)}) custom-call(bf16[128,2048]{1,0:T(8,128)(2,1)} %multiply_convert_fusion.1.refs_0_, f32[8,128]{1,0:T(8,128)} %copy-done.10), custom_call_target="tpu_custom_call" | custom-call | tf_op jit(solution)/shard_map/gather_all/pallas_call | solution.py:567
  277.9 5.7 fusion.89
  287.3 30.0 %spread.1 = (bf16[1536,2048]{1,0:T(8,128)(2,1)}, bf16[1536,2048]{1,0:T(8,128)(2,1)}, bf16[2048,256]{1,0:T(8,128)(2,1)}, bf16[2048,512]{1,0:T(8,128)(2,1)}, bf16[...) custom-call(bf16[2048,2048]{1,0:T(8,128)(2,1)} %bitcast.130, bf16[2048,2048]{1,0:T(8,128)(2,1)} %all-gather.21.cloned.1.call-done.up_ref, ...), custom_call_target="tpu_custom_call" | custom-call | flops 14495514624 | bytes 41943040 | tf_op jit(solution)/shard_map/spread/pallas_call | solution.py:299
  328.7 25.0 %fusion.4 = bf16[1536,2816]{1,0:T(8,128)(2,1)} fusion(bf16[1536,2048]{1,0:T(8,128)(2,1)} %get-tuple-element.93, bf16[1,2048,2816]{2,1,0:T(8,128)(2,1)} %all-gather.43.cloned.1.call-done), kind=kOutput, calls=%fused_computation.11 | convolution fusion | flops 17721065472 | bytes 26476544 | tf_op jit(solution)/shard_map/dot_general | solution.py:70
  353.7 22.1 %fusion.10 = (bf16[1536,1408]{1,0:T(8,128)(2,1)}, bf16[1536,1408]{1,0:T(8,128)(2,1)}, bf16[1536,1408]{1,0:T(8,128)(2,1)}) fusion(bf16[1536,2816]{1,0:T(8,128)(2,1)} %fusion.4, bf16[1536,2048]{1,0:T(8,128)(2,1)} %get-tuple-element.92, bf16[1,1408,2048]{2,1,0:T(8,128)(2,1)} %all-gather.45.cloned.1.call-done), kind=kOutput, calls=%fused_computation.17 | convolution fusion | flops 8897298432 | bytes 33685504 | tf_op jit(solution)/shard_map/dot_general | solution.py:78
  375.8 16.4 %convolution_convert_fusion.2.res_ref = bf16[1536,2048]{1,0:T(8,128)(2,1)} fusion(bf16[1536,1408]{1,0:T(8,128)(2,1)} %get-tuple-element.91, bf16[1,1408,2048]{2,1,0:T(8,128)(2,1)} %all-gather.45.cloned.1.call-done), kind=kOutput, calls=%fused_computation.33 | convolution fusion | flops 8861515776 | bytes 16384000 | tf_op jit(solution)/shard_map/dot_general | solution.py:70
  392.3 11.2 %collect_forward.1 = (bf16[2048,2048]{1,0:T(8,128)(2,1)}, f32[2048,1]{1,0:T(8,128)S(1)}) custom-call(bf16[1536,2048]{1,0:T(8,128)(2,1)} %convolution_convert_fusion.2.res_ref, bf16[2048,2048]{1,0:T(8,128)(2,1)} %all-gather.21.cloned.1.call-done.up_ref, s32[4,4,128]{2,1,0:T(4,128)S(1)} %copy-done.9, f32[2048,1]{1,0:T(8,128)S(1)} %get-tuple-element.118.gate_ref, ...), custom_call_target="tpu_custom_call" | custom-call | flops 2952790016 | bytes 25165824 | tf_op jit(solution)/shard_map/collect_forward/pallas_call | solution.py:332
  404.4 24.9 %fusion.23.rows_ref = bf16[1536,2048]{1,0:T(8,128)(2,1)} fusion(bf16[1,2048,2816]{2,1,0:T(8,128)(2,1)} %all-gather.43.cloned.1.call-done, bf16[1536,1408]{1,0:T(8,128)(2,1)} %get-tuple-element.95, bf16[1536,1408]{1,0:T(8,128)(2,1)} %get-tuple-element.94), kind=kOutput, calls=%fused_computation.31 | convolution fusion | flops 17737187328 | bytes 26476544 | tf_op jit(solution)/shard_map/dot_general | solution.py:78
  429.3 10.5 collect_backward.1
  439.8 226.5 %scatter_sum.2 = (f32[128,2048]{1,0:T(8,128)}, f32[128,2048]{1,0:T(8,128)}, f32[16,16,128]{2,1,0:T(8,128)}) custom-call(bf16[16,128,2048]{2,1,0:T(8,128)(2,1)} %bitcast.143, bf16[16,128,2048]{2,1,0:T(8,128)(2,1)} %bitcast.132, f32[16,128]{1,0:T(8,128)} %bitcast.157), custom_call_target="tpu_custom_call" | custom-call | tf_op jit(solution)/shard_map/scatter_sum/pallas_call | solution.py:768
  678.7 2.9 fusion.31
  683.6 6.5 all-to-all-start.1
  692.0 7.8 add_convert_fusion
  699.8 44.3 %scatter_sum.3 = f32[64,2048]{1,0:T(8,128)} custom-call(bf16[16,64,2048]{2,1,0:T(8,128)(2,1)} %bitcast.133), custom_call_target="tpu_custom_call" | custom-call | tf_op jit(solution)/shard_map/scatter_sum/pallas_call | solution.py:768
  748.4 12.5 %attention_backward.1 = bf16[2048,512]{1,0:T(8,128)(2,1)} custom-call(bf16[2048,192]{1,0:T(8,128)(2,1)S(1)} %copy-done.12, bf16[2048,192]{1,0:T(8,128)(2,1)S(1)} %copy-done.14, bf16[2048,128]{1,0:T(8,128)(2,1)S(1)} %copy-done.18, bf16[2048,128]{1,0:T(8,128)(2,1)S(1)} %bitcast.124, s32[2048,1]{1,0:T(8,128)S(1)} %copy-done.6, ...), custom_call_target="tpu_custom_call" | custom-call | flops 3489660928 | bytes 6291456 | tf_op jit(solution)/shard_map/attention_backward/pallas_call | solution.py:156
  763.1 6.3 convolution_convert_fusion.5
  772.7 5.2 all-to-all-start.2
  778.0 14.3 %convolution_convert_fusion.1 = bf16[1408,2048]{1,0:T(8,128)(2,1)} fusion(bf16[1536,1408]{1,0:T(8,128)(2,1)} %get-tuple-element.91, bf16[1536,2048]{1,0:T(8,128)(2,1)} %get-tuple-element.92), kind=kOutput, calls=%fused_computation.32 | convolution fusion | flops 8861253632 | bytes 16384000 | tf_op jit(solution)/shard_map/dot_general | solution.py:74
  792.2 24.4 %convolution_convert_fusion = bf16[2048,2816]{1,0:T(8,128)(2,1)} fusion(bf16[1536,2048]{1,0:T(8,128)(2,1)} %get-tuple-element.93, bf16[1536,1408]{1,0:T(8,128)(2,1)} %get-tuple-element.95, bf16[1536,1408]{1,0:T(8,128)(2,1)} %get-tuple-element.94), kind=kOutput, calls=%fused_computation.10 | convolution fusion | flops 17739808768 | bytes 26476544 | tf_op jit(solution)/shard_map/dot_general | solution.py:74
  816.7 26.1 %all-to-all-done.2 = bf16[16,128,512]{1,2,0:T(8,128)(2,1)S(1)} async-done(((bf16[16,128,512]{1,2,0:T(8,128)(2,1)}), bf16[16,128,512]{1,2,0:T(8,128)(2,1)S(1)}, u32[]{:S(2)}, u32[]{:S(2)}) %all-to-all-start.2) | async-done | bytes 2097184 | tf_op jit(solution)/shard_map/all_to_all | solution.py:1005
  845.5 3.8 multiply_reduce_fusion.3
  861.4 7.3 multiply_convert_fusion
  868.7 4.9 convolution_convert_fusion.7
  875.7 2.9 constant_dynamic-slice_fusion.1
  878.9 9.1 fusion.90
  889.8 8.7 convert_element_type.291
  898.5 8.2 collective-permute-start.3
  907.3 17.7 %turn_units.1 = f32[1024,5632]{1,0:T(8,128)} custom-call(bf16[16,4,88,1024]{3,2,1,0:T(8,128)(2,1)} %bitcast.134), custom_call_target="tpu_custom_call" | custom-call | bytes 34603008 | tf_op jit(solution)/shard_map/turn_units/pallas_call | solution.py:398
  925.0 6.7 convert_element_type.287
  931.7 6.3 collective-permute-start.4
  938.0 3.8 constant_dynamic-slice_fusion
  943.1 3.6 collective-permute-done.5
  946.8 8.4 convolution_convert_fusion.4
  959.6 6.4 add_bitcast_fusion.1
  966.0 23.3 %all-gather.39.cloned.1.call-done.in_ref = bf16[4096,256]{1,0:T(8,128)(2,1)} async-done(((bf16[256,256]{1,0:T(8,128)(2,1)}), bf16[4096,256]{1,0:T(8,128)(2,1)}) %all-gather.39.cloned.1.call-update) | async-done | bytes 2097168 | tf_op jit(solution)/shard_map/all_gather | solution.py:792
  990.9 3.9 turn_rows.3
  994.8 3.1 convert_add_fusion
  997.9 10.3 add_bitcast_fusion
  1008.2 76.5 %all-gather.35.cloned.1.call-done.in_ref = bf16[3072,1024]{1,0:T(8,128)(2,1)} async-done(((bf16[192,1024]{1,0:T(8,128)(2,1)}), bf16[3072,1024]{1,0:T(8,128)(2,1)}) %all-gather.35.cloned.1.call-update) | async-done | bytes 6291472 | tf_op jit(solution)/shard_map/all_gather | solution.py:792
  1084.8 9.4 turn_rows.2
  (328 shorter events, 105.0 us)
Async XLA Ops:
  7.2 139.8 %all-gather.19.cloned.1.call-start = ((), (), s32[]{:S(2)}) async-start(), calls=%async_computation.3 | async-start | bytes 4718592 | tf_op jit(solution)/shard_map/all_gather | solution.py:800
  13.1 161.8 %all-gather.21.cloned.1.call-start = ((), (), s32[]{:S(2)}) async-start(), calls=%async_computation.4 | async-start | bytes 8912896 | tf_op jit(solution)/shard_map/all_gather | solution.py:792
  13.5 129.4 %copy-start.53 = (pred[128]{0:T(512)(128)(4,1)}, pred[128]{0:T(512)(128)(4,1)S(1)}, u32[]{:S(2)}) copy-start(pred[128]{0:T(512)(128)(4,1)S(1)} %dynamic_slice.104) | copy-start | bytes 388
  14.4 180.0 %all-gather.23.cloned.1.call-start = ((), (), s32[]{:S(2)}) async-start(), calls=%async_computation.5 | async-start | bytes 12582912 | tf_op jit(solution)/shard_map/all_gather | solution.py:800
  15.2 272.2 %all-gather.25.cloned.1.call-start = ((), (), s32[]{:S(2)}) async-start(), calls=%async_computation.6 | async-start | bytes 3145728 | tf_op jit(solution)/shard_map/all_gather | solution.py:800
  143.2 20.5 %copy-start.5 = (s32[2048,1]{1,0:T(8,128)}, s32[2048,1]{1,0:T(8,128)S(1)}, u32[]{:S(2)}) copy-start(s32[2048,1]{1,0:T(8,128)S(1)} %add_select_fusion.segc_ref) | copy-start | bytes 24580
  180.8 147.9 %all-gather.43.cloned.1.call-start = ((), (), s32[]{:S(2)}) async-start(), calls=%async_computation.15 | async-start | bytes 17301504 | tf_op jit(solution)/shard_map/all_gather | solution.py:800
  182.4 19.0 %all-to-all-start = ((bf16[16,128,128]{1,2,0:T(8,128)(2,1)}), bf16[16,128,128]{1,2,0:T(8,128)(2,1)S(1)}, u32[]{:S(2)}, u32[]{:S(2)}) async-start(bf16[16,128,128]{1,2,0:T(8,128)(2,1)} %copy.106), calls=%async_computation | async-start | bytes 1048576 | tf_op jit(solution)/shard_map/all_to_all | solution.py:931
  186.0 167.7 %all-gather.45.cloned.1.call-start = ((), (), s32[]{:S(2)}) async-start(), calls=%async_computation.16 | async-start | bytes 8650752 | tf_op jit(solution)/shard_map/all_gather | solution.py:800
  186.6 253.2 %all-gather.27.cloned.1.call-start = ((), (), s32[]{:S(2)}) async-start(), calls=%async_computation.7 | async-start | bytes 6127616 | tf_op jit(solution)/shard_map/all_gather | solution.py:792
  187.1 90.8 %copy-start.32 = (bf16[2048,16]{1,0:T(8,128)(2,1)}, bf16[2048,16]{1,0:T(8,128)(2,1)S(1)}, u32[]{:S(2)}) copy-start(bf16[2048,16]{1,0:T(8,128)(2,1)S(1)} %reshape.285) | copy-start | bytes 196612
  206.4 77.2 %copy-start.59 = (f32[128]{0:T(128)}, f32[128]{0:T(128)S(1)}, u32[]{:S(2)}) copy-start(f32[128]{0:T(128)S(1)} %get-tuple-element.145) | copy-start | bytes 1540
  206.4 77.2 %copy-start.50 = (f32[128]{0:T(128)}, f32[128]{0:T(128)S(1)}, u32[]{:S(2)}) copy-start(f32[128]{0:T(128)S(1)} %fusion.73) | copy-start | bytes 1540
  283.6 33.7 %copy-start.41 = (f32[2048]{0:T(1024)}, f32[2048]{0:T(1024)S(1)}, u32[]{:S(2)}) copy-start(f32[2048]{0:T(1024)S(1)} %get-tuple-element.147) | copy-start | bytes 24580
  284.9 32.4 %copy-start.43 = (f32[2048]{0:T(1024)}, f32[2048]{0:T(1024)S(1)}, u32[]{:S(2)}) copy-start(f32[2048]{0:T(1024)S(1)} %fusion.47) | copy-start | bytes 24580
  319.3 2.9 collective-permute-start
  321.6 2.7 collective-permute-start.1
  326.6 419.4 %all-gather.29.cloned.1.call-start = ((), (), s32[]{:S(2)}) async-start(), calls=%async_computation.8 | async-start | bytes 12255232 | tf_op jit(solution)/shard_map/all_gather | solution.py:792
  327.4 518.2 %all-gather.33.cloned.1.call-start = ((), (), s32[]{:S(2)}) async-start(), calls=%async_computation.10 | async-start | bytes 6291456 | tf_op jit(solution)/shard_map/all_gather | solution.py:800
  328.1 550.8 %all-gather.31.cloned.1.call-start = ((), (), s32[]{:S(2)}) async-start(), calls=%async_computation.9 | async-start | bytes 18874368 | tf_op jit(solution)/shard_map/all_gather | solution.py:800
  404.4 24.9 %copy-start.2 = (bf16[2048,512]{1,0:T(8,128)(2,1)S(1)}, bf16[2048,512]{1,0:T(8,128)(2,1)}, u32[]{:S(2)}) copy-start(bf16[2048,512]{1,0:T(8,128)(2,1)} %all-gather.25.cloned.1.call-done.in_ref) | copy-start | bytes 6291460
  404.4 24.9 %copy-start.3 = (bf16[2048,512]{1,0:T(8,128)(2,1)S(1)}, bf16[2048,512]{1,0:T(8,128)(2,1)}, u32[]{:S(2)}) copy-start(bf16[2048,512]{1,0:T(8,128)(2,1)} %get-tuple-element.79.grad_ref) | copy-start | bytes 6291460
  439.8 227.9 %copy-start.21 = (f32[2048,16]{1,0:T(8,128)S(1)}, f32[2048,16]{1,0:T(8,128)}, u32[]{:S(2)}) copy-start(f32[2048,16]{1,0:T(8,128)} %copy-done.20) | copy-start | bytes 393220
  439.8 227.9 %copy-start.42 = (f32[2048]{0:T(1024)S(1)}, f32[2048]{0:T(1024)}, u32[]{:S(2)}) copy-start(f32[2048]{0:T(1024)} %copy-done.41) | copy-start | bytes 24580
  439.8 227.9 %copy-start.44 = (f32[2048]{0:T(1024)S(1)}, f32[2048]{0:T(1024)}, u32[]{:S(2)}) copy-start(f32[2048]{0:T(1024)} %copy-done.43) | copy-start | bytes 24580
  678.7 13.4 %collective-permute-start.10 = (bf16[1024,2048]{1,0:T(8,128)(2,1)}, bf16[1024,2048]{1,0:T(8,128)(2,1)}, u32[]{:S(2)}, u32[]{:S(2)}) collective-permute-start(bf16[1024,2048]{1,0:T(8,128)(2,1)} %constant_dynamic-slice_fusion.3), channel_id=1, source_target_pairs={{0,1},{1,0},{2,3},{3,2},{4,5},{5,4},{6,7},{7,6},{8,9},{9,8},{10,11... | collective-permute-start | bytes 12582920 | tf_op jit(solution)/shard_map/ppermute | solution.py:815
  683.6 62.3 %all-to-all-start.1 = ((bf16[128,16,128]{2,0,1:T(8,128)(2,1)}), bf16[128,16,128]{2,0,1:T(8,128)(2,1)S(1)}, u32[]{:S(2)}, u32[]{:S(2)}) async-start(bf16[128,16,128]{2,0,1:T(8,128)(2,1)} %bitcast.119), calls=%async_computation.1 | async-start | bytes 1048576 | tf_op jit(solution)/shard_map/all_to_all | solution.py:993
  690.1 234.9 %all-gather.41.cloned.1.call-start = ((), (), s32[]{:S(2)}) async-start(), calls=%async_computation.14 | async-start | bytes 4456448 | tf_op jit(solution)/shard_map/all_gather | solution.py:792
  699.8 46.1 %copy-start.6 = (s32[2048,1]{1,0:T(8,128)S(1)}, s32[2048,1]{1,0:T(8,128)}, u32[]{:S(2)}) copy-start(s32[2048,1]{1,0:T(8,128)} %copy-done.5) | copy-start | bytes 24580
  699.8 46.2 %copy-start.12 = (bf16[2048,192]{1,0:T(8,128)(2,1)S(1)}, bf16[2048,192]{1,0:T(8,128)(2,1)}, u32[]{:S(2)}) copy-start(bf16[2048,192]{1,0:T(8,128)(2,1)} %copy-done.11) | copy-start | bytes 2359300
  699.8 46.2 %copy-start.18 = (bf16[2048,128]{1,0:T(8,128)(2,1)S(1)}, bf16[2048,128]{1,0:T(8,128)(2,1)}, u32[]{:S(2)}) copy-start(bf16[2048,128]{1,0:T(8,128)(2,1)} %copy-done.17) | copy-start | bytes 1572868
  772.7 70.1 %all-to-all-start.2 = ((bf16[16,128,512]{1,2,0:T(8,128)(2,1)}), bf16[16,128,512]{1,2,0:T(8,128)(2,1)S(1)}, u32[]{:S(2)}, u32[]{:S(2)}) async-start(bf16[16,128,512]{1,2,0:T(8,128)(2,1)} %copy.112), calls=%async_computation.2 | async-start | bytes 4194304 | tf_op jit(solution)/shard_map/all_to_all | solution.py:1005
  777.9 168.9 %all-gather.37.cloned.1.call-start = ((), (), s32[]{:S(2)}) async-start(), calls=%async_computation.12 | async-start | bytes 2785280 | tf_op jit(solution)/shard_map/all_gather | solution.py:792
  816.6 32.7 %copy-start.56 = (f32[32]{0:T(128)S(1)}, f32[32]{0:T(128)}, u32[]{:S(2)}) copy-start(f32[32]{0:T(128)} %copy-done.55) | copy-start | bytes 388
  851.6 137.7 %all-gather.39.cloned.1.call-start = ((), (), s32[]{:S(2)}) async-start(), calls=%async_computation.13 | async-start | bytes 2228224 | tf_op jit(solution)/shard_map/all_gather | solution.py:792
  851.6 1.4 collective-permute-start.9
  853.8 231.0 %all-gather.35.cloned.1.call-start = ((), (), s32[]{:S(2)}) async-start(), calls=%async_computation.11 | async-start | bytes 6684672 | tf_op jit(solution)/shard_map/all_gather | solution.py:792
  855.1 1.8 collective-permute-start.7
  859.8 1.2 collective-permute-start.14
  878.6 119.3 %collective-permute-start.12 = (bf16[1024,2816]{1,0:T(8,128)(2,1)}, bf16[1024,2816]{1,0:T(8,128)(2,1)}, u32[]{:S(2)}, u32[]{:S(2)}) collective-permute-start(bf16[1024,2816]{1,0:T(8,128)(2,1)} %constant_dynamic-slice_fusion.1), channel_id=1, source_target_pairs={{0,1},{1,0},{2,3},{3,2},{4,5},{5,4},{6,7},{7,6},{8,9},{9,8},{10,11... | collective-permute-start | bytes 17301512 | tf_op jit(solution)/shard_map/ppermute | solution.py:815
  889.4 9.2 collective-permute-start.2
  889.8 16.9 %collective-permute-start.11 = (bf16[1024,16]{0,1:T(8,128)(2,1)S(1)}, bf16[1024,16]{0,1:T(8,128)(2,1)S(1)}, u32[]{:S(2)}, u32[]{:S(2)}) collective-permute-start(bf16[1024,16]{0,1:T(8,128)(2,1)S(1)} %constant_dynamic-slice_fusion.2), channel_id=1, source_target_pairs={{0,1},{1,0},{2,3},{3,2},{4,5},{5,4},{6,7},{7,6},{8,9},{9,8},{10,11... | collective-permute-start | bytes 98312 | tf_op jit(solution)/shard_map/ppermute | solution.py:815
  898.5 33.2 %collective-permute-start.3 = (f32[36,128]{1,0:T(8,128)S(1)}, f32[36,128]{1,0:T(8,128)S(1)}, u32[]{:S(2)}, u32[]{:S(2)}) collective-permute-start(f32[36,128]{1,0:T(8,128)S(1)} %fusion.82), channel_id=1, source_target_pairs={{0,4},{2,6},{4,0},{6,2},{8,12},{10,14},{12,8},{14,10},{16,20},{18,... | collective-permute-start | bytes 55304 | tf_op jit(solution)/shard_map/ppermute | solution.py:823
  931.7 10.0 collective-permute-start.4
  941.7 17.9 %collective-permute-start.13 = (bf16[704,2048]{1,0:T(8,128)(2,1)}, bf16[704,2048]{1,0:T(8,128)(2,1)}, u32[]{:S(2)}, u32[]{:S(2)}) collective-permute-start(bf16[704,2048]{1,0:T(8,128)(2,1)} %constant_dynamic-slice_fusion), channel_id=1, source_target_pairs={{0,1},{1,0},{2,3},{3,2},{4,5},{5,4},{6,7},{7,6},{8,9},{9,8},{10,11... | collective-permute-start | bytes 8650760 | tf_op jit(solution)/shard_map/ppermute | solution.py:815
  941.7 5.0 collective-permute-start.5
  946.8 11.5 %collective-permute-start.6 = (f32[36,128]{1,0:T(8,128)S(1)}, f32[36,128]{1,0:T(8,128)S(1)}, u32[]{:S(2)}, u32[]{:S(2)}) collective-permute-start(f32[36,128]{1,0:T(8,128)S(1)} %add.283), channel_id=1, source_target_pairs={{0,1},{1,0},{2,3},{3,2},{4,5},{5,4},{6,7},{7,6},{8,9},{9,8},{10,11... | collective-permute-start | bytes 55304 | tf_op jit(solution)/shard_map/ppermute | solution.py:815
  956.6 38.2 %collective-permute-start.8 = (bf16[1024,576]{0,1:T(8,128)(2,1)}, bf16[1024,576]{0,1:T(8,128)(2,1)}, u32[]{:S(2)}, u32[]{:S(2)}) collective-permute-start(bf16[1024,576]{0,1:T(8,128)(2,1)} %constant_dynamic-slice_fusion.5), channel_id=1, source_target_pairs={{0,1},{1,0},{2,3},{3,2},{4,5},{5,4},{6,7},{7,6},{8,9},{9,8},{10,11... | collective-permute-start | bytes 3538952 | tf_op jit(solution)/shard_map/ppermute | solution.py:815
  (53 other events, 367.8 us)
Sparse Core Ops, SparseCore 0:
  13.2 14.7 all-gather.18
  31.3 138.5 all-gather.20
  171.4 17.5 all-gather.22
  191.0 11.7 all-gather.24
  204.2 25.0 all-gather.42
  230.6 17.1 all-gather.44
  326.7 87.7 all-gather.26
  417.3 230.7 all-gather.28
  649.7 15.2 all-gather.32
  666.3 28.5 all-gather.30
  746.0 106.8 all-gather.40
  856.0 70.3 all-gather.36
  929.2 60.0 all-gather.38
  991.9 92.7 all-gather.34

commit v6 on v5

--- a/solution.py
+++ b/solution.py
@@ -466,14 +466,9 @@
     pl.semaphore_wait(barrier, count - 1)
 
 
-def gather_kernel(streams, n_main, n_small, *refs):
-    n = n_main + n_small
-    ins, outs = refs[:n], refs[n : 2 * n]
-    send_sems, recv_sems, small_send, small_recv, local_sems = refs[2 * n :]
+def gather_events(streams, ins, outs, send_sems, recv_sems):
     rank, z, y, x = place()
     count = lax.axis_size("seq")
-    greet_all()
-    locals_ = [pltpu.make_async_copy(ins[i], outs[i].at[rank], local_sems.at[i]) for i in range(n)]
     slots = {}
 
     def copy(stream, offset, step):
@@ -492,17 +487,6 @@
             device_id_type=MESH,
         )
 
-    def small_copy(i, k):
-        peer = lax.rem(rank + k, count)
-        return pltpu.make_async_remote_copy(
-            src_ref=ins[n_main + i],
-            dst_ref=outs[n_main + i].at[rank],
-            send_sem=small_send.at[i * count + k],
-            recv_sem=small_recv.at[i * count + rank],
-            device_id={"seq": peer},
-            device_id_type=MESH,
-        )
-
     def arrived(stream, offset):
         index, first, rows, order = streams[stream]
         source = rank_at(z, y, x, *offset)
@@ -520,22 +504,54 @@
         ((stream, offset) for stream in range(len(streams)) for offset in OFFSETS),
         key=lambda it: (hops(it[1]), it[0]),
     )
-    for stream, offset in todo:
-        def forward(stream=stream, offset=offset):
+
+    def act(stream, offset):
+        def forward():
             if hops(offset):
                 arrived(stream, offset)
             for step in onward(streams[stream][3], offset):
                 guarded(z, [step[0]], lambda: copy(stream, offset, step).start())
+
         guarded(z, [offset[0]], forward)
-        if stream == len(streams) - 1 and offset == (0, 0, 0):
+
+    def finish():
+        for stream, offset in todo:
+            for step in onward(streams[stream][3], offset):
+                guarded(z, [offset[0], step[0]], lambda: copy(stream, offset, step).wait_send())
+
+    return [functools.partial(act, *it) for it in todo], finish
+
+
+def gather_kernel(streams, n_main, n_small, *refs):
+    n = n_main + n_small
+    ins, outs = refs[:n], refs[n : 2 * n]
+    send_sems, recv_sems, small_send, small_recv, local_sems = refs[2 * n :]
+    rank = lax.axis_index("seq")
+    count = lax.axis_size("seq")
+    greet_all()
+    locals_ = [pltpu.make_async_copy(ins[i], outs[i].at[rank], local_sems.at[i]) for i in range(n)]
+
+    def small_copy(i, k):
+        peer = lax.rem(rank + k, count)
+        return pltpu.make_async_remote_copy(
+            src_ref=ins[n_main + i],
+            dst_ref=outs[n_main + i].at[rank],
+            send_sem=small_send.at[i * count + k],
+            recv_sem=small_recv.at[i * count + rank],
+            device_id={"seq": peer},
+            device_id_type=MESH,
+        )
+
+    actions, finish = gather_events(streams, ins, outs, send_sems, recv_sems)
+    for i, action in enumerate(actions):
+        action()
+        if i == len(streams) - 1:
             for c in locals_:
                 c.start()
-            for i in range(n_small):
+            for s in range(n_small):
                 for k in range(1, count):
-                    small_copy(i, k).start()
-    for stream, offset in todo:
-        for step in onward(streams[stream][3], offset):
-            guarded(z, [offset[0], step[0]], lambda: copy(stream, offset, step).wait_send())
+                    small_copy(s, k).start()
+    finish()
     for i in range(n_small):
         for k in range(1, count):
             small_copy(i, k).wait_send()
@@ -543,8 +559,12 @@
             source = lax.rem(rank + k, count)
             block = outs[n_main + i].at[source]
             pltpu.make_async_remote_copy(
-                src_ref=block, dst_ref=block, send_sem=small_send.at[0],
-                recv_sem=small_recv.at[i * count + source], device_id={"seq": rank}, device_id_type=MESH,
+                src_ref=block,
+                dst_ref=block,
+                send_sem=small_send.at[0],
+                recv_sem=small_recv.at[i * count + source],
+                device_id={"seq": rank},
+                device_id_type=MESH,
             ).wait_recv()
     for c in locals_:
         c.wait()
@@ -554,14 +574,18 @@
     return sum(len(onward(s[3], o)) for s in streams for o in OFFSETS)
 
 
-def gather_all(main, parts, small, collective_id, count=16):
+def streams_of(main, parts):
     streams = []
     for i, pieces in enumerate(parts):
         first = 0
         for rows, order in pieces:
             streams.append((i, first, rows, order))
             first += rows
-        assert first == main[i].shape[0]
+    return streams
+
+
+def gather_all(main, parts, small, collective_id, count=16):
+    streams = streams_of(main, parts)
     arrays = list(main) + list(small)
     any_spec = pl.BlockSpec(memory_space=pl.ANY)
     return pl.pallas_call(
@@ -750,13 +774,7 @@
 
 
 def scatter_sum(main, parts, small, collective_id, count=16):
-    streams = []
-    for i, pieces in enumerate(parts):
-        first = 0
-        for rows, order in pieces:
-            streams.append((i, first, rows, order))
-            first += rows
-        assert first == main[i].shape[1]
+    streams = streams_of(main, parts)
     arrays = list(main) + list(small)
     any_spec = pl.BlockSpec(memory_space=pl.ANY)
     vmem = pl.BlockSpec(memory_space=pltpu.VMEM)
@@ -788,6 +806,161 @@
     )(*arrays)
 
 
+COLS = 256
+PACE = 2
+
+
+def expert_kernel(
+    streams, n_main, x_ref, rg_ref, in_col_ref, out_row_ref, out_col_ref, in_row_ref, *refs
+):
+    ins, refs = refs[:n_main], refs[n_main:]
+    res_ref, back_ref, hidden_out, gate_out, up_out, refs = *refs[:5], refs[5:]
+    outs, refs = refs[:n_main], refs[n_main:]
+    gu, hidden, dgu, send_sems, recv_sems, local_sems, out_sems = refs
+    rank = lax.axis_index("seq")
+    i = pl.program_id(0)
+    spans = -(-FF // COLS)
+    ends = [2 * FF // COLS, 2 * FF // COLS + spans]
+    ends += [ends[1] + D // COLS, ends[1] + 2 * D // COLS]
+    actions, finish = gather_events(streams, ins, outs, send_sems, recv_sems)
+    own = [pltpu.make_async_copy(ins[k], outs[k].at[rank], local_sems.at[k]) for k in range(n_main)]
+    kept = [
+        pltpu.make_async_copy(hidden, hidden_out, out_sems.at[0]),
+        pltpu.make_async_copy(dgu.at[:, pl.ds(0, FF)], gate_out, out_sems.at[1]),
+        pltpu.make_async_copy(dgu.at[:, pl.ds(FF, FF)], up_out, out_sems.at[2]),
+    ]
+
+    @pl.when(i == 0)
+    def _():
+        greet_all()
+        for action in actions[: len(streams)]:
+            action()
+        for copy in own:
+            copy.start()
+
+    @pl.when(i < ends[0])
+    def _():
+        cols = pl.ds(pl.multiple_of(i * COLS, COLS), COLS)
+        gu[:, cols] = dot(x_ref[...], in_col_ref[...]).astype(BF16)
+
+    def back_span(first, width):
+        grad = dot_nt(rg_ref[...], out_row_ref[:width, :])
+        at, to = pl.ds(first, width), pl.ds(pl.multiple_of(FF + first, 128), width)
+        gate, up = gu[:, at].astype(F32), gu[:, to].astype(F32)
+        hidden[:, at] = (gate * jax.nn.sigmoid(gate) * up).astype(BF16)
+        gate_grad, up_grad = silu_grads(gate, up, grad)
+        dgu[:, at] = gate_grad.astype(BF16)
+        dgu[:, to] = up_grad.astype(BF16)
+
+    full = FF // COLS
+
+    @pl.when((i >= ends[0]) & (i < ends[0] + full))
+    def _():
+        back_span(pl.multiple_of((i - ends[0]) * COLS, COLS), COLS)
+
+    if FF % COLS:
+
+        @pl.when(i == ends[0] + full)
+        def _():
+            back_span(full * COLS, FF % COLS)
+
+    @pl.when(i == ends[1])
+    def _():
+        for copy in kept:
+            copy.start()
+
+    @pl.when((i >= ends[1]) & (i < ends[2]))
+    def _():
+        res_ref[...] = dot(hidden[...], out_col_ref[...]).astype(BF16)
+
+    @pl.when(i >= ends[2])
+    def _():
+        back_ref[...] = dot_nt(dgu[...], in_row_ref[...]).astype(BF16)
+
+    done = len(streams)
+    for step in range(ends[3] - 1):
+        some = actions[done : done + PACE]
+        done += len(some)
+        if some:
+
+            @pl.when(i == step)
+            def _(some=some):
+                for action in some:
+                    action()
+
+    @pl.when(i == ends[3] - 1)
+    def _():
+        for action in actions[done:]:
+            action()
+        finish()
+        for copy in own + kept:
+            copy.wait()
+
+
+def expert_block(x, rg, w_in, w_out, main, parts, collective_id, count=16):
+    rows = x.shape[0]
+    streams = streams_of(main, parts)
+    spans = -(-FF // COLS)
+    first = 2 * FF // COLS
+    second = first + spans
+    third = second + D // COLS
+    steps = third + D // COLS
+
+    def held(array):
+        return pl.BlockSpec(array.shape, lambda i: (0, 0), pipeline_mode=pl.Buffered(1))
+
+    def during(start, stop):
+        return lambda i: jnp.minimum(jnp.maximum(i - start, 0), stop - start - 1)
+
+    one, two, three, four = during(0, first), during(first, second), during(second, third), during(third, steps)
+    any_spec = pl.BlockSpec(memory_space=pl.ANY)
+    n = len(main)
+    results = pl.pallas_call(
+        functools.partial(expert_kernel, streams, n),
+        grid=(steps,),
+        in_specs=[
+            held(x),
+            held(rg),
+            pl.BlockSpec((D, COLS), lambda i: (0, one(i))),
+            pl.BlockSpec((COLS, D), lambda i: (two(i), 0)),
+            pl.BlockSpec((FF, COLS), lambda i: (0, three(i))),
+            pl.BlockSpec((COLS, 2 * FF), lambda i: (four(i), 0)),
+        ]
+        + [any_spec] * n,
+        out_specs=(
+            pl.BlockSpec((rows, COLS), lambda i: (0, three(i))),
+            pl.BlockSpec((rows, COLS), lambda i: (0, four(i))),
+            any_spec,
+            any_spec,
+            any_spec,
+        )
+        + (any_spec,) * n,
+        out_shape=(
+            jax.ShapeDtypeStruct((rows, D), BF16),
+            jax.ShapeDtypeStruct((rows, D), BF16),
+            jax.ShapeDtypeStruct((rows, FF), BF16),
+            jax.ShapeDtypeStruct((rows, FF), BF16),
+            jax.ShapeDtypeStruct((rows, FF), BF16),
+        )
+        + tuple(jax.ShapeDtypeStruct((count,) + a.shape, a.dtype) for a in main),
+        scratch_shapes=[
+            pltpu.VMEM((rows, 2 * FF), BF16),
+            pltpu.VMEM((rows, FF), BF16),
+            pltpu.VMEM((rows, 2 * FF), BF16),
+            pltpu.SemaphoreType.DMA((n_sends(streams),)),
+            pltpu.SemaphoreType.DMA((len(streams) * count,)),
+            pltpu.SemaphoreType.DMA((n,)),
+            pltpu.SemaphoreType.DMA((3,)),
+        ],
+        compiler_params=pltpu.CompilerParams(
+            collective_id=collective_id, has_side_effects=True, vmem_limit_bytes=60 * 2**20
+        ),
+        cost_estimate=pl.CostEstimate(flops=12 * rows * D * FF, bytes_accessed=100 * 2**20, transcendentals=2 * rows * FF),
+        name="expert_block",
+    )(x, rg, w_in, w_out, w_out, w_in, *main)
+    return results[:5], results[5:]
+
+
 def gather_seq(rows):
     return lax.all_gather(rows, "seq", axis=0, tiled=True)
 
@@ -831,10 +1004,10 @@
 ROW_PARTS = [(48, "zxy"), (48, "zyx"), (16, "xyz"), (16, "yxz")]
 
 
-def split_rows(rows):
+def split_rows(rows, part=8):
     tile = 16
     tiles = rows // tile
-    short = tiles // 8
+    short = tiles // part
     long = (tiles - 2 * short) // 2
     sizes = [tiles - 2 * short - long, long, short, short]
     orders = ["zxy", "zyx", "xyz", "yxz"]
@@ -951,24 +1124,24 @@
     part_shared_out = scatter_fsdp(grad_shared_out[:units]).astype(BF16)
     part_shared_in = jnp.concatenate([grad_shared_in[:units], grad_shared_in[lanes : lanes + units]], axis=0)
     part_shared_in = scatter_fsdp(part_shared_in, 1).astype(BF16)
-    arrived, part_shared_out, part_shared_in = lax.optimization_barrier(
-        (arrived, part_shared_out, part_shared_in)
-    )
-    all_shared_out = gather_seq(part_shared_out)
-    all_shared_in = gather_seq(part_shared_in)
-
-    gate_up = dot(arrived, expert_in).astype(BF16)
-    gate_part, up_part = gate_up[:, :FF].astype(F32), gate_up[:, FF:].astype(F32)
-    hidden = (jax.nn.silu(gate_part) * up_part).astype(BF16)
-    result = dot(hidden, expert_out).astype(BF16)
-    d_hidden = dot_nt(result_grad, expert_out)
-    d_gate, d_up = [g.astype(BF16) for g in silu_grads(gate_part, up_part, d_hidden)]
-    row_grad = dot_nt(jnp.concatenate([d_gate, d_up], axis=1), expert_in).astype(BF16)
+    part_shared_out = jnp.pad(part_shared_out, ((0, -unit % 16), (0, 0)))
+
+    (result, row_grad, hidden, d_gate, d_up), (all_shared_in, all_shared_out) = expert_block(
+        arrived,
+        result_grad,
+        expert_in,
+        expert_out,
+        [part_shared_in, part_shared_out],
+        [split_rows(part_shared_in.shape[0], 6), split_rows(part_shared_out.shape[0], 6)],
+        4,
+    )
     mixed_part, gate_grad = collect_forward(
         result, upstream_all, place, gates, shared_hidden, shared_out, capacity
     )
     ffn_part = collect_backward(row_grad, place, shared_grad, shared_in, capacity)
-    mixed_part, ffn_part, all_shared_out = lax.optimization_barrier((mixed_part, ffn_part, all_shared_out))
+    mixed_part, query_weight, expand_weight = lax.optimization_barrier(
+        (mixed_part, query_weight, expand_weight)
+    )
     mixed_sum, ffn_sum, prob_grads = scatter_sum(
         [part.reshape(seq_count, tok_count, D) for part in (mixed_part, ffn_part)],
         [ROW_PARTS, ROW_PARTS],
@@ -997,7 +1170,8 @@
         [grad_output.reshape(seq_count, output_rows, D)], [split_rows(output_rows)], [], 5
     )
 
-    head_grad, all_shared_in = lax.optimization_barrier((head_grad, all_shared_in))
+    head_grad, part_output = lax.optimization_barrier((head_grad, part_output.astype(BF16)))
+    all_output = gather_seq(part_output)
     head_back = attention_backward(query, key, value, head_grad, segment, log_total, cosines, sines)
     head_back, arrived, result_grad, hidden, d_gate, d_up = lax.optimization_barrier(
         (head_back, arrived, result_grad, hidden, d_gate, d_up)
@@ -1011,13 +1185,15 @@
     head_pre_grad = jnp.concatenate([head_back[:, :DN], head_back[:, rope_at : rope_at + DR]], axis=1)
     grad_query = dot_tn(head_pre_grad, normed_all).astype(BF16)
     grad_expand = dot_tn(head_back[:, DN:rope_at], latent_all).astype(BF16)
-    back, grad_expert_out, grad_expert_in, grad_query, grad_expand = lax.optimization_barrier(
-        (back, grad_expert_out, grad_expert_in, grad_query, grad_expand)
+    part_query = scatter_fsdp(grad_query, 1).astype(BF16)
+    part_expand = scatter_fsdp(grad_expand, 1).astype(BF16)
+    all_query = gather_seq(part_query)
+    all_expand = gather_seq(part_expand)
+    back, grad_expert_out, grad_expert_in, part_query, part_expand = lax.optimization_barrier(
+        (back, grad_expert_out, grad_expert_in, part_query, part_expand)
     )
     sum_expert_in = scatter_fsdp(grad_expert_in)[None]
     sum_expert_out = scatter_fsdp(grad_expert_out)[None]
-    part_query = scatter_fsdp(grad_query, 1).astype(BF16)
-    part_expand = scatter_fsdp(grad_expand, 1).astype(BF16)
 
     back = back.transpose(1, 0, 2)
     pre_grad = jnp.concatenate([back[..., :DN], back[..., rope_at : rope_at + DR]], axis=-1)
@@ -1028,11 +1204,13 @@
     latent_pull = jax.vjp(rms_norm, own(latent_full), gain_latent)[1]
     compressed_grad, grad_gain_latent = latent_pull(latent_grad)
     full_grad = jnp.concatenate([compressed_grad, rope_grad], axis=1).astype(BF16)
+    full_grad, all_output = lax.optimization_barrier((full_grad, all_output))
     full_all = gather_seq(full_grad)
     sum_latent = scatter_fsdp(dot_tn(normed_all, full_all).astype(BF16))
     spread_grad = jnp.pad(full_grad[:, :KVR], ((0, 0), (0, query_width + DR)))
     spread_grad = spread_grad + jnp.pad(full_grad[:, KVR:], ((0, 0), (KVR + query_width, 0)))
     normed_grad = dot_nt(pre_grad, query_weight) + dot_nt(spread_grad, head_weights)
+    normed_grad, all_query = lax.optimization_barrier((normed_grad, all_query))
     input_pull = jax.vjp(rms_norm, inputs, gain_attn)[1]
     input_norm_grad, grad_gain_attn = input_pull(normed_grad)
     grad_inputs = middle_grad + input_norm_grad
@@ -1040,11 +1218,11 @@
     gain_sum = sum_everywhere(
         jnp.concatenate([grad_gain_attn, grad_gain_latent, grad_gain_ffn]).reshape(-1, 128)
     ).reshape(-1)
-    sum_shared_out = all_shared_out.astype(F32)
+    sum_shared_out = all_shared_out[:, :unit].reshape(w_shared_out.shape).astype(F32)
     sum_shared_in = turn_units(all_shared_in.reshape(seq_count, 2 * fsdp_count, unit, row_part))
-    sum_query = turn_rows(gather_seq(part_query), 384)
-    sum_expand = turn_rows(gather_seq(part_expand), 512)
-    sum_output = gather_seq(part_output.astype(BF16)).astype(F32)
+    sum_query = turn_rows(all_query, 384)
+    sum_expand = turn_rows(all_expand, 512)
+    sum_output = all_output.astype(F32)
     fsdp_rank = lax.axis_index("fsdp")
 
     def own_part(first, like):

time: 1110 us -> 1080 us (0.973)
  matrix products: 180 us -> 92.2 us
  Pallas kernels: 577 us -> 631 us
  waiting for transfers between devices: 145 us -> 164 us
    pallas_call x0 -> x1, Pallas kernels: none -> 150 us  [expert_block(): pl.pallas_call(functools.partial(expert_kernel, streams, n), grid=(steps,...]
    pallas_call x2, Pallas kernels: 271 us -> 180 us  [scatter_sum(): pl.pallas_call(functools.partial(scatter_kernel, streams, len(main), len(...]
    dot_general x7 -> x5, matrix products: 66.2 us -> 18.7 us  [dot_nt(): lax.dot_general(left, right, (((1,), (1,)), ((), ())), preferred_element_...]
    dot_general x4 -> x2, matrix products: 52.1 us -> 13.1 us  [dot(): return jnp.dot(left, right, preferred_element_type=F32)]
    all_gather x7 -> x5, waiting for transfers between devices: 99.8 us -> 137 us  [gather_seq(): return lax.all_gather(rows, 'seq', axis=0, tiled=True)]
    all_to_all x1, waiting for transfers between devices: 26.1 us -> 11.8 us  [on_device(): lax.all_to_all(head_back.reshape(seq_count, tok_count, -1), 'seq', split_...]
  transfers between devices with their start and end apart: 32 -> 30, of which waited for: 9 -> 10; matrix products, arithmetic and copies ran while one was open for 28% -> 19% of each run, Pallas kernels for 52% -> 45%
where the time goes in v6:
time: 1080 us; the launch traced here: 1070 us
  Pallas kernels  631 us (58%)
  waiting for transfers between devices  164 us (15%)
  matrix products  92.2 us (9%)
  other arithmetic  78.6 us (7%)
  local copies, waits for them, and re-layouts  61.1 us (6%)
  starting transfers between devices  23.8 us (2%)
  between operations  15.8 us (1%)
    pallas_call x2, Pallas kernels, scatter_sum(): pl.pallas_call(functools.partial(scatter_kernel, streams, len(main), len(...  180 us
    pallas_call x2, Pallas kernels, gather_all(): pl.pallas_call(functools.partial(gather_kernel, streams, len(main), len(s...  180 us
    pallas_call x1, Pallas kernels, expert_block(): pl.pallas_call(functools.partial(expert_kernel, streams, n), grid=(steps,...  150 us
    all_gather x5, waiting for transfers between devices, gather_seq(): return lax.all_gather(rows, 'seq', axis=0, tiled=True)  137 us
    dot_general x7, matrix products, dot_tn(): lax.dot_general(left, right, (((0,), (0,)), ((), ())), preferred_element_...  60.4 us
    pallas_call x1, Pallas kernels, spread(): pl.pallas_call(spread_kernel, grid=(steps,), in_specs=[by_rows(t, D), by_...  31.8 us
  transfers between devices with their start and end apart: 30, of which 10 were waited for; matrix products, arithmetic and copies ran while one was open for 19% of the time, Pallas kernels for 45%

profile of v6, /device:TPU:0, one launch (start us, length us, event | category | flops | bytes accessed | tf_op | source)
XLA Modules:
  0.0 1073.8 jit_solution(15316606079024899982)
XLA Ops:
  20.4 112.3 %gather_all.2 = (bf16[16,128,2048]{2,1,0:T(8,128)(2,1)}, bf16[16,16,128]{2,1,0:T(8,128)(2,1)}) custom-call(bf16[128,2048]{1,0:T(8,128)(2,1)} %refs_0_.1, bf16[16,128]{1,0:T(8,128)(2,1)} %convert_element_type.214.refs_1_), custom_call_target="tpu_custom_call" | custom-call | tf_op jit(solution)/shard_map/gather_all/pallas_call | solution.py:591
  136.1 3.7 fusion.4
  139.9 16.7 %project.1 = (bf16[2048,2048]{1,0:T(8,128)(2,1)}, bf16[2048,192]{1,0:T(8,128)(2,1)S(1)}, bf16[2048,192]{1,0:T(8,128)(2,1)S(1)}, bf16[2048,128]{1,0:T(8,128)(2,1)...) custom-call(bf16[2048,2048]{1,0:T(8,128)(2,1)} %bitcast.155, f32[1,2048]{1,0:T(1,128)S(1)} %bitcast.111, ...), custom_call_target="tpu_custom_call" | custom-call | flops 7549747200 | bytes 25165824 | tf_op jit(solution)/shard_map/project/pallas_call | solution.py:199
  156.6 7.7 attention_forward.1
  171.0 3.3 concatenate.33
  178.0 3.8 all-to-all-start
  186.0 3.0 all_gather.51
  190.1 6.9 all-to-all-done
  197.0 5.7 multiply_reduce_fusion.2
  204.6 67.5 %gather_all.3 = (bf16[16,128,2048]{2,1,0:T(8,128)(2,1)}, f32[16,8,128]{2,1,0:T(8,128)}) custom-call(bf16[128,2048]{1,0:T(8,128)(2,1)} %multiply_convert_fusion.1.refs_0_, f32[8,128]{1,0:T(8,128)} %copy-done.11), custom_call_target="tpu_custom_call" | custom-call | tf_op jit(solution)/shard_map/gather_all/pallas_call | solution.py:591
  272.1 7.5 fusion.50
  282.8 31.8 %spread.1 = (bf16[1536,2048]{1,0:T(8,128)(2,1)}, bf16[1536,2048]{1,0:T(8,128)(2,1)}, bf16[2048,256]{1,0:T(8,128)(2,1)}, bf16[2048,512]{1,0:T(8,128)(2,1)}, bf16[...) custom-call(bf16[2048,2048]{1,0:T(8,128)(2,1)} %bitcast.116, bf16[2048,2048]{1,0:T(8,128)(2,1)} %all-gather.19.cloned.1.call-done.up_ref, ...), custom_call_target="tpu_custom_call" | custom-call | flops 14495514624 | bytes 41943040 | tf_op jit(solution)/shard_map/spread/pallas_call | solution.py:299
  323.9 149.7 %expert_block.1 = (bf16[1536,2048]{1,0:T(8,128)(2,1)}, bf16[1536,2048]{1,0:T(8,128)(2,1)}, bf16[1536,1408]{1,0:T(8,128)(2,1)}, bf16[1536,1408]{1,0:T(8,128)(2,1)...) custom-call(bf16[1536,2048]{1,0:T(8,128)(2,1)} %get-tuple-element.100.x_ref, ...), custom_call_target="tpu_custom_call" | custom-call | flops 53150220288 | bytes 104857600 | tf_op jit(solution)/shard_map/expert_block/pallas_call | solution.py:918
  473.6 11.2 %collect_forward.1 = (bf16[2048,2048]{1,0:T(8,128)(2,1)}, f32[2048,1]{1,0:T(8,128)S(1)}) custom-call(bf16[1536,2048]{1,0:T(8,128)(2,1)} %get-tuple-element.82.res_ref, bf16[2048,2048]{1,0:T(8,128)(2,1)} %all-gather.19.cloned.1.call-done.up_ref, s32[4,4,128]{2,1,0:T(4,128)S(1)} %copy-done.10, f32[2048,1]{1,0:T(8,128)S(1)} %get-tuple-element.130.gate_ref, ...), custom_call_target="tpu_custom_call" | custom-call | flops 2952790016 | bytes 25165824 | tf_op jit(solution)/shard_map/collect_forward/pallas_call | solution.py:332
  491.2 10.5 collect_backward.1
  501.7 134.7 %scatter_sum.2 = (f32[128,2048]{1,0:T(8,128)}, f32[128,2048]{1,0:T(8,128)}, f32[16,16,128]{2,1,0:T(8,128)}) custom-call(bf16[16,128,2048]{2,1,0:T(8,128)(2,1)} %bitcast.127, bf16[16,128,2048]{2,1,0:T(8,128)(2,1)} %bitcast.118, f32[16,128]{1,0:T(8,128)} %bitcast.143), custom_call_target="tpu_custom_call" | custom-call | tf_op jit(solution)/shard_map/scatter_sum/pallas_call | solution.py:786
  644.5 2.6 constant_dynamic-slice_fusion.6
  647.1 2.9 fusion.3
  650.9 4.5 all-to-all-start.1
  655.5 7.8 add_convert_fusion
  663.3 45.2 %scatter_sum.3 = f32[64,2048]{1,0:T(8,128)} custom-call(bf16[16,64,2048]{2,1,0:T(8,128)(2,1)} %bitcast.119), custom_call_target="tpu_custom_call" | custom-call | tf_op jit(solution)/shard_map/scatter_sum/pallas_call | solution.py:786
  713.3 12.5 %attention_backward.1 = bf16[2048,512]{1,0:T(8,128)(2,1)} custom-call(bf16[2048,192]{1,0:T(8,128)(2,1)S(1)} %copy-done.13, bf16[2048,192]{1,0:T(8,128)(2,1)S(1)} %copy-done.15, bf16[2048,128]{1,0:T(8,128)(2,1)S(1)} %copy-done.19, bf16[2048,128]{1,0:T(8,128)(2,1)S(1)} %bitcast.110, s32[2048,1]{1,0:T(8,128)S(1)} %copy-done.6, ...), custom_call_target="tpu_custom_call" | custom-call | flops 3489660928 | bytes 6291456 | tf_op jit(solution)/shard_map/attention_backward/pallas_call | solution.py:156
  727.9 5.3 convolution_convert_fusion.4
  739.8 7.4 multiply_convert_fusion
  747.2 4.8 convolution_convert_fusion.6
  752.3 17.4 %turn_units.1 = f32[1024,5632]{1,0:T(8,128)} custom-call(bf16[16,4,88,1024]{3,2,1,0:T(8,128)(2,1)} %bitcast.120), custom_call_target="tpu_custom_call" | custom-call | bytes 34603008 | tf_op jit(solution)/shard_map/turn_units/pallas_call | solution.py:398
  769.7 3.5 slice.90
  774.5 2.4 copy.100
  776.8 5.5 all-to-all-start.2
  782.4 24.4 %convolution_convert_fusion = bf16[2048,2816]{1,0:T(8,128)(2,1)} fusion(bf16[1536,2048]{1,0:T(8,128)(2,1)} %get-tuple-element.100.x_ref, bf16[1536,1408]{1,0:T(8,128)(2,1)} %get-tuple-element.102, bf16[1536,1408]{1,0:T(8,128)(2,1)} %get-tuple-element.101), kind=kOutput, calls=%fused_computation.2 | convolution fusion | flops 17739808768 | bytes 26476544 | tf_op jit(solution)/shard_map/dot_general | solution.py:74
  807.6 14.4 %convolution_convert_fusion.1 = bf16[1408,2048]{1,0:T(8,128)(2,1)} fusion(bf16[1536,1408]{1,0:T(8,128)(2,1)} %get-tuple-element.98, bf16[1536,2048]{1,0:T(8,128)(2,1)} %get-tuple-element.99.rg_ref), kind=kOutput, calls=%fused_computation.7 | convolution fusion | flops 8861253632 | bytes 16384000 | tf_op jit(solution)/shard_map/dot_general | solution.py:74
  822.1 11.8 %all-to-all-done.2 = bf16[16,128,512]{1,2,0:T(8,128)(2,1)S(1)} async-done(((bf16[16,128,512]{1,2,0:T(8,128)(2,1)}), bf16[16,128,512]{1,2,0:T(8,128)(2,1)S(1)}, u32[]{:S(2)}, u32[]{:S(2)}) %all-to-all-start.2) | async-done | bytes 2097184 | tf_op jit(solution)/shard_map/all_to_all | solution.py:1179
  833.9 3.7 constant_dynamic-slice_fusion
  837.6 5.5 constant_dynamic-slice_fusion.1
  844.9 4.1 multiply_reduce_fusion.3
  851.2 8.7 bitcast_convert_fusion
  860.1 10.0 fusion.51
  871.2 30.4 %all-gather.31.cloned.1.call-done.in_ref = bf16[3072,1024]{1,0:T(8,128)(2,1)} async-done(((bf16[192,1024]{1,0:T(8,128)(2,1)}), bf16[3072,1024]{1,0:T(8,128)(2,1)}) %all-gather.31.cloned.1.call-update) | async-done | bytes 6291472 | tf_op jit(solution)/shard_map/all_gather | solution.py:965
  904.2 59.3 %all-gather.35.cloned.1.call-done.in_ref = bf16[4096,256]{1,0:T(8,128)(2,1)} async-done(((bf16[256,256]{1,0:T(8,128)(2,1)}), bf16[4096,256]{1,0:T(8,128)(2,1)}) %all-gather.35.cloned.1.call-update) | async-done | bytes 2097168 | tf_op jit(solution)/shard_map/all_gather | solution.py:965
  965.1 4.1 turn_rows.3
  970.8 6.5 add_bitcast_fusion.1
  977.3 4.4 convert_element_type.260
  983.3 46.0 %all-gather.33.cloned.1.call-done = bf16[2048,576]{1,0:T(8,128)(2,1)} async-done(((bf16[128,576]{1,0:T(8,128)(2,1)}), bf16[2048,576]{1,0:T(8,128)(2,1)}) %all-gather.33.cloned.1.call-update) | async-done | bytes 2359312 | tf_op jit(solution)/shard_map/all_gather | solution.py:965
  1029.3 8.3 convolution_convert_fusion.3
  1037.9 10.1 add_bitcast_fusion
  1047.9 2.3 collective-permute-start.8
  1050.3 2.4 collective-permute-done.8
  1054.0 9.4 turn_rows.2
  (298 shorter events, 94.2 us)
Async XLA Ops:
  7.2 132.7 %all-gather.17.cloned.1.call-start = ((), (), s32[]{:S(2)}) async-start(), calls=%async_computation.3 | async-start | bytes 4718592 | tf_op jit(solution)/shard_map/all_gather | solution.py:973
  13.0 156.0 %all-gather.19.cloned.1.call-start = ((), (), s32[]{:S(2)}) async-start(), calls=%async_computation.4 | async-start | bytes 8912896 | tf_op jit(solution)/shard_map/all_gather | solution.py:965
  14.4 175.7 %all-gather.21.cloned.1.call-start = ((), (), s32[]{:S(2)}) async-start(), calls=%async_computation.5 | async-start | bytes 12582912 | tf_op jit(solution)/shard_map/all_gather | solution.py:973
  15.1 267.7 %all-gather.23.cloned.1.call-start = ((), (), s32[]{:S(2)}) async-start(), calls=%async_computation.6 | async-start | bytes 3145728 | tf_op jit(solution)/shard_map/all_gather | solution.py:973
  136.1 20.5 %copy-start.5 = (s32[2048,1]{1,0:T(8,128)}, s32[2048,1]{1,0:T(8,128)S(1)}, u32[]{:S(2)}) copy-start(s32[2048,1]{1,0:T(8,128)S(1)} %add_select_fusion.segc_ref) | copy-start | bytes 24580
  139.8 16.7 %copy-start.8 = (f32[2048,128]{1,0:T(8,128)}, f32[2048,128]{1,0:T(8,128)S(1)}, u32[]{:S(2)}) copy-start(f32[2048,128]{1,0:T(8,128)S(1)} %get-tuple-element.152.sin_ref) | copy-start | bytes 3145732
  139.8 16.7 %copy-start.9 = (f32[2048,128]{1,0:T(8,128)}, f32[2048,128]{1,0:T(8,128)S(1)}, u32[]{:S(2)}) copy-start(f32[2048,128]{1,0:T(8,128)S(1)} %get-tuple-element.153.cos_ref) | copy-start | bytes 3145732
  174.3 149.6 %all-gather.39.cloned.1.call-start = ((), (), s32[]{:S(2)}) async-start(), calls=%async_computation.14 | async-start | bytes 8650752 | tf_op jit(solution)/shard_map/all_gather | solution.py:973
  174.9 149.0 %all-gather.37.cloned.1.call-start = ((), (), s32[]{:S(2)}) async-start(), calls=%async_computation.13 | async-start | bytes 17301504 | tf_op jit(solution)/shard_map/all_gather | solution.py:973
  175.5 310.4 %all-gather.27.cloned.1.call-start = ((), (), s32[]{:S(2)}) async-start(), calls=%async_computation.8 | async-start | bytes 6291456 | tf_op jit(solution)/shard_map/all_gather | solution.py:973
  176.2 309.6 %all-gather.25.cloned.1.call-start = ((), (), s32[]{:S(2)}) async-start(), calls=%async_computation.7 | async-start | bytes 18874368 | tf_op jit(solution)/shard_map/all_gather | solution.py:973
  176.9 20.1 %copy-start.27 = (bf16[128,2048]{1,0:T(8,128)(2,1)S(1)}, bf16[128,2048]{1,0:T(8,128)(2,1)}, u32[]{:S(2)}) copy-start(bf16[128,2048]{1,0:T(8,128)(2,1)} %refs_0_.1) | copy-start | bytes 1572868
  178.0 19.0 %all-to-all-start = ((bf16[16,128,128]{1,2,0:T(8,128)(2,1)}), bf16[16,128,128]{1,2,0:T(8,128)(2,1)S(1)}, u32[]{:S(2)}, u32[]{:S(2)}) async-start(bf16[16,128,128]{1,2,0:T(8,128)(2,1)} %copy.96), calls=%async_computation | async-start | bytes 1048576 | tf_op jit(solution)/shard_map/all_to_all | solution.py:1104
  182.2 89.8 %copy-start.32 = (bf16[2048,16]{1,0:T(8,128)(2,1)}, bf16[2048,16]{1,0:T(8,128)(2,1)S(1)}, u32[]{:S(2)}) copy-start(bf16[2048,16]{1,0:T(8,128)(2,1)S(1)} %reshape.288) | copy-start | bytes 196612
  316.6 2.9 collective-permute-start.1
  319.0 2.7 collective-permute-start
  323.9 149.7 %copy-start = (bf16[256,2048]{1,0:T(8,128)(2,1)S(1)}, bf16[256,2048]{1,0:T(8,128)(2,1)}, u32[]{:S(2)}) copy-start(bf16[256,2048]{1,0:T(8,128)(2,1)} %pad.16.out_ref) | copy-start | bytes 3145732
  323.9 149.7 %copy-start.4 = (bf16[2048,256]{1,0:T(8,128)(2,1)S(1)}, bf16[2048,256]{1,0:T(8,128)(2,1)}, u32[]{:S(2)}) copy-start(bf16[2048,256]{1,0:T(8,128)(2,1)} %get-tuple-element.83.hidden_ref) | copy-start | bytes 3145732
  323.9 149.8 %copy-start.10 = (s32[4,4,128]{2,1,0:T(4,128)S(1)}, s32[4,4,128]{2,1,0:T(4,128)}, u32[]{:S(2)}) copy-start(s32[4,4,128]{2,1,0:T(4,128)} %add_select_fusion.1.place_ref) | copy-start | bytes 24580
  501.7 136.1 %copy-start.22 = (f32[2048,16]{1,0:T(8,128)S(1)}, f32[2048,16]{1,0:T(8,128)}, u32[]{:S(2)}) copy-start(f32[2048,16]{1,0:T(8,128)} %copy-done.21) | copy-start | bytes 393220
  647.0 8.5 collective-permute-start.2
  650.9 59.4 %all-to-all-start.1 = ((bf16[128,16,128]{2,0,1:T(8,128)(2,1)}), bf16[128,16,128]{2,0,1:T(8,128)(2,1)S(1)}, u32[]{:S(2)}, u32[]{:S(2)}) async-start(bf16[128,16,128]{2,0,1:T(8,128)(2,1)} %bitcast.105), calls=%async_computation.1 | async-start | bytes 1048576 | tf_op jit(solution)/shard_map/all_to_all | solution.py:1166
  655.5 195.8 %all-gather.29.cloned.1.call-start = ((), (), s32[]{:S(2)}) async-start(), calls=%async_computation.9 | async-start | bytes 4456448 | tf_op jit(solution)/shard_map/all_gather | solution.py:965
  663.3 47.5 %copy-start.6 = (s32[2048,1]{1,0:T(8,128)S(1)}, s32[2048,1]{1,0:T(8,128)}, u32[]{:S(2)}) copy-start(s32[2048,1]{1,0:T(8,128)} %copy-done.5) | copy-start | bytes 24580
  663.3 47.5 %copy-start.13 = (bf16[2048,192]{1,0:T(8,128)(2,1)S(1)}, bf16[2048,192]{1,0:T(8,128)(2,1)}, u32[]{:S(2)}) copy-start(bf16[2048,192]{1,0:T(8,128)(2,1)} %copy-done.12) | copy-start | bytes 2359300
  663.3 47.5 %copy-start.19 = (bf16[2048,128]{1,0:T(8,128)(2,1)S(1)}, bf16[2048,128]{1,0:T(8,128)(2,1)}, u32[]{:S(2)}) copy-start(bf16[2048,128]{1,0:T(8,128)(2,1)} %copy-done.18) | copy-start | bytes 1572868
  710.3 191.3 %all-gather.31.cloned.1.call-start = ((), (), s32[]{:S(2)}) async-start(), calls=%async_computation.10 | async-start | bytes 6684672 | tf_op jit(solution)/shard_map/all_gather | solution.py:965
  727.9 8.2 copy-start.28
  733.3 1.8 collective-permute-start.3
  738.3 1.2 collective-permute-start.14
  747.2 22.5 %slice-start.2 = ((s8[6291456]{0:T(1024)(128)(4,1)}), s8[4194304]{0:T(1024)(128)(4,1)S(1)}, s32[]{:S(2)}) async-start(s8[6291456]{0:T(1024)(128)(4,1)} %bitcast.128), calls=%async_computation.17 | async-start | bytes 8388608
  752.0 151.5 %collective-permute-start.11 = (bf16[1024,16]{0,1:T(8,128)(2,1)S(1)}, bf16[1024,16]{0,1:T(8,128)(2,1)S(1)}, u32[]{:S(2)}, u32[]{:S(2)}) collective-permute-start(bf16[1024,16]{0,1:T(8,128)(2,1)S(1)} %constant_dynamic-slice_fusion.2), channel_id=1, source_target_pairs={{0,1},{1,0},{2,3},{3,2},{4,5},{5,4},{6,7},{7,6},{8,9},{9,8},{10,11... | collective-permute-start | bytes 98312 | tf_op jit(solution)/shard_map/ppermute | solution.py:988
  752.3 17.4 %slice-start.3 = ((s8[6291456]{0:T(1024)(128)(4,1)}), s8[2097152]{0:T(1024)(128)(4,1)S(1)}, s32[]{:S(2)}) async-start(s8[6291456]{0:T(1024)(128)(4,1)} %bitcast.128), calls=%async_computation.18 | async-start | bytes 4194304
  774.0 32.8 %collective-permute-start.4 = (bf16[256,256]{1,0:T(8,128)(2,1)S(1)}, bf16[256,256]{1,0:T(8,128)(2,1)S(1)}, u32[]{:S(2)}, u32[]{:S(2)}) collective-permute-start(bf16[256,256]{1,0:T(8,128)(2,1)S(1)} %constant_dynamic-slice_fusion.4), channel_id=1, source_target_pairs={{0,1},{1,0},{2,3},{3,2},{4,5},{5,4},{6,7},{7,6},{8,9},{9,8},{10,11... | collective-permute-start | bytes 393224 | tf_op jit(solution)/shard_map/ppermute | solution.py:988
  776.8 57.1 %all-to-all-start.2 = ((bf16[16,128,512]{1,2,0:T(8,128)(2,1)}), bf16[16,128,512]{1,2,0:T(8,128)(2,1)S(1)}, u32[]{:S(2)}, u32[]{:S(2)}) async-start(bf16[16,128,512]{1,2,0:T(8,128)(2,1)} %copy.100), calls=%async_computation.2 | async-start | bytes 4194304 | tf_op jit(solution)/shard_map/all_to_all | solution.py:1179
  782.4 181.1 %all-gather.35.cloned.1.call-start = ((), (), s32[]{:S(2)}) async-start(), calls=%async_computation.12 | async-start | bytes 2228224 | tf_op jit(solution)/shard_map/all_gather | solution.py:965
  807.6 221.7 %all-gather.33.cloned.1.call-start = ((), (), s32[]{:S(2)}) async-start(), calls=%async_computation.11 | async-start | bytes 2785280 | tf_op jit(solution)/shard_map/all_gather | solution.py:965
  837.6 133.2 %collective-permute-start.13 = (bf16[704,2048]{1,0:T(8,128)(2,1)}, bf16[704,2048]{1,0:T(8,128)(2,1)}, u32[]{:S(2)}, u32[]{:S(2)}) collective-permute-start(bf16[704,2048]{1,0:T(8,128)(2,1)} %constant_dynamic-slice_fusion), channel_id=1, source_target_pairs={{0,1},{1,0},{2,3},{3,2},{4,5},{5,4},{6,7},{7,6},{8,9},{9,8},{10,11... | collective-permute-start | bytes 8650760 | tf_op jit(solution)/shard_map/ppermute | solution.py:988
  843.1 194.7 %collective-permute-start.12 = (bf16[1024,2816]{1,0:T(8,128)(2,1)}, bf16[1024,2816]{1,0:T(8,128)(2,1)}, u32[]{:S(2)}, u32[]{:S(2)}) collective-permute-start(bf16[1024,2816]{1,0:T(8,128)(2,1)} %constant_dynamic-slice_fusion.1), channel_id=1, source_target_pairs={{0,1},{1,0},{2,3},{3,2},{4,5},{5,4},{6,7},{7,6},{8,9},{9,8},{10,11... | collective-permute-start | bytes 17301512 | tf_op jit(solution)/shard_map/ppermute | solution.py:988
  860.1 10.0 copy-start.40
  860.1 10.0 copy-start.35
  902.0 67.2 %collective-permute-start.5 = (f32[36,128]{1,0:T(8,128)S(1)}, f32[36,128]{1,0:T(8,128)S(1)}, u32[]{:S(2)}, u32[]{:S(2)}) collective-permute-start(f32[36,128]{1,0:T(8,128)S(1)} %maximum_bitcast_fusion), channel_id=1, source_target_pairs={{0,2},{2,0},{4,6},{6,4},{8,10},{10,8},{12,14},{14,12},{16,18},{18,... | collective-permute-start | bytes 55304 | tf_op jit(solution)/shard_map/ppermute | solution.py:996
  969.2 12.5 %collective-permute-start.6 = (f32[36,128]{1,0:T(8,128)S(1)}, f32[36,128]{1,0:T(8,128)S(1)}, u32[]{:S(2)}, u32[]{:S(2)}) collective-permute-start(f32[36,128]{1,0:T(8,128)S(1)} %fusion.43), channel_id=1, source_target_pairs={{0,4},{2,6},{4,0},{6,2},{8,12},{10,14},{12,8},{14,10},{16,20},{18,... | collective-permute-start | bytes 55304 | tf_op jit(solution)/shard_map/ppermute | solution.py:996
  981.7 66.2 %collective-permute-start.7 = (f32[36,128]{1,0:T(8,128)S(1)}, f32[36,128]{1,0:T(8,128)S(1)}, u32[]{:S(2)}, u32[]{:S(2)}) collective-permute-start(f32[36,128]{1,0:T(8,128)S(1)} %fusion.73), channel_id=1, source_target_pairs={{0,8},{2,10},{4,12},{6,14},{8,0},{10,2},{12,4},{14,6},{16,24},{18,... | collective-permute-start | bytes 55304 | tf_op jit(solution)/shard_map/ppermute | solution.py:996
  1037.8 14.9 %copy-start.26 = (f32[128,2048]{1,0:T(8,128)S(1)}, f32[128,2048]{1,0:T(8,128)}, u32[]{:S(2)}) copy-start(f32[128,2048]{1,0:T(8,128)} %copy-done.25) | copy-start | bytes 3145732
  1037.8 26.9 %collective-permute-start.10 = (bf16[1024,576]{0,1:T(8,128)(2,1)S(1)}, bf16[1024,576]{0,1:T(8,128)(2,1)S(1)}, u32[]{:S(2)}, u32[]{:S(2)}) collective-permute-start(bf16[1024,576]{0,1:T(8,128)(2,1)S(1)} %constant_dynamic-slice_fusion.3), channel_id=1, source_target_pairs={{0,1},{1,0},{2,3},{3,2},{4,5},{5,4},{6,7},{7,6},{8,9},{9,8},{10,11... | collective-permute-start | bytes 3538952 | tf_op jit(solution)/shard_map/ppermute | solution.py:988
  1047.9 4.7 collective-permute-start.8
  1052.7 10.7 collective-permute-start.9
  (38 other events, 126.8 us)
Sparse Core Ops, SparseCore 0:
  13.1 14.7 all-gather.16
  31.3 137.7 all-gather.18
  170.6 18.5 all-gather.20
  191.1 11.7 all-gather.22
  204.3 17.1 all-gather.38
  222.9 25.0 all-gather.36
  249.5 14.8 all-gather.26
  266.0 26.0 all-gather.24
  710.5 75.8 all-gather.28
  788.9 112.6 all-gather.30
  904.4 59.0 all-gather.34
  966.6 62.6 all-gather.32

commit v7 on v6

--- a/solution.py
+++ b/solution.py
@@ -308,66 +308,6 @@
         cost_estimate=pl.CostEstimate(flops=flops, bytes_accessed=40 * 2**20, transcendentals=2 * count * units),
         name="spread",
     )(ffn, upstream, in_steps(place), in_steps(gates), shared_in, shared_out)
-
-
-def collect_forward_kernel(res_ref, up_ref, place_ref, gate_ref, hidden_ref, out_ref, mixed_ref, dots_ref):
-    blocks, tok = place_ref.shape
-    capacity = res_ref.shape[0] // blocks
-    for b in range(blocks):
-        pick = as_weights(pick_of(place_ref, b, capacity))
-        tokens, rows = pl.ds(b * tok, tok), pl.ds(b * capacity, capacity)
-        mine = dot_tn(pick, res_ref[rows, :])
-        dots_ref[tokens, :] = jnp.sum(up_ref[tokens, :].astype(F32) * mine, axis=1, keepdims=True)
-        shared = dot(hidden_ref[tokens, :], out_ref[...])
-        mixed_ref[tokens, :] = (gate_ref[tokens, :] * mine + shared).astype(BF16)
-
-
-def collect_forward(results, upstream, place, gates, hidden, shared_out, capacity):
-    count = upstream.shape[0]
-    seq, tok = place.shape
-    steps = seq // BLOCKS
-    t, rows = BLOCKS * tok, BLOCKS * capacity
-    units = shared_out.shape[0]
-    flops = 2 * seq * capacity * tok * D + 2 * count * D * units
-    return pl.pallas_call(
-        collect_forward_kernel,
-        grid=(steps,),
-        in_specs=[by_rows(rows, D), by_rows(t, D), by_step(tok), by_rows(t, 1), by_rows(t, units), whole(shared_out)],
-        out_specs=(by_rows(t, D), by_rows(t, 1)),
-        out_shape=(jax.ShapeDtypeStruct((count, D), BF16), jax.ShapeDtypeStruct((count, 1), F32)),
-        compiler_params=pltpu.CompilerParams(vmem_limit_bytes=48 * 2**20),
-        cost_estimate=pl.CostEstimate(flops=flops, bytes_accessed=24 * 2**20, transcendentals=0),
-        name="collect_forward",
-    )(results, upstream, in_steps(place), gates.reshape(-1, 1), hidden, shared_out)
-
-
-def collect_backward_kernel(rows_ref, place_ref, grad_ref, in_ref, back_ref):
-    blocks, tok = place_ref.shape
-    capacity = rows_ref.shape[0] // blocks
-    shared = dot_nt(grad_ref[...], in_ref[...])
-    for b in range(blocks):
-        pick = as_weights(pick_of(place_ref, b, capacity))
-        tokens, rows = pl.ds(b * tok, tok), pl.ds(b * capacity, capacity)
-        mine = dot_tn(pick, rows_ref[rows, :])
-        back_ref[tokens, :] = (mine + shared[b * tok : (b + 1) * tok]).astype(BF16)
-
-
-def collect_backward(row_grads, place, grads, shared_in, capacity):
-    count = grads.shape[0]
-    seq, tok = place.shape
-    steps = seq // BLOCKS
-    t, rows = BLOCKS * tok, BLOCKS * capacity
-    flops = 2 * seq * capacity * tok * D + 2 * count * D * grads.shape[1]
-    return pl.pallas_call(
-        collect_backward_kernel,
-        grid=(steps,),
-        in_specs=[by_rows(rows, D), by_step(tok), by_rows(t, grads.shape[1]), whole(shared_in)],
-        out_specs=by_rows(t, D),
-        out_shape=jax.ShapeDtypeStruct((count, D), BF16),
-        compiler_params=pltpu.CompilerParams(vmem_limit_bytes=48 * 2**20),
-        cost_estimate=pl.CostEstimate(flops=flops, bytes_accessed=18 * 2**20, transcendentals=0),
-        name="collect_backward",
-    )(row_grads, in_steps(place), grads, shared_in)
 
 
 def turn_kernel(in_ref, out_ref):
@@ -807,21 +747,31 @@
 
 
 COLS = 256
-PACE = 2
+PACE = 4
+
+
+def expert_phases():
+    ends, last = [], 0
+    for steps in (2 * FF // COLS, -(-FF // COLS), D // COLS, D // COLS):
+        last += steps
+        ends.append(last)
+    return ends
 
 
 def expert_kernel(
-    streams, n_main, x_ref, rg_ref, in_col_ref, out_row_ref, out_col_ref, in_row_ref, *refs
+    streams, n_main,
+    x_ref, rg_ref, in_col_ref, out_row_ref, out_col_ref, in_row_ref,
+    place_ref, gate_ref, shid_ref, sgrad_ref, sout_ref, sin_ref, up_ref, *refs
 ):
     ins, refs = refs[:n_main], refs[n_main:]
-    res_ref, back_ref, hidden_out, gate_out, up_out, refs = *refs[:5], refs[5:]
+    mixed_ref, back_ref, dots_ref, hidden_out, gate_out, up_out, refs = *refs[:6], refs[6:]
     outs, refs = refs[:n_main], refs[n_main:]
-    gu, hidden, dgu, send_sems, recv_sems, local_sems, out_sems = refs
+    gu, hidden, dgu, picks, send_sems, recv_sems, local_sems, out_sems = refs
     rank = lax.axis_index("seq")
     i = pl.program_id(0)
-    spans = -(-FF // COLS)
-    ends = [2 * FF // COLS, 2 * FF // COLS + spans]
-    ends += [ends[1] + D // COLS, ends[1] + 2 * D // COLS]
+    blocks, tok = place_ref.shape
+    capacity = x_ref.shape[0] // blocks
+    ends = expert_phases()
     actions, finish = gather_events(streams, ins, outs, send_sems, recv_sems)
     own = [pltpu.make_async_copy(ins[k], outs[k].at[rank], local_sems.at[k]) for k in range(n_main)]
     kept = [
@@ -837,6 +787,8 @@
             action()
         for copy in own:
             copy.start()
+        for b in range(blocks):
+            picks[pl.ds(b * capacity, capacity), :] = as_weights(pick_of(place_ref, b, capacity))
 
     @pl.when(i < ends[0])
     def _():
@@ -868,14 +820,27 @@
     def _():
         for copy in kept:
             copy.start()
+        dots_ref[...] = jnp.zeros_like(dots_ref)
 
     @pl.when((i >= ends[1]) & (i < ends[2]))
     def _():
-        res_ref[...] = dot(hidden[...], out_col_ref[...]).astype(BF16)
+        result = dot(hidden[...], out_col_ref[...]).astype(BF16)
+        shared = dot(shid_ref[...], sout_ref[...])
+        for b in range(blocks):
+            tokens, slots = pl.ds(b * tok, tok), pl.ds(b * capacity, capacity)
+            mine = dot_tn(picks[slots, :], result[b * capacity : (b + 1) * capacity])
+            dots_ref[tokens, :] += jnp.sum(up_ref[tokens, :].astype(F32) * mine, axis=1, keepdims=True)
+            both = gate_ref[tokens, :] * mine + shared[b * tok : (b + 1) * tok]
+            mixed_ref[tokens, :] = both.astype(BF16)
 
     @pl.when(i >= ends[2])
     def _():
-        back_ref[...] = dot_nt(dgu[...], in_row_ref[...]).astype(BF16)
+        row_grad = dot_nt(dgu[...], in_row_ref[...]).astype(BF16)
+        shared = dot_nt(sgrad_ref[...], sin_ref[...])
+        for b in range(blocks):
+            tokens, slots = pl.ds(b * tok, tok), pl.ds(b * capacity, capacity)
+            mine = dot_tn(picks[slots, :], row_grad[b * capacity : (b + 1) * capacity])
+            back_ref[tokens, :] = (mine + shared[b * tok : (b + 1) * tok]).astype(BF16)
 
     done = len(streams)
     for step in range(ends[3] - 1):
@@ -897,14 +862,14 @@
             copy.wait()
 
 
-def expert_block(x, rg, w_in, w_out, main, parts, collective_id, count=16):
-    rows = x.shape[0]
+def expert_block(
+    x, rg, w_in, w_out, place, gates, shared_hidden, shared_grad, shared_out, shared_in, upstream,
+    main, parts, collective_id, count=16,
+):
+    rows, tokens = x.shape[0], upstream.shape[0]
+    units = shared_out.shape[0]
     streams = streams_of(main, parts)
-    spans = -(-FF // COLS)
-    first = 2 * FF // COLS
-    second = first + spans
-    third = second + D // COLS
-    steps = third + D // COLS
+    ends = expert_phases()
 
     def held(array):
         return pl.BlockSpec(array.shape, lambda i: (0, 0), pipeline_mode=pl.Buffered(1))
@@ -912,12 +877,13 @@
     def during(start, stop):
         return lambda i: jnp.minimum(jnp.maximum(i - start, 0), stop - start - 1)
 
-    one, two, three, four = during(0, first), during(first, second), during(second, third), during(third, steps)
+    one, two, three, four = [during(a, b) for a, b in zip([0] + ends[:-1], ends)]
     any_spec = pl.BlockSpec(memory_space=pl.ANY)
     n = len(main)
+    gate_column = gates.reshape(-1, 1)
     results = pl.pallas_call(
         functools.partial(expert_kernel, streams, n),
-        grid=(steps,),
+        grid=(ends[-1],),
         in_specs=[
             held(x),
             held(rg),
@@ -925,19 +891,28 @@
             pl.BlockSpec((COLS, D), lambda i: (two(i), 0)),
             pl.BlockSpec((FF, COLS), lambda i: (0, three(i))),
             pl.BlockSpec((COLS, 2 * FF), lambda i: (four(i), 0)),
+            held(place),
+            held(gate_column),
+            held(shared_hidden),
+            held(shared_grad),
+            pl.BlockSpec((units, COLS), lambda i: (0, three(i))),
+            pl.BlockSpec((COLS, 2 * units), lambda i: (four(i), 0)),
+            pl.BlockSpec((tokens, COLS), lambda i: (0, three(i))),
         ]
         + [any_spec] * n,
         out_specs=(
-            pl.BlockSpec((rows, COLS), lambda i: (0, three(i))),
-            pl.BlockSpec((rows, COLS), lambda i: (0, four(i))),
+            pl.BlockSpec((tokens, COLS), lambda i: (0, three(i))),
+            pl.BlockSpec((tokens, COLS), lambda i: (0, four(i))),
+            pl.BlockSpec((tokens, 1), lambda i: (0, 0)),
             any_spec,
             any_spec,
             any_spec,
         )
         + (any_spec,) * n,
         out_shape=(
-            jax.ShapeDtypeStruct((rows, D), BF16),
-            jax.ShapeDtypeStruct((rows, D), BF16),
+            jax.ShapeDtypeStruct((tokens, D), BF16),
+            jax.ShapeDtypeStruct((tokens, D), BF16),
+            jax.ShapeDtypeStruct((tokens, 1), F32),
             jax.ShapeDtypeStruct((rows, FF), BF16),
             jax.ShapeDtypeStruct((rows, FF), BF16),
             jax.ShapeDtypeStruct((rows, FF), BF16),
@@ -947,18 +922,24 @@
             pltpu.VMEM((rows, 2 * FF), BF16),
             pltpu.VMEM((rows, FF), BF16),
             pltpu.VMEM((rows, 2 * FF), BF16),
+            pltpu.VMEM((rows, place.shape[1]), BF16),
             pltpu.SemaphoreType.DMA((n_sends(streams),)),
             pltpu.SemaphoreType.DMA((len(streams) * count,)),
             pltpu.SemaphoreType.DMA((n,)),
             pltpu.SemaphoreType.DMA((3,)),
         ],
         compiler_params=pltpu.CompilerParams(
-            collective_id=collective_id, has_side_effects=True, vmem_limit_bytes=60 * 2**20
+            collective_id=collective_id, has_side_effects=True, vmem_limit_bytes=62 * 2**20
         ),
-        cost_estimate=pl.CostEstimate(flops=12 * rows * D * FF, bytes_accessed=100 * 2**20, transcendentals=2 * rows * FF),
+        cost_estimate=pl.CostEstimate(
+            flops=12 * rows * D * FF, bytes_accessed=100 * 2**20, transcendentals=2 * rows * FF
+        ),
         name="expert_block",
-    )(x, rg, w_in, w_out, w_out, w_in, *main)
-    return results[:5], results[5:]
+    )(
+        x, rg, w_in, w_out, w_out, w_in,
+        place, gate_column, shared_hidden, shared_grad, shared_out, shared_in, upstream, *main,
+    )
+    return results[:6], results[6:]
 
 
 def gather_seq(rows):
@@ -986,19 +967,6 @@
 def shift_fsdp(rows, k):
     count = lax.axis_size("fsdp")
     return lax.ppermute(rows, "fsdp", [(i, (i + k) % count) for i in range(count)])
-
-
-def sum_everywhere(rows):
-    count = lax.axis_size("seq")
-    total = rows
-    bit = 1
-    while bit < count:
-        total = total + lax.ppermute(total, "seq", [(i, i ^ bit) for i in range(count)])
-        bit *= 2
-    kept = total
-    for k in range(1, lax.axis_size("fsdp")):
-        total = total + shift_fsdp(kept, k)
-    return total
 
 
 ROW_PARTS = [(48, "zxy"), (48, "zyx"), (16, "xyz"), (16, "yxz")]
@@ -1126,19 +1094,22 @@
     part_shared_in = scatter_fsdp(part_shared_in, 1).astype(BF16)
     part_shared_out = jnp.pad(part_shared_out, ((0, -unit % 16), (0, 0)))
 
-    (result, row_grad, hidden, d_gate, d_up), (all_shared_in, all_shared_out) = expert_block(
+    (mixed_part, ffn_part, gate_grad, hidden, d_gate, d_up), (all_shared_in, all_shared_out) = expert_block(
         arrived,
         result_grad,
         expert_in,
         expert_out,
+        place,
+        gates,
+        shared_hidden,
+        shared_grad,
+        shared_out,
+        shared_in,
+        upstream_all,
         [part_shared_in, part_shared_out],
         [split_rows(part_shared_in.shape[0], 6), split_rows(part_shared_out.shape[0], 6)],
         4,
     )
-    mixed_part, gate_grad = collect_forward(
-        result, upstream_all, place, gates, shared_hidden, shared_out, capacity
-    )
-    ffn_part = collect_backward(row_grad, place, shared_grad, shared_in, capacity)
     mixed_part, query_weight, expand_weight = lax.optimization_barrier(
         (mixed_part, query_weight, expand_weight)
     )
@@ -1187,8 +1158,6 @@
     grad_expand = dot_tn(head_back[:, DN:rope_at], latent_all).astype(BF16)
     part_query = scatter_fsdp(grad_query, 1).astype(BF16)
     part_expand = scatter_fsdp(grad_expand, 1).astype(BF16)
-    all_query = gather_seq(part_query)
-    all_expand = gather_seq(part_expand)
     back, grad_expert_out, grad_expert_in, part_query, part_expand = lax.optimization_barrier(
         (back, grad_expert_out, grad_expert_in, part_query, part_expand)
     )
@@ -1205,23 +1174,30 @@
     compressed_grad, grad_gain_latent = latent_pull(latent_grad)
     full_grad = jnp.concatenate([compressed_grad, rope_grad], axis=1).astype(BF16)
     full_grad, all_output = lax.optimization_barrier((full_grad, all_output))
-    full_all = gather_seq(full_grad)
-    sum_latent = scatter_fsdp(dot_tn(normed_all, full_all).astype(BF16))
     spread_grad = jnp.pad(full_grad[:, :KVR], ((0, 0), (0, query_width + DR)))
     spread_grad = spread_grad + jnp.pad(full_grad[:, KVR:], ((0, 0), (KVR + query_width, 0)))
     normed_grad = dot_nt(pre_grad, query_weight) + dot_nt(spread_grad, head_weights)
-    normed_grad, all_query = lax.optimization_barrier((normed_grad, all_query))
     input_pull = jax.vjp(rms_norm, inputs, gain_attn)[1]
     input_norm_grad, grad_gain_attn = input_pull(normed_grad)
     grad_inputs = middle_grad + input_norm_grad
 
-    gain_sum = sum_everywhere(
-        jnp.concatenate([grad_gain_attn, grad_gain_latent, grad_gain_ffn]).reshape(-1, 128)
-    ).reshape(-1)
+    gain_grads = jnp.concatenate([grad_gain_attn, grad_gain_latent, grad_gain_ffn]).reshape(-1, 128)
+    gain_grads = jnp.pad(gain_grads, ((0, -gain_grads.shape[0] % 8), (0, 0)))
+    last_parts = [part_query, part_expand, full_grad]
+    all_query, all_expand, full_all, gain_all = gather_all(
+        last_parts, [split_rows(part.shape[0]) for part in last_parts], [gain_grads], 6
+    )
+    full_all = full_all.reshape(group_size, -1)
+    sum_latent = scatter_fsdp(dot_tn(normed_all, full_all).astype(BF16))
+    gain_seq = jnp.sum(gain_all, axis=0)
+    gain_sum = gain_seq
+    for k in range(1, fsdp_count):
+        gain_sum = gain_sum + shift_fsdp(gain_seq, k)
+    gain_sum = gain_sum.reshape(-1)
     sum_shared_out = all_shared_out[:, :unit].reshape(w_shared_out.shape).astype(F32)
     sum_shared_in = turn_units(all_shared_in.reshape(seq_count, 2 * fsdp_count, unit, row_part))
-    sum_query = turn_rows(all_query, 384)
-    sum_expand = turn_rows(all_expand, 512)
+    sum_query = turn_rows(all_query.reshape(-1, row_part), 384)
+    sum_expand = turn_rows(all_expand.reshape(-1, w_kvb.shape[0]), 512)
     sum_output = all_output.astype(F32)
     fsdp_rank = lax.axis_index("fsdp")
 

time: 1080 us -> 1040 us (0.963)
  waiting for transfers between devices: 164 us -> 40.3 us
  Pallas kernels: 631 us -> 711 us
    all_gather x5 -> x2, waiting for transfers between devices: 137 us -> 20 us  [gather_seq(): return lax.all_gather(rows, 'seq', axis=0, tiled=True)]
    pallas_call x2 -> x3, Pallas kernels: 180 us -> 272 us  [gather_all(): pl.pallas_call(functools.partial(gather_kernel, streams, len(main), len(s...]
    pallas_call x3 -> x1, Pallas kernels: 171 us -> 162 us  [expert_block(): pl.pallas_call(functools.partial(expert_kernel, streams, n), grid=(ends[-...]
  transfers between devices with their start and end apart: 30 -> 23, of which waited for: 10 -> 3; matrix products, arithmetic and copies ran while one was open for 19% -> 21% of each run, Pallas kernels for 45% -> 67%
where the time goes in v7:
time: 1040 us
  Pallas kernels  711 us (68%)
  matrix products  99.6 us (10%)
  other arithmetic  79.7 us (8%)
  local copies, waits for them, and re-layouts  67.1 us (6%)
  waiting for transfers between devices  40.3 us (4%)
  starting transfers between devices  16.8 us (2%)
  between operations  15.2 us (1%)
    pallas_call x3, Pallas kernels, gather_all(): pl.pallas_call(functools.partial(gather_kernel, streams, len(main), len(s...  272 us
    pallas_call x2, Pallas kernels, scatter_sum(): pl.pallas_call(functools.partial(scatter_kernel, streams, len(main), len(...  178 us
    pallas_call x1, Pallas kernels, expert_block(): pl.pallas_call(functools.partial(expert_kernel, streams, n), grid=(ends[-...  162 us
    dot_general x7, matrix products, dot_tn(): lax.dot_general(left, right, (((0,), (0,)), ((), ())), preferred_element_...  62 us
    pallas_call x1, Pallas kernels, spread(): pl.pallas_call(spread_kernel, grid=(steps,), in_specs=[by_rows(t, D), by_...  30 us
    dot_general x5, matrix products, dot_nt(): lax.dot_general(left, right, (((1,), (1,)), ((), ())), preferred_element_...  24.3 us
  transfers between devices with their start and end apart: 23, of which 3 were waited for; matrix products, arithmetic and copies ran while one was open for 21% of the time, Pallas kernels for 67%

profile of v7, /device:TPU:0, one launch (start us, length us, event | category | flops | bytes accessed | tf_op | source)
XLA Modules:
  0.0 1036.6 jit_solution(17060888662354927524)
XLA Ops:
  19.5 112.3 %gather_all.3 = (bf16[16,128,2048]{2,1,0:T(8,128)(2,1)}, bf16[16,16,128]{2,1,0:T(8,128)(2,1)}) custom-call(bf16[128,2048]{1,0:T(8,128)(2,1)} %refs_0_.1, bf16[16,128]{1,0:T(8,128)(2,1)} %convert_element_type.215.refs_1_), custom_call_target="tpu_custom_call" | custom-call | tf_op jit(solution)/shard_map/gather_all/pallas_call | solution.py:531
  135.3 5.0 fusion.4
  141.9 16.1 %project.1 = (bf16[2048,2048]{1,0:T(8,128)(2,1)}, bf16[2048,192]{1,0:T(8,128)(2,1)S(1)}, bf16[2048,192]{1,0:T(8,128)(2,1)S(1)}, bf16[2048,128]{1,0:T(8,128)(2,1)...) custom-call(bf16[2048,2048]{1,0:T(8,128)(2,1)} %bitcast.155, f32[1,2048]{1,0:T(1,128)S(1)} %bitcast.115, ...), custom_call_target="tpu_custom_call" | custom-call | flops 7549747200 | bytes 25165824 | tf_op jit(solution)/shard_map/project/pallas_call | solution.py:199
  158.0 7.9 attention_forward.1
  170.8 3.3 concatenate.33
  178.8 3.6 all-to-all-start
  185.1 3.0 all_gather.42
  189.2 8.6 all-to-all-done
  197.8 5.6 multiply_reduce_fusion.2
  205.3 68.2 %gather_all.4 = (bf16[16,128,2048]{2,1,0:T(8,128)(2,1)}, f32[16,8,128]{2,1,0:T(8,128)}) custom-call(bf16[128,2048]{1,0:T(8,128)(2,1)} %multiply_convert_fusion.1.refs_0_, f32[8,128]{1,0:T(8,128)} %copy-done.3), custom_call_target="tpu_custom_call" | custom-call | tf_op jit(solution)/shard_map/gather_all/pallas_call | solution.py:531
  273.5 7.8 fusion.51
  284.9 30.0 %spread.1 = (bf16[1536,2048]{1,0:T(8,128)(2,1)}, bf16[1536,2048]{1,0:T(8,128)(2,1)}, bf16[2048,256]{1,0:T(8,128)(2,1)}, bf16[2048,512]{1,0:T(8,128)(2,1)}, bf16[...) custom-call(bf16[2048,2048]{1,0:T(8,128)(2,1)} %bitcast.118, bf16[2048,2048]{1,0:T(8,128)(2,1)} %all-gather.16.cloned.1.call-done.up_ref, ...), custom_call_target="tpu_custom_call" | custom-call | flops 14495514624 | bytes 41943040 | tf_op jit(solution)/shard_map/spread/pallas_call | solution.py:299
  328.3 161.8 %expert_block.1 = (bf16[2048,2048]{1,0:T(8,128)(2,1)}, bf16[2048,2048]{1,0:T(8,128)(2,1)}, f32[2048,1]{1,0:T(8,128)}, bf16[1536,1408]{1,0:T(8,128)(2,1)}, bf16[1...) custom-call(bf16[1536,2048]{1,0:T(8,128)(2,1)} %get-tuple-element.10, ...), custom_call_target="tpu_custom_call" | custom-call | flops 53150220288 | bytes 104857600 | tf_op jit(solution)/shard_map/expert_block/pallas_call | solution.py:884
  492.4 131.4 %scatter_sum.2 = (f32[128,2048]{1,0:T(8,128)}, f32[128,2048]{1,0:T(8,128)}, f32[16,16,128]{2,1,0:T(8,128)}) custom-call(bf16[16,128,2048]{2,1,0:T(8,128)(2,1)} %bitcast.126, bf16[16,128,2048]{2,1,0:T(8,128)(2,1)} %bitcast.127, f32[16,128]{1,0:T(8,128)} %bitcast.143), custom_call_target="tpu_custom_call" | custom-call | tf_op jit(solution)/shard_map/scatter_sum/pallas_call | solution.py:726
  626.1 2.4 fusion.14
  632.6 2.3 convolution_convert_fusion.2
  634.9 3.4 copy-done.10
  638.3 2.3 constant_dynamic-slice_fusion.6
  641.0 7.2 multiply_convert_fusion
  648.1 6.3 fusion.3
  655.4 5.9 all-to-all-start.1
  661.3 4.8 convolution_convert_fusion.6
  666.4 3.1 slice.90
  669.5 6.4 bitcast_convert_fusion
  675.9 18.1 %turn_units.1 = f32[1024,5632]{1,0:T(8,128)} custom-call(bf16[16,4,88,1024]{3,2,1,0:T(8,128)(2,1)} %bitcast.123), custom_call_target="tpu_custom_call" | custom-call | bytes 34603008 | tf_op jit(solution)/shard_map/turn_units/pallas_call | solution.py:338
  694.7 6.5 add_convert_fusion
  701.2 46.4 %scatter_sum.3 = f32[64,2048]{1,0:T(8,128)} custom-call(bf16[16,64,2048]{2,1,0:T(8,128)(2,1)} %bitcast.122), custom_call_target="tpu_custom_call" | custom-call | tf_op jit(solution)/shard_map/scatter_sum/pallas_call | solution.py:726
  753.1 13.3 %attention_backward.1 = bf16[2048,512]{1,0:T(8,128)(2,1)} custom-call(bf16[2048,192]{1,0:T(8,128)(2,1)S(1)} %copy-done.5, bf16[2048,192]{1,0:T(8,128)(2,1)S(1)} %copy-done.7, bf16[2048,128]{1,0:T(8,128)(2,1)S(1)} %get-tuple-element.73.v_ref, bf16[2048,128]{1,0:T(8,128)(2,1)S(1)} %bitcast.114, s32[2048,1]{1,0:T(8,128)S(1)} %add_select_fusion.segc_ref, ...), custom_call_target="tpu_custom_call" | custom-call | flops 3489660928 | bytes 6291456 | tf_op jit(solution)/shard_map/attention_backward/pallas_call | solution.py:156
  768.5 5.4 convolution_convert_fusion.4
  774.5 3.9 copy.106
  778.4 4.4 all-to-all-start.2
  783.6 24.4 %convolution_convert_fusion = bf16[2048,2816]{1,0:T(8,128)(2,1)} fusion(bf16[1536,2048]{1,0:T(8,128)(2,1)} %get-tuple-element.102.x_ref, bf16[1536,1408]{1,0:T(8,128)(2,1)} %get-tuple-element.104, bf16[1536,1408]{1,0:T(8,128)(2,1)} %get-tuple-element.103), kind=kOutput, calls=%fused_computation.2 | convolution fusion | flops 17739808768 | bytes 26476544 | tf_op jit(solution)/shard_map/dot_general | solution.py:74
  808.0 14.4 %convolution_convert_fusion.1 = bf16[1408,2048]{1,0:T(8,128)(2,1)} fusion(bf16[1536,1408]{1,0:T(8,128)(2,1)} %get-tuple-element.100, bf16[1536,2048]{1,0:T(8,128)(2,1)} %get-tuple-element.101.rg_ref), kind=kOutput, calls=%fused_computation.7 | convolution fusion | flops 8861253632 | bytes 16384000 | tf_op jit(solution)/shard_map/dot_general | solution.py:74
  824.0 7.7 all-to-all-done.2
  835.0 3.8 constant_dynamic-slice_fusion
  838.9 5.6 constant_dynamic-slice_fusion.1
  846.5 3.8 multiply_reduce_fusion.3
  851.7 9.6 fusion.52
  861.2 20.0 %all-gather.26.cloned.1.call-done = bf16[1024,2048]{1,0:T(8,128)(2,1)} async-done(((bf16[64,2048]{1,0:T(8,128)(2,1)}), bf16[1024,2048]{1,0:T(8,128)(2,1)}) %all-gather.26.cloned.1.call-update) | async-done | bytes 4194320 | tf_op jit(solution)/shard_map/all_gather | solution.py:946
  881.3 4.1 fusion.10
  886.1 91.9 %gather_all.5 = (bf16[16,192,1024]{2,1,0:T(8,128)(2,1)}, bf16[16,256,256]{2,1,0:T(8,128)(2,1)}, bf16[16,128,576]{2,1,0:T(8,128)(2,1)}, f32[16,40,128]{2,1,0:T(8,128)}) custom-call(bf16[192,1024]{1,0:T(8,128)(2,1)} %add_convert_fusion.3.refs_0_, bf16[256,256]{1,0:T(8,128)(2,1)} %add_convert_fusion.5.refs_1_, bf16[128,576]{1,0:T(8,128)(2,1)} %copy-done.29, ...), custom_call_target="tpu_custom_call" | custom-call | tf_op jit(solution)/shard_map/gather_all/pallas_call | solution.py:531
  978.0 8.6 convolution_convert_fusion.3
  989.2 6.5 add_bitcast_fusion.1
  997.5 9.6 turn_rows.2
  1007.1 3.9 turn_rows.3
  1011.0 4.5 convert_element_type.261
  1016.8 3.0 convert_add_fusion
  1019.8 10.0 add_bitcast_fusion
  (275 shorter events, 83.5 us)
Async XLA Ops:
  7.2 133.1 %all-gather.14.cloned.1.call-start = ((), (), s32[]{:S(2)}) async-start(), calls=%async_computation.3 | async-start | bytes 4718592 | tf_op jit(solution)/shard_map/all_gather | solution.py:954
  12.1 156.7 %all-gather.16.cloned.1.call-start = ((), (), s32[]{:S(2)}) async-start(), calls=%async_computation.4 | async-start | bytes 8912896 | tf_op jit(solution)/shard_map/all_gather | solution.py:946
  13.5 175.7 %all-gather.18.cloned.1.call-start = ((), (), s32[]{:S(2)}) async-start(), calls=%async_computation.5 | async-start | bytes 12582912 | tf_op jit(solution)/shard_map/all_gather | solution.py:954
  14.2 270.7 %all-gather.20.cloned.1.call-start = ((), (), s32[]{:S(2)}) async-start(), calls=%async_computation.6 | async-start | bytes 3145728 | tf_op jit(solution)/shard_map/all_gather | solution.py:954
  14.3 120.6 %copy-start.39 = (f32[32]{0:T(128)}, f32[32]{0:T(128)S(1)}, u32[]{:S(2)}) copy-start(f32[32]{0:T(128)S(1)} %negate_power_fusion) | copy-start | bytes 388
  140.3 17.7 %copy-start.1 = (f32[2048,128]{1,0:T(8,128)}, f32[2048,128]{1,0:T(8,128)S(1)}, u32[]{:S(2)}) copy-start(f32[2048,128]{1,0:T(8,128)S(1)} %get-tuple-element.160.sin_ref) | copy-start | bytes 3145732
  168.8 5.9 copy-start.3
  174.1 154.2 %all-gather.30.cloned.1.call-start = ((), (), s32[]{:S(2)}) async-start(), calls=%async_computation.11 | async-start | bytes 8650752 | tf_op jit(solution)/shard_map/all_gather | solution.py:954
  174.7 153.7 %all-gather.28.cloned.1.call-start = ((), (), s32[]{:S(2)}) async-start(), calls=%async_computation.10 | async-start | bytes 17301504 | tf_op jit(solution)/shard_map/all_gather | solution.py:954
  175.3 314.9 %all-gather.24.cloned.1.call-start = ((), (), s32[]{:S(2)}) async-start(), calls=%async_computation.8 | async-start | bytes 6291456 | tf_op jit(solution)/shard_map/all_gather | solution.py:954
  176.0 314.2 %all-gather.22.cloned.1.call-start = ((), (), s32[]{:S(2)}) async-start(), calls=%async_computation.7 | async-start | bytes 18874368 | tf_op jit(solution)/shard_map/all_gather | solution.py:954
  177.2 96.3 %copy-start.19 = (bf16[2048,16]{1,0:T(8,128)(2,1)}, bf16[2048,16]{1,0:T(8,128)(2,1)S(1)}, u32[]{:S(2)}) copy-start(bf16[2048,16]{1,0:T(8,128)(2,1)S(1)} %reshape.297) | copy-start | bytes 196612
  177.8 25.6 %copy-start.45 = (f32[128]{0:T(128)}, f32[128]{0:T(128)S(1)}, u32[]{:S(2)}) copy-start(f32[128]{0:T(128)S(1)} %fusion.7) | copy-start | bytes 1540
  178.8 19.0 %all-to-all-start = ((bf16[16,128,128]{1,2,0:T(8,128)(2,1)}), bf16[16,128,128]{1,2,0:T(8,128)(2,1)S(1)}, u32[]{:S(2)}, u32[]{:S(2)}) async-start(bf16[16,128,128]{1,2,0:T(8,128)(2,1)} %copy.101), calls=%async_computation | async-start | bytes 1048576 | tf_op jit(solution)/shard_map/all_to_all | solution.py:1072
  281.6 33.3 %copy-start.11 = (f32[2048,16]{1,0:T(8,128)}, f32[2048,16]{1,0:T(8,128)S(1)}, u32[]{:S(2)}) copy-start(f32[2048,16]{1,0:T(8,128)S(1)} %copy.103) | copy-start | bytes 393220
  316.1 7.9 collective-permute-start.1
  319.3 6.7 collective-permute-start
  322.1 168.0 %copy-start.48 = (f32[128]{0:T(128)}, f32[128]{0:T(128)S(1)}, u32[]{:S(2)}) copy-start(f32[128]{0:T(128)S(1)} %multiply_reduce_fusion.5) | copy-start | bytes 1540
  323.6 317.0 %collective-permute-start.10 = (f32[16,128]{1,0:T(8,128)S(1)}, f32[16,128]{1,0:T(8,128)S(1)}, u32[]{:S(2)}, u32[]{:S(2)}) collective-permute-start(f32[16,128]{1,0:T(8,128)S(1)} %bitcast.144), channel_id=1, source_target_pairs={{0,1},{1,0},{2,3},{3,2},{4,5},{5,4},{6,7},{7,6},{8,9},{9,8},{10,11... | collective-permute-start | bytes 24584 | tf_op jit(solution)/shard_map/ppermute | solution.py:969
  492.4 133.7 %copy-start.12 = (f32[2048,16]{1,0:T(8,128)S(1)}, f32[2048,16]{1,0:T(8,128)}, u32[]{:S(2)}) copy-start(f32[2048,16]{1,0:T(8,128)} %copy-done.11) | copy-start | bytes 393220
  623.8 6.8 copy-start.20
  640.6 54.0 %collective-permute-start.2 = (bf16[1024,2048]{1,0:T(8,128)(2,1)}, bf16[1024,2048]{1,0:T(8,128)(2,1)}, u32[]{:S(2)}, u32[]{:S(2)}) collective-permute-start(bf16[1024,2048]{1,0:T(8,128)(2,1)} %constant_dynamic-slice_fusion.6), channel_id=1, source_target_pairs={{0,1},{1,0},{2,3},{3,2},{4,5},{5,4},{6,7},{7,6},{8,9},{9,8},{10,11... | collective-permute-start | bytes 12582920 | tf_op jit(solution)/shard_map/ppermute | solution.py:969
  655.4 94.0 %all-to-all-start.1 = ((bf16[128,16,128]{2,0,1:T(8,128)(2,1)}), bf16[128,16,128]{2,0,1:T(8,128)(2,1)S(1)}, u32[]{:S(2)}, u32[]{:S(2)}) async-start(bf16[128,16,128]{2,0,1:T(8,128)(2,1)} %bitcast.132), calls=%async_computation.1 | async-start | bytes 1048576 | tf_op jit(solution)/shard_map/all_to_all | solution.py:1137
  666.1 27.9 %collective-permute-start.7 = (bf16[1024,16]{0,1:T(8,128)(2,1)S(1)}, bf16[1024,16]{0,1:T(8,128)(2,1)S(1)}, u32[]{:S(2)}, u32[]{:S(2)}) collective-permute-start(bf16[1024,16]{0,1:T(8,128)(2,1)S(1)} %constant_dynamic-slice_fusion.2), channel_id=1, source_target_pairs={{0,1},{1,0},{2,3},{3,2},{4,5},{5,4},{6,7},{7,6},{8,9},{9,8},{10,11... | collective-permute-start | bytes 98312 | tf_op jit(solution)/shard_map/ppermute | solution.py:969
  669.5 25.1 %slice-start = ((s8[8388608]{0:T(1024)(128)(4,1)}), s8[4194304]{0:T(1024)(128)(4,1)S(1)}, s32[]{:S(2)}) async-start(s8[8388608]{0:T(1024)(128)(4,1)} %bitcast.120), calls=%async_computation.12 | async-start | bytes 8388608
  675.9 18.7 %slice-start.1 = ((s8[8388608]{0:T(1024)(128)(4,1)}), s8[4194304]{0:T(1024)(128)(4,1)S(1)}, s32[]{:S(2)}) async-start(s8[8388608]{0:T(1024)(128)(4,1)} %bitcast.120), calls=%async_computation.13 | async-start | bytes 8388608
  753.1 13.3 %copy-start.51 = (bf16[2048,512]{1,0:T(8,128)(2,1)S(1)}, bf16[2048,512]{1,0:T(8,128)(2,1)}, u32[]{:S(2)}) copy-start(bf16[2048,512]{1,0:T(8,128)(2,1)} %get-tuple-element.106) | copy-start | bytes 6291460
  768.4 54.0 %collective-permute-start.4 = (bf16[256,256]{1,0:T(8,128)(2,1)S(1)}, bf16[256,256]{1,0:T(8,128)(2,1)S(1)}, u32[]{:S(2)}, u32[]{:S(2)}) collective-permute-start(bf16[256,256]{1,0:T(8,128)(2,1)S(1)} %constant_dynamic-slice_fusion.4), channel_id=1, source_target_pairs={{0,1},{1,0},{2,3},{3,2},{4,5},{5,4},{6,7},{7,6},{8,9},{9,8},{10,11... | collective-permute-start | bytes 393224 | tf_op jit(solution)/shard_map/ppermute | solution.py:969
  773.9 49.2 %collective-permute-start.3 = (bf16[192,1024]{1,0:T(8,128)(2,1)S(1)}, bf16[192,1024]{1,0:T(8,128)(2,1)S(1)}, u32[]{:S(2)}, u32[]{:S(2)}) collective-permute-start(bf16[192,1024]{1,0:T(8,128)(2,1)S(1)} %constant_dynamic-slice_fusion.5), channel_id=1, source_target_pairs={{0,1},{1,0},{2,3},{3,2},{4,5},{5,4},{6,7},{7,6},{8,9},{9,8},{10,11... | collective-permute-start | bytes 1179656 | tf_op jit(solution)/shard_map/ppermute | solution.py:969
  778.4 53.3 %all-to-all-start.2 = ((bf16[16,128,512]{1,2,0:T(8,128)(2,1)}), bf16[16,128,512]{1,2,0:T(8,128)(2,1)}, u32[]{:S(2)}, u32[]{:S(2)}) async-start(bf16[16,128,512]{1,2,0:T(8,128)(2,1)} %copy.106), calls=%async_computation.2 | async-start | bytes 4194304 | tf_op jit(solution)/shard_map/all_to_all | solution.py:1150
  782.8 98.4 %all-gather.26.cloned.1.call-start = ((), (), s32[]{:S(2)}) async-start(), calls=%async_computation.9 | async-start | bytes 4456448 | tf_op jit(solution)/shard_map/all_gather | solution.py:946
  838.8 7.4 copy-start.40
  838.8 7.4 copy-start.47
  838.8 7.7 copy-start.36
  838.8 7.7 copy-start.43
  838.8 150.4 %collective-permute-start.9 = (bf16[704,2048]{1,0:T(8,128)(2,1)}, bf16[704,2048]{1,0:T(8,128)(2,1)}, u32[]{:S(2)}, u32[]{:S(2)}) collective-permute-start(bf16[704,2048]{1,0:T(8,128)(2,1)} %constant_dynamic-slice_fusion), channel_id=1, source_target_pairs={{0,1},{1,0},{2,3},{3,2},{4,5},{5,4},{6,7},{7,6},{8,9},{9,8},{10,11... | collective-permute-start | bytes 8650760 | tf_op jit(solution)/shard_map/ppermute | solution.py:969
  844.5 5.9 copy-start.49
  844.5 175.3 %collective-permute-start.8 = (bf16[1024,2816]{1,0:T(8,128)(2,1)}, bf16[1024,2816]{1,0:T(8,128)(2,1)}, u32[]{:S(2)}, u32[]{:S(2)}) collective-permute-start(bf16[1024,2816]{1,0:T(8,128)(2,1)} %constant_dynamic-slice_fusion.1), channel_id=1, source_target_pairs={{0,1},{1,0},{2,3},{3,2},{4,5},{5,4},{6,7},{7,6},{8,9},{9,8},{10,11... | collective-permute-start | bytes 17301512 | tf_op jit(solution)/shard_map/ppermute | solution.py:969
  851.5 29.7 %copy-start.29 = (bf16[128,576]{1,0:T(8,128)(2,1)}, bf16[128,576]{1,0:T(8,128)(2,1)S(1)}, u32[]{:S(2)}) copy-start(bf16[128,576]{1,0:T(8,128)(2,1)S(1)} %pad_maximum_fusion.2.refs_2_) | copy-start | bytes 442372
  851.6 29.7 %copy-start.16 = (bf16[128,2048]{1,0:T(8,128)(2,1)S(1)}, bf16[128,2048]{1,0:T(8,128)(2,1)}, u32[]{:S(2)}) copy-start(bf16[128,2048]{1,0:T(8,128)(2,1)} %refs_0_.1) | copy-start | bytes 1572868
  851.6 29.7 %copy-start.33 = (f32[1,8,2,128]{3,1,2,0:T(8,128)S(1)}, f32[1,8,2,128]{3,1,2,0:T(8,128)}, u32[]{:S(2)}) copy-start(f32[1,8,2,128]{3,1,2,0:T(8,128)} %copy.128) | copy-start | bytes 24580
  851.6 29.7 %copy-start.38 = (f32[128]{0:T(128)S(1)}, f32[128]{0:T(128)}, u32[]{:S(2)}) copy-start(f32[128]{0:T(128)} %fusion.40) | copy-start | bytes 1540
  989.2 6.6 copy-start.32
  989.2 7.0 copy-start.46
  989.2 7.1 copy-start.22
  989.2 27.6 %collective-permute-start.6 = (bf16[1024,576]{0,1:T(8,128)(2,1)}, bf16[1024,576]{0,1:T(8,128)(2,1)}, u32[]{:S(2)}, u32[]{:S(2)}) collective-permute-start(bf16[1024,576]{0,1:T(8,128)(2,1)} %constant_dynamic-slice_fusion.3), channel_id=1, source_target_pairs={{0,1},{1,0},{2,3},{3,2},{4,5},{5,4},{6,7},{7,6},{8,9},{9,8},{10,11... | collective-permute-start | bytes 3538952 | tf_op jit(solution)/shard_map/ppermute | solution.py:969
  995.8 19.7 %collective-permute-start.5 = (f32[40,128]{1,0:T(8,128)S(1)}, f32[40,128]{1,0:T(8,128)S(1)}, u32[]{:S(2)}, u32[]{:S(2)}) collective-permute-start(f32[40,128]{1,0:T(8,128)S(1)} %reduce_sum.183), channel_id=1, source_target_pairs={{0,1},{1,0},{2,3},{3,2},{4,5},{5,4},{6,7},{7,6},{8,9},{9,8},{10,11... | collective-permute-start | bytes 61448 | tf_op jit(solution)/shard_map/ppermute | solution.py:969
  997.5 9.6 copy-start
  (32 other events, 85.8 us)
Sparse Core Ops, SparseCore 0:
  12.2 14.7 all-gather.13
  30.3 137.7 all-gather.15
  169.6 18.2 all-gather.17
  190.0 11.9 all-gather.19
  203.3 17.1 all-gather.29
  221.9 25.0 all-gather.27
  248.5 14.8 all-gather.23
  265.0 26.0 all-gather.21
  786.4 94.7 all-gather.25

commit v8 on v7

--- a/solution.py
+++ b/solution.py
@@ -329,24 +329,6 @@
     )(rows)
 
 
-def turn_units(parts):
-    seq_count, groups, unit, columns = parts.shape
-    if unit % 8 or (seq_count * unit) % 128:
-        return parts.transpose(3, 1, 0, 2).reshape(columns, -1).astype(F32)
-    wide = seq_count * unit
-    tile = 256
-    return pl.pallas_call(
-        turn_kernel,
-        grid=(groups, columns // tile),
-        in_specs=[pl.BlockSpec((seq_count, None, unit, tile), lambda g, i: (0, g, 0, i))],
-        out_specs=pl.BlockSpec((tile, wide), lambda g, i: (i, g)),
-        out_shape=jax.ShapeDtypeStruct((columns, groups * wide), F32),
-        compiler_params=pltpu.CompilerParams(vmem_limit_bytes=48 * 2**20),
-        cost_estimate=pl.CostEstimate(flops=0, bytes_accessed=6 * parts.size, transcendentals=0),
-        name="turn_units",
-    )(parts)
-
-
 LINE = 4
 MESH = pl.DeviceIdType.MESH
 
@@ -462,6 +444,44 @@
     return [functools.partial(act, *it) for it in todo], finish
 
 
+def small_events(ins, outs, small_send, small_recv):
+    rank, count = lax.axis_index("seq"), lax.axis_size("seq")
+
+    def copy(i, k):
+        peer = lax.rem(rank + k, count)
+        return pltpu.make_async_remote_copy(
+            src_ref=ins[i],
+            dst_ref=outs[i].at[rank],
+            send_sem=small_send.at[i * count + k],
+            recv_sem=small_recv.at[i * count + rank],
+            device_id={"seq": peer},
+            device_id_type=MESH,
+        )
+
+    def send():
+        for i in range(len(ins)):
+            for k in range(1, count):
+                copy(i, k).start()
+
+    def finish():
+        for i in range(len(ins)):
+            for k in range(1, count):
+                copy(i, k).wait_send()
+            for k in range(1, count):
+                source = lax.rem(rank + k, count)
+                block = outs[i].at[source]
+                pltpu.make_async_remote_copy(
+                    src_ref=block,
+                    dst_ref=block,
+                    send_sem=small_send.at[0],
+                    recv_sem=small_recv.at[i * count + source],
+                    device_id={"seq": rank},
+                    device_id_type=MESH,
+                ).wait_recv()
+
+    return send, finish
+
+
 def gather_kernel(streams, n_main, n_small, *refs):
     n = n_main + n_small
     ins, outs = refs[:n], refs[n : 2 * n]
@@ -470,48 +490,32 @@
     count = lax.axis_size("seq")
     greet_all()
     locals_ = [pltpu.make_async_copy(ins[i], outs[i].at[rank], local_sems.at[i]) for i in range(n)]
-
-    def small_copy(i, k):
-        peer = lax.rem(rank + k, count)
-        return pltpu.make_async_remote_copy(
-            src_ref=ins[n_main + i],
-            dst_ref=outs[n_main + i].at[rank],
-            send_sem=small_send.at[i * count + k],
-            recv_sem=small_recv.at[i * count + rank],
-            device_id={"seq": peer},
-            device_id_type=MESH,
-        )
-
     actions, finish = gather_events(streams, ins, outs, send_sems, recv_sems)
+    send_small, finish_small = small_events(ins[n_main:], outs[n_main:], small_send, small_recv)
     for i, action in enumerate(actions):
         action()
         if i == len(streams) - 1:
             for c in locals_:
                 c.start()
-            for s in range(n_small):
-                for k in range(1, count):
-                    small_copy(s, k).start()
+            send_small()
     finish()
-    for i in range(n_small):
-        for k in range(1, count):
-            small_copy(i, k).wait_send()
-        for k in range(1, count):
-            source = lax.rem(rank + k, count)
-            block = outs[n_main + i].at[source]
-            pltpu.make_async_remote_copy(
-                src_ref=block,
-                dst_ref=block,
-                send_sem=small_send.at[0],
-                recv_sem=small_recv.at[i * count + source],
-                device_id={"seq": rank},
-                device_id_type=MESH,
-            ).wait_recv()
+    finish_small()
     for c in locals_:
         c.wait()
 
 
 def n_sends(streams):
     return sum(len(onward(s[3], o)) for s in streams for o in OFFSETS)
+
+
+def gather_scratch(streams, n_small, n, count):
+    return [
+        pltpu.SemaphoreType.DMA((n_sends(streams),)),
+        pltpu.SemaphoreType.DMA((len(streams) * count,)),
+        pltpu.SemaphoreType.DMA((max(1, n_small) * count,)),
+        pltpu.SemaphoreType.DMA((max(1, n_small) * count,)),
+        pltpu.SemaphoreType.DMA((n,)),
+    ]
 
 
 def streams_of(main, parts):
@@ -533,13 +537,7 @@
         out_shape=tuple(jax.ShapeDtypeStruct((count,) + a.shape, a.dtype) for a in arrays),
         in_specs=[any_spec] * len(arrays),
         out_specs=tuple([any_spec] * len(arrays)),
-        scratch_shapes=[
-            pltpu.SemaphoreType.DMA((n_sends(streams),)),
-            pltpu.SemaphoreType.DMA((len(streams) * count,)),
-            pltpu.SemaphoreType.DMA((max(1, len(small)) * count,)),
-            pltpu.SemaphoreType.DMA((max(1, len(small)) * count,)),
-            pltpu.SemaphoreType.DMA((len(arrays),)),
-        ],
+        scratch_shapes=gather_scratch(streams, len(small), len(arrays), count),
         compiler_params=pltpu.CompilerParams(collective_id=collective_id, has_side_effects=True),
         name="gather_all",
     )(*arrays)
@@ -747,7 +745,7 @@
 
 
 COLS = 256
-PACE = 4
+PACE = 3
 
 
 def expert_phases():
@@ -942,6 +940,72 @@
     return results[:6], results[6:]
 
 
+def turn_gather_kernel(streams, n_main, n_small, steps, *refs):
+    n = n_main + n_small
+    parts_ref, ins, refs = refs[0], refs[1 : n + 1], refs[n + 1 :]
+    turned_ref, outs, refs = refs[0], refs[1 : n + 1], refs[n + 1 :]
+    send_sems, recv_sems, small_send, small_recv, local_sems = refs
+    i = pl.program_id(0)
+    rank = lax.axis_index("seq")
+    actions, finish = gather_events(streams, ins, outs, send_sems, recv_sems)
+    own = [pltpu.make_async_copy(ins[k], outs[k].at[rank], local_sems.at[k]) for k in range(n)]
+    send_small, finish_small = small_events(ins[n_main:], outs[n_main:], small_send, small_recv)
+
+    @pl.when(i == 0)
+    def _():
+        greet_all()
+        for action in actions[: len(streams)]:
+            action()
+        for copy in own:
+            copy.start()
+        send_small()
+
+    block = parts_ref[...].astype(F32)
+    turned_ref[...] = block.reshape(-1, block.shape[-1]).T
+    rest = actions[len(streams) :]
+    for step in range(steps):
+
+        @pl.when(i == step)
+        def _(step=step):
+            for action in rest[step * len(rest) // steps : (step + 1) * len(rest) // steps]:
+                action()
+
+    @pl.when(i == steps - 1)
+    def _():
+        finish()
+        finish_small()
+        for copy in own:
+            copy.wait()
+
+
+def turn_and_gather(turned, main, parts, small, collective_id, count=16):
+    seq_count, groups, unit, columns = turned.shape
+    wide = seq_count * unit
+    if unit % 8 or wide % 128 or columns % 256:
+        rows = turned.transpose(3, 1, 0, 2).reshape(columns, -1).astype(F32)
+        return (rows, *gather_all(main, parts, small, collective_id, count))
+    tile = 256
+    across = columns // tile
+    streams = streams_of(main, parts)
+    arrays = list(main) + list(small)
+    any_spec = pl.BlockSpec(memory_space=pl.ANY)
+    return pl.pallas_call(
+        functools.partial(turn_gather_kernel, streams, len(main), len(small), groups * across),
+        grid=(groups * across,),
+        in_specs=[pl.BlockSpec((seq_count, None, unit, tile), lambda i: (0, i // across, 0, i % across))]
+        + [any_spec] * len(arrays),
+        out_specs=(pl.BlockSpec((tile, wide), lambda i: (i % across, i // across)),)
+        + (any_spec,) * len(arrays),
+        out_shape=(jax.ShapeDtypeStruct((columns, groups * wide), F32),)
+        + tuple(jax.ShapeDtypeStruct((count,) + a.shape, a.dtype) for a in arrays),
+        scratch_shapes=gather_scratch(streams, len(small), len(arrays), count),
+        compiler_params=pltpu.CompilerParams(
+            collective_id=collective_id, has_side_effects=True, vmem_limit_bytes=40 * 2**20
+        ),
+        name="turn_and_gather",
+    )(turned, *arrays)
+
+
 def gather_seq(rows):
     return lax.all_gather(rows, "seq", axis=0, tiled=True)
 
@@ -980,6 +1044,10 @@
     sizes = [tiles - 2 * short - long, long, short, short]
     orders = ["zxy", "zyx", "xyz", "yxz"]
     return [(n * tile, order) for n, order in zip(sizes, orders) if n]
+
+
+def in_halves(rows):
+    return split_rows(rows, rows)
 
 
 def on_device(
@@ -1107,7 +1175,7 @@
         shared_in,
         upstream_all,
         [part_shared_in, part_shared_out],
-        [split_rows(part_shared_in.shape[0], 6), split_rows(part_shared_out.shape[0], 6)],
+        [split_rows(part_shared_in.shape[0], 5), in_halves(part_shared_out.shape[0])],
         4,
     )
     mixed_part, query_weight, expand_weight = lax.optimization_barrier(
@@ -1173,7 +1241,6 @@
     latent_pull = jax.vjp(rms_norm, own(latent_full), gain_latent)[1]
     compressed_grad, grad_gain_latent = latent_pull(latent_grad)
     full_grad = jnp.concatenate([compressed_grad, rope_grad], axis=1).astype(BF16)
-    full_grad, all_output = lax.optimization_barrier((full_grad, all_output))
     spread_grad = jnp.pad(full_grad[:, :KVR], ((0, 0), (0, query_width + DR)))
     spread_grad = spread_grad + jnp.pad(full_grad[:, KVR:], ((0, 0), (KVR + query_width, 0)))
     normed_grad = dot_nt(pre_grad, query_weight) + dot_nt(spread_grad, head_weights)
@@ -1181,11 +1248,15 @@
     input_norm_grad, grad_gain_attn = input_pull(normed_grad)
     grad_inputs = middle_grad + input_norm_grad
 
+    full_grad, all_output = lax.optimization_barrier((full_grad, all_output))
     gain_grads = jnp.concatenate([grad_gain_attn, grad_gain_latent, grad_gain_ffn]).reshape(-1, 128)
     gain_grads = jnp.pad(gain_grads, ((0, -gain_grads.shape[0] % 8), (0, 0)))
-    last_parts = [part_query, part_expand, full_grad]
-    all_query, all_expand, full_all, gain_all = gather_all(
-        last_parts, [split_rows(part.shape[0]) for part in last_parts], [gain_grads], 6
+    sum_shared_in, all_query, all_expand, full_all, gain_all = turn_and_gather(
+        all_shared_in.reshape(seq_count, 2 * fsdp_count, unit, row_part),
+        [part_query, part_expand, full_grad],
+        [split_rows(part.shape[0]) for part in (part_query, part_expand, full_grad)],
+        [gain_grads],
+        6,
     )
     full_all = full_all.reshape(group_size, -1)
     sum_latent = scatter_fsdp(dot_tn(normed_all, full_all).astype(BF16))
@@ -1195,7 +1266,6 @@
         gain_sum = gain_sum + shift_fsdp(gain_seq, k)
     gain_sum = gain_sum.reshape(-1)
     sum_shared_out = all_shared_out[:, :unit].reshape(w_shared_out.shape).astype(F32)
-    sum_shared_in = turn_units(all_shared_in.reshape(seq_count, 2 * fsdp_count, unit, row_part))
     sum_query = turn_rows(all_query.reshape(-1, row_part), 384)
     sum_expand = turn_rows(all_expand.reshape(-1, w_kvb.shape[0]), 512)
     sum_output = all_output.astype(F32)

time: 1040 us -> 1030 us (level)
  Pallas kernels: 711 us -> 689 us
  local copies, waits for them, and re-layouts: 67.1 us -> 82.3 us
    pallas_call x3 -> x2, Pallas kernels: 272 us -> 182 us  [gather_all(): pl.pallas_call(functools.partial(gather_kernel, streams, len(main), len(s...]
    pallas_call x1, Pallas kernels: 18.1 us -> 95.1 us  [turn_and_gather(): pl.pallas_call(functools.partial(turn_gather_kernel, streams, len(main),...]
    unnamed x120 -> x131, local copies, waits for them, and re-layouts: 17.4 us -> 32.8 us
    pallas_call x1, Pallas kernels: 162 us -> 151 us  [expert_block(): pl.pallas_call(functools.partial(expert_kernel, streams, n), grid=(ends[-...]
  transfers between devices with their start and end apart: 23 -> 23, of which waited for: 3 -> 3; matrix products, arithmetic and copies ran while one was open for 21% -> 21% of each run, Pallas kernels for 67% -> 66%
where the time goes in v8:
time: 1030 us
  Pallas kernels  689 us (67%)
  matrix products  100 us (10%)
  local copies, waits for them, and re-layouts  82.3 us (8%)
  other arithmetic  78.7 us (8%)
  waiting for transfers between devices  38.6 us (4%)
  starting transfers between devices  15.5 us (2%)
  between operations  15.2 us (1%)
    pallas_call x2, Pallas kernels, gather_all(): pl.pallas_call(functools.partial(gather_kernel, streams, len(main), len(s...  182 us
    pallas_call x2, Pallas kernels, scatter_sum(): pl.pallas_call(functools.partial(scatter_kernel, streams, len(main), len(...  181 us
    pallas_call x1, Pallas kernels, expert_block(): pl.pallas_call(functools.partial(expert_kernel, streams, n), grid=(ends[-...  151 us
    pallas_call x1, Pallas kernels, turn_and_gather(): pl.pallas_call(functools.partial(turn_gather_kernel, streams, len(main),...  95.1 us
    dot_general x7, matrix products, dot_tn(): lax.dot_general(left, right, (((0,), (0,)), ((), ())), preferred_element_...  63.8 us
    unnamed x131, local copies, waits for them, and re-layouts  32.8 us
    pallas_call x1, Pallas kernels, spread(): pl.pallas_call(spread_kernel, grid=(steps,), in_specs=[by_rows(t, D), by_...  30 us
    dot_general x5, matrix products, dot_nt(): lax.dot_general(left, right, (((1,), (1,)), ((), ())), preferred_element_...  24.1 us
  transfers between devices with their start and end apart: 23, of which 3 were waited for; matrix products, arithmetic and copies ran while one was open for 21% of the time, Pallas kernels for 66%

profile of v8, /device:TPU:0, one launch (start us, length us, event | category | flops | bytes accessed | tf_op | source)
XLA Modules:
  0.0 1026.1 jit_solution(6935712338126232019)
XLA Ops:
  19.5 112.3 %gather_all.2 = (bf16[16,128,2048]{2,1,0:T(8,128)(2,1)}, bf16[16,16,128]{2,1,0:T(8,128)(2,1)}) custom-call(bf16[128,2048]{1,0:T(8,128)(2,1)} %refs_0_.1, bf16[16,128]{1,0:T(8,128)(2,1)} %convert_element_type.215.refs_1_), custom_call_target="tpu_custom_call" | custom-call | tf_op jit(solution)/shard_map/gather_all/pallas_call | solution.py:535
  135.4 5.0 fusion.4
  142.0 16.1 %project.1 = (bf16[2048,2048]{1,0:T(8,128)(2,1)}, bf16[2048,192]{1,0:T(8,128)(2,1)S(1)}, bf16[2048,192]{1,0:T(8,128)(2,1)S(1)}, bf16[2048,128]{1,0:T(8,128)(2,1)...) custom-call(bf16[2048,2048]{1,0:T(8,128)(2,1)} %bitcast.159, f32[1,2048]{1,0:T(1,128)S(1)} %bitcast.116, ...), custom_call_target="tpu_custom_call" | custom-call | flops 7549747200 | bytes 25165824 | tf_op jit(solution)/shard_map/project/pallas_call | solution.py:199
  158.1 7.8 attention_forward.1
  168.9 2.6 constant_dynamic-slice_fusion.9
  171.5 3.8 concatenate.36
  180.8 3.6 all-to-all-start
  187.1 2.8 all_gather.42
  191.0 8.8 all-to-all-done
  199.8 4.9 multiply_reduce_fusion.2
  206.7 69.7 %gather_all.3 = (bf16[16,128,2048]{2,1,0:T(8,128)(2,1)}, f32[16,8,128]{2,1,0:T(8,128)}) custom-call(bf16[128,2048]{1,0:T(8,128)(2,1)} %multiply_convert_fusion.1.refs_0_, f32[8,128]{1,0:T(8,128)} %copy-done.3), custom_call_target="tpu_custom_call" | custom-call | tf_op jit(solution)/shard_map/gather_all/pallas_call | solution.py:535
  276.3 7.2 fusion.61
  287.2 30.0 %spread.1 = (bf16[1536,2048]{1,0:T(8,128)(2,1)}, bf16[1536,2048]{1,0:T(8,128)(2,1)}, bf16[2048,256]{1,0:T(8,128)(2,1)}, bf16[2048,512]{1,0:T(8,128)(2,1)}, bf16[...) custom-call(bf16[2048,2048]{1,0:T(8,128)(2,1)} %bitcast.120, bf16[2048,2048]{1,0:T(8,128)(2,1)} %all-gather.16.cloned.1.call-done.up_ref, ...), custom_call_target="tpu_custom_call" | custom-call | flops 14495514624 | bytes 41943040 | tf_op jit(solution)/shard_map/spread/pallas_call | solution.py:299
  330.6 150.6 %expert_block.1 = (bf16[2048,2048]{1,0:T(8,128)(2,1)}, bf16[2048,2048]{1,0:T(8,128)(2,1)}, f32[2048,1]{1,0:T(8,128)}, bf16[1536,1408]{1,0:T(8,128)(2,1)}, bf16[1...) custom-call(bf16[1536,2048]{1,0:T(8,128)(2,1)} %get-tuple-element.10, ...), custom_call_target="tpu_custom_call" | custom-call | flops 53150220288 | bytes 104857600 | tf_op jit(solution)/shard_map/expert_block/pallas_call | solution.py:882
  483.5 134.6 %scatter_sum.2 = (f32[128,2048]{1,0:T(8,128)}, f32[128,2048]{1,0:T(8,128)}, f32[16,16,128]{2,1,0:T(8,128)}) custom-call(bf16[16,128,2048]{2,1,0:T(8,128)(2,1)} %bitcast.132, bf16[16,128,2048]{2,1,0:T(8,128)(2,1)} %bitcast.133, f32[16,128]{1,0:T(8,128)} %bitcast.147), custom_call_target="tpu_custom_call" | custom-call | tf_op jit(solution)/shard_map/scatter_sum/pallas_call | solution.py:724
  620.4 2.4 fusion.14
  627.9 2.3 convolution_convert_fusion.2
  630.2 3.4 copy-done.10
  633.6 2.3 constant_dynamic-slice_fusion.6
  636.3 7.2 multiply_convert_fusion
  643.5 6.3 fusion.3
  650.7 5.0 all-to-all-start.1
  655.6 4.7 convolution_convert_fusion.6
  660.6 3.3 slice.88
  664.0 6.4 bitcast_convert_fusion
  671.0 6.1 add_convert_fusion
  677.1 46.4 %scatter_sum.3 = f32[64,2048]{1,0:T(8,128)} custom-call(bf16[16,64,2048]{2,1,0:T(8,128)(2,1)} %bitcast.124), custom_call_target="tpu_custom_call" | custom-call | tf_op jit(solution)/shard_map/scatter_sum/pallas_call | solution.py:724
  729.0 12.7 %attention_backward.1 = bf16[2048,512]{1,0:T(8,128)(2,1)} custom-call(bf16[2048,192]{1,0:T(8,128)(2,1)S(1)} %copy-done.5, bf16[2048,192]{1,0:T(8,128)(2,1)S(1)} %copy-done.7, bf16[2048,128]{1,0:T(8,128)(2,1)S(1)} %get-tuple-element.74.v_ref, bf16[2048,128]{1,0:T(8,128)(2,1)S(1)} %bitcast.115, s32[2048,1]{1,0:T(8,128)S(1)} %add_select_fusion.segc_ref, ...), custom_call_target="tpu_custom_call" | custom-call | flops 3489660928 | bytes 6291456 | tf_op jit(solution)/shard_map/attention_backward/pallas_call | solution.py:156
  744.5 5.5 convolution_convert_fusion.4
  752.2 2.4 copy.106
  754.6 4.1 all-to-all-start.2
  759.4 24.4 %convolution_convert_fusion = bf16[2048,2816]{1,0:T(8,128)(2,1)} fusion(bf16[1536,2048]{1,0:T(8,128)(2,1)} %get-tuple-element.103.x_ref, bf16[1536,1408]{1,0:T(8,128)(2,1)} %get-tuple-element.105, bf16[1536,1408]{1,0:T(8,128)(2,1)} %get-tuple-element.104), kind=kOutput, calls=%fused_computation.2 | convolution fusion | flops 17739808768 | bytes 26476544 | tf_op jit(solution)/shard_map/dot_general | solution.py:74
  783.8 14.5 %convolution_convert_fusion.1 = bf16[1408,2048]{1,0:T(8,128)(2,1)} fusion(bf16[1536,1408]{1,0:T(8,128)(2,1)} %get-tuple-element.101, bf16[1536,2048]{1,0:T(8,128)(2,1)} %get-tuple-element.102.rg_ref), kind=kOutput, calls=%fused_computation.7 | convolution fusion | flops 8861253632 | bytes 16384000 | tf_op jit(solution)/shard_map/dot_general | solution.py:74
  799.4 8.2 all-to-all-done.2
  809.4 3.8 constant_dynamic-slice_fusion
  813.3 5.5 constant_dynamic-slice_fusion.1
  820.9 4.1 multiply_reduce_fusion.3
  826.2 9.7 fusion.62
  838.3 17.7 %all-gather.26.cloned.1.call-done = bf16[1024,2048]{1,0:T(8,128)(2,1)} async-done(((bf16[64,2048]{1,0:T(8,128)(2,1)}), bf16[1024,2048]{1,0:T(8,128)(2,1)}) %all-gather.26.cloned.1.call-update) | async-done | bytes 4194320 | tf_op jit(solution)/shard_map/all_gather | solution.py:1010
  856.0 95.1 %turn_and_gather.1 = (f32[1024,5632]{1,0:T(8,128)}, bf16[16,192,1024]{2,1,0:T(8,128)(2,1)S(1)}, bf16[16,256,256]{2,1,0:T(8,128)(2,1)S(1)}, bf16[16,128,576]{2,1,0:T(8,128)(2,1)S(1)}, f32[16,40,128]{2,1,0:T(8,128)S(1)}) custom-call(bf16[16,4,88,1024]{3,2,1,0:T(8,128)(2,1)} %bitcast.125, bf16[192,1024]{1,0:T(8,128)(2,1)S(1)} %add_convert_fusion.3.refs_1_, ...), custom_call_target="tpu_custom_call" | custom-call | tf_op jit(solution)/shard_map/turn_and_gather/pallas_call | solution.py:992
  951.1 10.3 %convolution_convert_fusion.3 = bf16[2048,576]{0,1:T(8,128)(2,1)S(1)} fusion(bf16[2048,2048]{1,0:T(8,128)(2,1)} %get-tuple-element.106, bf16[2048,576]{1,0:T(8,128)(2,1)S(1)} %bitcast.118), kind=kOutput, calls=%fused_computation.11 | convolution fusion | flops 4833017856 | bytes 13107200 | tf_op jit(solution)/shard_map/dot_general | solution.py:74
  964.7 6.4 add_bitcast_fusion.1
  971.1 9.4 turn_rows.2
  980.5 3.9 turn_rows.3
  984.4 4.5 convert_element_type.261
  990.2 3.1 convert_add_fusion
  993.3 10.0 add_bitcast_fusion
  1003.3 16.0 %copy.131 = f32[1024,5632]{1,0:T(8,128)} copy(f32[1024,5632]{1,0:T(8,128)} %get-tuple-element.198) | data formatting | bytes 46137344
  (283 shorter events, 84.2 us)
Async XLA Ops:
  7.2 133.2 %all-gather.14.cloned.1.call-start = ((), (), s32[]{:S(2)}) async-start(), calls=%async_computation.3 | async-start | bytes 4718592 | tf_op jit(solution)/shard_map/all_gather | solution.py:1018
  12.1 156.8 %all-gather.16.cloned.1.call-start = ((), (), s32[]{:S(2)}) async-start(), calls=%async_computation.4 | async-start | bytes 8912896 | tf_op jit(solution)/shard_map/all_gather | solution.py:1010
  13.5 177.6 %all-gather.18.cloned.1.call-start = ((), (), s32[]{:S(2)}) async-start(), calls=%async_computation.5 | async-start | bytes 12582912 | tf_op jit(solution)/shard_map/all_gather | solution.py:1018
  14.2 273.0 %all-gather.20.cloned.1.call-start = ((), (), s32[]{:S(2)}) async-start(), calls=%async_computation.6 | async-start | bytes 3145728 | tf_op jit(solution)/shard_map/all_gather | solution.py:1018
  14.3 126.1 %copy-start.44 = (f32[32]{0:T(128)}, f32[32]{0:T(128)S(1)}, u32[]{:S(2)}) copy-start(f32[32]{0:T(128)S(1)} %negate_power_fusion) | copy-start | bytes 388
  140.4 17.7 %copy-start.1 = (f32[2048,128]{1,0:T(8,128)}, f32[2048,128]{1,0:T(8,128)S(1)}, u32[]{:S(2)}) copy-start(f32[2048,128]{1,0:T(8,128)S(1)} %get-tuple-element.162.sin_ref) | copy-start | bytes 3145732
  168.9 7.0 copy-start.3
  175.3 155.3 %all-gather.30.cloned.1.call-start = ((), (), s32[]{:S(2)}) async-start(), calls=%async_computation.11 | async-start | bytes 8650752 | tf_op jit(solution)/shard_map/all_gather | solution.py:1018
  175.9 154.7 %all-gather.28.cloned.1.call-start = ((), (), s32[]{:S(2)}) async-start(), calls=%async_computation.10 | async-start | bytes 17301504 | tf_op jit(solution)/shard_map/all_gather | solution.py:1018
  176.5 304.8 %all-gather.24.cloned.1.call-start = ((), (), s32[]{:S(2)}) async-start(), calls=%async_computation.8 | async-start | bytes 6291456 | tf_op jit(solution)/shard_map/all_gather | solution.py:1018
  177.3 304.1 %all-gather.22.cloned.1.call-start = ((), (), s32[]{:S(2)}) async-start(), calls=%async_computation.7 | async-start | bytes 18874368 | tf_op jit(solution)/shard_map/all_gather | solution.py:1018
  179.8 24.9 %copy-start.50 = (f32[128]{0:T(128)}, f32[128]{0:T(128)S(1)}, u32[]{:S(2)}) copy-start(f32[128]{0:T(128)S(1)} %fusion.7) | copy-start | bytes 1540
  180.8 19.0 %all-to-all-start = ((bf16[16,128,128]{1,2,0:T(8,128)(2,1)}), bf16[16,128,128]{1,2,0:T(8,128)(2,1)S(1)}, u32[]{:S(2)}, u32[]{:S(2)}) async-start(bf16[16,128,128]{1,2,0:T(8,128)(2,1)} %copy.101), calls=%async_computation | async-start | bytes 1048576 | tf_op jit(solution)/shard_map/all_to_all | solution.py:1140
  283.9 33.3 %copy-start.11 = (f32[2048,16]{1,0:T(8,128)}, f32[2048,16]{1,0:T(8,128)S(1)}, u32[]{:S(2)}) copy-start(f32[2048,16]{1,0:T(8,128)S(1)} %copy.103) | copy-start | bytes 393220
  318.5 8.0 collective-permute-start.1
  321.7 6.7 collective-permute-start
  325.9 310.0 %collective-permute-start.10 = (f32[16,128]{1,0:T(8,128)S(1)}, f32[16,128]{1,0:T(8,128)S(1)}, u32[]{:S(2)}, u32[]{:S(2)}) collective-permute-start(f32[16,128]{1,0:T(8,128)S(1)} %bitcast.148), channel_id=1, source_target_pairs={{0,1},{1,0},{2,3},{3,2},{4,5},{5,4},{6,7},{7,6},{8,9},{9,8},{10,11... | collective-permute-start | bytes 24584 | tf_op jit(solution)/shard_map/ppermute | solution.py:1033
  483.5 136.8 %copy-start.12 = (f32[2048,16]{1,0:T(8,128)S(1)}, f32[2048,16]{1,0:T(8,128)}, u32[]{:S(2)}) copy-start(f32[2048,16]{1,0:T(8,128)} %copy-done.11) | copy-start | bytes 393220
  627.9 15.6 %copy-start.15 = (f32[128,2048]{1,0:T(8,128)}, f32[128,2048]{1,0:T(8,128)S(1)}, u32[]{:S(2)}) copy-start(f32[128,2048]{1,0:T(8,128)S(1)} %get-tuple-element.149) | copy-start | bytes 3145732
  635.9 35.1 %collective-permute-start.2 = (bf16[1024,2048]{1,0:T(8,128)(2,1)}, bf16[1024,2048]{1,0:T(8,128)(2,1)}, u32[]{:S(2)}, u32[]{:S(2)}) collective-permute-start(bf16[1024,2048]{1,0:T(8,128)(2,1)} %constant_dynamic-slice_fusion.6), channel_id=1, source_target_pairs={{0,1},{1,0},{2,3},{3,2},{4,5},{5,4},{6,7},{7,6},{8,9},{9,8},{10,11... | collective-permute-start | bytes 12582920 | tf_op jit(solution)/shard_map/ppermute | solution.py:1033
  650.7 74.7 %all-to-all-start.1 = ((bf16[128,16,128]{2,0,1:T(8,128)(2,1)}), bf16[128,16,128]{2,0,1:T(8,128)(2,1)S(1)}, u32[]{:S(2)}, u32[]{:S(2)}) async-start(bf16[128,16,128]{2,0,1:T(8,128)(2,1)} %bitcast.108), calls=%async_computation.1 | async-start | bytes 1048576 | tf_op jit(solution)/shard_map/all_to_all | solution.py:1205
  660.3 10.0 collective-permute-start.7
  660.6 10.4 %slice-start = ((s8[8388608]{0:T(1024)(128)(4,1)}), s8[4194304]{0:T(1024)(128)(4,1)S(1)}, s32[]{:S(2)}) async-start(s8[8388608]{0:T(1024)(128)(4,1)} %bitcast.122), calls=%async_computation.12 | async-start | bytes 8388608
  663.9 7.1 slice-start.1
  729.0 12.7 %copy-start.56 = (bf16[2048,512]{1,0:T(8,128)(2,1)S(1)}, bf16[2048,512]{1,0:T(8,128)(2,1)}, u32[]{:S(2)}) copy-start(bf16[2048,512]{1,0:T(8,128)(2,1)} %get-tuple-element.107) | copy-start | bytes 6291460
  744.5 53.8 %collective-permute-start.4 = (bf16[256,256]{1,0:T(8,128)(2,1)}, bf16[256,256]{1,0:T(8,128)(2,1)}, u32[]{:S(2)}, u32[]{:S(2)}) collective-permute-start(bf16[256,256]{1,0:T(8,128)(2,1)} %constant_dynamic-slice_fusion.4), channel_id=1, source_target_pairs={{0,1},{1,0},{2,3},{3,2},{4,5},{5,4},{6,7},{7,6},{8,9},{9,8},{10,11... | collective-permute-start | bytes 393224 | tf_op jit(solution)/shard_map/ppermute | solution.py:1033
  744.5 7.7 copy-start.22
  751.7 47.6 %collective-permute-start.3 = (bf16[192,1024]{1,0:T(8,128)(2,1)}, bf16[192,1024]{1,0:T(8,128)(2,1)S(1)}, u32[]{:S(2)}, u32[]{:S(2)}) collective-permute-start(bf16[192,1024]{1,0:T(8,128)(2,1)} %constant_dynamic-slice_fusion.5), channel_id=1, source_target_pairs={{0,1},{1,0},{2,3},{3,2},{4,5},{5,4},{6,7},{7,6},{8,9},{9,8},{10,11... | collective-permute-start | bytes 1179656 | tf_op jit(solution)/shard_map/ppermute | solution.py:1033
  754.6 53.1 %all-to-all-start.2 = ((bf16[16,128,512]{1,2,0:T(8,128)(2,1)}), bf16[16,128,512]{1,2,0:T(8,128)(2,1)S(1)}, u32[]{:S(2)}, u32[]{:S(2)}) async-start(bf16[16,128,512]{1,2,0:T(8,128)(2,1)} %copy.106), calls=%async_computation.2 | async-start | bytes 4194304 | tf_op jit(solution)/shard_map/all_to_all | solution.py:1218
  758.7 97.3 %all-gather.26.cloned.1.call-start = ((), (), s32[]{:S(2)}) async-start(), calls=%async_computation.9 | async-start | bytes 4456448 | tf_op jit(solution)/shard_map/all_gather | solution.py:1010
  783.8 14.5 %copy-start.37 = (bf16[256,512]{1,0:T(8,128)(2,1)S(1)}, bf16[256,512]{1,0:T(8,128)(2,1)}, u32[]{:S(2)}) copy-start(bf16[256,512]{1,0:T(8,128)(2,1)} %copy-done.36) | copy-start | bytes 786436
  783.8 15.5 %copy-start.26 = (bf16[192,2048]{1,0:T(8,128)(2,1)S(1)}, bf16[192,2048]{1,0:T(8,128)(2,1)}, u32[]{:S(2)}) copy-start(bf16[192,2048]{1,0:T(8,128)(2,1)} %copy-done.25) | copy-start | bytes 2359300
  813.2 7.3 copy-start.45
  813.2 7.3 copy-start.52
  813.2 7.7 copy-start.41
  813.2 7.7 copy-start.48
  813.2 151.5 %collective-permute-start.9 = (bf16[704,2048]{1,0:T(8,128)(2,1)}, bf16[704,2048]{1,0:T(8,128)(2,1)}, u32[]{:S(2)}, u32[]{:S(2)}) collective-permute-start(bf16[704,2048]{1,0:T(8,128)(2,1)} %constant_dynamic-slice_fusion), channel_id=1, source_target_pairs={{0,1},{1,0},{2,3},{3,2},{4,5},{5,4},{6,7},{7,6},{8,9},{9,8},{10,11... | collective-permute-start | bytes 8650760 | tf_op jit(solution)/shard_map/ppermute | solution.py:1033
  818.8 174.6 %collective-permute-start.8 = (bf16[1024,2816]{1,0:T(8,128)(2,1)}, bf16[1024,2816]{1,0:T(8,128)(2,1)}, u32[]{:S(2)}, u32[]{:S(2)}) collective-permute-start(bf16[1024,2816]{1,0:T(8,128)(2,1)} %constant_dynamic-slice_fusion.1), channel_id=1, source_target_pairs={{0,1},{1,0},{2,3},{3,2},{4,5},{5,4},{6,7},{7,6},{8,9},{9,8},{10,11... | collective-permute-start | bytes 17301512 | tf_op jit(solution)/shard_map/ppermute | solution.py:1033
  826.1 9.7 copy-start.18
  826.1 9.7 copy-start.27
  826.2 9.7 copy-start.38
  826.2 9.7 copy-start.43
  951.1 10.4 %copy-start = (bf16[16,192,1024]{2,1,0:T(8,128)(2,1)}, bf16[16,192,1024]{2,1,0:T(8,128)(2,1)S(1)}, u32[]{:S(2)}) copy-start(bf16[16,192,1024]{2,1,0:T(8,128)(2,1)S(1)} %get-tuple-element.118) | copy-start | bytes 18874372
  951.1 11.7 %copy-start.16 = (f32[128,2048]{1,0:T(8,128)S(1)}, f32[128,2048]{1,0:T(8,128)}, u32[]{:S(2)}) copy-start(f32[128,2048]{1,0:T(8,128)} %copy-done.15) | copy-start | bytes 3145732
  951.1 11.7 %copy-start.19 = (bf16[128,2048]{1,0:T(8,128)(2,1)S(1)}, bf16[128,2048]{1,0:T(8,128)(2,1)}, u32[]{:S(2)}) copy-start(bf16[128,2048]{1,0:T(8,128)(2,1)} %refs_0_.1) | copy-start | bytes 1572868
  951.1 11.7 %copy-start.24 = (f32[128,2048]{1,0:T(8,128)S(1)}, f32[128,2048]{1,0:T(8,128)}, u32[]{:S(2)}) copy-start(f32[128,2048]{1,0:T(8,128)} %get-tuple-element.172) | copy-start | bytes 3145732
  962.8 27.4 %collective-permute-start.6 = (bf16[1024,576]{0,1:T(8,128)(2,1)}, bf16[1024,576]{0,1:T(8,128)(2,1)}, u32[]{:S(2)}, u32[]{:S(2)}) collective-permute-start(bf16[1024,576]{0,1:T(8,128)(2,1)} %constant_dynamic-slice_fusion.3), channel_id=1, source_target_pairs={{0,1},{1,0},{2,3},{3,2},{4,5},{5,4},{6,7},{7,6},{8,9},{9,8},{10,11... | collective-permute-start | bytes 3538952 | tf_op jit(solution)/shard_map/ppermute | solution.py:1033
  964.1 24.8 %collective-permute-start.5 = (f32[40,128]{1,0:T(8,128)S(1)}, f32[40,128]{1,0:T(8,128)S(1)}, u32[]{:S(2)}, u32[]{:S(2)}) collective-permute-start(f32[40,128]{1,0:T(8,128)S(1)} %reduce_sum.183), channel_id=1, source_target_pairs={{0,1},{1,0},{2,3},{3,2},{4,5},{5,4},{6,7},{7,6},{8,9},{9,8},{10,11... | collective-permute-start | bytes 61448 | tf_op jit(solution)/shard_map/ppermute | solution.py:1033
  (37 other events, 104.4 us)
Sparse Core Ops, SparseCore 0:
  12.2 14.7 all-gather.13
  30.3 137.7 all-gather.15
  169.6 18.0 all-gather.17
  189.7 11.7 all-gather.19
  202.9 17.1 all-gather.29
  221.5 25.0 all-gather.27
  248.1 14.8 all-gather.23
  264.5 26.0 all-gather.21
  762.3 93.6 all-gather.25

commit v9 on v8

--- a/solution.py
+++ b/solution.py
@@ -961,7 +961,7 @@
         send_small()
 
     block = parts_ref[...].astype(F32)
-    turned_ref[...] = block.reshape(-1, block.shape[-1]).T
+    turned_ref[...] = block.reshape(-1, block.shape[-1]).T.astype(turned_ref.dtype)
     rest = actions[len(streams) :]
     for step in range(steps):
 
@@ -982,7 +982,7 @@
     seq_count, groups, unit, columns = turned.shape
     wide = seq_count * unit
     if unit % 8 or wide % 128 or columns % 256:
-        rows = turned.transpose(3, 1, 0, 2).reshape(columns, -1).astype(F32)
+        rows = turned.transpose(3, 1, 0, 2).reshape(columns, -1)
         return (rows, *gather_all(main, parts, small, collective_id, count))
     tile = 256
     across = columns // tile
@@ -996,7 +996,7 @@
         + [any_spec] * len(arrays),
         out_specs=(pl.BlockSpec((tile, wide), lambda i: (i % across, i // across)),)
         + (any_spec,) * len(arrays),
-        out_shape=(jax.ShapeDtypeStruct((columns, groups * wide), F32),)
+        out_shape=(jax.ShapeDtypeStruct((columns, groups * wide), turned.dtype),)
         + tuple(jax.ShapeDtypeStruct((count,) + a.shape, a.dtype) for a in arrays),
         scratch_shapes=gather_scratch(streams, len(small), len(arrays), count),
         compiler_params=pltpu.CompilerParams(
@@ -1226,8 +1226,19 @@
     grad_expand = dot_tn(head_back[:, DN:rope_at], latent_all).astype(BF16)
     part_query = scatter_fsdp(grad_query, 1).astype(BF16)
     part_expand = scatter_fsdp(grad_expand, 1).astype(BF16)
-    back, grad_expert_out, grad_expert_in, part_query, part_expand = lax.optimization_barrier(
-        (back, grad_expert_out, grad_expert_in, part_query, part_expand)
+    grad_expert_in, global_max = lax.optimization_barrier((grad_expert_in, global_max))
+    clip_gamma = CLIP_LIMIT / jnp.maximum(global_max, CLIP_LIMIT)
+    clip_root = jnp.sqrt(clip_gamma)
+    query_factor = jnp.concatenate(
+        [
+            jnp.broadcast_to(clip_root[:, None], (H, DN)),
+            jnp.broadcast_to(clip_gamma[:, None], (H, DR)),
+        ],
+        axis=1,
+    ).reshape(1, -1)
+    clipped_query = (w_q.astype(F32) * query_factor).astype(BF16)
+    back, grad_expert_out, grad_expert_in, part_query, part_expand, clipped_query = lax.optimization_barrier(
+        (back, grad_expert_out, grad_expert_in, part_query, part_expand, clipped_query)
     )
     sum_expert_in = scatter_fsdp(grad_expert_in)[None]
     sum_expert_out = scatter_fsdp(grad_expert_out)[None]
@@ -1248,7 +1259,9 @@
     input_norm_grad, grad_gain_attn = input_pull(normed_grad)
     grad_inputs = middle_grad + input_norm_grad
 
-    full_grad, all_output = lax.optimization_barrier((full_grad, all_output))
+    full_grad, all_output, sum_expert_in, sum_expert_out = lax.optimization_barrier(
+        (full_grad, all_output, sum_expert_in, sum_expert_out)
+    )
     gain_grads = jnp.concatenate([grad_gain_attn, grad_gain_latent, grad_gain_ffn]).reshape(-1, 128)
     gain_grads = jnp.pad(gain_grads, ((0, -gain_grads.shape[0] % 8), (0, 0)))
     sum_shared_in, all_query, all_expand, full_all, gain_all = turn_and_gather(
@@ -1266,6 +1279,7 @@
         gain_sum = gain_sum + shift_fsdp(gain_seq, k)
     gain_sum = gain_sum.reshape(-1)
     sum_shared_out = all_shared_out[:, :unit].reshape(w_shared_out.shape).astype(F32)
+    sum_shared_in = sum_shared_in.astype(F32)
     sum_query = turn_rows(all_query.reshape(-1, row_part), 384)
     sum_expand = turn_rows(all_expand.reshape(-1, w_kvb.shape[0]), 512)
     sum_output = all_output.astype(F32)
@@ -1278,16 +1292,6 @@
     sum_gain_latent = own_part(D, g_kv)
     sum_gain_ffn = own_part(D + KVR, g_ffn)
 
-    clip_gamma = CLIP_LIMIT / jnp.maximum(global_max, CLIP_LIMIT)
-    clip_root = jnp.sqrt(clip_gamma)
-    query_factor = jnp.concatenate(
-        [
-            jnp.broadcast_to(clip_root[:, None], (H, DN)),
-            jnp.broadcast_to(clip_gamma[:, None], (H, DR)),
-        ],
-        axis=1,
-    ).reshape(1, -1)
-    clipped_query = (w_q.astype(F32) * query_factor).astype(BF16)
     return (
         mixed,
         grad_inputs,

time: 1030 us -> 1040 us (level)
  other arithmetic: 78.7 us -> 97.2 us
  local copies, waits for them, and re-layouts: 82.3 us -> 67.1 us
  Pallas kernels: 689 us -> 702 us
    all_gather x2, waiting for transfers between devices: 17.7 us -> 0.01 us  [gather_seq(): return lax.all_gather(rows, 'seq', axis=0, tiled=True)]
    unnamed x131 -> x118, local copies, waits for them, and re-layouts: 32.8 us -> 15.8 us
    pallas_call x1, Pallas kernels: 95.1 us -> 111 us  [turn_and_gather(): pl.pallas_call(functools.partial(turn_gather_kernel, streams, len(main),...]
    convert_element_type x0 -> x1, other arithmetic: none -> 13 us  [on_device(): sum_shared_in = sum_shared_in.astype(F32)]
  transfers between devices with their start and end apart: 23 -> 23, of which waited for: 3 -> 3; matrix products, arithmetic and copies ran while one was open for 21% -> 19% of each run, Pallas kernels for 66% -> 54%
where the time goes in v9:
time: 1040 us
  Pallas kernels  702 us (68%)
  matrix products  102 us (10%)
  other arithmetic  97.2 us (9%)
  local copies, waits for them, and re-layouts  67.1 us (6%)
  waiting for transfers between devices  29.7 us (3%)
  starting transfers between devices  16.3 us (2%)
  between operations  15.1 us (1%)
    pallas_call x2, Pallas kernels, gather_all(): pl.pallas_call(functools.partial(gather_kernel, streams, len(main), len(s...  181 us
    pallas_call x2, Pallas kernels, scatter_sum(): pl.pallas_call(functools.partial(scatter_kernel, streams, len(main), len(...  179 us
    pallas_call x1, Pallas kernels, expert_block(): pl.pallas_call(functools.partial(expert_kernel, streams, n), grid=(ends[-...  151 us
    pallas_call x1, Pallas kernels, turn_and_gather(): pl.pallas_call(functools.partial(turn_gather_kernel, streams, len(main),...  111 us
    dot_general x7, matrix products, dot_tn(): lax.dot_general(left, right, (((0,), (0,)), ((), ())), preferred_element_...  64.2 us
    pallas_call x1, Pallas kernels, spread(): pl.pallas_call(spread_kernel, grid=(steps,), in_specs=[by_rows(t, D), by_...  30 us
    dot_general x5, matrix products, dot_nt(): lax.dot_general(left, right, (((1,), (1,)), ((), ())), preferred_element_...  24.2 us
  transfers between devices with their start and end apart: 23, of which 3 were waited for; matrix products, arithmetic and copies ran while one was open for 19% of the time, Pallas kernels for 54%

profile of v9, /device:TPU:0, one launch (start us, length us, event | category | flops | bytes accessed | tf_op | source)
XLA Modules:
  0.0 1036.4 jit_solution(3630122145197062220)
XLA Ops:
  19.5 112.3 %gather_all.2 = (bf16[16,128,2048]{2,1,0:T(8,128)(2,1)}, bf16[16,16,128]{2,1,0:T(8,128)(2,1)}) custom-call(bf16[128,2048]{1,0:T(8,128)(2,1)} %refs_0_.1, bf16[16,128]{1,0:T(8,128)(2,1)} %convert_element_type.218.refs_1_), custom_call_target="tpu_custom_call" | custom-call | tf_op jit(solution)/shard_map/gather_all/pallas_call | solution.py:535
  135.4 5.0 fusion.4
  142.0 16.1 %project.1 = (bf16[2048,2048]{1,0:T(8,128)(2,1)}, bf16[2048,192]{1,0:T(8,128)(2,1)S(1)}, bf16[2048,192]{1,0:T(8,128)(2,1)S(1)}, bf16[2048,128]{1,0:T(8,128)(2,1)...) custom-call(bf16[2048,2048]{1,0:T(8,128)(2,1)} %bitcast.161, f32[1,2048]{1,0:T(1,128)S(1)} %bitcast.116, ...), custom_call_target="tpu_custom_call" | custom-call | flops 7549747200 | bytes 25165824 | tf_op jit(solution)/shard_map/project/pallas_call | solution.py:199
  158.1 7.9 attention_forward.1
  169.0 2.6 constant_dynamic-slice_fusion.9
  171.6 3.8 concatenate.36
  179.1 3.6 all-to-all-start
  186.5 2.8 all_gather.42
  190.4 7.7 all-to-all-done
  198.2 5.3 multiply_reduce_fusion.2
  205.4 68.7 %gather_all.3 = (bf16[16,128,2048]{2,1,0:T(8,128)(2,1)}, f32[16,8,128]{2,1,0:T(8,128)}) custom-call(bf16[128,2048]{1,0:T(8,128)(2,1)} %multiply_convert_fusion.1.refs_0_, f32[8,128]{1,0:T(8,128)} %copy-done.3), custom_call_target="tpu_custom_call" | custom-call | tf_op jit(solution)/shard_map/gather_all/pallas_call | solution.py:535
  274.1 8.0 fusion.61
  285.7 30.0 %spread.1 = (bf16[1536,2048]{1,0:T(8,128)(2,1)}, bf16[1536,2048]{1,0:T(8,128)(2,1)}, bf16[2048,256]{1,0:T(8,128)(2,1)}, bf16[2048,512]{1,0:T(8,128)(2,1)}, bf16[...) custom-call(bf16[2048,2048]{1,0:T(8,128)(2,1)} %bitcast.120, bf16[2048,2048]{1,0:T(8,128)(2,1)} %all-gather.16.cloned.1.call-done.up_ref, ...), custom_call_target="tpu_custom_call" | custom-call | flops 14495514624 | bytes 41943040 | tf_op jit(solution)/shard_map/spread/pallas_call | solution.py:299
  324.9 150.8 %expert_block.1 = (bf16[2048,2048]{1,0:T(8,128)(2,1)}, bf16[2048,2048]{1,0:T(8,128)(2,1)}, f32[2048,1]{1,0:T(8,128)}, bf16[1536,1408]{1,0:T(8,128)(2,1)}, bf16[1...) custom-call(bf16[1536,2048]{1,0:T(8,128)(2,1)} %get-tuple-element.10, ...), custom_call_target="tpu_custom_call" | custom-call | flops 53150220288 | bytes 104857600 | tf_op jit(solution)/shard_map/expert_block/pallas_call | solution.py:882
  477.9 134.4 %scatter_sum.2 = (f32[128,2048]{1,0:T(8,128)}, f32[128,2048]{1,0:T(8,128)}, f32[16,16,128]{2,1,0:T(8,128)}) custom-call(bf16[16,128,2048]{2,1,0:T(8,128)(2,1)} %bitcast.130, bf16[16,128,2048]{2,1,0:T(8,128)(2,1)} %bitcast.131, f32[16,128]{1,0:T(8,128)} %bitcast.149), custom_call_target="tpu_custom_call" | custom-call | tf_op jit(solution)/shard_map/scatter_sum/pallas_call | solution.py:724
  614.6 2.7 fusion.14
  619.3 2.4 multiply_reduce_fusion
  623.0 2.3 convolution_convert_fusion.2
  625.3 3.4 copy-done.10
  628.7 2.3 constant_dynamic-slice_fusion.6
  636.4 6.3 fusion.3
  643.6 5.0 all-to-all-start.1
  649.3 7.8 add_convert_fusion
  657.1 44.3 %scatter_sum.3 = f32[64,2048]{1,0:T(8,128)} custom-call(bf16[16,64,2048]{2,1,0:T(8,128)(2,1)} %bitcast.122), custom_call_target="tpu_custom_call" | custom-call | tf_op jit(solution)/shard_map/scatter_sum/pallas_call | solution.py:724
  706.9 13.1 %attention_backward.1 = bf16[2048,512]{1,0:T(8,128)(2,1)} custom-call(bf16[2048,192]{1,0:T(8,128)(2,1)S(1)} %copy-done.5, bf16[2048,192]{1,0:T(8,128)(2,1)S(1)} %copy-done.7, bf16[2048,128]{1,0:T(8,128)(2,1)S(1)} %get-tuple-element.79.v_ref, bf16[2048,128]{1,0:T(8,128)(2,1)S(1)} %bitcast.115, s32[2048,1]{1,0:T(8,128)S(1)} %add_select_fusion.segc_ref, ...), custom_call_target="tpu_custom_call" | custom-call | flops 3489660928 | bytes 6291456 | tf_op jit(solution)/shard_map/attention_backward/pallas_call | solution.py:156
  723.7 24.7 %convolution_convert_fusion = bf16[2048,2816]{1,0:T(8,128)(2,1)} fusion(bf16[1536,2048]{1,0:T(8,128)(2,1)} %get-tuple-element.108.x_ref, bf16[1536,1408]{1,0:T(8,128)(2,1)} %get-tuple-element.110, bf16[1536,1408]{1,0:T(8,128)(2,1)} %get-tuple-element.109), kind=kOutput, calls=%fused_computation.2 | convolution fusion | flops 17739808768 | bytes 26476544 | tf_op jit(solution)/shard_map/dot_general | solution.py:74
  752.3 2.4 copy.106
  754.7 5.5 all-to-all-start.2
  760.2 5.5 convolution_convert_fusion.4
  766.9 7.1 multiply_convert_fusion
  773.9 14.7 %convolution_convert_fusion.1 = bf16[1408,2048]{1,0:T(8,128)(2,1)} fusion(bf16[1536,1408]{1,0:T(8,128)(2,1)} %get-tuple-element.106, bf16[1536,2048]{1,0:T(8,128)(2,1)} %get-tuple-element.107.rg_ref), kind=kOutput, calls=%fused_computation.7 | convolution fusion | flops 8861253632 | bytes 16384000 | tf_op jit(solution)/shard_map/dot_general | solution.py:74
  790.8 18.2 %all-to-all-done.2 = bf16[16,128,512]{1,2,0:T(8,128)(2,1)S(1)} async-done(((bf16[16,128,512]{1,2,0:T(8,128)(2,1)}), bf16[16,128,512]{1,2,0:T(8,128)(2,1)S(1)}, u32[]{:S(2)}, u32[]{:S(2)}) %all-to-all-start.2) | async-done | bytes 2097184 | tf_op jit(solution)/shard_map/all_to_all | solution.py:1218
  809.0 5.5 constant_dynamic-slice_fusion.3
  814.5 4.6 convolution_convert_fusion.6
  819.7 3.3 slice.90
  823.1 6.4 bitcast_convert_fusion
  832.8 4.1 multiply_reduce_fusion.3
  839.7 9.1 fusion.62
  851.3 5.3 add_bitcast_fusion.1
  856.6 10.0 add_bitcast_fusion
  866.6 111.3 %turn_and_gather.1 = (bf16[1024,5632]{1,0:T(8,128)(2,1)}, bf16[16,192,1024]{2,1,0:T(8,128)(2,1)S(1)}, bf16[16,256,256]{2,1,0:T(8,128)(2,1)S(1)}, bf16[16,128,576]{2,1,0:T(8,128)(2,1)S(1)}, f32[16,40,128]{2,1,0:T(8,128)S(1)}) custom-call(bf16[16,4,88,1024]{3,2,1,0:T(8,128)(2,1)} %bitcast.123, bf16[192,1024]{1,0:T(8,128)(2,1)S(1)} %add_convert_fusion.3.refs_1_, ...), custom_call_target="tpu_custom_call" | custom-call | tf_op jit(solution)/shard_map/turn_and_gather/pallas_call | solution.py:992
  978.0 9.9 convolution_convert_fusion.3
  991.7 2.8 fusion.6
  994.5 13.0 %convert_element_type.274 = f32[1024,5632]{1,0:T(8,128)} convert(bf16[1024,5632]{1,0:T(8,128)(2,1)} %get-tuple-element.132) | non-fusion elementwise | flops 5767168 | bytes 34603008 | tf_op jit(solution)/shard_map/convert_element_type | solution.py:1282
  1007.5 9.4 turn_rows.2
  1016.9 3.9 turn_rows.3
  1020.8 4.5 convert_element_type.270
  1026.6 3.0 convert_add_fusion
  (271 shorter events, 88.3 us)
Async XLA Ops:
  7.2 133.2 %all-gather.14.cloned.1.call-start = ((), (), s32[]{:S(2)}) async-start(), calls=%async_computation.3 | async-start | bytes 4718592 | tf_op jit(solution)/shard_map/all_gather | solution.py:1018
  12.1 156.9 %all-gather.16.cloned.1.call-start = ((), (), s32[]{:S(2)}) async-start(), calls=%async_computation.4 | async-start | bytes 8912896 | tf_op jit(solution)/shard_map/all_gather | solution.py:1010
  13.5 177.0 %all-gather.18.cloned.1.call-start = ((), (), s32[]{:S(2)}) async-start(), calls=%async_computation.5 | async-start | bytes 12582912 | tf_op jit(solution)/shard_map/all_gather | solution.py:1018
  14.2 271.5 %all-gather.20.cloned.1.call-start = ((), (), s32[]{:S(2)}) async-start(), calls=%async_computation.6 | async-start | bytes 3145728 | tf_op jit(solution)/shard_map/all_gather | solution.py:1018
  140.4 17.7 %copy-start.1 = (f32[2048,128]{1,0:T(8,128)}, f32[2048,128]{1,0:T(8,128)S(1)}, u32[]{:S(2)}) copy-start(f32[2048,128]{1,0:T(8,128)S(1)} %get-tuple-element.172.sin_ref) | copy-start | bytes 3145732
  169.0 7.1 copy-start.3
  175.4 149.5 %all-gather.30.cloned.1.call-start = ((), (), s32[]{:S(2)}) async-start(), calls=%async_computation.11 | async-start | bytes 8650752 | tf_op jit(solution)/shard_map/all_gather | solution.py:1018
  176.0 148.9 %all-gather.28.cloned.1.call-start = ((), (), s32[]{:S(2)}) async-start(), calls=%async_computation.10 | async-start | bytes 17301504 | tf_op jit(solution)/shard_map/all_gather | solution.py:1018
  176.6 299.1 %all-gather.24.cloned.1.call-start = ((), (), s32[]{:S(2)}) async-start(), calls=%async_computation.8 | async-start | bytes 6291456 | tf_op jit(solution)/shard_map/all_gather | solution.py:1018
  177.3 6.6 copy-start.34
  177.4 298.4 %all-gather.22.cloned.1.call-start = ((), (), s32[]{:S(2)}) async-start(), calls=%async_computation.7 | async-start | bytes 18874368 | tf_op jit(solution)/shard_map/all_gather | solution.py:1018
  178.1 20.0 %copy-start.16 = (bf16[128,2048]{1,0:T(8,128)(2,1)S(1)}, bf16[128,2048]{1,0:T(8,128)(2,1)}, u32[]{:S(2)}) copy-start(bf16[128,2048]{1,0:T(8,128)(2,1)} %refs_0_.1) | copy-start | bytes 1572868
  179.1 19.0 %all-to-all-start = ((bf16[16,128,128]{1,2,0:T(8,128)(2,1)}), bf16[16,128,128]{1,2,0:T(8,128)(2,1)S(1)}, u32[]{:S(2)}, u32[]{:S(2)}) async-start(bf16[16,128,128]{1,2,0:T(8,128)(2,1)} %copy.101), calls=%async_computation | async-start | bytes 1048576 | tf_op jit(solution)/shard_map/all_to_all | solution.py:1140
  198.1 5.4 copy-start.19
  282.4 33.3 %copy-start.11 = (f32[2048,16]{1,0:T(8,128)}, f32[2048,16]{1,0:T(8,128)S(1)}, u32[]{:S(2)}) copy-start(f32[2048,16]{1,0:T(8,128)S(1)} %copy.103) | copy-start | bytes 393220
  317.0 3.2 collective-permute-start.1
  320.2 2.5 collective-permute-start
  477.9 136.6 %copy-start.12 = (f32[2048,16]{1,0:T(8,128)S(1)}, f32[2048,16]{1,0:T(8,128)}, u32[]{:S(2)}) copy-start(f32[2048,16]{1,0:T(8,128)} %copy-done.11) | copy-start | bytes 393220
  614.5 7.2 copy-start.31
  614.6 7.2 copy-start.33
  623.0 13.4 %copy-start.15 = (f32[128,2048]{1,0:T(8,128)}, f32[128,2048]{1,0:T(8,128)S(1)}, u32[]{:S(2)}) copy-start(f32[128,2048]{1,0:T(8,128)S(1)} %get-tuple-element.159) | copy-start | bytes 3145732
  631.0 18.3 %collective-permute-start.2 = (bf16[1024,2048]{1,0:T(8,128)(2,1)}, bf16[1024,2048]{1,0:T(8,128)(2,1)}, u32[]{:S(2)}, u32[]{:S(2)}) collective-permute-start(bf16[1024,2048]{1,0:T(8,128)(2,1)} %constant_dynamic-slice_fusion.6), channel_id=1, source_target_pairs={{0,1},{1,0},{2,3},{3,2},{4,5},{5,4},{6,7},{7,6},{8,9},{9,8},{10,11... | collective-permute-start | bytes 12582920 | tf_op jit(solution)/shard_map/ppermute | solution.py:1033
  635.0 13.6 %copy-start.47 = (f32[128]{0:T(128)}, f32[128]{0:T(128)S(1)}, u32[]{:S(2)}) copy-start(f32[128]{0:T(128)S(1)} %multiply_reduce_fusion.5) | copy-start | bytes 1540
  635.9 13.3 %collective-permute-start.3 = (f32[16,128]{1,0:T(8,128)S(1)}, f32[16,128]{1,0:T(8,128)S(1)}, u32[]{:S(2)}, u32[]{:S(2)}) collective-permute-start(f32[16,128]{1,0:T(8,128)S(1)} %bitcast.150), channel_id=1, source_target_pairs={{0,1},{1,0},{2,3},{3,2},{4,5},{5,4},{6,7},{7,6},{8,9},{9,8},{10,11... | collective-permute-start | bytes 24584 | tf_op jit(solution)/shard_map/ppermute | solution.py:1033
  643.6 59.6 %all-to-all-start.1 = ((bf16[128,16,128]{2,0,1:T(8,128)(2,1)}), bf16[128,16,128]{2,0,1:T(8,128)(2,1)S(1)}, u32[]{:S(2)}, u32[]{:S(2)}) async-start(bf16[128,16,128]{2,0,1:T(8,128)(2,1)} %bitcast.108), calls=%async_computation.1 | async-start | bytes 1048576 | tf_op jit(solution)/shard_map/all_to_all | solution.py:1205
  723.7 25.6 %copy-start.21 = (bf16[2048,512]{1,0:T(8,128)(2,1)S(1)}, bf16[2048,512]{1,0:T(8,128)(2,1)}, u32[]{:S(2)}) copy-start(bf16[2048,512]{1,0:T(8,128)(2,1)} %attention_backward.1) | copy-start | bytes 6291460
  752.3 36.4 %collective-permute-start.5 = (bf16[256,256]{1,0:T(8,128)(2,1)}, bf16[256,256]{1,0:T(8,128)(2,1)}, u32[]{:S(2)}, u32[]{:S(2)}) collective-permute-start(bf16[256,256]{1,0:T(8,128)(2,1)} %constant_dynamic-slice_fusion.4), channel_id=1, source_target_pairs={{0,1},{1,0},{2,3},{3,2},{4,5},{5,4},{6,7},{7,6},{8,9},{9,8},{10,11... | collective-permute-start | bytes 393224 | tf_op jit(solution)/shard_map/ppermute | solution.py:1033
  754.7 54.3 %all-to-all-start.2 = ((bf16[16,128,512]{1,2,0:T(8,128)(2,1)}), bf16[16,128,512]{1,2,0:T(8,128)(2,1)S(1)}, u32[]{:S(2)}, u32[]{:S(2)}) async-start(bf16[16,128,512]{1,2,0:T(8,128)(2,1)} %copy.106), calls=%async_computation.2 | async-start | bytes 4194304 | tf_op jit(solution)/shard_map/all_to_all | solution.py:1218
  760.1 106.4 %all-gather.26.cloned.1.call-start = ((), (), s32[]{:S(2)}) async-start(), calls=%async_computation.9 | async-start | bytes 4456448 | tf_op jit(solution)/shard_map/all_gather | solution.py:1010
  765.7 8.2 copy-start.23
  766.6 23.0 %collective-permute-start.4 = (bf16[192,1024]{1,0:T(8,128)(2,1)}, bf16[192,1024]{1,0:T(8,128)(2,1)S(1)}, u32[]{:S(2)}, u32[]{:S(2)}) collective-permute-start(bf16[192,1024]{1,0:T(8,128)(2,1)} %constant_dynamic-slice_fusion.5), channel_id=1, source_target_pairs={{0,1},{1,0},{2,3},{3,2},{4,5},{5,4},{6,7},{7,6},{8,9},{9,8},{10,11... | collective-permute-start | bytes 1179656 | tf_op jit(solution)/shard_map/ppermute | solution.py:1033
  790.8 23.7 %copy-start.29 = (bf16[2048,16]{1,0:T(8,128)(2,1)S(1)}, bf16[2048,16]{1,0:T(8,128)(2,1)}, u32[]{:S(2)}) copy-start(bf16[2048,16]{1,0:T(8,128)(2,1)} %copy-done.28) | copy-start | bytes 196612
  814.5 42.1 %collective-permute-start.6 = (bf16[1024,2816]{1,0:T(8,128)(2,1)}, bf16[1024,2816]{1,0:T(8,128)(2,1)}, u32[]{:S(2)}, u32[]{:S(2)}) collective-permute-start(bf16[1024,2816]{1,0:T(8,128)(2,1)} %constant_dynamic-slice_fusion.3), channel_id=1, source_target_pairs={{0,1},{1,0},{2,3},{3,2},{4,5},{5,4},{6,7},{7,6},{8,9},{9,8},{10,11... | collective-permute-start | bytes 17301512 | tf_op jit(solution)/shard_map/ppermute | solution.py:1033
  819.2 170.5 %collective-permute-start.10 = (bf16[1024,16]{0,1:T(8,128)(2,1)S(1)}, bf16[1024,16]{0,1:T(8,128)(2,1)}, u32[]{:S(2)}, u32[]{:S(2)}) collective-permute-start(bf16[1024,16]{0,1:T(8,128)(2,1)S(1)} %constant_dynamic-slice_fusion), channel_id=1, source_target_pairs={{0,1},{1,0},{2,3},{3,2},{4,5},{5,4},{6,7},{7,6},{8,9},{9,8},{10,11... | collective-permute-start | bytes 98312 | tf_op jit(solution)/shard_map/ppermute | solution.py:1033
  819.7 10.9 %slice-start = ((s8[5767168]{0:T(1024)(128)(4,1)}), s8[4194304]{0:T(1024)(128)(4,1)S(1)}, s32[]{:S(2)}) async-start(s8[5767168]{0:T(1024)(128)(4,1)} %bitcast.132), calls=%async_computation.12 | async-start | bytes 8388608
  823.1 7.5 slice-start.1
  832.4 18.8 %collective-permute-start.7 = (bf16[704,2048]{1,0:T(8,128)(2,1)}, bf16[704,2048]{1,0:T(8,128)(2,1)}, u32[]{:S(2)}, u32[]{:S(2)}) collective-permute-start(bf16[704,2048]{1,0:T(8,128)(2,1)} %constant_dynamic-slice_fusion.2), channel_id=1, source_target_pairs={{0,1},{1,0},{2,3},{3,2},{4,5},{5,4},{6,7},{7,6},{8,9},{9,8},{10,11... | collective-permute-start | bytes 8650760 | tf_op jit(solution)/shard_map/ppermute | solution.py:1033
  839.6 11.6 %slice-start.2 = ((s8[5767168]{0:T(1024)(128)(4,1)}), s8[4194304]{0:T(1024)(128)(4,1)S(1)}, s32[]{:S(2)}) async-start(s8[5767168]{0:T(1024)(128)(4,1)} %bitcast.134), calls=%async_computation.14 | async-start | bytes 8388608
  839.6 9.2 copy-start.17
  839.7 9.2 copy-start.24
  839.7 9.2 copy-start.39
  839.7 11.6 %slice-start.3 = ((s8[5767168]{0:T(1024)(128)(4,1)}), s8[1572864]{0:T(1024)(128)(4,1)S(1)}, s32[]{:S(2)}) async-start(s8[5767168]{0:T(1024)(128)(4,1)} %bitcast.134), calls=%async_computation.15 | async-start | bytes 3145728
  977.9 10.0 copy-start
  977.9 13.2 %copy-start.46 = (f32[128]{0:T(128)S(1)}, f32[128]{0:T(128)}, u32[]{:S(2)}) copy-start(f32[128]{0:T(128)} %copy-done.45) | copy-start | bytes 1540
  977.9 13.8 %copy-start.18 = (bf16[128,2048]{1,0:T(8,128)(2,1)S(1)}, bf16[128,2048]{1,0:T(8,128)(2,1)}, u32[]{:S(2)}) copy-start(bf16[128,2048]{1,0:T(8,128)(2,1)} %refs_0_.1) | copy-start | bytes 1572868
  989.7 37.0 %collective-permute-start.9 = (bf16[1024,576]{0,1:T(8,128)(2,1)}, bf16[1024,576]{0,1:T(8,128)(2,1)}, u32[]{:S(2)}, u32[]{:S(2)}) collective-permute-start(bf16[1024,576]{0,1:T(8,128)(2,1)} %constant_dynamic-slice_fusion.1), channel_id=1, source_target_pairs={{0,1},{1,0},{2,3},{3,2},{4,5},{5,4},{6,7},{7,6},{8,9},{9,8},{10,11... | collective-permute-start | bytes 3538952 | tf_op jit(solution)/shard_map/ppermute | solution.py:1033
  991.1 34.2 %collective-permute-start.8 = (f32[40,128]{1,0:T(8,128)S(1)}, f32[40,128]{1,0:T(8,128)S(1)}, u32[]{:S(2)}, u32[]{:S(2)}) collective-permute-start(f32[40,128]{1,0:T(8,128)S(1)} %reduce_sum.183), channel_id=1, source_target_pairs={{0,1},{1,0},{2,3},{3,2},{4,5},{5,4},{6,7},{7,6},{8,9},{9,8},{10,11... | collective-permute-start | bytes 61448 | tf_op jit(solution)/shard_map/ppermute | solution.py:1033
  1020.8 5.8 copy-start.27
  (29 other events, 73.5 us)
Sparse Core Ops, SparseCore 0:
  12.2 14.7 all-gather.13
  30.3 137.7 all-gather.15
  169.6 18.0 all-gather.17
  189.7 11.7 all-gather.19
  202.9 17.1 all-gather.29
  221.5 25.0 all-gather.27
  248.1 14.8 all-gather.23
  264.5 26.0 all-gather.21
  767.0 93.6 all-gather.25
